TPU v7x, 128 devices: a whole 4x4x4 slice. The times are simulated.
128 devices in a mesh: tok: 16 (over y, x_lo, core), mdl: 8 (over x_hi, z).
Axes of the slice: x: 4 (x_hi: 2, x_lo: 2; x = x_hi * 2 + x_lo), y: 4, z: 4, core: 2. Of those that a mesh axis runs over, the one named last changes fastest.
Arguments:
- tokens: bfloat16 [12288, 2048], P('tok', 'mdl'), may hold values from -6 to 6
- segments: int32 [16, 768], P('tok'), may hold values from 0 to 5, never falling along the last dimension, each value on 1 to 576 neighbouring positions
- gain_attn: bfloat16 [2048], P('tok'), may hold values from 0.5 to 1.5
- w_query: bfloat16 [2048, 2048], P('tok', 'mdl'), may hold values from -2 to 2
- key_weight_matrix: bfloat16 [2048, 1024], P('tok', 'mdl'), may hold values from -2 to 2
- value_weight_matrix: bfloat16 [2048, 1024], P('tok', 'mdl'), may hold values from -0.125 to 0.125
- w_output: bfloat16 [2048, 2048], P('tok', 'mdl'), may hold values from -0.5 to 0.5
- gain_ffn: bfloat16 [2048], P('tok'), may hold values from 0.5 to 1.5
- w_gate: bfloat16 [2048, 8192], P('tok', 'mdl'), may hold values from -0.125 to 0.125
- w_up: bfloat16 [2048, 8192], P('tok', 'mdl'), may hold values from -0.125 to 0.125
- w_down: bfloat16 [2048, 8192], P('tok', 'mdl'), may hold values from -0.09375 to 0.09375
- cotangent: bfloat16 [12288, 2048], P('tok', 'mdl'), may hold values from -6 to 6
Outputs:
- output: bfloat16 [12288, 2048], P('tok', 'mdl')
- grad_input: float32 [12288, 2048], P('tok', 'mdl')
- grad_gain_attn: float32 [2048], P('tok')
- grad_w_query: float32 [2048, 2048], P('tok', 'mdl')
- grad_w_key: float32 [2048, 1024], P('tok', 'mdl')
- grad_w_value: float32 [2048, 1024], P('tok', 'mdl')
- grad_w_output: float32 [2048, 2048], P('tok', 'mdl')
- grad_gain_ffn: float32 [2048], P('tok')
- grad_w_gate: float32 [2048, 8192], P('tok', 'mdl')
- grad_w_up: float32 [2048, 8192], P('tok', 'mdl')
- grad_w_down: float32 [2048, 8192], P('tok', 'mdl')
- clipped_query: bfloat16 [2048, 2048], P('tok', 'mdl')
- clipped_key: bfloat16 [2048, 1024], P('tok', 'mdl')
Inputs may be any that keep to these rules, and one draw needn't show every extreme that they name: `segments`: segment numbers never fall along a sequence; each of the 6 documents of a sequence has 1 to 576 tokens, and one has exactly that many.
All inputs are finite; a program needn't handle non-finite values.
Results may differ from a plain program's by a relative error of at most 0.025.
Values may be sent and summed in bfloat16 or wider, within the bound.
No kernel may reach another device: no remote copies, remote signals or barrier semaphores. Data moves between devices by JAX's collectives and lax.ppermute only.
A program may use at most 192 MiB of HBM per device.

v0:
```python
import math

import jax
import jax.numpy as jnp
from jax import lax
from jax.sharding import Mesh
from jax.sharding import PartitionSpec as P

QUERY_HEADS = 8
KEY_VALUE_HEADS = 4
HEAD_WIDTH = 256
MDL = ("mdl_0", "mdl_1")
TOK = ("tok_0", "tok_1", "tok_2")
TOK_MDL = ("tok_0", "tok_1", "tok_2", "mdl_0", "mdl_1")


norm_epsilon = 1e-06
rope_base = 1000042.0
logit_ceiling = 4.0
masked_value = -1e30
peak_floor_epsilon = 1e-06
contract_last = (((1,), (1,)), ((), ()))
contract_first = (((0,), (0,)), ((), ()))


def in_one_piece(arrays, axis, dim, along):
    columns = [a.reshape(*a.shape[:along], -1) for a in arrays]
    both = jnp.concatenate(columns, axis=along)
    whole, at, done = (lax.all_gather(both, axis, axis=dim, tiled=True), 0, [])
    for a, column in zip(arrays, columns):
        piece = whole[..., at : at + column.shape[along]]
        done.append(piece.reshape(*piece.shape[:along], *a.shape[along:]))
        at += column.shape[along]
    return tuple(done)


def from_partner(value, axis, apart):
    mask = 2**apart
    pairs = [(source, source ^ mask) for source in range(lax.axis_size(axis))]
    return lax.ppermute(value, axis, pairs)


def one_axis_at_a_time(value, axes):
    for axis in axes:
        value = lax.pmax(value, axis)
    return value


def in_one_piece_2(arrays, axis, dim, along):
    columns = [a.reshape(*a.shape[:along], -1) for a in arrays]
    both = jnp.concatenate(columns, axis=along)
    whole, at, done = (lax.psum_scatter(both, axis, scatter_dimension=dim, tiled=True), 0, [])
    for a, column in zip(arrays, columns):
        piece = whole[..., at : at + column.shape[along]]
        done.append(piece.reshape(*piece.shape[:along], *a.shape[along:]))
        at += column.shape[along]
    return tuple(done)


def rope_tables(segment_row, head_size):
    token_length = segment_row.shape[0]
    earlier = jnp.sum((segment_row[None, :] < segment_row[:, None]).astype(jnp.int32), axis=1)
    places = jnp.arange(token_length, dtype=jnp.int32) - earlier
    half_size = head_size // 2
    inverse = jnp.exp(
        jnp.arange(half_size, dtype=jnp.float32) * (-2.0 * math.log(rope_base) / head_size)
    )
    angles = places.astype(jnp.float32)[:, None] * inverse[None, :]
    return (jnp.cos(angles), jnp.sin(angles))


def apply_rotary_heads(values, cosine_lookup, sine_lookup, turn_sign):
    half_size = values.shape[-1] // 2
    shape_tail = (cosine_lookup.shape[0],) + (1,) * (values.ndim - 2) + (half_size,)
    cos_part = cosine_lookup.reshape(shape_tail)
    sin_part = sine_lookup.reshape(shape_tail) * turn_sign
    first_half = values[..., :half_size]
    second_half = values[..., half_size:]
    return jnp.concatenate(
        [
            first_half * cos_part - second_half * sin_part,
            second_half * cos_part + first_half * sin_part,
        ],
        axis=-1,
    )


def allowed_pairs(segment_row):
    index_row = jnp.arange(segment_row.shape[0], dtype=jnp.int32)
    return (segment_row[:, None] == segment_row[None, :]) & (
        index_row[:, None] >= index_row[None, :]
    )


def norm_back(upstream, inputs, factor, gain_full):
    scaled = upstream * gain_full
    return factor * scaled - inputs * factor**3 * jnp.mean(scaled * inputs, axis=1, keepdims=True)


def column_scales(scale_table, first_column, count_columns, head_size):
    head_of = (first_column + jnp.arange(count_columns, dtype=jnp.int32)) // head_size
    table_index = jnp.arange(scale_table.shape[0], dtype=jnp.int32)
    return jnp.sum(
        jnp.where(head_of[:, None] == table_index[None, :], scale_table[None, :], 0.0), axis=1
    )


def on_device(
    tokens,
    segments,
    gain_attn,
    w_query,
    key_weight_matrix,
    value_weight_matrix,
    w_output,
    gain_ffn,
    w_gate,
    w_up,
    w_down,
    cotangent,
):
    model_index = lax.axis_index(MDL)
    segment_row = segments[0]
    token_length = segment_row.shape[0]
    feature_cols = tokens.shape[1]
    first_col = model_index * feature_cols
    inputs = lax.all_gather(tokens, MDL, axis=1, tiled=True).astype(jnp.float32)
    gain_one, query_w, key_w, value_w, output_w, gain_two, gate_w, up_w, down_w = in_one_piece(
        (
            gain_attn,
            w_query,
            key_weight_matrix,
            value_weight_matrix,
            w_output,
            gain_ffn,
            w_gate,
            w_up,
            w_down,
        ),
        TOK,
        0,
        1,
    )
    gain_one = gain_one.astype(jnp.float32)
    gain_two = gain_two.astype(jnp.float32)
    factor_attn = lax.rsqrt(jnp.mean(inputs * inputs, axis=1, keepdims=True) + norm_epsilon)
    normed_attn = (inputs * factor_attn * gain_one).astype(jnp.bfloat16)
    query_unrotated = jnp.dot(normed_attn, query_w, preferred_element_type=jnp.float32)
    key_unrotated = jnp.dot(normed_attn, key_w, preferred_element_type=jnp.float32)
    value_reduced = jnp.dot(normed_attn, value_w, preferred_element_type=jnp.float32).astype(
        jnp.bfloat16
    )
    own_kv = key_unrotated.shape[1]
    shared = own_kv < HEAD_WIDTH
    lower_half = model_index % 2 == 0
    other_key, other_value = from_partner(
        (key_unrotated, value_reduced.astype(jnp.float32)), MDL, 0
    )
    other_value = other_value.astype(jnp.bfloat16)
    key_full = jnp.where(
        lower_half,
        jnp.concatenate([key_unrotated, other_key], 1),
        jnp.concatenate([other_key, key_unrotated], 1),
    )
    value_full = jnp.where(
        lower_half,
        jnp.concatenate([value_reduced, other_value], 1),
        jnp.concatenate([other_value, value_reduced], 1),
    )
    heads_here = query_w.shape[1] // HEAD_WIDTH
    kv_heads = key_full.shape[1] // HEAD_WIDTH
    group_here = heads_here // kv_heads
    cosine_lookup, sine_lookup = rope_tables(segment_row, HEAD_WIDTH)
    query_rotated = apply_rotary_heads(
        query_unrotated.reshape(token_length, kv_heads, group_here, HEAD_WIDTH),
        cosine_lookup,
        sine_lookup,
        1.0,
    ).astype(jnp.bfloat16)
    key_rotated = apply_rotary_heads(
        key_full.reshape(token_length, kv_heads, HEAD_WIDTH), cosine_lookup, sine_lookup, 1.0
    ).astype(jnp.bfloat16)
    value_head_rows = value_full.reshape(token_length, kv_heads, HEAD_WIDTH)
    allowed = allowed_pairs(segment_row)
    head_scale = HEAD_WIDTH ** (-0.5)
    scores = (
        jnp.einsum("qjgd,kjd->jgqk", query_rotated, key_rotated, preferred_element_type=jnp.float32)
        * head_scale
    )
    masked = jnp.where(allowed, scores, masked_value)
    row_top = jnp.max(masked, axis=-1, keepdims=True)
    log_total = row_top + jnp.log(jnp.sum(jnp.exp(masked - row_top), axis=-1, keepdims=True))
    probs_low = jnp.exp(masked - log_total).astype(jnp.bfloat16)
    attended = jnp.einsum(
        "jgqk,kjd->qjgd", probs_low, value_head_rows, preferred_element_type=jnp.float32
    )
    attended = attended.reshape(token_length, heads_here * HEAD_WIDTH).astype(jnp.bfloat16)
    local_peaks = jnp.max(jnp.where(allowed, jnp.abs(scores), 0.0), axis=(2, 3)).reshape(heads_here)
    peak_start = jnp.zeros((QUERY_HEADS,), jnp.float32)
    head_logit_peaks = one_axis_at_a_time(
        lax.dynamic_update_slice(peak_start, local_peaks, (model_index * heads_here,)), TOK_MDL
    )
    attn_part = lax.dot_general(
        attended, output_w, contract_last, preferred_element_type=jnp.float32
    )
    attn_out = lax.psum(attn_part, MDL)
    hidden_res = inputs + attn_out
    factor_ffn = lax.rsqrt(jnp.mean(hidden_res * hidden_res, axis=1, keepdims=True) + norm_epsilon)
    normed_ffn = (hidden_res * factor_ffn * gain_two).astype(jnp.bfloat16)
    hidden_share = lax.dynamic_slice_in_dim(hidden_res, first_col, feature_cols, 1)
    gate_pre = jnp.dot(normed_ffn, gate_w, preferred_element_type=jnp.float32)
    up_pre = jnp.dot(normed_ffn, up_w, preferred_element_type=jnp.float32)
    gate_sig = jax.nn.sigmoid(gate_pre)
    gate_act = gate_pre * gate_sig
    hidden_low = (gate_act * up_pre).astype(jnp.bfloat16)
    ffn_part = lax.dot_general(
        hidden_low, down_w, contract_last, preferred_element_type=jnp.float32
    )
    ffn_share = lax.psum_scatter(
        ffn_part.astype(jnp.bfloat16), MDL, scatter_dimension=1, tiled=True
    ).astype(jnp.float32)
    result = (hidden_share + ffn_share).astype(jnp.bfloat16)
    upstream_low = lax.all_gather(cotangent, MDL, axis=1, tiled=True)
    grad_hidden = jnp.dot(upstream_low, down_w, preferred_element_type=jnp.float32)
    grad_down = lax.dot_general(
        upstream_low, hidden_low, contract_first, preferred_element_type=jnp.float32
    )
    grad_gate_pre = (grad_hidden * up_pre * gate_sig * (1.0 + gate_pre * (1.0 - gate_sig))).astype(
        jnp.bfloat16
    )
    grad_up_pre = (grad_hidden * gate_act).astype(jnp.bfloat16)
    grad_gate = lax.dot_general(
        normed_ffn, grad_gate_pre, contract_first, preferred_element_type=jnp.float32
    )
    grad_up = lax.dot_general(
        normed_ffn, grad_up_pre, contract_first, preferred_element_type=jnp.float32
    )
    normed_grad_part = lax.dot_general(
        grad_gate_pre, gate_w, contract_last, preferred_element_type=jnp.float32
    )
    normed_grad_part = normed_grad_part + lax.dot_general(
        grad_up_pre, up_w, contract_last, preferred_element_type=jnp.float32
    )
    normed_grad = lax.psum(normed_grad_part, MDL)
    grad_gain_ffn = jnp.sum(normed_grad * hidden_res * factor_ffn, axis=0)
    grad_res = upstream_low.astype(jnp.float32) + norm_back(
        normed_grad, hidden_res, factor_ffn, gain_two
    )
    grad_res_low = grad_res.astype(jnp.bfloat16)
    grad_output = lax.dot_general(
        grad_res_low, attended, contract_first, preferred_element_type=jnp.float32
    )
    grad_attended = jnp.dot(grad_res_low, output_w, preferred_element_type=jnp.float32).astype(
        jnp.bfloat16
    )
    grad_attended = grad_attended.reshape(token_length, kv_heads, group_here, HEAD_WIDTH)
    scores_again = (
        jnp.einsum("qjgd,kjd->jgqk", query_rotated, key_rotated, preferred_element_type=jnp.float32)
        * head_scale
    )
    probs_again = jnp.exp(jnp.where(allowed, scores_again, masked_value) - log_total)
    probs_again_low = probs_again.astype(jnp.bfloat16)
    grad_probs = jnp.einsum(
        "qjgd,kjd->jgqk", grad_attended, value_head_rows, preferred_element_type=jnp.float32
    )
    grad_value_full = jnp.einsum(
        "jgqk,qjgd->kjd", probs_again_low, grad_attended, preferred_element_type=jnp.float32
    )
    row_delta = jnp.sum(grad_probs * probs_again, axis=-1, keepdims=True)
    grad_scores = (probs_again * (grad_probs - row_delta)).astype(jnp.bfloat16)
    grad_query_rot = (
        jnp.einsum("jgqk,kjd->qjgd", grad_scores, key_rotated, preferred_element_type=jnp.float32)
        * head_scale
    )
    grad_key_rot = (
        jnp.einsum("jgqk,qjgd->kjd", grad_scores, query_rotated, preferred_element_type=jnp.float32)
        * head_scale
    )
    other_gkey, other_gvalue = (
        from_partner(grad_key_rot.astype(jnp.bfloat16), MDL, 0).astype(grad_key_rot.dtype),
        from_partner(grad_value_full.astype(jnp.bfloat16), MDL, 0).astype(grad_value_full.dtype),
    )
    grad_key_rot = grad_key_rot + other_gkey
    grad_value_full = grad_value_full + other_gvalue
    grad_query_pre = (
        apply_rotary_heads(grad_query_rot, cosine_lookup, sine_lookup, -1.0)
        .reshape(token_length, heads_here * HEAD_WIDTH)
        .astype(jnp.bfloat16)
    )
    grad_key_whole = apply_rotary_heads(grad_key_rot, cosine_lookup, sine_lookup, -1.0).reshape(
        token_length, kv_heads * HEAD_WIDTH
    )
    grad_value_whole = grad_value_full.reshape(token_length, kv_heads * HEAD_WIDTH)
    half_start = model_index % 2 * own_kv
    grad_key_whole = lax.dynamic_slice_in_dim(grad_key_whole, half_start, own_kv, 1)
    grad_value_whole = lax.dynamic_slice_in_dim(grad_value_whole, half_start, own_kv, 1)
    grad_key_pre = grad_key_whole.astype(jnp.bfloat16)
    grad_value_pre = grad_value_whole.astype(jnp.bfloat16)
    grad_query = lax.dot_general(
        normed_attn, grad_query_pre, contract_first, preferred_element_type=jnp.float32
    )
    grad_key = lax.dot_general(
        normed_attn, grad_key_pre, contract_first, preferred_element_type=jnp.float32
    )
    grad_value = lax.dot_general(
        normed_attn, grad_value_pre, contract_first, preferred_element_type=jnp.float32
    )
    attn_grad_part = lax.dot_general(
        grad_query_pre, query_w, contract_last, preferred_element_type=jnp.float32
    )
    attn_grad_part = attn_grad_part + lax.dot_general(
        grad_key_pre, key_w, contract_last, preferred_element_type=jnp.float32
    )
    attn_grad_part = attn_grad_part + lax.dot_general(
        grad_value_pre, value_w, contract_last, preferred_element_type=jnp.float32
    )
    attn_grad = lax.psum(attn_grad_part.astype(jnp.bfloat16), MDL).astype(jnp.float32)
    grad_gain_attn = jnp.sum(attn_grad * inputs * factor_attn, axis=0)
    grad_inputs = grad_res + norm_back(attn_grad, inputs, factor_attn, gain_one)
    grad_share = lax.dynamic_slice_in_dim(grad_inputs, first_col, feature_cols, 1)
    summed = tuple(
        (
            part.astype(jnp.float32)
            for part in in_one_piece_2(
                (
                    grad_gain_attn.astype(jnp.bfloat16),
                    grad_query.astype(jnp.bfloat16),
                    grad_key.astype(jnp.bfloat16),
                    grad_value.astype(jnp.bfloat16),
                    grad_output.astype(jnp.bfloat16),
                    grad_gain_ffn.astype(jnp.bfloat16),
                    grad_gate.astype(jnp.bfloat16),
                    grad_up.astype(jnp.bfloat16),
                    grad_down.astype(jnp.bfloat16),
                ),
                TOK,
                0,
                1,
            )
        )
    )
    scale_query = jnp.sqrt(logit_ceiling / (head_logit_peaks + peak_floor_epsilon))
    key_clip_scale = jnp.sqrt(
        logit_ceiling
        / (
            jnp.max(
                head_logit_peaks.reshape(KEY_VALUE_HEADS, QUERY_HEADS // KEY_VALUE_HEADS), axis=1
            )
            + peak_floor_epsilon
        )
    )
    query_cols = w_query.shape[1]
    key_cols = key_weight_matrix.shape[1]
    query_factors = column_scales(scale_query, model_index * query_cols, query_cols, HEAD_WIDTH)
    key_factors = column_scales(key_clip_scale, model_index * key_cols, key_cols, HEAD_WIDTH)
    clipped_query = (w_query.astype(jnp.float32) * query_factors[None, :]).astype(jnp.bfloat16)
    clipped_key = (key_weight_matrix.astype(jnp.float32) * key_factors[None, :]).astype(
        jnp.bfloat16
    )
    return (
        result,
        grad_share,
        summed[0],
        summed[1],
        summed[2],
        summed[3],
        summed[4],
        summed[5],
        summed[6],
        summed[7],
        summed[8],
        clipped_query,
        clipped_key,
    )


def solution(mesh):
    torus = Mesh(mesh.devices.reshape(4, 2, 2, 2, 4), ("tok_0", "tok_1", "tok_2", "mdl_0", "mdl_1"))
    placed = (
        P(TOK, MDL),
        P(TOK, None),
        P(TOK),
        P(TOK, MDL),
        P(TOK, MDL),
        P(TOK, MDL),
        P(TOK, MDL),
        P(TOK),
        P(TOK, MDL),
        P(TOK, MDL),
        P(TOK, MDL),
        P(TOK, MDL),
    )
    return jax.shard_map(
        on_device,
        mesh=torus,
        in_specs=placed,
        out_specs=(
            P(TOK, MDL),
            P(TOK, MDL),
            P(TOK),
            P(TOK, MDL),
            P(TOK, MDL),
            P(TOK, MDL),
            P(TOK, MDL),
            P(TOK),
            P(TOK, MDL),
            P(TOK, MDL),
            P(TOK, MDL),
            P(TOK, MDL),
            P(TOK, MDL),
        ),
        check_vma=False,
    )
```

profile of v0, /device:TPU:1, one launch (start us, length us, event | category | flops | bytes accessed | tf_op | source)
XLA Modules:
  0.0 1015.6 jit_solution(2704055574395189015)
XLA Ops:
  9.5 2.7 concatenate.73
  13.5 63.6 %all-gather.4.cloned.1.call-done = bf16[768,2048]{1,0:T(8,128)(2,1)} async-done(((bf16[768,256]{1,0:T(8,128)(2,1)}), bf16[768,2048]{1,0:T(8,128)(2,1)}) %all-gather.4.cloned.1.call-update) | async-done | bytes 3145744 | tf_op jit(solution)/shard_map/all_gather | solution.py:127
  77.1 2.7 fusion
  80.4 86.2 %all-gather.6.cloned.1.call-done = bf16[2048,3842]{1,0:T(8,128)(2,1)} async-done(((bf16[128,3842]{1,0:T(8,128)(2,1)}), bf16[2048,3842]{1,0:T(8,128)(2,1)}) %all-gather.6.cloned.1.call-update) | async-done | bytes 15736848 | tf_op jit(solution)/shard_map/all_gather | solution.py:29
  166.6 1.8 convert_reduce_fusion.1
  169.2 3.3 convolution_convert_fusion.7
  172.5 1.4 collective-permute-start
  173.8 2.5 fusion.75
  176.8 2.9 convolution_bitcast_fusion.1
  179.7 1.7 fusion.101
  181.4 7.9 collective-permute-done.1
  189.3 2.3 fusion.103
  192.3 1.3 fusion.30
  194.2 0.9 fusion.44
  195.8 5.5 fusion.48
  201.6 32.2 %all-gather.8.cloned.1.call-done = bf16[768,2048]{1,0:T(8,128)(2,1)} async-done(((bf16[768,256]{1,0:T(8,128)(2,1)}), bf16[768,2048]{1,0:T(8,128)(2,1)}) %all-gather.8.cloned.1.call-update) | async-done | bytes 3145744 | tf_op jit(solution)/shard_map/all_gather | solution.py:223
  233.8 8.4 fusion.6
  242.2 138.8 %all-reduce.4.cloned.1.call-done = f32[768,2048]{1,0:T(8,128)} async-done(((f32[768,2048]{1,0:T(8,128)}), f32[768,2048]{1,0:T(8,128)}) %all-reduce.4.cloned.1.call-update) | async-done | bytes 6291472 | tf_op jit(solution)/shard_map/psum | solution.py:206
  381.0 3.7 multiply_reduce_fusion.2
  385.9 1.5 copy-done
  387.4 8.7 fusion.16
  396.1 9.7 fusion.26
  405.9 7.4 fusion.10
  413.3 7.4 fusion.18
  420.8 143.9 %all-reduce.6.cloned.1.call-done = f32[768,2048]{1,0:T(8,128)} async-done(((f32[768,2048]{1,0:T(8,128)}), f32[768,2048]{1,0:T(8,128)}) %all-reduce.6.cloned.1.call-update) | async-done | bytes 6291472 | tf_op jit(solution)/shard_map/psum | solution.py:244
  564.8 6.2 multiply_reduce_fusion
  571.2 0.9 copy-done.10
  572.1 3.9 subtract_add_fusion
  576.1 3.9 fusion.41
  581.6 1.0 fusion.31
  584.1 1.5 collective-permute-start.2
  586.1 1.7 fusion.81
  587.8 12.1 %collective-permute-done.2 = bf16[768,1,256]{0,2,1:T(8,128)(2,1)S(1)} collective-permute-done((bf16[768,1,256]{0,2,1:T(8,128)(2,1)S(1)}, bf16[768,1,256]{0,2,1:T(8,128)(2,1)S(1)}, u32[]{:S(2)}, u32[]{:S(2)}) %collective-permute-start.2) | collective-permute-done | bytes 393248 | tf_op jit(solution)/shard_map/ppermute | solution.py:40
  600.0 1.7 fusion.84
  601.8 2.3 fusion.77
  604.1 2.4 fusion.73
  606.5 4.8 add_convert_fusion
  611.3 8.1 fusion.21
  619.7 7.9 convolution_convert_fusion.1
  627.7 5.3 convolution_convert_fusion
  633.0 5.1 convert_bitcast_fusion
  638.7 2.0 convolution_convert_fusion.3
  640.7 2.0 convolution_convert_fusion.2
  642.7 1.5 convolution_convert_fusion.5
  644.2 1.4 convolution_convert_fusion.4
  645.6 59.8 %all-reduce.8.cloned.1.call-done = bf16[768,2048]{1,0:T(8,128)(2,1)} async-done(((bf16[768,2048]{1,0:T(8,128)(2,1)}), bf16[768,2048]{1,0:T(8,128)(2,1)}) %all-reduce.8.cloned.1.call-update) | async-done | bytes 3145744 | tf_op jit(solution)/shard_map/psum | solution.py:317
  705.3 5.3 fusion.5
  710.6 87.1 %concatenate.88 = bf16[2048,3842]{0,1:T(8,128)(2,1)} concatenate(bf16[2048,1]{0,1:T(2,128)(2,1)S(1)} %convert_element_type.272, bf16[2048,256]{0,1:T(8,128)(2,1)} %convolution_convert_fusion.3, bf16[2048,128]{0,1:T(8,128)(2,1)} %convolution_convert_fusion.5, bf16[2048,128]{0,1:T(8,128)(2,1)} %convolution_convert_fusion.4, bf16[2048,256]{0,1:T(8,128)(2,1)} %convolution_convert_fusion.2, ...), dimensions={1} | concatenate | bytes 31473664 | tf_op jit(solution)/shard_map/concatenate | solution.py:51
  797.8 20.8 %copy.66 = bf16[2048,3842]{1,0:T(8,128)(2,1)} copy(bf16[2048,3842]{0,1:T(8,128)(2,1)} %concatenate.88) | data formatting | bytes 31473664
  819.4 8.7 pmax.35
  828.1 3.8 pmax.36
  831.9 10.0 pmax.37
  841.9 5.9 pmax.38
  847.8 3.5 convert_element_type.233
  851.3 7.1 pmax.39
  860.1 2.1 add_convert_fusion.1
  862.3 2.9 dynamic-slice_add_fusion
  865.2 131.3 %reduce-scatter.7.cloned.1.call-done = bf16[128,3842]{1,0:T(8,128)(2,1)} async-done(((bf16[2048,3842]{1,0:T(8,128)(2,1)}), bf16[128,3842]{1,0:T(8,128)(2,1)}) %reduce-scatter.7.cloned.1.call-update) | async-done | bytes 983568
  997.5 1.1 fusion.116
  999.5 1.0 fusion.117
  1003.1 1.5 fusion.114
  1004.8 0.9 copy.62
  1005.9 0.9 copy.63
  1007.0 0.9 copy.64
  (181 shorter events, 21.9 us)
Async XLA Ops:
  7.2 5.9 copy-start.42
  7.2 69.9 %all-gather.4.cloned.1.call-start = ((), (), s32[]{:S(2)}) async-start(), calls=%async_computation.2 | async-start | bytes 3538944 | tf_op jit(solution)/shard_map/all_gather | solution.py:127
  7.9 158.7 %all-gather.6.cloned.1.call-start = ((), (), s32[]{:S(2)}) async-start(), calls=%async_computation.3 | async-start | bytes 17268736 | tf_op jit(solution)/shard_map/all_gather | solution.py:29
  12.2 221.5 %all-gather.8.cloned.1.call-start = ((), (), s32[]{:S(2)}) async-start(), calls=%async_computation.6 | async-start | bytes 3538944 | tf_op jit(solution)/shard_map/all_gather | solution.py:223
  13.0 368.0 %all-reduce.4.cloned.1.call-start = ((), (), s32[]{:S(2)}) async-start(), calls=%async_computation.4 | async-start | bytes 12582912 | tf_op jit(solution)/shard_map/psum | solution.py:206
  13.1 166.6 %copy-start.40 = (f32[128]{0:T(128)}, f32[128]{0:T(128)S(1)}, u32[]{:S(2)}) copy-start(f32[128]{0:T(128)S(1)} %multiply_exponential_fusion) | copy-start | bytes 1540
  77.1 91.3 %copy-start.1 = (bf16[768,2048]{1,0:T(8,128)(2,1)S(1)}, bf16[768,2048]{1,0:T(8,128)(2,1)}, u32[]{:S(2)}) copy-start(bf16[768,2048]{1,0:T(8,128)(2,1)} %all-gather.4.cloned.1.call-done) | copy-start | bytes 9437188
  80.4 88.7 %copy-start.30 = (f32[768]{0:T(1024)}, f32[768]{0:T(1024)S(1)}, u32[]{:S(2)}) copy-start(f32[768]{0:T(1024)S(1)} %get-tuple-element.97) | copy-start | bytes 9220
  169.2 7.6 copy-start.2
  172.5 21.1 %copy-start.25 = (bf16[768,128]{0,1:T(8,128)(2,1)}, bf16[768,128]{0,1:T(8,128)(2,1)S(1)}, u32[]{:S(2)}) copy-start(bf16[768,128]{0,1:T(8,128)(2,1)S(1)} %convolution_convert_fusion.7) | copy-start | bytes 589828
  172.5 21.1 %collective-permute-start = (bf16[768,128]{0,1:T(8,128)(2,1)S(1)}, bf16[768,128]{0,1:T(8,128)(2,1)S(1)}, u32[]{:S(2)}, u32[]{:S(2)}) collective-permute-start(bf16[768,128]{0,1:T(8,128)(2,1)S(1)} %convolution_convert_fusion.7), channel_id=1, source_target_pairs={{0,1},{1,0},{2,3},{3,2},{4,5},{5,4},{6,7},{7,6},{8,9},{9,8},{10,11... | collective-permute-start | bytes 589832 | tf_op jit(solution)/shard_map/ppermute | solution.py:40
  176.3 12.9 %collective-permute-start.1 = (f32[768,128]{0,1:T(8,128)S(1)}, f32[768,128]{0,1:T(8,128)S(1)}, u32[]{:S(2)}, u32[]{:S(2)}) collective-permute-start(f32[768,128]{0,1:T(8,128)S(1)} %fusion.75), channel_id=1, source_target_pairs={{0,1},{1,0},{2,3},{3,2},{4,5},{5,4},{6,7},{7,6},{8,9},{9,8},{10,11... | collective-permute-start | bytes 1179656 | tf_op jit(solution)/shard_map/ppermute | solution.py:40
  181.3 10.9 %copy-start.20 = (bf16[768,128]{0,1:T(8,128)(2,1)}, bf16[768,128]{0,1:T(8,128)(2,1)S(1)}, u32[]{:S(2)}) copy-start(bf16[768,128]{0,1:T(8,128)(2,1)S(1)} %get-tuple-element.94) | copy-start | bytes 589828
  181.4 10.9 %copy-start.22 = (bf16[768,128]{0,1:T(8,128)(2,1)}, bf16[768,128]{0,1:T(8,128)(2,1)S(1)}, u32[]{:S(2)}) copy-start(bf16[768,128]{0,1:T(8,128)(2,1)S(1)} %get-tuple-element.95) | copy-start | bytes 589828
  192.3 1.4 copy-start.6
  194.2 0.9 copy-start.43
  201.4 363.4 %all-reduce.6.cloned.1.call-start = ((), (), s32[]{:S(2)}) async-start(), calls=%async_computation.7 | async-start | bytes 12582912 | tf_op jit(solution)/shard_map/psum | solution.py:244
  384.6 2.7 copy-start
  385.3 2.1 copy-start.32
  387.4 8.8 copy-start.8
  387.4 8.8 copy-start.45
  387.4 18.5 %slice-start.2 = ((s8[16252928]{0:T(1024)(128)(4,1)}), s8[3670016]{0:T(1024)(128)(4,1)S(1)}, s32[]{:S(2)}) async-start(s8[16252928]{0:T(1024)(128)(4,1)} %bitcast.135), calls=%async_computation.12 | async-start | bytes 7340032
  387.4 18.5 %slice-start.3 = ((s8[16252928]{0:T(1024)(128)(4,1)}), s8[4194304]{0:T(1024)(128)(4,1)S(1)}, s32[]{:S(2)}) async-start(s8[16252928]{0:T(1024)(128)(4,1)} %bitcast.135), calls=%async_computation.13 | async-start | bytes 8388608
  396.1 9.8 slice-start.4
  396.1 9.8 slice-start.5
  405.9 7.5 copy-start.46
  420.8 284.6 %all-reduce.8.cloned.1.call-start = ((), (), s32[]{:S(2)}) async-start(), calls=%async_computation.8 | async-start | bytes 6291456 | tf_op jit(solution)/shard_map/psum | solution.py:317
  564.8 6.4 copy-start.5
  564.8 7.4 copy-start.10
  564.8 7.4 copy-start.33
  564.8 7.4 copy-start.39
  576.1 4.0 copy-start.4
  576.1 4.4 copy-start.7
  576.1 4.4 copy-start.38
  580.5 1.0 copy-start.26
  580.5 1.1 copy-start.44
  581.3 20.4 %collective-permute-start.3 = (bf16[768,1,256]{0,2,1:T(8,128)(2,1)S(1)}, bf16[768,1,256]{0,2,1:T(8,128)(2,1)S(1)}, u32[]{:S(2)}, u32[]{:S(2)}) collective-permute-start(bf16[768,1,256]{0,2,1:T(8,128)(2,1)S(1)} %get-tuple-element.102), channel_id=1, source_target_pairs={{0,1},{1,0},{2,3},{3,2},{4,5},{5,4},{6,7},{7,6},{8,9},{9,8},{10,11... | collective-permute-start | bytes 1179656 | tf_op jit(solution)/shard_map/ppermute | solution.py:40
  582.6 0.9 copy-start.21
  582.6 1.0 copy-start.23
  583.6 2.5 copy-start.41
  584.1 15.8 %collective-permute-start.2 = (bf16[768,1,256]{0,2,1:T(8,128)(2,1)S(1)}, bf16[768,1,256]{0,2,1:T(8,128)(2,1)S(1)}, u32[]{:S(2)}, u32[]{:S(2)}) collective-permute-start(bf16[768,1,256]{0,2,1:T(8,128)(2,1)S(1)} %get-tuple-element.106), channel_id=1, source_target_pairs={{0,1},{1,0},{2,3},{3,2},{4,5},{5,4},{6,7},{7,6},{8,9},{9,8},{10,11... | collective-permute-start | bytes 1179656 | tf_op jit(solution)/shard_map/ppermute | solution.py:40
  587.8 18.6 %copy-start.16 = (bf16[768,1,1,128]{0,3,2,1:T(8,128)(2,1)}, bf16[768,1,1,128]{0,3,2,1:T(8,128)(2,1)S(1)}, u32[]{:S(2)}) copy-start(bf16[768,1,1,128]{0,3,2,1:T(8,128)(2,1)S(1)} %get-tuple-element.88) | copy-start | bytes 589828
  587.8 18.6 %copy-start.18 = (bf16[768,1,1,128]{0,3,2,1:T(8,128)(2,1)}, bf16[768,1,1,128]{0,3,2,1:T(8,128)(2,1)S(1)}, u32[]{:S(2)}) copy-start(bf16[768,1,1,128]{0,3,2,1:T(8,128)(2,1)S(1)} %get-tuple-element.89) | copy-start | bytes 589828
  601.7 2.4 copy-start.14
  611.3 248.9 %reduce-scatter.5.cloned.1.call-start = ((), (), s32[]{:S(2)}) async-start(), calls=%async_computation.5 | async-start | bytes 3538944 | tf_op jit(solution)/shard_map/reduce_scatter | solution.py:219
  619.4 377.1 %reduce-scatter.7.cloned.1.call-start = ((), (), s32[]{:S(2)}) async-start(), calls=%async_computation.9 | async-start | bytes 17268736
  619.7 8.0 copy-start.9
  619.7 7.9 copy-start.47
  627.6 5.3 copy-start.11
  627.6 5.3 copy-start.48
  627.6 13.0 %slice-start = ((s8[6291456]{0:T(1024)(128)(4,1)}), s8[2097152]{0:T(1024)(128)(4,1)S(1)}, s32[]{:S(2)}) async-start(s8[6291456]{0:T(1024)(128)(4,1)} %bitcast.133), calls=%async_computation.10 | async-start | bytes 4194304
  633.0 5.1 copy-start.36
  633.0 5.7 copy-start.3
  633.0 5.7 copy-start.17
  633.0 5.7 copy-start.19
  633.0 7.7 slice-start.1
  638.1 2.6 copy-start.13
  640.7 2.0 copy-start.15
  642.7 62.6 %copy-start.29 = (f32[2048]{0:T(1024)S(1)}, f32[2048]{0:T(1024)}, u32[]{:S(2)}) copy-start(f32[2048]{0:T(1024)} %copy-done.28) | copy-start | bytes 24580
  642.7 62.6 %copy-start.31 = (f32[768]{0:T(1024)S(1)}, f32[768]{0:T(1024)}, u32[]{:S(2)}) copy-start(f32[768]{0:T(1024)} %copy-done.30) | copy-start | bytes 9220
  645.6 65.1 %copy-start.34 = (bf16[2048,1]{0,1:T(2,128)(2,1)S(1)}, bf16[2048,1]{0,1:T(2,128)(2,1)}, u32[]{:S(2)}) copy-start(bf16[2048,1]{0,1:T(2,128)(2,1)} %convert_element_type.278) | copy-start | bytes 12292
  847.8 11.1 %copy-start.27 = (bf16[128,128]{1,0:T(8,128)(2,1)S(1)}, bf16[128,128]{1,0:T(8,128)(2,1)}, u32[]{:S(2)}) copy-start(bf16[128,128]{1,0:T(8,128)(2,1)} %param.16) | copy-start | bytes 98308
  847.8 11.7 %copy-start.24 = (bf16[128,256]{1,0:T(8,128)(2,1)S(1)}, bf16[128,256]{1,0:T(8,128)(2,1)}, u32[]{:S(2)}) copy-start(bf16[128,256]{1,0:T(8,128)(2,1)} %param.15) | copy-start | bytes 196612
  847.8 14.5 %copy-start.35 = (f32[768]{0:T(1024)S(1)}, f32[768]{0:T(1024)}, u32[]{:S(2)}) copy-start(f32[768]{0:T(1024)} %get-tuple-element.96) | copy-start | bytes 9220
  (3 other events, 2.2 us)
Sparse Core Ops, SparseCore 0:
  10.2 66.8 all-gather.3
  78.8 87.7 all-gather.5
  168.8 64.9 all-gather.7
  236.2 144.7 all-reduce.3
  420.9 143.8 all-reduce.5
  611.4 93.9 all-reduce.7
  709.2 80.6 reduce-scatter.4
  818.7 177.7 reduce-scatter.6
where the time goes:
time: 1020 us
  waiting for transfers between devices  677 us (66%)
  local copies, waits for them, and re-layouts  130 us (13%)
  matrix products  107 us (10%)
  other arithmetic  46.8 us (5%)
  blocking collectives  35.6 us (3%)
  between operations  15.2 us (1%)
    psum x1, waiting for transfers between devices, on_device(): normed_grad = lax.psum(normed_grad_part, MDL)  144 us
    psum x1, waiting for transfers between devices, on_device(): attn_out = lax.psum(attn_part, MDL)  139 us
    unnamed x9, waiting for transfers between devices  133 us
    concatenate x1, local copies, waits for them, and re-layouts, in_one_piece_2(): both = jnp.concatenate(columns, axis=along)  87.1 us
    all_gather x1, waiting for transfers between devices, in_one_piece(): whole, at, done = (lax.all_gather(both, axis, axis=dim, tiled=True), 0, [])  86.2 us
    all_gather x1, waiting for transfers between devices, on_device(): inputs = lax.all_gather(tokens, MDL, axis=1, tiled=True).astype(jnp.float32)  63.6 us
    psum x1, waiting for transfers between devices, on_device(): lax.psum(attn_grad_part.astype(jnp.bfloat16), MDL).astype(jnp.float32)  59.8 us
    pmax x5, blocking collectives, one_axis_at_a_time(): value = lax.pmax(value, axis)  35.6 us
  transfers between devices with their start and end apart: 12, of which 9 were waited for; matrix products, arithmetic and copies ran while one was open for 20% of the time, Pallas kernels for 0%

commit v1 on v0

v1 whole, which is shorter than its diff:
```python
import functools
import math

import jax
import jax.numpy as jnp
from jax import lax
from jax.experimental import pallas as pl
from jax.experimental.pallas import tpu as pltpu
from jax.sharding import Mesh
from jax.sharding import PartitionSpec as P

QUERY_HEADS = 8
HEAD = 256
WIDTH = 2048
LEN = 768
OWN = 96
FF = 1024
Y, XLO, CORE, XHI, Z = "tok_0", "tok_1", "tok_2", "mdl_0", "mdl_1"
TOK = (Y, XLO, CORE)
MDL = (XHI, Z)

norm_epsilon = 1e-06
rope_base = 1000042.0
logit_ceiling = 4.0
masked_value = -1e30
peak_floor_epsilon = 1e-06
SCALE = HEAD ** (-0.5)
nt = (((1,), (1,)), ((), ()))
tn = (((0,), (0,)), ((), ()))
f32 = jnp.float32
bf16 = jnp.bfloat16


def dot(a, b, dims=(((1,), (0,)), ((), ()))):
    return lax.dot_general(a, b, dims, preferred_element_type=f32)


def swap(a):
    got = lax.ppermute(a, (CORE, XHI), [(1, 2), (2, 1)])
    return jnp.where(lax.axis_index(CORE) == lax.axis_index(XHI), a, got)


def other_core(a):
    return lax.ppermute(a, CORE, [(0, 1), (1, 0)])


def shift(a, axis, by):
    return lax.ppermute(a, axis, [(i, (i + by) % 4) for i in range(4)])


def z_other(a, mask):
    return lax.ppermute(a, Z, [(i, i ^ mask) for i in range(4)])


def y_other(a, mask):
    return lax.ppermute(a, Y, [(i, i ^ mask) for i in range(4)])


def kv_partner(a):
    return lax.ppermute(a, Z, [(0, 1), (1, 0), (2, 3), (3, 2)])


def plane_pairs(flip_lo, flip_core):
    pairs = []
    for lo in range(2):
        for core in range(2):
            for hi in range(2):
                pairs.append((lo * 4 + core * 2 + hi, (lo ^ flip_lo) * 4 + hi * 2 + (core ^ flip_core)))
    return pairs


def x_pairs(flip_lo, flip_core, back):
    pairs = plane_pairs(flip_lo, flip_core)
    return [(there, here) if back else (here, there) for here, there in pairs if here != there]


def x_in(a, flip_lo, flip_core):
    return lax.ppermute(a, (XLO, CORE, XHI), x_pairs(flip_lo, flip_core, False))


def x_out(a, flip_lo, flip_core):
    return lax.ppermute(a, (XLO, CORE, XHI), x_pairs(flip_lo, flip_core, True))


def own_or(got, own):
    return jnp.where(lax.axis_index(CORE) == lax.axis_index(XHI), own, got)


FLIPS = ((0, 0), (0, 1), (1, 0), (1, 1))


def from_y(a):
    return [a, shift(a, Y, -1), shift(a, Y, 2), shift(a, Y, 1)]


def from_z(a):
    return [a, shift(a, Z, -1), shift(a, Z, 2), shift(a, Z, 1)]


def x_ring(a, mask):
    return lax.ppermute(a, (XLO, XHI), [(i, i ^ mask) for i in range(4)])


def total(pieces, cols=slice(None)):
    return sum(piece[:, cols].astype(f32) for piece in pieces)


def team_gather(own):
    return lax.all_gather(own, (CORE, Z), axis=0, tiled=True)


def team_scatter(give, keep):
    both = (keep.astype(f32) + other_core(give).astype(f32)).astype(bf16)
    return lax.psum_scatter(both, Z, scatter_dimension=0, tiled=True).astype(f32)


def after(value, *others):
    return lax.optimization_barrier((value, *others))[0]


def rope_tables(segment_row):
    earlier = jnp.sum((segment_row[None, :] < segment_row[:, None]).astype(jnp.int32), axis=1)
    places = jnp.arange(LEN, dtype=jnp.int32) - earlier
    half = HEAD // 2
    inverse = jnp.exp(jnp.arange(half, dtype=f32) * (-2.0 * math.log(rope_base) / HEAD))
    angles = places.astype(f32)[:, None] * inverse[None, :]
    return jnp.cos(angles), jnp.sin(angles)


def position(r, at):
    return (((r >> 2) - at[0]) & 3) * 4 + (((r >> 1) & 1) ^ at[1]) * 2 + ((r & 1) ^ at[2])


def lanes(index, size):
    return pl.ds(pl.multiple_of(index * size, size), size)


def owner(at, there, dz):
    return (at[3] ^ there) * 4 + ((at[4] + dz) & 3)


def kdot(a, b, dims=(((1,), (0,)), ((), ()))):
    return lax.dot_general(a, b, dims, preferred_element_type=f32)


def in_vmem(n):
    return [pl.BlockSpec(memory_space=pltpu.VMEM)] * n


def call(body, name, inputs, outs, scratch, flops, megabytes=56, anywhere=0):
    moved = sum(v.size * v.dtype.itemsize for v in inputs[1:])
    moved += sum(math.prod(s) * jnp.dtype(d).itemsize for s, d in outs)
    specs = [pl.BlockSpec(memory_space=pltpu.SMEM)] + in_vmem(len(inputs) - 1 - anywhere)
    specs += [pl.BlockSpec(memory_space=pl.ANY)] * anywhere
    return list(pl.pallas_call(
        body,
        name=name,
        out_shape=[jax.ShapeDtypeStruct(s, d) for s, d in outs],
        in_specs=specs,
        out_specs=in_vmem(len(outs)),
        scratch_shapes=scratch,
        cost_estimate=pl.CostEstimate(flops=int(flops), bytes_accessed=int(moved), transcendentals=0),
        compiler_params=pltpu.CompilerParams(vmem_limit_bytes=megabytes * 2**20),
    )(*inputs))


def turn(values, cosine, sine):
    first, second = values[:, :128], values[:, 128:]
    return first * cosine - second * sine, second * cosine + first * sine


def attention_weights(a_refs, b_refs, w_qkv, w_o, sem):
    copies = []

    def move(source, to):
        copies.append(pltpu.make_async_copy(source, to, sem.at[len(copies)]))
        copies[-1].start()

    for i in range(4):
        for dy in range(4):
            rows = pl.ds((dy * 4 + i) * 128, 128)
            move(b_refs[i].at[pl.ds(dy * 144, 128), pl.ds(256, 256)], w_o.at[rows])
    for dy in range(4):
        for i in range(4):
            rows = pl.ds((dy * 4 + i) * 128, 128)
            move(b_refs[i].at[pl.ds(dy * 144, 128), pl.ds(0, 256)], w_qkv.at[rows, pl.ds(0, 256)])
            move(a_refs[dy].at[pl.ds(i * 128, 128)], w_qkv.at[rows, pl.ds(256, 512)])
    return copies


def pack_body(at, *refs):
    xs, ys, to_y, to_x, sem = refs[:4], refs[4:8], refs[8], refs[9], refs[10]
    pairs = [(ref.at[pl.ds(0, 128)], to_y.at[pl.ds(128 * i, 128)]) for i, ref in enumerate(xs)]
    pairs += [(ref.at[pl.ds(0, 144)], to_x.at[pl.ds(144 * i, 144)]) for i, ref in enumerate(ys)]
    copies = [pltpu.make_async_copy(a, b, sem.at[i]) for i, (a, b) in enumerate(pairs)]
    for copy in copies:
        copy.start()
    for copy in copies:
        copy.wait()


def riders_body(at, *refs):
    xs, ys = refs[:4], refs[4:8]
    a_wide, b_wide, a_down, b_down, sem = refs[8:]
    copies = []
    for ref, row, wide, down in [(xs, 128, a_wide, a_down), (ys, 144, b_wide, b_down)]:
        for i in range(4):
            for j in range(3):
                source = ref[i].at[pl.ds(row + j * 128, 128)]
                rows = pl.ds(i * 128, 128)
                to = down.at[rows] if j == 2 else wide.at[rows, pl.ds(j * 512, 512)]
                copies.append(pltpu.make_async_copy(source, to, sem.at[len(copies)]))
    for copy in copies:
        copy.start()
    for copy in copies:
        copy.wait()


def allowed_block(i, seg_col, seg_row):
    rows, cols = 256, (i + 1) * 256
    same = seg_col[i * 256 : (i + 1) * 256, :] == seg_row[:, :cols]
    row = i * 256 + lax.broadcasted_iota(jnp.int32, (rows, cols), 0)
    return same & (row >= lax.broadcasted_iota(jnp.int32, (rows, cols), 1))


def forward_body(at, *refs):
    x, cosine, sine, seg_row, seg_col = refs[:5]
    a_refs, b_refs = refs[5:9], refs[9:13]
    a1, r1, x_mine, qr, kr, v, o, lse, peak, gains, give, keep = refs[13:25]
    w_qkv, w_o, gain_rows, sem, gain_sem = refs[25:]
    gain_copies = []
    for dy in range(4):
        for i in range(4):
            source = b_refs[i].at[pl.ds(dy * 144 + 128, 16), pl.ds(0, 128)]
            to = gain_rows.at[:, pl.ds((dy * 4 + i) * 128, 128)]
            gain_copies.append(pltpu.make_async_copy(source, to, gain_sem.at[len(gain_copies)]))
            gain_copies[-1].start()
    copies = attention_weights(a_refs, b_refs, w_qkv, w_o, sem)
    for copy in gain_copies:
        copy.wait()
    gains[...] = gain_rows[...].astype(f32)[:8]
    own = at[3] * 4 + at[4]
    for r in range(16):
        rows = pl.ds(pl.multiple_of((r // 2) * LEN + own * OWN, OWN), OWN)
        x_mine[:, lanes(position(r, at), 128)] = x[rows, (r % 2) * 128 : (r % 2 + 1) * 128]

    def norm(step, carry):
        rows = pl.ds(pl.multiple_of(step * 128, 128), 128)
        total = jnp.zeros((128, 1), f32)
        for m in range(8):
            value = x[pl.ds(pl.multiple_of(m * LEN + step * 128, 128), 128), :].astype(f32)
            total = total + jnp.sum(value * value, axis=1, keepdims=True)
        factor = lax.rsqrt(total / WIDTH + norm_epsilon)
        r1[rows, :] = factor
        for r in range(16):
            at_lanes = lanes(position(r, at), 128)
            from_rows = pl.ds(pl.multiple_of((r // 2) * LEN + step * 128, 128), 128)
            value = x[from_rows, (r % 2) * 128 : (r % 2 + 1) * 128].astype(f32)
            a1[rows, at_lanes] = (value * factor * gains[0:1, at_lanes]).astype(bf16)
        return carry

    lax.fori_loop(0, 6, norm, 0)
    for copy in copies:
        copy.wait()
    for i in range(3):
        rows = slice(i * 256, (i + 1) * 256)
        qk = kdot(a1[rows, :], w_qkv[:, :512])
        cos_i, sin_i = cosine[rows, :], sine[rows, :]
        for ref, at_col in ((qr, 0), (kr, 256)):
            one, two = turn(qk[:, at_col : at_col + 256], cos_i, sin_i)
            ref[rows, :128] = one.astype(bf16)
            ref[rows, 128:] = two.astype(bf16)
        v[rows, :] = kdot(a1[rows, :], w_qkv[:, 512:]).astype(bf16)
    largest = jnp.zeros((1, 1), f32)
    for i in range(3):
        rows, cols = slice(i * 256, (i + 1) * 256), (i + 1) * 256
        allowed = allowed_block(i, seg_col, seg_row)
        scores = kdot(qr[rows, :], kr[:cols, :], nt) * SCALE
        masked = jnp.where(allowed, scores, masked_value)
        size = jnp.where(allowed, jnp.abs(scores), 0.0)
        largest = jnp.maximum(largest, jnp.max(jnp.max(size, axis=1, keepdims=True), axis=0, keepdims=True))
        top = jnp.max(masked, axis=1, keepdims=True)
        log_total = top + jnp.log(jnp.sum(jnp.exp(masked - top), axis=1, keepdims=True))
        lse[rows, :] = log_total
        probs = jnp.exp(masked - log_total).astype(bf16)
        o[rows, :] = kdot(probs, v[:cols, :]).astype(bf16)
    peak[...] = jnp.broadcast_to(largest, (8, 128))
    for ref, c in ((give, 1 - at[3]), (keep, at[3])):
        rows = pl.ds(pl.multiple_of(c * 384, 384), 384)
        for half in range(2):
            cols = slice(half * 1024, (half + 1) * 1024)
            ref[:, cols] = kdot(o[rows, :], w_o[cols, :], nt).astype(bf16)


def reorder_body(at, whole, out):
    for r in range(16):
        rows = slice((r // 2) * LEN, (r // 2 + 1) * LEN)
        out[:, lanes(position(r, at), 128)] = whole[rows, (r % 2) * 128 : (r % 2 + 1) * 128]


def start_either(at, own, got, to, sem):
    mine = at[2] == at[3]

    @pl.when(mine)
    def _():
        pltpu.make_async_copy(own, to, sem).start()

    @pl.when(jnp.logical_not(mine))
    def _():
        pltpu.make_async_copy(got, to, sem).start()

    return pltpu.make_async_copy(got, to, sem)


def rows_a(refs, to_ref, cols, sem, copies):
    for i, ref in enumerate(refs):
        to = to_ref.at[pl.ds(i * 512, 512), cols]
        copies.append(pltpu.make_async_copy(ref, to, sem.at[len(copies)]))
        copies[-1].start()


def rows_b(at, own, refs, to_ref, cols, sem, copies):
    for i, ref in enumerate(refs):
        for j in range(4):
            to = to_ref.at[pl.ds((j * 4 + i) * 128, 128), cols]
            rows = pl.ds(j * 128, 128)
            if i == 0:
                copies.append(start_either(at, own.at[rows], ref.at[rows], to, sem.at[len(copies)]))
            else:
                copies.append(pltpu.make_async_copy(ref.at[rows], to, sem.at[len(copies)]))
                copies[-1].start()


def ffn_body(at, *refs):
    h, gains, dy = refs[:3]
    wide_a, down_a, wide_b, down_b = [refs[3 + 4 * i : 7 + 4 * i] for i in range(4)]
    own_wide, own_down = refs[19:21]
    a2, hid, dgate, dup, h_cols, give, keep = refs[21:28]
    w_gate, w_up, w_down, sem = refs[28:]
    copies = []
    rows_a(wide_a, w_gate, pl.ds(0, FF), sem, copies)
    rows_b(at, own_wide, wide_b, w_up, pl.ds(0, FF), sem, copies)
    rows_a(down_a, w_down, pl.ds(0, 512), sem, copies)
    rows_b(at, own_down, down_b, w_down, pl.ds(512, 512), sem, copies)
    own = at[3] * 4 + at[4]
    for j in range(2):
        h_cols[:, j * 128 : (j + 1) * 128] = h[:, lanes(position(2 * own + j, at), 128)]
    for i in range(6):
        rows = slice(i * 128, (i + 1) * 128)
        value = h[rows, :].astype(f32)
        factor = lax.rsqrt(jnp.mean(value * value, axis=1, keepdims=True) + norm_epsilon)
        a2[rows, :] = (value * factor * gains[1:2, :]).astype(bf16)
    for copy in copies:
        copy.wait()
    for half in range(2):
        rows = slice(half * 384, (half + 1) * 384)
        for j in range(4):
            cols = slice(j * 256, (j + 1) * 256)
            gate = kdot(a2[rows, :], w_gate[:, cols])
            up = kdot(a2[rows, :], w_up[:, cols])
            grad = kdot(dy[rows, :], w_down[:, cols])
            sig = 1.0 / (1.0 + jnp.exp(-gate))
            act = gate * sig
            hid[rows, cols] = (act * up).astype(bf16)
            dgate[rows, cols] = (grad * up * sig * (1.0 + gate * (1.0 - sig))).astype(bf16)
            dup[rows, cols] = (grad * act).astype(bf16)
    for ref, c in ((give, 1 - at[3]), (keep, at[3])):
        rows = pl.ds(pl.multiple_of(c * 384, 384), 384)
        for j in range(4):
            cols = slice(j * 512, (j + 1) * 512)
            ref[:, cols] = (
                kdot(dgate[rows, :], w_gate[cols, :], nt) + kdot(dup[rows, :], w_up[cols, :], nt)
            ).astype(bf16)


def ffn_out_body(at, hid, *refs):
    down_a, down_b, own_down = refs[:4], refs[4:8], refs[8]
    give, keep, w_down, sem = refs[9:]
    copies = []
    rows_a(down_a, w_down, pl.ds(0, 512), sem, copies)
    rows_b(at, own_down, down_b, w_down, pl.ds(512, 512), sem, copies)
    for copy in copies:
        copy.wait()
    for ref, c in ((give, 1 - at[3]), (keep, at[3])):
        for dz in range(4):
            m = c * 4 + dz
            pair = pl.ds(pl.multiple_of((position(2 * m, at) >> 1) * 256, 256), 256)
            value = kdot(hid[...], w_down[pair, :], nt)
            rows = slice(dz * LEN, (dz + 1) * LEN)
            for j in range(2):
                ref[rows, lanes(at[2] ^ j, 128)] = value[:, j * 128 : (j + 1) * 128].astype(bf16)


def weight_gate_body(blocks, at, a2, dgate, *outs):
    for i, out in zip(blocks, outs):
        for j in range(2):
            n = slice(j * 512, (j + 1) * 512)
            out[:, n] = kdot(a2[:, i * 512 : (i + 1) * 512], dgate[:, n], tn).astype(bf16)


def weight_up_body(first, at, a2, dup, *outs):
    for i in range(4):
        cols = slice((i * 4 + first) * 128, (i * 4 + first + 2) * 128)
        for j in range(2):
            n = slice(j * 512, (j + 1) * 512)
            value = kdot(a2[:, cols], dup[:, n], tn).astype(bf16)
            for k in range(2):
                outs[k][i * 128 : (i + 1) * 128, n] = value[k * 128 : (k + 1) * 128]


def weight_rest_body(at, a2, dy, dgate, dup, hid, *outs):
    a_wide, b_wide, a_down, b_down = outs[:2], outs[2:4], outs[4:8], outs[8:]
    for i in range(4):
        cols, rows = slice(i * 512, (i + 1) * 512), slice(i * 128, (i + 1) * 128)
        for j in range(2):
            n = slice(j * 512, (j + 1) * 512)
            value = kdot(a2[:, i * 512 : i * 512 + 256], dup[:, n], tn).astype(bf16)
            for k in range(2):
                b_wide[k][rows, n] = value[k * 128 : (k + 1) * 128]
            if i % 2 == 0:
                a_wide[i // 2][:, n] = kdot(a2[:, cols], dgate[:, n], tn).astype(bf16)
        a_down[i][...] = kdot(dy[:, cols], hid[:, :512], tn).astype(bf16)
        value = kdot(dy[:, cols], hid[:, 512:], tn).astype(bf16)
        for k in range(4):
            b_down[k][rows, :] = value[k * 128 : (k + 1) * 128]


def backward_body(at, *refs):
    db, cosine, sine, seg_row, seg_col, qr, kr, v, lse, a1, gains = refs[:11]
    a_refs, b_refs = refs[11:15], refs[15:19]
    db_cols, dqkv, row_part, gain_part, give, keep = refs[19:25]
    w_qkv, w_o, d_o, dk_sum, dv_sum, sem = refs[25:]
    copies = attention_weights(a_refs, b_refs, w_qkv, w_o, sem)
    own = at[3] * 4 + at[4]
    for j in range(2):
        db_cols[:, j * 128 : (j + 1) * 128] = db[:, lanes(position(2 * own + j, at), 128)]
    for copy in copies:
        copy.wait()
    for i in range(3):
        rows = slice(i * 256, (i + 1) * 256)
        d_o[rows, :] = kdot(db[rows, :], w_o[...]).astype(bf16)
    for i in (2, 1, 0):
        rows, cols = slice(i * 256, (i + 1) * 256), (i + 1) * 256
        allowed = allowed_block(i, seg_col, seg_row)
        scores = kdot(qr[rows, :], kr[:cols, :], nt) * SCALE
        probs = jnp.exp(jnp.where(allowed, scores, masked_value) - lse[rows, :])
        low = probs.astype(bf16)
        dp = kdot(d_o[rows, :], v[:cols, :], nt)
        delta = jnp.sum(dp * probs, axis=1, keepdims=True)
        ds = (probs * (dp - delta)).astype(bf16)
        dq = kdot(ds, kr[:cols, :]) * SCALE
        row_part[rows, :] = jnp.sum(dq * qr[rows, :].astype(f32), axis=1, keepdims=True)
        one, two = turn(dq, cosine[rows, :], -sine[rows, :])
        dqkv[rows, :128] = one.astype(bf16)
        dqkv[rows, 128:256] = two.astype(bf16)
        dk_new = kdot(ds, qr[rows, :], tn)
        dv_new = kdot(low, d_o[rows, :], tn)
        if i == 2:
            dk_sum[...] = dk_new
            dv_sum[...] = dv_new
        else:
            dk_sum[:cols, :] = dk_sum[:cols, :] + dk_new
            dv_sum[:cols, :] = dv_sum[:cols, :] + dv_new
    for i in range(3):
        rows = slice(i * 256, (i + 1) * 256)
        dk = dk_sum[rows, :] * SCALE
        dv_i = dv_sum[rows, :]
        row_part[rows, :] = (
            row_part[rows, :]
            + jnp.sum(dk * kr[rows, :].astype(f32), axis=1, keepdims=True)
            + jnp.sum(dv_i * v[rows, :].astype(f32), axis=1, keepdims=True)
        )
        one, two = turn(dk, cosine[rows, :], -sine[rows, :])
        dqkv[rows, 256:384] = one.astype(bf16)
        dqkv[rows, 384:512] = two.astype(bf16)
        dqkv[rows, 512:] = dv_i.astype(bf16)
    for m, ref in [(j, give) for j in range(4)] + [(j, keep) for j in range(4)]:
        half = 1 - at[3] if ref is give else at[3]
        pair = lanes(position(2 * (half * 4 + m), at) >> 1, 256)
        value = kdot(dqkv[...], w_qkv[pair, :], nt)
        gain_part[:, pair] = jnp.sum(value * a1[:, pair].astype(f32), axis=0, keepdims=True) / gains[0:1, pair]
        rows = slice(m * LEN, (m + 1) * LEN)
        for j in range(2):
            ref[rows, lanes(at[2] ^ j, 128)] = value[:, j * 128 : (j + 1) * 128].astype(bf16)


def attention_weight_body(at, a1, dqkv, db, o, *outs):
    a_outs, b_outs = outs[:4], outs[4:]
    for i in range(4):
        cols, rows = slice(i * 512, (i + 1) * 512), slice(i * 128, (i + 1) * 128)
        a_outs[i][...] = kdot(a1[:, cols], dqkv[:, 256:], tn).astype(bf16)
        for n, left, right in ((slice(0, 256), a1, dqkv.at[:, :256]), (slice(256, 512), db, o)):
            value = kdot(left[:, cols], right[...], tn).astype(bf16)
            for k in range(4):
                b_outs[k][rows, n] = value[k * 128 : (k + 1) * 128]


def ffn_sum_body(at, *refs):
    wide_a, down_a, wide_b, down_b = [refs[4 * i : 4 * i + 4] for i in range(4)]
    own_wide, own_down, out_a, out_b = refs[16:]
    mine = at[2] == at[3]
    for cols, a, b, own in ((slice(0, FF), wide_a, wide_b, own_wide), (slice(FF, 1536), down_a, down_b, own_down)):
        value = a[0][...].astype(f32) + a[1][...].astype(f32) + a[2][...].astype(f32) + a[3][...].astype(f32)
        out_a[:, cols] = value.astype(bf16)
        value = jnp.where(mine, own[...], b[0][...]).astype(f32) + b[1][...].astype(f32)
        value = value + b[2][...].astype(f32) + b[3][...].astype(f32)
        out_b[:, cols] = value.astype(bf16)


def join_body(at, *refs):
    ffn_a, ffn_b, a, b, own, outs = refs[0], refs[1], refs[2:6], refs[6:10], refs[10], refs[11:]
    for i in range(4):
        rows = slice(i * 128, (i + 1) * 128)
        outs[i][:, :1536] = ffn_a[rows, :]
        outs[4 + i][:, :1536] = ffn_b[rows, :]
        value = a[0][rows, :].astype(f32) + a[1][rows, :].astype(f32) + a[2][rows, :].astype(f32)
        outs[i][:, 1536:] = (value + a[3][rows, :].astype(f32)).astype(bf16)
        head = jnp.where(at[2] == at[3], own[rows, :], b[0][rows, :])
        value = head.astype(f32) + b[1][rows, :].astype(f32) + b[2][rows, :].astype(f32)
        outs[4 + i][:, 1536:] = (value + b[3][rows, :].astype(f32)).astype(bf16)


def finish_body(at, *refs):
    own, a, b = refs[0], refs[1:5], refs[5:9]
    gate, up, down, query, output = refs[9:]
    mine = at[2] == at[3]

    def sum_a(cols):
        head = jnp.where(mine, own[:, cols], a[0][:, cols])
        return head.astype(f32) + a[1][:, cols].astype(f32) + a[2][:, cols].astype(f32) + a[3][:, cols].astype(f32)

    def sum_b(cols):
        return b[0][:, cols].astype(f32) + b[1][:, cols].astype(f32) + b[2][:, cols].astype(f32) + b[3][:, cols].astype(f32)

    for j in range(4):
        cols = slice(j * 256, (j + 1) * 256)
        gate[:, cols] = sum_a(cols)
        up[:, cols] = sum_b(cols)
    for j in range(2):
        cols = slice(FF + j * 256, FF + (j + 1) * 256)
        down[:, j * 256 : (j + 1) * 256] = sum_a(cols)
        down[:, 512 + j * 256 : 512 + (j + 1) * 256] = sum_b(cols)
    query[...] = sum_b(slice(1536, 1792))
    output[...] = sum_b(slice(1792, 2048))


def on_device(
    tokens,
    segments,
    gain_attn,
    w_query,
    w_key,
    w_value,
    w_output,
    gain_ffn,
    w_gate,
    w_up,
    w_down,
    cotangent,
):
    y, lo, core = lax.axis_index(Y), lax.axis_index(XLO), lax.axis_index(CORE)
    hi, z = lax.axis_index(XHI), lax.axis_index(Z)
    at = jnp.stack([y, lo, hi, core, z]).astype(jnp.int32)
    mine = core * 4 + z

    riders = jnp.zeros((16, HEAD), bf16).at[:3].set(segments.reshape(3, HEAD).astype(bf16))
    gains = jnp.zeros((16, 2 * HEAD), bf16)
    gains = gains.at[0, :128].set(gain_attn).at[1, :128].set(gain_ffn)
    hf = FF // 2
    kv_own = jnp.concatenate([w_key, w_value], 1)
    kv_other = kv_partner(kv_own)
    got = swap(jnp.concatenate([tokens, riders, cotangent], 0))
    along_y = jnp.concatenate([w_query, w_output], 1)
    along_y = from_y(jnp.concatenate([along_y, gains, w_up[:, :hf], w_up[:, hf:], w_down[:, hf:]], 0))
    odd = z % 2 == 1
    half = HEAD // 2
    low_kv, high_kv = jnp.where(odd, kv_other, kv_own), jnp.where(odd, kv_own, kv_other)
    along_x = jnp.concatenate([low_kv[:, :half], high_kv[:, :half], low_kv[:, half:], high_kv[:, half:]], 1)
    along_x = jnp.concatenate([along_x, w_gate[:, :hf], w_gate[:, hf:], w_down[:, :hf]], 0)
    along_x = [own_or(x_in(along_x, 0, 0), along_x)] + [x_in(along_x, *flip) for flip in FLIPS[1:]]
    got, *rest = lax.optimization_barrier((got, *along_x, *along_y))
    to_y, to_x = call(
        pack_body,
        "pack",
        [at, *rest],
        [((512, 2 * HEAD), bf16), ((576, 2 * HEAD), bf16)],
        [pltpu.SemaphoreType.DMA((8,))],
        0,
        anywhere=8,
    )
    a_wide, b_wide, a_down, b_down = call(
        riders_body,
        "riders",
        [at, *rest],
        [((512, FF), bf16)] * 2 + [((512, hf), bf16)] * 2,
        [pltpu.SemaphoreType.DMA((24,))],
        0,
        anywhere=8,
    )
    x_own = got[:LEN]
    x_all = team_gather(x_own)
    upstream = team_gather(after(got[784:1552], to_x))
    segment_row = got[LEN : LEN + 3].astype(f32).reshape(1, LEN)
    segment_col = segment_row.reshape(LEN, 1)
    cosine, sine = rope_tables(segment_row[0])
    first = [shift(to_y, Y, -1), shift(to_y, Y, 1)]
    second = [x_in(to_x, *flip) for flip in FLIPS[2:]]
    late_y, late_x, *rest = lax.optimization_barrier((to_y, to_x, *first, *second))
    first, second = rest[:2], rest[2:]
    first = [to_y, first[0], shift(late_y, Y, 2), first[1]]
    second = [own_or(x_in(late_x, 0, 0), to_x), x_in(late_x, *FLIPS[1])] + second
    x_all, cosine, sine, segment_row, segment_col, *rest = lax.optimization_barrier(
        (x_all, cosine, sine, segment_row, segment_col, *first, *second, a_wide, b_wide, a_down, b_down)
    )
    first, second, (a_wide, b_wide, a_down, b_down) = rest[:4], rest[4:8], rest[8:]
    wide_a = [shift(a_wide, Y, -1), shift(a_wide, Y, 1)]
    wide_b = [x_in(b_wide, *flip) for flip in FLIPS[2:]]

    part = ((LEN // 2, WIDTH), bf16)
    act, low, col = ((LEN, WIDTH), bf16), ((LEN, HEAD), bf16), ((LEN, 1), f32)
    a1, r1, x_mine, qr, kr, v, o, lse, peak, gain_rows, give, keep = call(
        forward_body,
        "attention_forward",
        [at, x_all, cosine, sine, segment_row, segment_col, *first, *second],
        [act, col, ((OWN, WIDTH), bf16), low, low, low, low, col, ((8, 128), f32), ((8, WIDTH), f32), part, part],
        [
            pltpu.VMEM((WIDTH, 3 * HEAD), bf16),
            pltpu.VMEM((WIDTH, HEAD), bf16),
            pltpu.VMEM((16, WIDTH), bf16),
            pltpu.SemaphoreType.DMA((48,)),
            pltpu.SemaphoreType.DMA((16,)),
        ],
        2 * LEN * WIDTH * 1024,
        anywhere=8,
    )
    give, keep, upstream, *done = lax.optimization_barrier(
        (give, keep, upstream, *wide_a, *wide_b, a_wide, b_wide, a_down, b_down)
    )
    wide_a, wide_b, (a_wide, b_wide, a_down, b_down) = done[:2], done[2:4], done[4:]
    attn_own = team_scatter(give, keep)
    wide_a = [a_wide, wide_a[0], shift(a_wide, Y, 2), wide_a[1]]
    wide_b = [x_in(b_wide, *flip) for flip in FLIPS[:2]] + wide_b
    down_a = [shift(a_down, Y, -1), shift(a_down, Y, 1)]
    (dy,) = call(reorder_body, "order_upstream", [at, upstream], [((LEN, WIDTH), bf16)], [], 0)


    attn_own, dy, *done = lax.optimization_barrier((attn_own, dy, *wide_a, *wide_b, *down_a, b_wide, a_down, b_down))
    wide_a, wide_b, down_a, (b_wide, a_down, b_down) = done[:4], done[4:8], done[8:10], done[10:]
    down_b = [x_in(b_down, *flip) for flip in FLIPS]
    down_a = [a_down, down_a[0], shift(a_down, Y, 2), down_a[1]]
    hidden_own = x_mine.astype(f32) + attn_own
    hidden = team_gather(hidden_own.astype(bf16))
    wide = ((LEN, FF), bf16)
    a2, hid, dgate, dup, h_cols, give, keep = call(
        ffn_body,
        "feed_forward",
        [at, hidden, gain_rows, dy, *wide_a, *down_a, *wide_b, *down_b, b_wide, b_down],
        [act, wide, wide, wide, low, part, part],
        [
            pltpu.VMEM((WIDTH, FF), bf16),
            pltpu.VMEM((WIDTH, FF), bf16),
            pltpu.VMEM((WIDTH, FF), bf16),
            pltpu.SemaphoreType.DMA((40,)),
        ],
        10 * LEN * WIDTH * FF,
        anywhere=18,
    )
    other = other_core(give)
    wide_out, stack = ((512, FF), bf16), ((4 * LEN, HEAD), bf16)
    work = 2 * LEN * WIDTH * FF
    up_a = call(functools.partial(weight_up_body, 2), "weight_up_first", [at, a2, dup], [wide_out] * 2, [], work / 2)
    keep, other, *up_a = lax.optimization_barrier((keep, other, *up_a))
    both = (keep.astype(f32) + other.astype(f32)).astype(bf16)
    normed_grad = lax.psum_scatter(both, Z, scatter_dimension=0, tiled=True).astype(f32)
    dgate, dup, hid = lax.optimization_barrier((dgate, dup, hid, both))[:3]
    gate_a = call(
        functools.partial(weight_gate_body, (1, 3)), "weight_gate_first", [at, a2, dgate], [wide_out] * 2, [], work / 2
    )
    got_up = [x_out(block, *flip) for block, flip in zip(up_a, FLIPS[2:])]
    got_gate = [shift(gate_a[0], Y, 1), shift(gate_a[1], Y, 3)]
    rest = call(
        weight_rest_body,
        "weight_rest",
        [at, a2, dy, after(dgate, gate_a[0]), dup, hid],
        [wide_out] * 4 + [((512, hf), bf16)] * 8,
        [],
        work * 2,
    )
    out_give, out_keep = call(
        ffn_out_body,
        "feed_forward_out",
        [at, after(hid, rest[0]), *down_a, *down_b, b_down],
        [stack, stack],
        [pltpu.VMEM((WIDTH, FF), bf16), pltpu.SemaphoreType.DMA((20,))],
        work,
        anywhere=9,
    )
    normed_grad, out_give, out_keep, *got = lax.optimization_barrier(
        (normed_grad, out_give, out_keep, *got_up, *got_gate, *rest)
    )
    got_up, got_gate, gate_b, up_b = [got[2 * i : 2 * i + 2] for i in range(4)]
    down_g = got[8:]

    gain_two = gain_rows[1:2]
    factor_own = lax.rsqrt(jnp.mean(hidden_own * hidden_own, axis=1, keepdims=True) + norm_epsilon)
    grad_gain_two = jnp.sum(normed_grad * hidden_own * factor_own, axis=0)
    scaled = normed_grad * gain_two
    grad_res = (
        lax.dynamic_slice_in_dim(dy, mine * OWN, OWN, 0).astype(f32)
        + factor_own * scaled
        - hidden_own * factor_own**3 * jnp.mean(scaled * hidden_own, axis=1, keepdims=True)
    )
    grad_low = grad_res.astype(bf16)
    db = team_gather(grad_low)
    got_gate = [gate_b[0], shift(gate_b[1], Y, 2)] + got_gate
    got_up = [x_out(up_b[0], 0, 0), x_out(up_b[1], *FLIPS[1])] + got_up
    out_both = (out_keep.astype(f32) + other_core(out_give).astype(f32)).astype(bf16)
    db, out_both, *got = lax.optimization_barrier((db, out_both, *got_gate, *got_up, *down_g))
    got_gate, got_up, down_g = got[:4], got[4:8], got[8:]
    got_down_a = [shift(down_g[1], Y, 1), shift(down_g[3], Y, 3)]
    got_down_b = [x_out(block, *flip) for block, flip in zip(down_g[6:], FLIPS[2:])]

    db_cols, dqkv, row_part, gain_part, part_give, part_keep = call(
        backward_body,
        "attention_backward",
        [at, db, cosine, sine, segment_row, segment_col, qr, kr, v, lse, a1, gain_rows, *first, *second],
        [low, ((LEN, 3 * HEAD), bf16), col, ((1, WIDTH), f32), stack, stack],
        [
            pltpu.VMEM((WIDTH, 3 * HEAD), bf16),
            pltpu.VMEM((WIDTH, HEAD), bf16),
            pltpu.VMEM((LEN, HEAD), bf16),
            pltpu.VMEM((LEN, HEAD), f32),
            pltpu.VMEM((LEN, HEAD), f32),
            pltpu.SemaphoreType.DMA((48,)),
        ],
        2 * LEN * WIDTH * 1024,
        anywhere=8,
    )
    part_give, part_keep, dqkv, down_y, down_0, down_1, *got = lax.optimization_barrier(
        (part_give, part_keep, dqkv, down_g[2], down_g[4], down_g[5], *got_down_a, *got_down_b)
    )
    got_down_a = [down_g[0], shift(down_y, Y, 2), *got[:2]]
    got_down_b = [x_out(down_0, 0, 0), x_out(down_1, *FLIPS[1]), *got[2:]]
    part_other = other_core(part_give)
    blocks = call(
        attention_weight_body,
        "attention_weights",
        [at, a1, dqkv, db, o],
        [((512, 512), bf16)] * 8,
        [],
        2 * LEN * WIDTH * 1024,
    )
    part_keep, part_other, *got = lax.optimization_barrier((part_keep, part_other, *blocks, *got_down_a, *got_down_b))
    blocks, got_down_a, got_down_b = got[:8], got[8:12], got[12:]
    part_both = (part_keep.astype(f32) + part_other.astype(f32)).astype(bf16)
    attn_grad = lax.psum_scatter(part_both, Z, scatter_dimension=0, tiled=True).astype(f32)
    got_attn_a = [shift(blocks[1], Y, 1), shift(blocks[3], Y, 3)]
    got_attn_b = [x_out(blocks[4 + i], *FLIPS[i]) for i in (2, 3)]
    row_part = after(row_part, part_both)

    block_at = jnp.stack([((r // 4 - y) % 4) * 4 + ((r // 2 % 2) ^ lo) * 2 + ((r % 2) ^ hi) for r in range(16)])
    pick = (block_at[:, None] == jnp.arange(16)[None, :]).astype(f32)
    gain_parts = jnp.concatenate([gain_part.reshape(16, 128), grad_gain_two.reshape(16, 128)], 1)
    gain_parts = jnp.dot(pick, gain_parts, precision=lax.Precision.HIGHEST)
    peaks = jnp.where((jnp.arange(QUERY_HEADS) == mine)[:, None], peak, 0.0)
    small = jnp.concatenate([row_part.reshape(6, 128), gain_parts[:, :128], gain_parts[:, 128:], peaks], 0)
    is_peak = (jnp.arange(46) >= 38)[:, None]

    def join(values):
        total, most = values[0], values[0]
        for value in values[1:]:
            total, most = total + value, jnp.maximum(most, value)
        return jnp.where(is_peak[-total.shape[0] :], most, total)

    small = join([small, other_core(small)])
    small = join([small, z_other(small, 1)])

    rest = lax.optimization_barrier((blocks[2], blocks[4], blocks[5], small, got_up[2], *got_attn_a, *got_attn_b))
    (block_y, block_0, block_1, small, got_up[2]), got_attn_a, got_attn_b = rest[:5], rest[5:7], rest[7:]
    got_attn_a = [blocks[0], shift(block_y, Y, 2), *got_attn_a]
    got_attn_b = [x_out(block_0, 0, 0), x_out(block_1, *FLIPS[1]), *got_attn_b]
    out_late = after(out_both, part_both)
    ffn_a, ffn_b = call(
        ffn_sum_body,
        "feed_forward_sums",
        [at, *got_gate, *got_down_a, *got_up, *got_down_b, up_b[0], down_0],
        [((512, 1536), bf16)] * 2,
        [],
        0,
    )

    small = join([small, z_other(small, 2)])
    row_sum = small[:6].reshape(LEN, 1)
    small = small[6:]
    small = join([small, y_other(small, 1)])
    got_attn_a, got_attn_b, ffn_a, ffn_b, small, attn_grad = lax.optimization_barrier(
        (got_attn_a, got_attn_b, ffn_a, ffn_b, small, attn_grad)
    )
    sums = call(
        join_body,
        "join_sums",
        [at, ffn_a, ffn_b, *got_attn_a, *got_attn_b, block_0],
        [((128, WIDTH), bf16)] * 8,
        [],
        0,
    )
    sums_a, sums_b = sums[:4], sums[4:]
    sum_b = [shift(sums_b[i], Y, i) for i in (1, 3)]
    sum_a = [x_out(sums_a[i], *FLIPS[i]) for i in (2, 3)]
    small = join([small, y_other(small, 2)])
    small = join([small, x_ring(small, 1)])
    rest = lax.optimization_barrier((*sum_b, *sum_a, sums_b[2], sums_a[0], sums_a[1], small))
    sum_b, sum_a, (late_y, late_0, late_1, small) = rest[:2], rest[2:4], rest[4:]
    sum_b = [sums_b[0], shift(late_y, Y, 2), *sum_b]
    sum_a = [x_out(late_0, 0, 0), x_out(late_1, *FLIPS[1]), *sum_a]
    ffn_own = lax.psum_scatter(out_late, Z, scatter_dimension=0, tiled=True).astype(f32)
    ffn_own = after(ffn_own, small)

    gain_pair = jnp.dot(pick, gain_rows[0].reshape(16, 128), precision=lax.Precision.HIGHEST)
    gain_cols = lax.dynamic_slice(gain_pair, (mine * 2, 0), (2, 128)).reshape(1, HEAD)
    grad_inputs = (
        db_cols.astype(f32) + r1 * attn_grad * gain_cols - x_own.astype(f32) * r1**2 * (row_sum / WIDTH)
    )
    home = [(h_cols.astype(f32) + ffn_own).astype(bf16), grad_inputs.astype(bf16)]
    home = swap(jnp.concatenate(home, 0))
    small = join([small, x_ring(small, 2)])
    sum_a, sum_b, home, small = lax.optimization_barrier((sum_a, sum_b, home, small))
    kv_sum = total([own_or(sum_a[0], sums_a[0]), *sum_a[1:]], slice(1536, None))
    first_halves = jnp.concatenate([kv_sum[:, :half], kv_sum[:, HEAD : HEAD + half]], 1)
    second_halves = jnp.concatenate([kv_sum[:, half:HEAD], kv_sum[:, HEAD + half :]], 1)
    kv_done = jnp.where(odd, second_halves, first_halves) + kv_partner(
        jnp.where(odd, first_halves, second_halves).astype(bf16)
    ).astype(f32)
    grads = call(
        finish_body,
        "finish",
        [at, sums_a[0], *sum_a, *sum_b],
        [((128, FF), f32)] * 3 + [((128, HEAD), f32)] * 2,
        [],
        0,
    )
    tok = y * 4 + lo * 2 + core
    gains_mine = lax.dynamic_slice(small[:32].reshape(2, 16, 128), (0, tok, 0), (2, 1, 128)).reshape(2, 128)
    peaks = small[32:, 0]

    head = hi * 4 + z
    peak_q = lax.dynamic_slice(peaks, (head,), (1,))
    pair = lax.dynamic_slice(peaks, (head // 2 * 2,), (2,))
    scale_q = jnp.sqrt(logit_ceiling / (peak_q + peak_floor_epsilon))
    scale_k = jnp.sqrt(logit_ceiling / (jnp.max(pair, keepdims=True) + peak_floor_epsilon))
    clipped_query = (w_query.astype(f32) * scale_q[None, :]).astype(bf16)
    clipped_key = (w_key.astype(f32) * scale_k[None, :]).astype(bf16)
    return (
        home[:LEN],
        home[LEN:].astype(f32),
        gains_mine[0],
        grads[3],
        kv_done[:, :half],
        kv_done[:, half:],
        grads[4],
        gains_mine[1],
        grads[0],
        grads[1],
        grads[2],
        clipped_query,
        clipped_key,
    )


def solution(mesh):
    torus = Mesh(mesh.devices.reshape(4, 2, 2, 2, 4), (Y, XLO, CORE, XHI, Z))
    both, rows = P(TOK, MDL), P(TOK)
    return jax.shard_map(
        on_device,
        mesh=torus,
        in_specs=(both, P(TOK, None), rows, both, both, both, both, rows, both, both, both, both),
        out_specs=(both, both, rows, both, both, both, both, rows, both, both, both, both, both),
        check_vma=False,
    )
```

time: 1020 us -> 476 us (0.47)
  waiting for transfers between devices: 677 us -> 153 us
  Pallas kernels: 0 us -> 126 us
  local copies, waits for them, and re-layouts: 130 us -> 15.9 us
  starting transfers between devices: 4.32 us -> 117 us
  matrix products: 107 us -> 0.37 us
  blocking collectives: 35.6 us -> 0 us
    psum x3 -> x0, waiting for transfers between devices: 342 us -> none  [the longest x1 144 us: on_device(): normed_grad = lax.psum(normed_grad_part, MDL)]
    all_gather x3 -> x4, waiting for transfers between devices: 182 us -> 0.03 us  [team_gather(): return lax.all_gather(own, (CORE, Z), axis=0, tiled=True)]
    unnamed x9 -> x8, waiting for transfers between devices: 133 us -> 0.82 us
    pallas_call x0 -> x14, Pallas kernels: none -> 126 us  [call(): pl.pallas_call(body, name=name, out_shape=[jax.ShapeDtypeStruct(s, d) for...]
    ppermute x4 -> x71, waiting for transfers between devices: 20 us -> 141 us  [the longest x24 60.9 us: shift(): return lax.ppermute(a, axis, [(i, (i + by) % 4) for i in range(4)])]
    ppermute x4 -> x71, starting transfers between devices: 3.57 us -> 117 us  [the longest x16 32.4 us: x_in(): return lax.ppermute(a, (XLO, CORE, XHI), x_pairs(flip_lo, flip_core, False))]
    dot_general x27 -> x2, matrix products: 107 us -> 0.37 us  [the longest x1 0.19 us: on_device(): gain_parts = jnp.dot(pick, gain_parts, precision=lax.Precision.HIGHEST)]
    concatenate x2, local copies, waits for them, and re-layouts: 89.8 us -> 1.76 us  [the longest x1 0.99 us: on_device(): jnp.concatenate([along_y, gains, w_up[:, :hf], w_up[:, hf:], w_down[:, hf...]
  transfers between devices with their start and end apart: 12 -> 79, of which waited for: 9 -> 31; matrix products, arithmetic and copies ran while one was open for 20% -> 7% of each run, Pallas kernels for 0% -> 21%
where the time goes in v1:
time: 476 us; the launch traced here: 468 us
  waiting for transfers between devices  153 us (32%)
  Pallas kernels  126 us (26%)
  starting transfers between devices  117 us (25%)
  other arithmetic  37.5 us (8%)
  between operations  17.3 us (4%)
  local copies, waits for them, and re-layouts  15.9 us (3%)
    pallas_call x14, Pallas kernels, call(): pl.pallas_call(body, name=name, out_shape=[jax.ShapeDtypeStruct(s, d) for...  126 us
    ppermute x24, waiting for transfers between devices, shift(): return lax.ppermute(a, axis, [(i, (i + by) % 4) for i in range(4)])  60.9 us
    ppermute x16, waiting for transfers between devices, x_in(): return lax.ppermute(a, (XLO, CORE, XHI), x_pairs(flip_lo, flip_core, False))  43 us
    ppermute x16, starting transfers between devices, x_in(): return lax.ppermute(a, (XLO, CORE, XHI), x_pairs(flip_lo, flip_core, False))  32.4 us
    ppermute x24, starting transfers between devices, shift(): return lax.ppermute(a, axis, [(i, (i + by) % 4) for i in range(4)])  30.6 us
    ppermute x16, starting transfers between devices, x_out(): return lax.ppermute(a, (XLO, CORE, XHI), x_pairs(flip_lo, flip_core, True))  28.8 us
    ppermute x16, waiting for transfers between devices, x_out(): return lax.ppermute(a, (XLO, CORE, XHI), x_pairs(flip_lo, flip_core, True))  17.2 us
    ppermute x2, waiting for transfers between devices, x_ring(): return lax.ppermute(a, (XLO, XHI), [(i, i ^ mask) for i in range(4)])  13 us
  transfers between devices with their start and end apart: 79, of which 31 were waited for; matrix products, arithmetic and copies ran while one was open for 7% of the time, Pallas kernels for 21%

profile of v1, /device:TPU:1, one launch (start us, length us, event | category | flops | bytes accessed | tf_op | source)
XLA Modules:
  0.0 467.9 jit_solution(679891275103505668)
XLA Ops:
  8.9 2.5 collective-permute-start.1
  19.6 5.8 %collective-permute-start = (bf16[1552,256]{1,0:T(8,128)(2,1)}, bf16[1552,256]{1,0:T(8,128)(2,1)}, u32[]{:S(2)}, u32[]{:S(2)}) collective-permute-start(bf16[1552,256]{1,0:T(8,128)(2,1)} %fusion.3), channel_id=1, source_target_pairs={{4,8},{8,4},{5,9},{9,5},{6,10},{10,6},{7,11},{11,7},{20,24},{24,20... | collective-permute-start | bytes 2383880 | tf_op jit(solution)/shard_map/ppermute | solution.py:39
  28.3 2.7 collective-permute-start.7
  32.1 3.5 collective-permute-start.4
  35.6 10.6 %collective-permute-done.2 = bf16[512,512]{1,0:T(8,128)(2,1)} collective-permute-done((bf16[512,512]{1,0:T(8,128)(2,1)}, bf16[512,512]{1,0:T(8,128)(2,1)}, u32[]{:S(2)}, u32[]{:S(2)}) %collective-permute-start.2) | collective-permute-done | bytes 524320 | tf_op jit(solution)/shard_map/ppermute | solution.py:78
  46.3 3.9 collective-permute-start.5
  53.6 5.7 %collective-permute-done.3.refs_1_ = bf16[512,512]{1,0:T(8,128)(2,1)} collective-permute-done((bf16[512,512]{1,0:T(8,128)(2,1)}, bf16[512,512]{1,0:T(8,128)(2,1)}, u32[]{:S(2)}, u32[]{:S(2)}) %collective-permute-start.3) | collective-permute-done | bytes 524320 | tf_op jit(solution)/shard_map/ppermute | solution.py:78
  59.4 2.5 collective-permute-done.5.refs_3_
  63.6 3.0 pack.1
  66.7 2.6 collective-permute-start.12
  70.6 2.1 collective-permute-start.10
  73.3 12.0 %collective-permute-done.10.refs_8_.refs_14_ = bf16[512,512]{1,0:T(8,128)(2,1)S(1)} collective-permute-done((bf16[512,512]{1,0:T(8,128)(2,1)}, bf16[512,512]{1,0:T(8,128)(2,1)S(1)}, u32[]{:S(2)}, u32[]{:S(2)}) %collective-permute-start.10) | collective-permute-done | bytes 524320 | tf_op jit(solution)/shard_map/ppermute | solution.py:48
  86.0 4.0 collective-permute-start.14
  92.5 4.6 riders.1
  97.1 2.5 multiply_sine_fusion
  99.7 3.9 collective-permute-done.14
  108.3 2.8 collective-permute-start.19
  112.2 15.7 %attention_forward.1 = (bf16[768,2048]{1,0:T(8,128)(2,1)}, f32[768,1]{1,0:T(8,128)}, bf16[96,2048]{1,0:T(8,128)(2,1)}, bf16[768,256]{1,0:T(8,128)(2,1)}, bf16[76...) custom-call(s32[5]{0:T(128)} %stack.74.at, ...), custom_call_target="tpu_custom_call" | custom-call | flops 3221225472 | bytes 16728064 | tf_op jit(solution)/shard_map/attention_forward/pallas_call | solution.py:155
  127.9 2.5 collective-permute-done.17.refs_6_
  130.4 3.3 collective-permute-done.19.refs_14_
  135.8 3.2 collective-permute-done.20
  139.1 3.1 add_convert_fusion.3
  144.0 4.4 collective-permute-start.22
  148.4 2.7 collective-permute-start.24
  151.1 4.7 %order_upstream.1.refs_2_.dy = bf16[768,2048]{1,0:T(8,128)(2,1)} custom-call(s32[5]{0:T(128)} %stack.74.at, bf16[6144,256]{1,0:T(8,128)(2,1)} %all-gather.7.cloned.1.call-done.whole), custom_call_target="tpu_custom_call" | custom-call | bytes 6291456 | tf_op jit(solution)/shard_map/order_upstream/pallas_call | solution.py:155
  155.8 12.1 %reduce-scatter.5.cloned.1.call-done = bf16[96,2048]{1,0:T(8,128)(2,1)} async-done(((bf16[384,2048]{1,0:T(8,128)(2,1)}), bf16[96,2048]{1,0:T(8,128)(2,1)}) %reduce-scatter.5.cloned.1.call-update) | async-done | bytes 393232 | tf_op jit(solution)/shard_map/reduce_scatter | solution.py:114
  168.9 11.4 %collective-permute-done.25.refs_10_.refs_3_ = bf16[512,512]{1,0:T(8,128)(2,1)} collective-permute-done((bf16[512,512]{1,0:T(8,128)(2,1)S(1)}, bf16[512,512]{1,0:T(8,128)(2,1)}, u32[]{:S(2)}, u32[]{:S(2)}) %collective-permute-start.25) | collective-permute-done | bytes 524320 | tf_op jit(solution)/shard_map/ppermute | solution.py:48
  182.4 2.6 collective-permute-start.30
  186.9 2.7 collective-permute-start.27
  189.6 6.4 %collective-permute-done.26.refs_9_.refs_2_ = bf16[512,512]{1,0:T(8,128)(2,1)S(1)} collective-permute-done((bf16[512,512]{1,0:T(8,128)(2,1)S(1)}, bf16[512,512]{1,0:T(8,128)(2,1)S(1)}, u32[]{:S(2)}, u32[]{:S(2)}) %collective-permute-start.26) | collective-permute-done | bytes 524320 | tf_op jit(solution)/shard_map/ppermute | solution.py:48
  196.1 13.3 %collective-permute-done.29.refs_17_.refs_6_ = bf16[512,512]{1,0:T(8,128)(2,1)} collective-permute-done((bf16[512,512]{1,0:T(8,128)(2,1)}, bf16[512,512]{1,0:T(8,128)(2,1)}, u32[]{:S(2)}, u32[]{:S(2)}) %collective-permute-start.29) | collective-permute-done | bytes 524320 | tf_op jit(solution)/shard_map/ppermute | solution.py:78
  210.8 26.5 %feed_forward.1 = (bf16[768,2048]{1,0:T(8,128)(2,1)}, bf16[768,1024]{1,0:T(8,128)(2,1)}, bf16[768,1024]{1,0:T(8,128)(2,1)}, bf16[768,1024]{1,0:T(8,128)(2,1)}, b...) custom-call(s32[5]{0:T(128)} %stack.74.at, ...), custom_call_target="tpu_custom_call" | custom-call | flops 16106127360 | bytes 31916032 | tf_op jit(solution)/shard_map/feed_forward/pallas_call | solution.py:155
  237.6 5.6 %weight_up_first.1 = (bf16[512,1024]{1,0:T(8,128)(2,1)}, bf16[512,1024]{1,0:T(8,128)(2,1)}) custom-call(s32[5]{0:T(128)} %stack.74.at, bf16[768,2048]{1,0:T(8,128)(2,1)} %get-tuple-element.367.a2, bf16[768,1024]{1,0:T(8,128)(2,1)} %get-tuple-element.379.dup), custom_call_target="tpu_custom_call" | custom-call | flops 1610612736 | bytes 6815744 | tf_op jit(solution)/shard_map/weight_up_first/pallas_call | solution.py:155
  246.7 3.2 collective-permute-start.32
  250.0 5.2 %weight_gate_first.1 = (bf16[512,1024]{1,0:T(8,128)(2,1)}, bf16[512,1024]{1,0:T(8,128)(2,1)}) custom-call(s32[5]{0:T(128)} %stack.74.at, bf16[768,2048]{1,0:T(8,128)(2,1)} %get-tuple-element.367.a2, bf16[768,1024]{1,0:T(8,128)(2,1)} %get-tuple-element.378.dgate), custom_call_target="tpu_custom_call" | custom-call | flops 1610612736 | bytes 6815744 | tf_op jit(solution)/shard_map/weight_gate_first/pallas_call | solution.py:155
  257.6 12.9 %weight_rest.1 = (bf16[512,1024]{1,0:T(8,128)(2,1)}, bf16[512,1024]{1,0:T(8,128)(2,1)}, bf16[512,1024]{1,0:T(8,128)(2,1)}, bf16[512,1024]{1,0:T(8,128)(2,1)}, bf...) custom-call(s32[5]{0:T(128)} %stack.74.at, ...), custom_call_target="tpu_custom_call" | custom-call | flops 6442450944 | bytes 19398656 | tf_op jit(solution)/shard_map/weight_rest/pallas_call | solution.py:155
  270.5 8.6 %feed_forward_out.1 = (bf16[3072,256]{1,0:T(8,128)(2,1)}, bf16[3072,256]{1,0:T(8,128)(2,1)}) custom-call(s32[5]{0:T(128)} %stack.74.at, bf16[768,1024]{1,0:T(8,128)(2,1)} %get-tuple-element.381.hid, bf16[512,512]{1,0:T(8,128)(2,1)} %get-tuple-element.356.refs_7_.refs_0_, bf16[512,512]{1,0:T(8,128)(2,1)} %collective-permute-done.24.refs_8_.refs_1_, ...), custom_call_target="tpu_custom_call" | custom-call | flops 3221225472 | bytes 9437184 | tf_op jit(solution)/shard_map/feed_forward_out/pallas_call | solution.py:155
  280.3 2.9 collective-permute-done.34.refs_2_
  284.0 2.3 subtract_convert_fusion.1
  288.6 4.1 collective-permute-start.38
  294.4 19.5 %collective-permute-done.37.refs_1_ = bf16[512,1024]{1,0:T(8,128)(2,1)S(1)} collective-permute-done((bf16[512,1024]{1,0:T(8,128)(2,1)}, bf16[512,1024]{1,0:T(8,128)(2,1)S(1)}, u32[]{:S(2)}, u32[]{:S(2)}) %collective-permute-start.37) | collective-permute-done | bytes 1048608 | tf_op jit(solution)/shard_map/ppermute | solution.py:48
  319.3 14.0 %attention_backward.1 = (bf16[768,256]{1,0:T(8,128)(2,1)}, bf16[768,768]{1,0:T(8,128)(2,1)}, f32[768,1]{1,0:T(8,128)}, f32[1,2048]{1,0:T(1,128)}, bf16[3072,256]{1,0:T(8,128)(2,1)}, /*index=5*/bf16[3072,256]{1,0:T(8,128)(2,1)}) custom-call(s32[5]{0:T(128)} %stack.74.at, bf16[768,2048]{1,0:T(8,128)(2,1)} %all-gather.11.cloned.1.call-done.refs_0_.db, ...), custom_call_target="tpu_custom_call" | custom-call | flops 3221225472 | bytes 17518592 | tf_op jit(solution)/shard_map/attention_backward/pallas_call | solution.py:155
  336.6 2.3 collective-permute-start.47
  338.9 3.0 collective-permute-start.46
  341.9 8.1 %attention_weights.1 = (bf16[512,512]{1,0:T(8,128)(2,1)}, bf16[512,512]{1,0:T(8,128)(2,1)}, bf16[512,512]{1,0:T(8,128)(2,1)}, bf16[512,512]{1,0:T(8,128)(2,1)}, ...) custom-call(s32[5]{0:T(128)} %stack.74.at, ...), custom_call_target="tpu_custom_call" | custom-call | flops 3221225472 | bytes 12058624 | tf_op jit(solution)/shard_map/attention_weights/pallas_call | solution.py:155
  350.0 2.5 collective-permute-done.46.refs_12_
  356.6 2.9 collective-permute-start.51
  362.4 3.1 collective-permute-done.49
  365.6 5.5 %collective-permute-done.50.refs_4_ = bf16[512,512]{1,0:T(8,128)(2,1)S(1)} collective-permute-done((bf16[512,512]{1,0:T(8,128)(2,1)}, bf16[512,512]{1,0:T(8,128)(2,1)S(1)}, u32[]{:S(2)}, u32[]{:S(2)}) %collective-permute-start.50) | collective-permute-done | bytes 524320 | tf_op jit(solution)/shard_map/ppermute | solution.py:48
  371.2 4.1 collective-permute-done.53.refs_9_
  375.3 2.3 collective-permute-start.57
  379.8 5.7 %collective-permute-start.55 = (bf16[512,512]{1,0:T(8,128)(2,1)S(1)}, bf16[512,512]{1,0:T(8,128)(2,1)}, u32[]{:S(2)}, u32[]{:S(2)}) collective-permute-start(bf16[512,512]{1,0:T(8,128)(2,1)S(1)} %copy-done.28), channel_id=1, source_target_pairs={{8,4},{4,8},{24,20},{20,24},{9,5},{5,9},{25,21},{21,25},{10,6},{6,... | collective-permute-start | bytes 1572872 | tf_op jit(solution)/shard_map/ppermute | solution.py:82
  386.0 8.1 %feed_forward_sums.1 = (bf16[512,1536]{1,0:T(8,128)(2,1)}, bf16[512,1536]{1,0:T(8,128)(2,1)}) custom-call(s32[5]{0:T(128)} %stack.74.at, bf16[512,1024]{1,0:T(8,128)(2,1)} %get-tuple-element.475.refs_0_, bf16[512,1024]{1,0:T(8,128)(2,1)} %copy-done.11, bf16[512,1024]{1,0:T(8,128)(2,1)} %collective-permute-done.34.refs_2_, ...), custom_call_target="tpu_custom_call" | custom-call | bytes 17301504 | tf_op jit(solution)/shard_map/feed_forward_sums/pallas_call | solution.py:155
  396.4 2.6 collective-permute-start.63
  399.0 5.5 %join_sums.1 = (bf16[128,2048]{1,0:T(8,128)(2,1)}, bf16[128,2048]{1,0:T(8,128)(2,1)}, bf16[128,2048]{1,0:T(8,128)(2,1)}, bf16[128,2048]{1,0:T(8,128)(2,1)}, bf16...) custom-call(s32[5]{0:T(128)} %stack.74.at, ...), custom_call_target="tpu_custom_call" | custom-call | bytes 12058624 | tf_op jit(solution)/shard_map/join_sums/pallas_call | solution.py:155
  404.5 2.7 collective-permute-start.60
  408.6 2.9 collective-permute-start.64
  412.9 7.1 %collective-permute-done.64 = f32[40,128]{1,0:T(8,128)S(1)} collective-permute-done((f32[40,128]{1,0:T(8,128)S(1)}, f32[40,128]{1,0:T(8,128)S(1)}, u32[]{:S(2)}, u32[]{:S(2)}) %collective-permute-start.64) | collective-permute-done | bytes 20512 | tf_op jit(solution)/shard_map/ppermute | solution.py:101
  422.4 4.8 %collective-permute-start.68 = (bf16[1536,256]{1,0:T(8,128)(2,1)S(1)}, bf16[1536,256]{1,0:T(8,128)(2,1)}, u32[]{:S(2)}, u32[]{:S(2)}) collective-permute-start(bf16[1536,256]{1,0:T(8,128)(2,1)S(1)} %pad_maximum_fusion), channel_id=1, source_target_pairs={{4,8},{8,4},{5,9},{9,5},{6,10},{10,6},{7,11},{11,7},{20,24},{24,20... | collective-permute-start | bytes 2359304 | tf_op jit(solution)/shard_map/ppermute | solution.py:39
  427.9 2.8 collective-permute-start.65
  432.0 5.9 %collective-permute-done.69 = f32[40,128]{1,0:T(8,128)S(1)} collective-permute-done((f32[40,128]{1,0:T(8,128)S(1)}, f32[40,128]{1,0:T(8,128)S(1)}, u32[]{:S(2)}, u32[]{:S(2)}) %collective-permute-start.69) | collective-permute-done | bytes 20512 | tf_op jit(solution)/shard_map/ppermute | solution.py:101
  439.4 4.3 collective-permute-done.65.refs_1_
  444.5 3.4 collective-permute-done.66.refs_2_
  455.8 3.7 finish.1
  (314 shorter events, 89.9 us)
Async XLA Ops:
  7.2 98.4 %all-gather.5.cloned.1.call-start = ((), (), s32[]{:S(2)}) async-start(), calls=%async_computation.4 | async-start | bytes 3538944 | tf_op jit(solution)/shard_map/all_gather | solution.py:109
  8.9 16.6 %collective-permute-start.1 = (bf16[128,256]{1,0:T(8,128)(2,1)S(1)}, bf16[128,256]{1,0:T(8,128)(2,1)S(1)}, u32[]{:S(2)}, u32[]{:S(2)}) collective-permute-start(bf16[128,256]{1,0:T(8,128)(2,1)S(1)} %constant_dynamic-update-slice_fusion), channel_id=1, source_target_pairs={{0,1},{1,0},{2,3},{3,2},{4,5},{5,4},{6,7},{7,6},{8,9},{9,8},{10,11... | collective-permute-start | bytes 196616 | tf_op jit(solution)/shard_map/ppermute | solution.py:60
  16.6 15.5 %collective-permute-start.8 = (bf16[528,512]{1,0:T(8,128)(2,1)S(1)}, bf16[528,512]{1,0:T(8,128)(2,1)S(1)}, u32[]{:S(2)}, u32[]{:S(2)}) collective-permute-start(bf16[528,512]{1,0:T(8,128)(2,1)S(1)} %get-tuple-element.301.refs_4_), channel_id=1, source_target_pairs={{0,32},{32,64},{64,96},{96,0},{1,33},{33,65},{65,97},{97,1},{2,34}... | collective-permute-start | bytes 1622024 | tf_op jit(solution)/shard_map/ppermute | solution.py:48
  19.6 26.6 %collective-permute-start = (bf16[1552,256]{1,0:T(8,128)(2,1)}, bf16[1552,256]{1,0:T(8,128)(2,1)}, u32[]{:S(2)}, u32[]{:S(2)}) collective-permute-start(bf16[1552,256]{1,0:T(8,128)(2,1)} %fusion.3), channel_id=1, source_target_pairs={{4,8},{8,4},{5,9},{9,5},{6,10},{10,6},{7,11},{11,7},{20,24},{24,20... | collective-permute-start | bytes 2383880 | tf_op jit(solution)/shard_map/ppermute | solution.py:39
  26.4 19.9 %collective-permute-start.2 = (bf16[512,512]{1,0:T(8,128)(2,1)}, bf16[512,512]{1,0:T(8,128)(2,1)}, u32[]{:S(2)}, u32[]{:S(2)}) collective-permute-start(bf16[512,512]{1,0:T(8,128)(2,1)} %pad_maximum_fusion.1), channel_id=1, source_target_pairs={{4,8},{8,4},{20,24},{24,20},{5,9},{9,5},{21,25},{25,21},{6,10},{10... | collective-permute-start | bytes 1572872 | tf_op jit(solution)/shard_map/ppermute | solution.py:78
  28.3 25.3 %collective-permute-start.7 = (bf16[528,512]{1,0:T(8,128)(2,1)S(1)}, bf16[528,512]{1,0:T(8,128)(2,1)S(1)}, u32[]{:S(2)}, u32[]{:S(2)}) collective-permute-start(bf16[528,512]{1,0:T(8,128)(2,1)S(1)} %get-tuple-element.301.refs_4_), channel_id=1, source_target_pairs={{0,64},{32,96},{64,0},{96,32},{1,65},{33,97},{65,1},{97,33},{2,66}... | collective-permute-start | bytes 1622024 | tf_op jit(solution)/shard_map/ppermute | solution.py:48
  31.0 22.6 %collective-permute-start.6 = (bf16[528,512]{1,0:T(8,128)(2,1)S(1)}, bf16[528,512]{1,0:T(8,128)(2,1)S(1)}, u32[]{:S(2)}, u32[]{:S(2)}) collective-permute-start(bf16[528,512]{1,0:T(8,128)(2,1)S(1)} %get-tuple-element.301.refs_4_), channel_id=1, source_target_pairs={{0,96},{32,0},{64,32},{96,64},{1,97},{33,1},{65,33},{97,65},{2,98}... | collective-permute-start | bytes 1622024 | tf_op jit(solution)/shard_map/ppermute | solution.py:48
  32.1 21.5 %collective-permute-start.4 = (bf16[512,512]{1,0:T(8,128)(2,1)}, bf16[512,512]{1,0:T(8,128)(2,1)}, u32[]{:S(2)}, u32[]{:S(2)}) collective-permute-start(bf16[512,512]{1,0:T(8,128)(2,1)} %pad_maximum_fusion.1), channel_id=1, source_target_pairs={{0,16},{4,24},{8,20},{12,28},{16,0},{20,8},{24,4},{28,12},{1,17},{... | collective-permute-start | bytes 1572872 | tf_op jit(solution)/shard_map/ppermute | solution.py:78
  46.3 15.6 %collective-permute-start.5 = (bf16[512,512]{1,0:T(8,128)(2,1)}, bf16[512,512]{1,0:T(8,128)(2,1)}, u32[]{:S(2)}, u32[]{:S(2)}) collective-permute-start(bf16[512,512]{1,0:T(8,128)(2,1)} %pad_maximum_fusion.1), channel_id=1, source_target_pairs={{0,20},{4,28},{8,16},{12,24},{16,4},{20,12},{24,0},{28,8},{1,21},{... | collective-permute-start | bytes 1572872 | tf_op jit(solution)/shard_map/ppermute | solution.py:78
  62.8 65.1 %all-gather.7.cloned.1.call-start = ((), (), s32[]{:S(2)}) async-start(), calls=%async_computation.5 | async-start | bytes 3538944 | tf_op jit(solution)/shard_map/all_gather | solution.py:109
  66.6 101.3 %reduce-scatter.5.cloned.1.call-start = ((), (), s32[]{:S(2)}) async-start(), calls=%async_computation.6 | async-start | bytes 1966080 | tf_op jit(solution)/shard_map/reduce_scatter | solution.py:114
  66.7 19.3 %collective-permute-start.12 = (bf16[576,512]{1,0:T(8,128)(2,1)}, bf16[576,512]{1,0:T(8,128)(2,1)S(1)}, u32[]{:S(2)}, u32[]{:S(2)}) collective-permute-start(bf16[576,512]{1,0:T(8,128)(2,1)} %get-tuple-element.310), channel_id=1, source_target_pairs={{0,20},{4,28},{8,16},{12,24},{16,4},{20,12},{24,0},{28,8},{1,21},{... | collective-permute-start | bytes 1769480 | tf_op jit(solution)/shard_map/ppermute | solution.py:78
  69.2 16.7 %collective-permute-start.11 = (bf16[576,512]{1,0:T(8,128)(2,1)}, bf16[576,512]{1,0:T(8,128)(2,1)S(1)}, u32[]{:S(2)}, u32[]{:S(2)}) collective-permute-start(bf16[576,512]{1,0:T(8,128)(2,1)} %get-tuple-element.310), channel_id=1, source_target_pairs={{0,16},{4,24},{8,20},{12,28},{16,0},{20,8},{24,4},{28,12},{1,17},{... | collective-permute-start | bytes 1769480 | tf_op jit(solution)/shard_map/ppermute | solution.py:78
  70.6 14.7 %collective-permute-start.10 = (bf16[512,512]{1,0:T(8,128)(2,1)}, bf16[512,512]{1,0:T(8,128)(2,1)S(1)}, u32[]{:S(2)}, u32[]{:S(2)}) collective-permute-start(bf16[512,512]{1,0:T(8,128)(2,1)} %get-tuple-element.322.refs_5_.refs_11_), channel_id=1, source_target_pairs={{0,32},{32,64},{64,96},{96,0},{1,33},{33,65},{65,97},{97,1},{2,34}... | collective-permute-start | bytes 1572872 | tf_op jit(solution)/shard_map/ppermute | solution.py:48
  72.7 13.3 %collective-permute-start.9 = (bf16[512,512]{1,0:T(8,128)(2,1)}, bf16[512,512]{1,0:T(8,128)(2,1)S(1)}, u32[]{:S(2)}, u32[]{:S(2)}) collective-permute-start(bf16[512,512]{1,0:T(8,128)(2,1)} %get-tuple-element.322.refs_5_.refs_11_), channel_id=1, source_target_pairs={{0,96},{32,0},{64,32},{96,64},{1,97},{33,1},{65,33},{97,65},{2,98}... | collective-permute-start | bytes 1572872 | tf_op jit(solution)/shard_map/ppermute | solution.py:48
  86.0 17.5 %collective-permute-start.14 = (bf16[576,512]{1,0:T(8,128)(2,1)}, bf16[576,512]{1,0:T(8,128)(2,1)S(1)}, u32[]{:S(2)}, u32[]{:S(2)}) collective-permute-start(bf16[576,512]{1,0:T(8,128)(2,1)} %get-tuple-element.310), channel_id=1, source_target_pairs={{4,8},{8,4},{20,24},{24,20},{5,9},{9,5},{21,25},{25,21},{6,10},{10... | collective-permute-start | bytes 1769480 | tf_op jit(solution)/shard_map/ppermute | solution.py:78
  90.4 15.2 %collective-permute-start.15 = (bf16[576,512]{1,0:T(8,128)(2,1)}, bf16[576,512]{1,0:T(8,128)(2,1)S(1)}, u32[]{:S(2)}, u32[]{:S(2)}) collective-permute-start(bf16[576,512]{1,0:T(8,128)(2,1)} %get-tuple-element.310), channel_id=1, source_target_pairs={{0,4},{4,12},{8,0},{12,8},{16,20},{20,28},{24,16},{28,24},{1,5},{5... | collective-permute-start | bytes 1769480 | tf_op jit(solution)/shard_map/ppermute | solution.py:78
  90.5 13.9 %collective-permute-start.13 = (bf16[512,512]{1,0:T(8,128)(2,1)}, bf16[512,512]{1,0:T(8,128)(2,1)}, u32[]{:S(2)}, u32[]{:S(2)}) collective-permute-start(bf16[512,512]{1,0:T(8,128)(2,1)} %get-tuple-element.322.refs_5_.refs_11_), channel_id=1, source_target_pairs={{0,64},{32,96},{64,0},{96,32},{1,65},{33,97},{65,1},{97,33},{2,66}... | collective-permute-start | bytes 1572872 | tf_op jit(solution)/shard_map/ppermute | solution.py:48
  105.6 24.8 %collective-permute-start.17 = (bf16[512,1024]{1,0:T(8,128)(2,1)S(1)}, bf16[512,1024]{1,0:T(8,128)(2,1)}, u32[]{:S(2)}, u32[]{:S(2)}) collective-permute-start(bf16[512,1024]{1,0:T(8,128)(2,1)S(1)} %copy-done.51), channel_id=1, source_target_pairs={{0,32},{32,64},{64,96},{96,0},{1,33},{33,65},{65,97},{97,1},{2,34}... | collective-permute-start | bytes 3145736 | tf_op jit(solution)/shard_map/ppermute | solution.py:48
  106.7 23.7 %collective-permute-start.16 = (bf16[512,1024]{1,0:T(8,128)(2,1)S(1)}, bf16[512,1024]{1,0:T(8,128)(2,1)}, u32[]{:S(2)}, u32[]{:S(2)}) collective-permute-start(bf16[512,1024]{1,0:T(8,128)(2,1)S(1)} %copy-done.51), channel_id=1, source_target_pairs={{0,96},{32,0},{64,32},{96,64},{1,97},{33,1},{65,33},{97,65},{2,98}... | collective-permute-start | bytes 3145736 | tf_op jit(solution)/shard_map/ppermute | solution.py:48
  108.3 25.4 %collective-permute-start.19 = (bf16[512,1024]{1,0:T(8,128)(2,1)}, bf16[512,1024]{1,0:T(8,128)(2,1)}, u32[]{:S(2)}, u32[]{:S(2)}) collective-permute-start(bf16[512,1024]{1,0:T(8,128)(2,1)} %get-tuple-element.364.refs_19_), channel_id=1, source_target_pairs={{0,20},{4,28},{8,16},{12,24},{16,4},{20,12},{24,0},{28,8},{1,21},{... | collective-permute-start | bytes 3145736 | tf_op jit(solution)/shard_map/ppermute | solution.py:78
  111.1 23.6 %collective-permute-start.18 = (bf16[512,1024]{1,0:T(8,128)(2,1)}, bf16[512,1024]{1,0:T(8,128)(2,1)}, u32[]{:S(2)}, u32[]{:S(2)}) collective-permute-start(bf16[512,1024]{1,0:T(8,128)(2,1)} %get-tuple-element.364.refs_19_), channel_id=1, source_target_pairs={{0,16},{4,24},{8,20},{12,28},{16,0},{20,8},{24,4},{28,12},{1,17},{... | collective-permute-start | bytes 3145736 | tf_op jit(solution)/shard_map/ppermute | solution.py:78
  142.2 68.6 %all-gather.9.cloned.1.call-start = ((), (), s32[]{:S(2)}) async-start(), calls=%async_computation.7 | async-start | bytes 3538944 | tf_op jit(solution)/shard_map/all_gather | solution.py:109
  142.3 38.1 %collective-permute-start.21 = (bf16[512,1024]{1,0:T(8,128)(2,1)S(1)}, bf16[512,1024]{1,0:T(8,128)(2,1)}, u32[]{:S(2)}, u32[]{:S(2)}) collective-permute-start(bf16[512,1024]{1,0:T(8,128)(2,1)S(1)} %copy-done.52), channel_id=1, source_target_pairs={{0,64},{32,96},{64,0},{96,32},{1,65},{33,97},{65,1},{97,33},{2,66}... | collective-permute-start | bytes 3145736 | tf_op jit(solution)/shard_map/ppermute | solution.py:48
  143.3 37.0 %collective-permute-start.23 = (bf16[512,1024]{1,0:T(8,128)(2,1)}, bf16[512,1024]{1,0:T(8,128)(2,1)}, u32[]{:S(2)}, u32[]{:S(2)}) collective-permute-start(bf16[512,1024]{1,0:T(8,128)(2,1)} %get-tuple-element.364.refs_19_), channel_id=1, source_target_pairs={{0,4},{4,12},{8,0},{12,8},{16,20},{20,28},{24,16},{28,24},{1,5},{5... | collective-permute-start | bytes 3145736 | tf_op jit(solution)/shard_map/ppermute | solution.py:78
  144.0 36.4 %collective-permute-start.22 = (bf16[512,1024]{1,0:T(8,128)(2,1)}, bf16[512,1024]{1,0:T(8,128)(2,1)}, u32[]{:S(2)}, u32[]{:S(2)}) collective-permute-start(bf16[512,1024]{1,0:T(8,128)(2,1)} %get-tuple-element.364.refs_19_), channel_id=1, source_target_pairs={{4,8},{8,4},{20,24},{24,20},{5,9},{9,5},{21,25},{25,21},{6,10},{10... | collective-permute-start | bytes 3145736 | tf_op jit(solution)/shard_map/ppermute | solution.py:78
  148.4 32.0 %collective-permute-start.25 = (bf16[512,512]{1,0:T(8,128)(2,1)S(1)}, bf16[512,512]{1,0:T(8,128)(2,1)}, u32[]{:S(2)}, u32[]{:S(2)}) collective-permute-start(bf16[512,512]{1,0:T(8,128)(2,1)S(1)} %copy-done.53), channel_id=1, source_target_pairs={{0,32},{32,64},{64,96},{96,0},{1,33},{33,65},{65,97},{97,1},{2,34}... | collective-permute-start | bytes 1572872 | tf_op jit(solution)/shard_map/ppermute | solution.py:48
  148.4 31.9 %collective-permute-start.24 = (bf16[512,512]{1,0:T(8,128)(2,1)S(1)}, bf16[512,512]{1,0:T(8,128)(2,1)}, u32[]{:S(2)}, u32[]{:S(2)}) collective-permute-start(bf16[512,512]{1,0:T(8,128)(2,1)S(1)} %copy-done.53), channel_id=1, source_target_pairs={{0,96},{32,0},{64,32},{96,64},{1,97},{33,1},{65,33},{97,65},{2,98}... | collective-permute-start | bytes 1572872 | tf_op jit(solution)/shard_map/ppermute | solution.py:48
  181.4 97.8 %reduce-scatter.7.cloned.1.call-start = ((), (), s32[]{:S(2)}) async-start(), calls=%async_computation.8 | async-start | bytes 1966080 | tf_op jit(solution)/shard_map/reduce_scatter | solution.py:674
  181.4 14.6 %collective-permute-start.26 = (bf16[512,512]{1,0:T(8,128)(2,1)S(1)}, bf16[512,512]{1,0:T(8,128)(2,1)S(1)}, u32[]{:S(2)}, u32[]{:S(2)}) collective-permute-start(bf16[512,512]{1,0:T(8,128)(2,1)S(1)} %copy-done.53), channel_id=1, source_target_pairs={{0,64},{32,96},{64,0},{96,32},{1,65},{33,97},{65,1},{97,33},{2,66}... | collective-permute-start | bytes 1572872 | tf_op jit(solution)/shard_map/ppermute | solution.py:48
  182.4 13.7 %collective-permute-start.30 = (bf16[512,512]{1,0:T(8,128)(2,1)}, bf16[512,512]{1,0:T(8,128)(2,1)S(1)}, u32[]{:S(2)}, u32[]{:S(2)}) collective-permute-start(bf16[512,512]{1,0:T(8,128)(2,1)} %get-tuple-element.363.refs_20_.refs_8_), channel_id=1, source_target_pairs={{0,20},{4,28},{8,16},{12,24},{16,4},{20,12},{24,0},{28,8},{1,21},{... | collective-permute-start | bytes 1572872 | tf_op jit(solution)/shard_map/ppermute | solution.py:78
  185.0 24.4 %collective-permute-start.29 = (bf16[512,512]{1,0:T(8,128)(2,1)}, bf16[512,512]{1,0:T(8,128)(2,1)}, u32[]{:S(2)}, u32[]{:S(2)}) collective-permute-start(bf16[512,512]{1,0:T(8,128)(2,1)} %get-tuple-element.363.refs_20_.refs_8_), channel_id=1, source_target_pairs={{0,16},{4,24},{8,20},{12,28},{16,0},{20,8},{24,4},{28,12},{1,17},{... | collective-permute-start | bytes 1572872 | tf_op jit(solution)/shard_map/ppermute | solution.py:78
  186.6 23.8 %collective-permute-start.28 = (bf16[512,512]{1,0:T(8,128)(2,1)}, bf16[512,512]{1,0:T(8,128)(2,1)}, u32[]{:S(2)}, u32[]{:S(2)}) collective-permute-start(bf16[512,512]{1,0:T(8,128)(2,1)} %get-tuple-element.363.refs_20_.refs_8_), channel_id=1, source_target_pairs={{0,4},{4,12},{8,0},{12,8},{16,20},{20,28},{24,16},{28,24},{1,5},{5... | collective-permute-start | bytes 1572872 | tf_op jit(solution)/shard_map/ppermute | solution.py:78
  186.9 23.9 %collective-permute-start.27 = (bf16[512,512]{1,0:T(8,128)(2,1)}, bf16[512,512]{1,0:T(8,128)(2,1)}, u32[]{:S(2)}, u32[]{:S(2)}) collective-permute-start(bf16[512,512]{1,0:T(8,128)(2,1)} %get-tuple-element.363.refs_20_.refs_8_), channel_id=1, source_target_pairs={{4,8},{8,4},{20,24},{24,20},{5,9},{9,5},{21,25},{25,21},{6,10},{10... | collective-permute-start | bytes 1572872 | tf_op jit(solution)/shard_map/ppermute | solution.py:78
  245.1 69.7 %all-gather.11.cloned.1.call-start = ((), (), s32[]{:S(2)}) async-start(), calls=%async_computation.9 | async-start | bytes 3538944 | tf_op jit(solution)/shard_map/all_gather | solution.py:109
  246.7 33.6 %collective-permute-start.32 = (bf16[512,1024]{1,0:T(8,128)(2,1)}, bf16[512,1024]{1,0:T(8,128)(2,1)S(1)}, u32[]{:S(2)}, u32[]{:S(2)}) collective-permute-start(bf16[512,1024]{1,0:T(8,128)(2,1)} %get-tuple-element.384), channel_id=1, source_target_pairs={{16,0},{24,4},{20,8},{28,12},{0,16},{8,20},{4,24},{12,28},{17,1},{... | collective-permute-start | bytes 3145736 | tf_op jit(solution)/shard_map/ppermute | solution.py:82
  249.9 30.4 %collective-permute-start.33 = (bf16[512,1024]{1,0:T(8,128)(2,1)}, bf16[512,1024]{1,0:T(8,128)(2,1)}, u32[]{:S(2)}, u32[]{:S(2)}) collective-permute-start(bf16[512,1024]{1,0:T(8,128)(2,1)} %get-tuple-element.385), channel_id=1, source_target_pairs={{20,0},{28,4},{16,8},{24,12},{4,16},{12,20},{0,24},{8,28},{21,1},{... | collective-permute-start | bytes 3145736 | tf_op jit(solution)/shard_map/ppermute | solution.py:82
  255.2 25.1 %collective-permute-start.35 = (bf16[512,1024]{1,0:T(8,128)(2,1)}, bf16[512,1024]{1,0:T(8,128)(2,1)}, u32[]{:S(2)}, u32[]{:S(2)}) collective-permute-start(bf16[512,1024]{1,0:T(8,128)(2,1)} %get-tuple-element.386), channel_id=1, source_target_pairs={{0,96},{32,0},{64,32},{96,64},{1,97},{33,1},{65,33},{97,65},{2,98}... | collective-permute-start | bytes 3145736 | tf_op jit(solution)/shard_map/ppermute | solution.py:48
  256.9 26.3 %collective-permute-start.34 = (bf16[512,1024]{1,0:T(8,128)(2,1)}, bf16[512,1024]{1,0:T(8,128)(2,1)}, u32[]{:S(2)}, u32[]{:S(2)}) collective-permute-start(bf16[512,1024]{1,0:T(8,128)(2,1)} %get-tuple-element.377), channel_id=1, source_target_pairs={{0,32},{32,64},{64,96},{96,0},{1,33},{33,65},{65,97},{97,1},{2,34}... | collective-permute-start | bytes 3145736 | tf_op jit(solution)/shard_map/ppermute | solution.py:48
  286.4 107.8 %reduce-scatter.9.cloned.1.call-start = ((), (), s32[]{:S(2)}) async-start(), calls=%async_computation.10 | async-start | bytes 1966080 | tf_op jit(solution)/shard_map/reduce_scatter | solution.py:756
  287.5 26.4 %collective-permute-start.37 = (bf16[512,1024]{1,0:T(8,128)(2,1)}, bf16[512,1024]{1,0:T(8,128)(2,1)S(1)}, u32[]{:S(2)}, u32[]{:S(2)}) collective-permute-start(bf16[512,1024]{1,0:T(8,128)(2,1)} %get-tuple-element.402), channel_id=1, source_target_pairs={{0,64},{32,96},{64,0},{96,32},{1,65},{33,97},{65,1},{97,33},{2,66}... | collective-permute-start | bytes 3145736 | tf_op jit(solution)/shard_map/ppermute | solution.py:48
  287.5 26.4 %collective-permute-start.39 = (bf16[512,1024]{1,0:T(8,128)(2,1)}, bf16[512,1024]{1,0:T(8,128)(2,1)}, u32[]{:S(2)}, u32[]{:S(2)}) collective-permute-start(bf16[512,1024]{1,0:T(8,128)(2,1)} %get-tuple-element.406), channel_id=1, source_target_pairs={{4,0},{12,4},{0,8},{8,12},{20,16},{28,20},{16,24},{24,28},{5,1},{1... | collective-permute-start | bytes 3145736 | tf_op jit(solution)/shard_map/ppermute | solution.py:82
  288.6 26.2 %collective-permute-start.38 = (bf16[512,1024]{1,0:T(8,128)(2,1)}, bf16[512,1024]{1,0:T(8,128)(2,1)}, u32[]{:S(2)}, u32[]{:S(2)}) collective-permute-start(bf16[512,1024]{1,0:T(8,128)(2,1)} %get-tuple-element.405.refs_16_), channel_id=1, source_target_pairs={{8,4},{4,8},{24,20},{20,24},{9,5},{5,9},{25,21},{21,25},{10,6},{6,... | collective-permute-start | bytes 3145736 | tf_op jit(solution)/shard_map/ppermute | solution.py:82
  314.8 18.5 %collective-permute-start.40 = (bf16[512,512]{1,0:T(8,128)(2,1)}, bf16[512,512]{1,0:T(8,128)(2,1)S(1)}, u32[]{:S(2)}, u32[]{:S(2)}) collective-permute-start(bf16[512,512]{1,0:T(8,128)(2,1)} %get-tuple-element.429), channel_id=1, source_target_pairs={{0,32},{32,64},{64,96},{96,0},{1,33},{33,65},{65,97},{97,1},{2,34}... | collective-permute-start | bytes 1572872 | tf_op jit(solution)/shard_map/ppermute | solution.py:48
  315.8 17.5 %collective-permute-start.41 = (bf16[512,512]{1,0:T(8,128)(2,1)}, bf16[512,512]{1,0:T(8,128)(2,1)S(1)}, u32[]{:S(2)}, u32[]{:S(2)}) collective-permute-start(bf16[512,512]{1,0:T(8,128)(2,1)} %get-tuple-element.430), channel_id=1, source_target_pairs={{0,96},{32,0},{64,32},{96,64},{1,97},{33,1},{65,33},{97,65},{2,98}... | collective-permute-start | bytes 1572872 | tf_op jit(solution)/shard_map/ppermute | solution.py:48
  317.5 15.8 %collective-permute-start.42 = (bf16[512,512]{1,0:T(8,128)(2,1)}, bf16[512,512]{1,0:T(8,128)(2,1)S(1)}, u32[]{:S(2)}, u32[]{:S(2)}) collective-permute-start(bf16[512,512]{1,0:T(8,128)(2,1)} %get-tuple-element.431), channel_id=1, source_target_pairs={{16,0},{24,4},{20,8},{28,12},{0,16},{8,20},{4,24},{12,28},{17,1},{... | collective-permute-start | bytes 1572872 | tf_op jit(solution)/shard_map/ppermute | solution.py:82
  319.0 14.3 %collective-permute-start.43 = (bf16[512,512]{1,0:T(8,128)(2,1)}, bf16[512,512]{1,0:T(8,128)(2,1)S(1)}, u32[]{:S(2)}, u32[]{:S(2)}) collective-permute-start(bf16[512,512]{1,0:T(8,128)(2,1)} %get-tuple-element.432), channel_id=1, source_target_pairs={{20,0},{28,4},{16,8},{24,12},{4,16},{12,20},{0,24},{8,28},{21,1},{... | collective-permute-start | bytes 1572872 | tf_op jit(solution)/shard_map/ppermute | solution.py:82
  334.4 18.1 %collective-permute-start.44 = (bf16[3072,256]{1,0:T(8,128)(2,1)}, bf16[3072,256]{1,0:T(8,128)(2,1)S(1)}, u32[]{:S(2)}, u32[]{:S(2)}) collective-permute-start(bf16[3072,256]{1,0:T(8,128)(2,1)} %get-tuple-element.434), channel_id=1, source_target_pairs={{0,8},{8,0},{1,9},{9,1},{2,10},{10,2},{3,11},{11,3},{4,12},{12,4},... | collective-permute-start | bytes 4718600 | tf_op jit(solution)/shard_map/ppermute | solution.py:44
  334.7 15.3 %collective-permute-start.45 = (bf16[512,512]{1,0:T(8,128)(2,1)}, bf16[512,512]{1,0:T(8,128)(2,1)S(1)}, u32[]{:S(2)}, u32[]{:S(2)}) collective-permute-start(bf16[512,512]{1,0:T(8,128)(2,1)} %get-tuple-element.446), channel_id=1, source_target_pairs={{0,64},{32,96},{64,0},{96,32},{1,65},{33,97},{65,1},{97,33},{2,66}... | collective-permute-start | bytes 1572872 | tf_op jit(solution)/shard_map/ppermute | solution.py:48
  336.6 13.4 %collective-permute-start.47 = (bf16[512,512]{1,0:T(8,128)(2,1)S(1)}, bf16[512,512]{1,0:T(8,128)(2,1)S(1)}, u32[]{:S(2)}, u32[]{:S(2)}) collective-permute-start(bf16[512,512]{1,0:T(8,128)(2,1)S(1)} %copy-done.54), channel_id=1, source_target_pairs={{4,0},{12,4},{0,8},{8,12},{20,16},{28,20},{16,24},{24,28},{5,1},{1... | collective-permute-start | bytes 1572872 | tf_op jit(solution)/shard_map/ppermute | solution.py:82
  338.9 13.6 %collective-permute-start.46 = (bf16[512,512]{1,0:T(8,128)(2,1)S(1)}, bf16[512,512]{1,0:T(8,128)(2,1)S(1)}, u32[]{:S(2)}, u32[]{:S(2)}) collective-permute-start(bf16[512,512]{1,0:T(8,128)(2,1)S(1)} %copy-done.21), channel_id=1, source_target_pairs={{8,4},{4,8},{24,20},{20,24},{9,5},{5,9},{25,21},{21,25},{10,6},{6,... | collective-permute-start | bytes 1572872 | tf_op jit(solution)/shard_map/ppermute | solution.py:82
  355.0 56.9 %reduce-scatter.11.cloned.1.call-start = ((), (), s32[]{:S(2)}) async-start(), calls=%async_computation.11 | async-start | bytes 1966080 | tf_op jit(solution)/shard_map/reduce_scatter | solution.py:816
  356.6 14.5 %collective-permute-start.50 = (bf16[512,512]{1,0:T(8,128)(2,1)}, bf16[512,512]{1,0:T(8,128)(2,1)S(1)}, u32[]{:S(2)}, u32[]{:S(2)}) collective-permute-start(bf16[512,512]{1,0:T(8,128)(2,1)} %get-tuple-element.464), channel_id=1, source_target_pairs={{0,32},{32,64},{64,96},{96,0},{1,33},{33,65},{65,97},{97,1},{2,34}... | collective-permute-start | bytes 1572872 | tf_op jit(solution)/shard_map/ppermute | solution.py:48
  356.6 14.5 %collective-permute-start.51 = (bf16[512,512]{1,0:T(8,128)(2,1)}, bf16[512,512]{1,0:T(8,128)(2,1)S(1)}, u32[]{:S(2)}, u32[]{:S(2)}) collective-permute-start(bf16[512,512]{1,0:T(8,128)(2,1)} %get-tuple-element.465), channel_id=1, source_target_pairs={{0,96},{32,0},{64,32},{96,64},{1,97},{33,1},{65,33},{97,65},{2,98}... | collective-permute-start | bytes 1572872 | tf_op jit(solution)/shard_map/ppermute | solution.py:48
  361.2 14.1 %collective-permute-start.53 = (bf16[512,512]{1,0:T(8,128)(2,1)}, bf16[512,512]{1,0:T(8,128)(2,1)S(1)}, u32[]{:S(2)}, u32[]{:S(2)}) collective-permute-start(bf16[512,512]{1,0:T(8,128)(2,1)} %get-tuple-element.467), channel_id=1, source_target_pairs={{20,0},{28,4},{16,8},{24,12},{4,16},{12,20},{0,24},{8,28},{21,1},{... | collective-permute-start | bytes 1572872 | tf_op jit(solution)/shard_map/ppermute | solution.py:82
  378.9 16.4 %collective-permute-start.54 = (bf16[512,512]{1,0:T(8,128)(2,1)}, bf16[512,512]{1,0:T(8,128)(2,1)}, u32[]{:S(2)}, u32[]{:S(2)}) collective-permute-start(bf16[512,512]{1,0:T(8,128)(2,1)} %get-tuple-element.468), channel_id=1, source_target_pairs={{0,64},{32,96},{64,0},{96,32},{1,65},{33,97},{65,1},{97,33},{2,66}... | collective-permute-start | bytes 1572872 | tf_op jit(solution)/shard_map/ppermute | solution.py:48
  379.0 16.3 %collective-permute-start.56 = (bf16[512,512]{1,0:T(8,128)(2,1)}, bf16[512,512]{1,0:T(8,128)(2,1)}, u32[]{:S(2)}, u32[]{:S(2)}) collective-permute-start(bf16[512,512]{1,0:T(8,128)(2,1)} %get-tuple-element.472), channel_id=1, source_target_pairs={{4,0},{12,4},{0,8},{8,12},{20,16},{28,20},{16,24},{24,28},{5,1},{1... | collective-permute-start | bytes 1572872 | tf_op jit(solution)/shard_map/ppermute | solution.py:82
  379.8 16.6 %collective-permute-start.55 = (bf16[512,512]{1,0:T(8,128)(2,1)S(1)}, bf16[512,512]{1,0:T(8,128)(2,1)}, u32[]{:S(2)}, u32[]{:S(2)}) collective-permute-start(bf16[512,512]{1,0:T(8,128)(2,1)S(1)} %copy-done.28), channel_id=1, source_target_pairs={{8,4},{4,8},{24,20},{20,24},{9,5},{5,9},{25,21},{21,25},{10,6},{6,... | collective-permute-start | bytes 1572872 | tf_op jit(solution)/shard_map/ppermute | solution.py:82
  404.5 15.5 %collective-permute-start.59 = (bf16[128,2048]{1,0:T(8,128)(2,1)}, bf16[128,2048]{1,0:T(8,128)(2,1)S(1)}, u32[]{:S(2)}, u32[]{:S(2)}) collective-permute-start(bf16[128,2048]{1,0:T(8,128)(2,1)} %get-tuple-element.504), channel_id=1, source_target_pairs={{0,32},{32,64},{64,96},{96,0},{1,33},{33,65},{65,97},{97,1},{2,34}... | collective-permute-start | bytes 1572872 | tf_op jit(solution)/shard_map/ppermute | solution.py:48
  404.5 15.5 %collective-permute-start.60 = (bf16[128,2048]{1,0:T(8,128)(2,1)}, bf16[128,2048]{1,0:T(8,128)(2,1)S(1)}, u32[]{:S(2)}, u32[]{:S(2)}) collective-permute-start(bf16[128,2048]{1,0:T(8,128)(2,1)} %get-tuple-element.505), channel_id=1, source_target_pairs={{0,96},{32,0},{64,32},{96,64},{1,97},{33,1},{65,33},{97,65},{2,98}... | collective-permute-start | bytes 1572872 | tf_op jit(solution)/shard_map/ppermute | solution.py:48
  422.4 15.6 %collective-permute-start.68 = (bf16[1536,256]{1,0:T(8,128)(2,1)S(1)}, bf16[1536,256]{1,0:T(8,128)(2,1)}, u32[]{:S(2)}, u32[]{:S(2)}) collective-permute-start(bf16[1536,256]{1,0:T(8,128)(2,1)S(1)} %pad_maximum_fusion), channel_id=1, source_target_pairs={{4,8},{8,4},{5,9},{9,5},{6,10},{10,6},{7,11},{11,7},{20,24},{24,20... | collective-permute-start | bytes 2359304 | tf_op jit(solution)/shard_map/ppermute | solution.py:39
  427.9 15.8 %collective-permute-start.65 = (bf16[128,2048]{1,0:T(8,128)(2,1)S(1)}, bf16[128,2048]{1,0:T(8,128)(2,1)S(1)}, u32[]{:S(2)}, u32[]{:S(2)}) collective-permute-start(bf16[128,2048]{1,0:T(8,128)(2,1)S(1)} %copy-done.12), channel_id=1, source_target_pairs={{8,4},{4,8},{24,20},{20,24},{9,5},{5,9},{25,21},{21,25},{10,6},{6,... | collective-permute-start | bytes 1572872 | tf_op jit(solution)/shard_map/ppermute | solution.py:82
  430.7 17.2 %collective-permute-start.66 = (bf16[128,2048]{1,0:T(8,128)(2,1)}, bf16[128,2048]{1,0:T(8,128)(2,1)S(1)}, u32[]{:S(2)}, u32[]{:S(2)}) collective-permute-start(bf16[128,2048]{1,0:T(8,128)(2,1)} %get-tuple-element.513), channel_id=1, source_target_pairs={{4,0},{12,4},{0,8},{8,12},{20,16},{28,20},{16,24},{24,28},{5,1},{1... | collective-permute-start | bytes 1572872 | tf_op jit(solution)/shard_map/ppermute | solution.py:82
  430.8 17.9 %collective-permute-start.67 = (bf16[128,2048]{1,0:T(8,128)(2,1)}, bf16[128,2048]{1,0:T(8,128)(2,1)S(1)}, u32[]{:S(2)}, u32[]{:S(2)}) collective-permute-start(bf16[128,2048]{1,0:T(8,128)(2,1)} %get-tuple-element.517), channel_id=1, source_target_pairs={{0,64},{32,96},{64,0},{96,32},{1,65},{33,97},{65,1},{97,33},{2,66}... | collective-permute-start | bytes 1572872 | tf_op jit(solution)/shard_map/ppermute | solution.py:48
  (74 other events, 852.1 us)
Sparse Core Ops, SparseCore 0:
  63.0 31.8 all-gather.4
  97.1 27.8 all-gather.6
  142.3 25.5 reduce-scatter.4
  181.5 28.8 all-gather.8
  245.2 25.1 reduce-scatter.6
  286.5 26.3 all-gather.10
  355.1 23.8 reduce-scatter.8
  381.4 25.8 reduce-scatter.10

commit v2 on v1

--- a/solution.py
+++ b/solution.py
@@ -147,7 +147,7 @@
     return [pl.BlockSpec(memory_space=pltpu.VMEM)] * n
 
 
-def call(body, name, inputs, outs, scratch, flops, megabytes=56, anywhere=0):
+def call(body, name, inputs, outs, scratch, flops, megabytes=56, anywhere=0, outs_anywhere=0):
     moved = sum(v.size * v.dtype.itemsize for v in inputs[1:])
     moved += sum(math.prod(s) * jnp.dtype(d).itemsize for s, d in outs)
     specs = [pl.BlockSpec(memory_space=pltpu.SMEM)] + in_vmem(len(inputs) - 1 - anywhere)
@@ -157,7 +157,7 @@
         name=name,
         out_shape=[jax.ShapeDtypeStruct(s, d) for s, d in outs],
         in_specs=specs,
-        out_specs=in_vmem(len(outs)),
+        out_specs=in_vmem(len(outs) - outs_anywhere) + [pl.BlockSpec(memory_space=pl.ANY)] * outs_anywhere,
         scratch_shapes=scratch,
         cost_estimate=pl.CostEstimate(flops=int(flops), bytes_accessed=int(moved), transcendentals=0),
         compiler_params=pltpu.CompilerParams(vmem_limit_bytes=megabytes * 2**20),
@@ -186,6 +186,49 @@
             move(b_refs[i].at[pl.ds(dy * 144, 128), pl.ds(0, 256)], w_qkv.at[rows, pl.ds(0, 256)])
             move(a_refs[dy].at[pl.ds(i * 128, 128)], w_qkv.at[rows, pl.ds(256, 512)])
     return copies
+
+
+def along_y_body(at, *refs):
+    riders, gain_one, gain_two = refs[:3]
+    tokens, cotangent, w_query, w_output, w_up, w_down, out, mixed, sem = refs[3:]
+    pairs = [
+        (w_query, out.at[pl.ds(0, 128), pl.ds(0, 256)]),
+        (w_output, out.at[pl.ds(0, 128), pl.ds(256, 256)]),
+        (w_up.at[:, pl.ds(0, 512)], out.at[pl.ds(144, 128)]),
+        (w_up.at[:, pl.ds(512, 512)], out.at[pl.ds(272, 128)]),
+        (w_down.at[:, pl.ds(512, 512)], out.at[pl.ds(400, 128)]),
+        (tokens, mixed.at[pl.ds(0, 768)]),
+        (cotangent, mixed.at[pl.ds(784, 768)]),
+    ]
+    copies = [pltpu.make_async_copy(a, b, sem.at[i]) for i, (a, b) in enumerate(pairs)]
+    for copy in copies:
+        copy.start()
+    row = lax.broadcasted_iota(jnp.int32, (16, 128), 0)
+    gains = jnp.where(row == 0, gain_one[...], jnp.where(row == 1, gain_two[...], 0.0))
+    out[128:144, :128] = gains.astype(bf16)
+    out[128:144, 128:] = jnp.zeros((16, 384), bf16)
+    mixed[768:784, :] = riders[...]
+    for copy in copies:
+        copy.wait()
+
+
+def along_x_body(at, *refs):
+    key, value, other, w_gate, w_down, out, sem = refs
+    pairs = [
+        (w_gate.at[:, pl.ds(0, 512)], out.at[pl.ds(128, 128)]),
+        (w_gate.at[:, pl.ds(512, 512)], out.at[pl.ds(256, 128)]),
+        (w_down.at[:, pl.ds(0, 512)], out.at[pl.ds(384, 128)]),
+    ]
+    copies = [pltpu.make_async_copy(a, b, sem.at[i]) for i, (a, b) in enumerate(pairs)]
+    for copy in copies:
+        copy.start()
+    odd = at[4] & 1
+    out[:128, lanes(odd, 128)] = key[...]
+    out[:128, lanes(1 - odd, 128)] = other[:, :128]
+    out[:128, lanes(2 + odd, 128)] = value[...]
+    out[:128, lanes(3 - odd, 128)] = other[:, 128:]
+    for copy in copies:
+        copy.wait()
 
 
 def pack_body(at, *refs):
@@ -332,16 +375,29 @@
 
 
 def ffn_body(at, *refs):
-    h, gains, dy = refs[:3]
+    gains, h_in, dy_in = refs[:3]
     wide_a, down_a, wide_b, down_b = [refs[3 + 4 * i : 7 + 4 * i] for i in range(4)]
     own_wide, own_down = refs[19:21]
-    a2, hid, dgate, dup, h_cols, give, keep = refs[21:28]
-    w_gate, w_up, w_down, sem = refs[28:]
+    h_cols, a2_out, hid_out, dgate_out, dup_out, give_out, keep_out = refs[21:28]
+    up_outs, gate_outs = refs[28:30], refs[30:32]
+    h, dy, a2, hid, dgate, dup, give, keep, up_0, up_1, gate_0, gate_1 = refs[32:44]
+    w_gate, w_up, w_down, sem, out_sem = refs[44:]
+    h_copy = pltpu.make_async_copy(h_in, h, out_sem.at[14])
+    h_copy.start()
     copies = []
     rows_a(wide_a, w_gate, pl.ds(0, FF), sem, copies)
     rows_b(at, own_wide, wide_b, w_up, pl.ds(0, FF), sem, copies)
     rows_a(down_a, w_down, pl.ds(0, 512), sem, copies)
     rows_b(at, own_down, down_b, w_down, pl.ds(512, 512), sem, copies)
+    copies.append(pltpu.make_async_copy(dy_in, dy, out_sem.at[15]))
+    copies[-1].start()
+    sent = []
+
+    def send(source, to):
+        sent.append(pltpu.make_async_copy(source, to, out_sem.at[len(sent)]))
+        sent[-1].start()
+
+    h_copy.wait()
     own = at[3] * 4 + at[4]
     for j in range(2):
         h_cols[:, j * 128 : (j + 1) * 128] = h[:, lanes(position(2 * own + j, at), 128)]
@@ -350,6 +406,7 @@
         value = h[rows, :].astype(f32)
         factor = lax.rsqrt(jnp.mean(value * value, axis=1, keepdims=True) + norm_epsilon)
         a2[rows, :] = (value * factor * gains[1:2, :]).astype(bf16)
+    send(a2, a2_out)
     for copy in copies:
         copy.wait()
     for half in range(2):
@@ -364,13 +421,32 @@
             hid[rows, cols] = (act * up).astype(bf16)
             dgate[rows, cols] = (grad * up * sig * (1.0 + gate * (1.0 - sig))).astype(bf16)
             dup[rows, cols] = (grad * act).astype(bf16)
-    for ref, c in ((give, 1 - at[3]), (keep, at[3])):
+    for source, to in ((hid, hid_out), (dgate, dgate_out), (dup, dup_out)):
+        send(source, to)
+    for ref, to, c in ((give, give_out, 1 - at[3]), (keep, keep_out, at[3])):
         rows = pl.ds(pl.multiple_of(c * 384, 384), 384)
         for j in range(4):
             cols = slice(j * 512, (j + 1) * 512)
             ref[:, cols] = (
                 kdot(dgate[rows, :], w_gate[cols, :], nt) + kdot(dup[rows, :], w_up[cols, :], nt)
             ).astype(bf16)
+        send(ref, to)
+    for i, ref, to in ((1, gate_0, gate_outs[0]), (3, gate_1, gate_outs[1])):
+        for j in range(2):
+            n = slice(j * 512, (j + 1) * 512)
+            ref[:, n] = kdot(a2[:, i * 512 : (i + 1) * 512], dgate[:, n], tn).astype(bf16)
+        send(ref, to)
+    for i in range(4):
+        cols = slice((i * 4 + 2) * 128, (i * 4 + 4) * 128)
+        for j in range(2):
+            n = slice(j * 512, (j + 1) * 512)
+            value = kdot(a2[:, cols], dup[:, n], tn).astype(bf16)
+            up_0[i * 128 : (i + 1) * 128, n] = value[:128]
+            up_1[i * 128 : (i + 1) * 128, n] = value[128:]
+    send(up_0, up_outs[0])
+    send(up_1, up_outs[1])
+    for copy in sent:
+        copy.wait()
 
 
 def ffn_out_body(at, hid, *refs):
@@ -389,23 +465,6 @@
             rows = slice(dz * LEN, (dz + 1) * LEN)
             for j in range(2):
                 ref[rows, lanes(at[2] ^ j, 128)] = value[:, j * 128 : (j + 1) * 128].astype(bf16)
-
-
-def weight_gate_body(blocks, at, a2, dgate, *outs):
-    for i, out in zip(blocks, outs):
-        for j in range(2):
-            n = slice(j * 512, (j + 1) * 512)
-            out[:, n] = kdot(a2[:, i * 512 : (i + 1) * 512], dgate[:, n], tn).astype(bf16)
-
-
-def weight_up_body(first, at, a2, dup, *outs):
-    for i in range(4):
-        cols = slice((i * 4 + first) * 128, (i * 4 + first + 2) * 128)
-        for j in range(2):
-            n = slice(j * 512, (j + 1) * 512)
-            value = kdot(a2[:, cols], dup[:, n], tn).astype(bf16)
-            for k in range(2):
-                outs[k][i * 128 : (i + 1) * 128, n] = value[k * 128 : (k + 1) * 128]
 
 
 def weight_rest_body(at, a2, dy, dgate, dup, hid, *outs):
@@ -564,21 +623,46 @@
     mine = core * 4 + z
 
     riders = jnp.zeros((16, HEAD), bf16).at[:3].set(segments.reshape(3, HEAD).astype(bf16))
-    gains = jnp.zeros((16, 2 * HEAD), bf16)
-    gains = gains.at[0, :128].set(gain_attn).at[1, :128].set(gain_ffn)
     hf = FF // 2
-    kv_own = jnp.concatenate([w_key, w_value], 1)
-    kv_other = kv_partner(kv_own)
-    got = swap(jnp.concatenate([tokens, riders, cotangent], 0))
-    along_y = jnp.concatenate([w_query, w_output], 1)
-    along_y = from_y(jnp.concatenate([along_y, gains, w_up[:, :hf], w_up[:, hf:], w_down[:, hf:]], 0))
     odd = z % 2 == 1
     half = HEAD // 2
-    low_kv, high_kv = jnp.where(odd, kv_other, kv_own), jnp.where(odd, kv_own, kv_other)
-    along_x = jnp.concatenate([low_kv[:, :half], high_kv[:, :half], low_kv[:, half:], high_kv[:, half:]], 1)
-    along_x = jnp.concatenate([along_x, w_gate[:, :hf], w_gate[:, hf:], w_down[:, :hf]], 0)
-    along_x = [own_or(x_in(along_x, 0, 0), along_x)] + [x_in(along_x, *flip) for flip in FLIPS[1:]]
-    got, *rest = lax.optimization_barrier((got, *along_x, *along_y))
+    kv_other = kv_partner(jnp.concatenate([w_key, w_value], 1))
+    y_rows, mixed = call(
+        along_y_body,
+        "lay_out_y",
+        [
+            at,
+            riders,
+            gain_attn.astype(f32).reshape(1, 128),
+            gain_ffn.astype(f32).reshape(1, 128),
+            tokens,
+            cotangent,
+            w_query,
+            w_output,
+            w_up,
+            w_down,
+        ],
+        [((528, 2 * HEAD), bf16), ((1552, HEAD), bf16)],
+        [pltpu.SemaphoreType.DMA((7,))],
+        0,
+        anywhere=6,
+    )
+    (x_rows,) = call(
+        along_x_body,
+        "lay_out_x",
+        [at, w_key, w_value, kv_other, w_gate, w_down],
+        [((512, 2 * HEAD), bf16)],
+        [pltpu.SemaphoreType.DMA((3,))],
+        0,
+        anywhere=2,
+    )
+    got = swap(mixed)
+    along_y = [shift(y_rows, Y, -1), shift(y_rows, Y, 1)]
+    along_x = [x_in(x_rows, *flip) for flip in FLIPS[2:]]
+    got, late_y, late_x, *rest = lax.optimization_barrier((got, y_rows, x_rows, *along_y, *along_x))
+    along_y = [y_rows, rest[0], shift(late_y, Y, 2), rest[1]]
+    along_x = [own_or(x_in(late_x, 0, 0), x_rows), x_in(late_x, *FLIPS[1]), *rest[2:]]
+    rest = lax.optimization_barrier((*along_x, *along_y))
     to_y, to_x = call(
         pack_body,
         "pack",
@@ -651,37 +735,36 @@
     hidden_own = x_mine.astype(f32) + attn_own
     hidden = team_gather(hidden_own.astype(bf16))
     wide = ((LEN, FF), bf16)
-    a2, hid, dgate, dup, h_cols, give, keep = call(
+    block = ((512, FF), bf16)
+    h_cols, a2, hid, dgate, dup, give, keep, up_2, up_3, gate_1, gate_3 = call(
         ffn_body,
         "feed_forward",
-        [at, hidden, gain_rows, dy, *wide_a, *down_a, *wide_b, *down_b, b_wide, b_down],
-        [act, wide, wide, wide, low, part, part],
+        [at, gain_rows, hidden, dy, *wide_a, *down_a, *wide_b, *down_b, b_wide, b_down],
+        [low, act, wide, wide, wide, part, part, block, block, block, block],
         [
+            *[pltpu.VMEM(*v) for v in (act, act, act, wide, wide, wide, part, part, block, block, block, block)],
             pltpu.VMEM((WIDTH, FF), bf16),
             pltpu.VMEM((WIDTH, FF), bf16),
             pltpu.VMEM((WIDTH, FF), bf16),
             pltpu.SemaphoreType.DMA((40,)),
+            pltpu.SemaphoreType.DMA((16,)),
         ],
-        10 * LEN * WIDTH * FF,
-        anywhere=18,
+        14 * LEN * WIDTH * FF,
+        anywhere=20,
+        outs_anywhere=10,
     )
     other = other_core(give)
     wide_out, stack = ((512, FF), bf16), ((4 * LEN, HEAD), bf16)
     work = 2 * LEN * WIDTH * FF
-    up_a = call(functools.partial(weight_up_body, 2), "weight_up_first", [at, a2, dup], [wide_out] * 2, [], work / 2)
-    keep, other, *up_a = lax.optimization_barrier((keep, other, *up_a))
     both = (keep.astype(f32) + other.astype(f32)).astype(bf16)
     normed_grad = lax.psum_scatter(both, Z, scatter_dimension=0, tiled=True).astype(f32)
     dgate, dup, hid = lax.optimization_barrier((dgate, dup, hid, both))[:3]
-    gate_a = call(
-        functools.partial(weight_gate_body, (1, 3)), "weight_gate_first", [at, a2, dgate], [wide_out] * 2, [], work / 2
-    )
-    got_up = [x_out(block, *flip) for block, flip in zip(up_a, FLIPS[2:])]
-    got_gate = [shift(gate_a[0], Y, 1), shift(gate_a[1], Y, 3)]
+    got_up = [x_out(up_2, *FLIPS[2]), x_out(up_3, *FLIPS[3])]
+    got_gate = [shift(gate_1, Y, 1), shift(gate_3, Y, 3)]
     rest = call(
         weight_rest_body,
         "weight_rest",
-        [at, a2, dy, after(dgate, gate_a[0]), dup, hid],
+        [at, a2, dy, dgate, dup, hid],
         [wide_out] * 4 + [((512, hf), bf16)] * 8,
         [],
         work * 2,

time: 476 us -> 472 us (level)
  waiting for transfers between devices: 153 us -> 163 us
  starting transfers between devices: 117 us -> 108 us
    ppermute x16, starting transfers between devices: 32.4 us -> 21.8 us  [x_in(): return lax.ppermute(a, (XLO, CORE, XHI), x_pairs(flip_lo, flip_core, False))]
  transfers between devices with their start and end apart: 79 -> 79, of which waited for: 31 -> 31; matrix products, arithmetic and copies ran while one was open for 7% -> 4% of each run, Pallas kernels for 21% -> 20%
where the time goes in v2:
time: 472 us; the launch traced here: 463 us
  waiting for transfers between devices  163 us (35%)
  Pallas kernels  126 us (27%)
  starting transfers between devices  108 us (23%)
  other arithmetic  34.5 us (7%)
  between operations  17.2 us (4%)
  local copies, waits for them, and re-layouts  13.6 us (3%)
    pallas_call x14, Pallas kernels, call(): pl.pallas_call(body, name=name, out_shape=[jax.ShapeDtypeStruct(s, d) for...  126 us
    ppermute x24, waiting for transfers between devices, shift(): return lax.ppermute(a, axis, [(i, (i + by) % 4) for i in range(4)])  63.1 us
    ppermute x16, waiting for transfers between devices, x_in(): return lax.ppermute(a, (XLO, CORE, XHI), x_pairs(flip_lo, flip_core, False))  43.5 us
    ppermute x24, starting transfers between devices, shift(): return lax.ppermute(a, axis, [(i, (i + by) % 4) for i in range(4)])  34.4 us
    ppermute x16, starting transfers between devices, x_out(): return lax.ppermute(a, (XLO, CORE, XHI), x_pairs(flip_lo, flip_core, True))  28.8 us
    ppermute x16, starting transfers between devices, x_in(): return lax.ppermute(a, (XLO, CORE, XHI), x_pairs(flip_lo, flip_core, False))  21.8 us
    ppermute x16, waiting for transfers between devices, x_out(): return lax.ppermute(a, (XLO, CORE, XHI), x_pairs(flip_lo, flip_core, True))  19.2 us
    ppermute x2, waiting for transfers between devices, x_ring(): return lax.ppermute(a, (XLO, XHI), [(i, i ^ mask) for i in range(4)])  13.6 us
  transfers between devices with their start and end apart: 79, of which 31 were waited for; matrix products, arithmetic and copies ran while one was open for 4% of the time, Pallas kernels for 20%

profile of v2, /device:TPU:1, one launch (start us, length us, event | category | flops | bytes accessed | tf_op | source)
XLA Modules:
  0.0 463.3 jit_solution(5999353555165530244)
XLA Ops:
  10.4 3.3 lay_out_y.1
  13.8 6.2 %collective-permute-start = (bf16[1552,256]{1,0:T(8,128)(2,1)}, bf16[1552,256]{1,0:T(8,128)(2,1)S(1)}, u32[]{:S(2)}, u32[]{:S(2)}) collective-permute-start(bf16[1552,256]{1,0:T(8,128)(2,1)} %get-tuple-element.275), channel_id=1, source_target_pairs={{4,8},{8,4},{5,9},{9,5},{6,10},{10,6},{7,11},{11,7},{20,24},{24,20... | collective-permute-start | bytes 2383880 | tf_op jit(solution)/shard_map/ppermute | solution.py:39
  25.8 2.7 lay_out_x.1
  30.2 4.6 collective-permute-done.3.refs_7_
  35.5 7.6 %collective-permute-done.5.refs_3_ = bf16[512,512]{1,0:T(8,128)(2,1)} collective-permute-done((bf16[512,512]{1,0:T(8,128)(2,1)}, bf16[512,512]{1,0:T(8,128)(2,1)}, u32[]{:S(2)}, u32[]{:S(2)}) %collective-permute-start.5) | collective-permute-done | bytes 524320 | tf_op jit(solution)/shard_map/ppermute | solution.py:78
  44.8 2.6 collective-permute-start.6
  47.4 3.0 collective-permute-start.8
  50.4 9.0 %collective-permute-done.6 = bf16[512,512]{1,0:T(8,128)(2,1)S(1)} collective-permute-done((bf16[512,512]{1,0:T(8,128)(2,1)}, bf16[512,512]{1,0:T(8,128)(2,1)S(1)}, u32[]{:S(2)}, u32[]{:S(2)}) %collective-permute-start.6) | collective-permute-done | bytes 524320 | tf_op jit(solution)/shard_map/ppermute | solution.py:78
  60.3 2.4 collective-permute-done.7.refs_1_
  64.3 3.0 pack.1
  67.5 2.1 collective-permute-start.11
  70.0 2.3 collective-permute-start.9
  72.3 11.9 %collective-permute-done.10.refs_8_.refs_14_ = bf16[512,512]{1,0:T(8,128)(2,1)S(1)} collective-permute-done((bf16[512,512]{1,0:T(8,128)(2,1)}, bf16[512,512]{1,0:T(8,128)(2,1)S(1)}, u32[]{:S(2)}, u32[]{:S(2)}) %collective-permute-start.10) | collective-permute-done | bytes 524320 | tf_op jit(solution)/shard_map/ppermute | solution.py:48
  84.3 2.3 collective-permute-start.14
  87.0 2.8 collective-permute-start.13
  89.8 2.5 multiply_sine_fusion
  92.3 4.7 %riders.1 = (bf16[512,1024]{1,0:T(8,128)(2,1)}, bf16[512,1024]{1,0:T(8,128)(2,1)}, bf16[512,512]{1,0:T(8,128)(2,1)}, bf16[512,512]{1,0:T(8,128)(2,1)}) custom-call(s32[5]{0:T(128)} %stack.74.at, bf16[512,512]{1,0:T(8,128)(2,1)} %broadcast_select_fusion.3.refs_0_, bf16[512,512]{1,0:T(8,128)(2,1)} %copy-done.5, ...), custom_call_target="tpu_custom_call" | custom-call | bytes 7405568 | tf_op jit(solution)/shard_map/riders/pallas_call | solution.py:155
  97.0 6.2 %collective-permute-done.14 = bf16[576,512]{1,0:T(8,128)(2,1)S(1)} collective-permute-done((bf16[576,512]{1,0:T(8,128)(2,1)}, bf16[576,512]{1,0:T(8,128)(2,1)S(1)}, u32[]{:S(2)}, u32[]{:S(2)}) %collective-permute-start.14) | collective-permute-done | bytes 589856 | tf_op jit(solution)/shard_map/ppermute | solution.py:78
  104.6 2.7 collective-permute-start.16
  110.6 15.7 %attention_forward.1 = (bf16[768,2048]{1,0:T(8,128)(2,1)}, f32[768,1]{1,0:T(8,128)}, bf16[96,2048]{1,0:T(8,128)(2,1)}, bf16[768,256]{1,0:T(8,128)(2,1)}, bf16[76...) custom-call(s32[5]{0:T(128)} %stack.74.at, ...), custom_call_target="tpu_custom_call" | custom-call | flops 3221225472 | bytes 16728064 | tf_op jit(solution)/shard_map/attention_forward/pallas_call | solution.py:155
  126.3 3.7 collective-permute-done.17.refs_6_
  131.2 2.5 collective-permute-done.18.refs_13_
  133.7 3.6 collective-permute-done.20
  137.3 3.0 add_convert_fusion.3
  141.7 3.7 collective-permute-start.22
  148.2 4.8 %order_upstream.1.refs_2_.dy = bf16[768,2048]{1,0:T(8,128)(2,1)} custom-call(s32[5]{0:T(128)} %stack.74.at, bf16[6144,256]{1,0:T(8,128)(2,1)} %all-gather.7.cloned.1.call-done.whole), custom_call_target="tpu_custom_call" | custom-call | bytes 6291456 | tf_op jit(solution)/shard_map/order_upstream/pallas_call | solution.py:155
  153.0 12.5 %reduce-scatter.5.cloned.1.call-done = bf16[96,2048]{1,0:T(8,128)(2,1)} async-done(((bf16[384,2048]{1,0:T(8,128)(2,1)}), bf16[96,2048]{1,0:T(8,128)(2,1)}) %reduce-scatter.5.cloned.1.call-update) | async-done | bytes 393232 | tf_op jit(solution)/shard_map/reduce_scatter | solution.py:114
  166.6 11.9 %collective-permute-done.25.refs_10_.refs_3_ = bf16[512,512]{1,0:T(8,128)(2,1)} collective-permute-done((bf16[512,512]{1,0:T(8,128)(2,1)S(1)}, bf16[512,512]{1,0:T(8,128)(2,1)}, u32[]{:S(2)}, u32[]{:S(2)}) %collective-permute-start.25) | collective-permute-done | bytes 524320 | tf_op jit(solution)/shard_map/ppermute | solution.py:48
  184.3 2.7 collective-permute-start.27
  187.0 7.2 %collective-permute-done.26.refs_9_.refs_2_ = bf16[512,512]{1,0:T(8,128)(2,1)S(1)} collective-permute-done((bf16[512,512]{1,0:T(8,128)(2,1)S(1)}, bf16[512,512]{1,0:T(8,128)(2,1)S(1)}, u32[]{:S(2)}, u32[]{:S(2)}) %collective-permute-start.26) | collective-permute-done | bytes 524320 | tf_op jit(solution)/shard_map/ppermute | solution.py:48
  194.2 12.4 %collective-permute-done.29.refs_17_.refs_6_ = bf16[512,512]{1,0:T(8,128)(2,1)} collective-permute-done((bf16[512,512]{1,0:T(8,128)(2,1)}, bf16[512,512]{1,0:T(8,128)(2,1)}, u32[]{:S(2)}, u32[]{:S(2)}) %collective-permute-start.29) | collective-permute-done | bytes 524320 | tf_op jit(solution)/shard_map/ppermute | solution.py:78
  208.2 31.0 %feed_forward.1 = (bf16[768,256]{1,0:T(8,128)(2,1)}, bf16[768,2048]{1,0:T(8,128)(2,1)}, bf16[768,1024]{1,0:T(8,128)(2,1)}, bf16[768,1024]{1,0:T(8,128)(2,1)}, bf...) custom-call(s32[5]{0:T(128)} %stack.74.at, ...), custom_call_target="tpu_custom_call" | custom-call | flops 22548578304 | bytes 36110336 | tf_op jit(solution)/shard_map/feed_forward/pallas_call | solution.py:155
  239.6 3.4 collective-permute-done.31
  243.0 3.1 add_convert_fusion.2
  247.7 3.4 collective-permute-start.32
  251.8 2.2 collective-permute-start.35
  254.4 13.1 %weight_rest.1 = (bf16[512,1024]{1,0:T(8,128)(2,1)}, bf16[512,1024]{1,0:T(8,128)(2,1)}, bf16[512,1024]{1,0:T(8,128)(2,1)}, bf16[512,1024]{1,0:T(8,128)(2,1)}, bf...) custom-call(s32[5]{0:T(128)} %stack.74.at, ...), custom_call_target="tpu_custom_call" | custom-call | flops 6442450944 | bytes 19398656 | tf_op jit(solution)/shard_map/weight_rest/pallas_call | solution.py:155
  267.5 8.7 %feed_forward_out.1 = (bf16[3072,256]{1,0:T(8,128)(2,1)}, bf16[3072,256]{1,0:T(8,128)(2,1)}) custom-call(s32[5]{0:T(128)} %stack.74.at, bf16[768,1024]{1,0:T(8,128)(2,1)} %get-tuple-element.362.hid, bf16[512,512]{1,0:T(8,128)(2,1)} %get-tuple-element.343.refs_7_.refs_0_, bf16[512,512]{1,0:T(8,128)(2,1)} %collective-permute-done.24.refs_8_.refs_1_, ...), custom_call_target="tpu_custom_call" | custom-call | flops 3221225472 | bytes 9437184 | tf_op jit(solution)/shard_map/feed_forward_out/pallas_call | solution.py:155
  278.4 2.3 subtract_convert_fusion.1
  281.2 2.3 collective-permute-start.37
  284.6 4.2 collective-permute-start.38
  290.6 16.9 %collective-permute-done.37.refs_1_ = bf16[512,1024]{1,0:T(8,128)(2,1)S(1)} collective-permute-done((bf16[512,1024]{1,0:T(8,128)(2,1)}, bf16[512,1024]{1,0:T(8,128)(2,1)S(1)}, u32[]{:S(2)}, u32[]{:S(2)}) %collective-permute-start.37) | collective-permute-done | bytes 1048608 | tf_op jit(solution)/shard_map/ppermute | solution.py:48
  307.5 3.5 collective-permute-done.38.refs_8_
  315.8 14.0 %attention_backward.1 = (bf16[768,256]{1,0:T(8,128)(2,1)}, bf16[768,768]{1,0:T(8,128)(2,1)}, f32[768,1]{1,0:T(8,128)}, f32[1,2048]{1,0:T(1,128)}, bf16[3072,256]{1,0:T(8,128)(2,1)}, /*index=5*/bf16[3072,256]{1,0:T(8,128)(2,1)}) custom-call(s32[5]{0:T(128)} %stack.74.at, bf16[768,2048]{1,0:T(8,128)(2,1)} %all-gather.11.cloned.1.call-done.refs_0_.db, ...), custom_call_target="tpu_custom_call" | custom-call | flops 3221225472 | bytes 17518592 | tf_op jit(solution)/shard_map/attention_backward/pallas_call | solution.py:155
  334.0 4.4 collective-permute-start.46
  338.4 8.0 %attention_weights.1 = (bf16[512,512]{1,0:T(8,128)(2,1)}, bf16[512,512]{1,0:T(8,128)(2,1)}, bf16[512,512]{1,0:T(8,128)(2,1)}, bf16[512,512]{1,0:T(8,128)(2,1)}, ...) custom-call(s32[5]{0:T(128)} %stack.74.at, ...), custom_call_target="tpu_custom_call" | custom-call | flops 3221225472 | bytes 12058624 | tf_op jit(solution)/shard_map/attention_weights/pallas_call | solution.py:155
  346.4 2.5 collective-permute-done.46.refs_12_
  353.4 2.6 collective-permute-start.51
  358.4 3.1 collective-permute-done.49
  361.5 6.1 %collective-permute-done.50.refs_4_ = bf16[512,512]{1,0:T(8,128)(2,1)S(1)} collective-permute-done((bf16[512,512]{1,0:T(8,128)(2,1)}, bf16[512,512]{1,0:T(8,128)(2,1)S(1)}, u32[]{:S(2)}, u32[]{:S(2)}) %collective-permute-start.50) | collective-permute-done | bytes 524320 | tf_op jit(solution)/shard_map/ppermute | solution.py:48
  367.6 4.1 collective-permute-done.53.refs_9_
  374.9 5.7 %collective-permute-start.55 = (bf16[512,512]{1,0:T(8,128)(2,1)S(1)}, bf16[512,512]{1,0:T(8,128)(2,1)}, u32[]{:S(2)}, u32[]{:S(2)}) collective-permute-start(bf16[512,512]{1,0:T(8,128)(2,1)S(1)} %copy-done.27), channel_id=1, source_target_pairs={{8,4},{4,8},{24,20},{20,24},{9,5},{5,9},{25,21},{21,25},{10,6},{6,... | collective-permute-start | bytes 1572872 | tf_op jit(solution)/shard_map/ppermute | solution.py:82
  381.6 8.0 %feed_forward_sums.1 = (bf16[512,1536]{1,0:T(8,128)(2,1)}, bf16[512,1536]{1,0:T(8,128)(2,1)}) custom-call(s32[5]{0:T(128)} %stack.74.at, bf16[512,1024]{1,0:T(8,128)(2,1)} %get-tuple-element.457.refs_0_, bf16[512,1024]{1,0:T(8,128)(2,1)} %copy-done.9, bf16[512,1024]{1,0:T(8,128)(2,1)} %collective-permute-done.34.refs_2_, ...), custom_call_target="tpu_custom_call" | custom-call | bytes 17301504 | tf_op jit(solution)/shard_map/feed_forward_sums/pallas_call | solution.py:155
  391.3 2.2 collective-permute-start.63
  393.5 5.5 %join_sums.1 = (bf16[128,2048]{1,0:T(8,128)(2,1)}, bf16[128,2048]{1,0:T(8,128)(2,1)}, bf16[128,2048]{1,0:T(8,128)(2,1)}, bf16[128,2048]{1,0:T(8,128)(2,1)}, bf16...) custom-call(s32[5]{0:T(128)} %stack.74.at, ...), custom_call_target="tpu_custom_call" | custom-call | bytes 12058624 | tf_op jit(solution)/shard_map/join_sums/pallas_call | solution.py:155
  399.0 2.7 collective-permute-start.60
  403.0 3.0 collective-permute-start.64
  407.4 7.1 %collective-permute-done.64 = f32[40,128]{1,0:T(8,128)S(1)} collective-permute-done((f32[40,128]{1,0:T(8,128)S(1)}, f32[40,128]{1,0:T(8,128)S(1)}, u32[]{:S(2)}, u32[]{:S(2)}) %collective-permute-start.64) | collective-permute-done | bytes 20512 | tf_op jit(solution)/shard_map/ppermute | solution.py:101
  416.9 5.6 %collective-permute-start.68 = (bf16[1536,256]{1,0:T(8,128)(2,1)S(1)}, bf16[1536,256]{1,0:T(8,128)(2,1)}, u32[]{:S(2)}, u32[]{:S(2)}) collective-permute-start(bf16[1536,256]{1,0:T(8,128)(2,1)S(1)} %pad_maximum_fusion), channel_id=1, source_target_pairs={{4,8},{8,4},{5,9},{9,5},{6,10},{10,6},{7,11},{11,7},{20,24},{24,20... | collective-permute-start | bytes 2359304 | tf_op jit(solution)/shard_map/ppermute | solution.py:39
  422.9 2.8 collective-permute-start.65
  426.5 6.4 %collective-permute-done.69 = f32[40,128]{1,0:T(8,128)S(1)} collective-permute-done((f32[40,128]{1,0:T(8,128)S(1)}, f32[40,128]{1,0:T(8,128)S(1)}, u32[]{:S(2)}, u32[]{:S(2)}) %collective-permute-start.69) | collective-permute-done | bytes 20512 | tf_op jit(solution)/shard_map/ppermute | solution.py:101
  434.4 4.1 collective-permute-done.65.refs_1_
  439.2 3.7 collective-permute-done.66.refs_2_
  451.2 3.7 finish.1
  (307 shorter events, 81.2 us)
Async XLA Ops:
  7.2 96.9 %all-gather.5.cloned.1.call-start = ((), (), s32[]{:S(2)}) async-start(), calls=%async_computation.4 | async-start | bytes 3538944 | tf_op jit(solution)/shard_map/all_gather | solution.py:109
  13.8 16.3 %collective-permute-start = (bf16[1552,256]{1,0:T(8,128)(2,1)}, bf16[1552,256]{1,0:T(8,128)(2,1)S(1)}, u32[]{:S(2)}, u32[]{:S(2)}) collective-permute-start(bf16[1552,256]{1,0:T(8,128)(2,1)} %get-tuple-element.275), channel_id=1, source_target_pairs={{4,8},{8,4},{5,9},{9,5},{6,10},{10,6},{7,11},{11,7},{20,24},{24,20... | collective-permute-start | bytes 2383880 | tf_op jit(solution)/shard_map/ppermute | solution.py:39
  22.4 12.3 %collective-permute-start.3 = (bf16[528,512]{1,0:T(8,128)(2,1)}, bf16[528,512]{1,0:T(8,128)(2,1)S(1)}, u32[]{:S(2)}, u32[]{:S(2)}) collective-permute-start(bf16[528,512]{1,0:T(8,128)(2,1)} %get-tuple-element.288.refs_4_), channel_id=1, source_target_pairs={{0,32},{32,64},{64,96},{96,0},{1,33},{33,65},{65,97},{97,1},{2,34}... | collective-permute-start | bytes 1622024 | tf_op jit(solution)/shard_map/ppermute | solution.py:48
  28.6 14.6 %collective-permute-start.5 = (bf16[512,512]{1,0:T(8,128)(2,1)}, bf16[512,512]{1,0:T(8,128)(2,1)}, u32[]{:S(2)}, u32[]{:S(2)}) collective-permute-start(bf16[512,512]{1,0:T(8,128)(2,1)} %lay_out_x.1), channel_id=1, source_target_pairs={{0,20},{4,28},{8,16},{12,24},{16,4},{20,12},{24,0},{28,8},{1,21},{... | collective-permute-start | bytes 1572872 | tf_op jit(solution)/shard_map/ppermute | solution.py:78
  28.6 15.2 %collective-permute-start.4 = (bf16[512,512]{1,0:T(8,128)(2,1)}, bf16[512,512]{1,0:T(8,128)(2,1)}, u32[]{:S(2)}, u32[]{:S(2)}) collective-permute-start(bf16[512,512]{1,0:T(8,128)(2,1)} %lay_out_x.1), channel_id=1, source_target_pairs={{0,16},{4,24},{8,20},{12,28},{16,0},{20,8},{24,4},{28,12},{1,17},{... | collective-permute-start | bytes 1572872 | tf_op jit(solution)/shard_map/ppermute | solution.py:78
  44.8 81.5 %all-gather.7.cloned.1.call-start = ((), (), s32[]{:S(2)}) async-start(), calls=%async_computation.5 | async-start | bytes 3538944 | tf_op jit(solution)/shard_map/all_gather | solution.py:109
  44.8 14.6 %collective-permute-start.6 = (bf16[512,512]{1,0:T(8,128)(2,1)}, bf16[512,512]{1,0:T(8,128)(2,1)S(1)}, u32[]{:S(2)}, u32[]{:S(2)}) collective-permute-start(bf16[512,512]{1,0:T(8,128)(2,1)} %lay_out_x.1), channel_id=1, source_target_pairs={{4,8},{8,4},{20,24},{24,20},{5,9},{9,5},{21,25},{25,21},{6,10},{10... | collective-permute-start | bytes 1572872 | tf_op jit(solution)/shard_map/ppermute | solution.py:78
  47.4 15.3 %collective-permute-start.8 = (bf16[528,512]{1,0:T(8,128)(2,1)S(1)}, bf16[528,512]{1,0:T(8,128)(2,1)S(1)}, u32[]{:S(2)}, u32[]{:S(2)}) collective-permute-start(bf16[528,512]{1,0:T(8,128)(2,1)S(1)} %copy-done.1), channel_id=1, source_target_pairs={{0,64},{32,96},{64,0},{96,32},{1,65},{33,97},{65,1},{97,33},{2,66}... | collective-permute-start | bytes 1622024 | tf_op jit(solution)/shard_map/ppermute | solution.py:48
  67.4 98.1 %reduce-scatter.5.cloned.1.call-start = ((), (), s32[]{:S(2)}) async-start(), calls=%async_computation.6 | async-start | bytes 1966080 | tf_op jit(solution)/shard_map/reduce_scatter | solution.py:114
  67.4 16.8 %collective-permute-start.12 = (bf16[576,512]{1,0:T(8,128)(2,1)}, bf16[576,512]{1,0:T(8,128)(2,1)S(1)}, u32[]{:S(2)}, u32[]{:S(2)}) collective-permute-start(bf16[576,512]{1,0:T(8,128)(2,1)} %get-tuple-element.297), channel_id=1, source_target_pairs={{0,20},{4,28},{8,16},{12,24},{16,4},{20,12},{24,0},{28,8},{1,21},{... | collective-permute-start | bytes 1769480 | tf_op jit(solution)/shard_map/ppermute | solution.py:78
  67.5 16.8 %collective-permute-start.11 = (bf16[576,512]{1,0:T(8,128)(2,1)}, bf16[576,512]{1,0:T(8,128)(2,1)S(1)}, u32[]{:S(2)}, u32[]{:S(2)}) collective-permute-start(bf16[576,512]{1,0:T(8,128)(2,1)} %get-tuple-element.297), channel_id=1, source_target_pairs={{0,16},{4,24},{8,20},{12,28},{16,0},{20,8},{24,4},{28,12},{1,17},{... | collective-permute-start | bytes 1769480 | tf_op jit(solution)/shard_map/ppermute | solution.py:78
  69.6 14.6 %collective-permute-start.10 = (bf16[512,512]{1,0:T(8,128)(2,1)}, bf16[512,512]{1,0:T(8,128)(2,1)S(1)}, u32[]{:S(2)}, u32[]{:S(2)}) collective-permute-start(bf16[512,512]{1,0:T(8,128)(2,1)} %get-tuple-element.309.refs_5_.refs_11_), channel_id=1, source_target_pairs={{0,32},{32,64},{64,96},{96,0},{1,33},{33,65},{65,97},{97,1},{2,34}... | collective-permute-start | bytes 1572872 | tf_op jit(solution)/shard_map/ppermute | solution.py:48
  70.0 14.2 %collective-permute-start.9 = (bf16[512,512]{1,0:T(8,128)(2,1)}, bf16[512,512]{1,0:T(8,128)(2,1)S(1)}, u32[]{:S(2)}, u32[]{:S(2)}) collective-permute-start(bf16[512,512]{1,0:T(8,128)(2,1)} %get-tuple-element.309.refs_5_.refs_11_), channel_id=1, source_target_pairs={{0,96},{32,0},{64,32},{96,64},{1,97},{33,1},{65,33},{97,65},{2,98}... | collective-permute-start | bytes 1572872 | tf_op jit(solution)/shard_map/ppermute | solution.py:48
  84.3 18.9 %collective-permute-start.14 = (bf16[576,512]{1,0:T(8,128)(2,1)}, bf16[576,512]{1,0:T(8,128)(2,1)S(1)}, u32[]{:S(2)}, u32[]{:S(2)}) collective-permute-start(bf16[576,512]{1,0:T(8,128)(2,1)} %get-tuple-element.297), channel_id=1, source_target_pairs={{4,8},{8,4},{20,24},{24,20},{5,9},{9,5},{21,25},{25,21},{6,10},{10... | collective-permute-start | bytes 1769480 | tf_op jit(solution)/shard_map/ppermute | solution.py:78
  87.0 17.1 %collective-permute-start.15 = (bf16[576,512]{1,0:T(8,128)(2,1)}, bf16[576,512]{1,0:T(8,128)(2,1)S(1)}, u32[]{:S(2)}, u32[]{:S(2)}) collective-permute-start(bf16[576,512]{1,0:T(8,128)(2,1)} %get-tuple-element.297), channel_id=1, source_target_pairs={{0,4},{4,12},{8,0},{12,8},{16,20},{20,28},{24,16},{28,24},{1,5},{5... | collective-permute-start | bytes 1769480 | tf_op jit(solution)/shard_map/ppermute | solution.py:78
  87.0 17.0 %collective-permute-start.13 = (bf16[512,512]{1,0:T(8,128)(2,1)}, bf16[512,512]{1,0:T(8,128)(2,1)}, u32[]{:S(2)}, u32[]{:S(2)}) collective-permute-start(bf16[512,512]{1,0:T(8,128)(2,1)} %get-tuple-element.309.refs_5_.refs_11_), channel_id=1, source_target_pairs={{0,64},{32,96},{64,0},{96,32},{1,65},{33,97},{65,1},{97,33},{2,66}... | collective-permute-start | bytes 1572872 | tf_op jit(solution)/shard_map/ppermute | solution.py:48
  104.6 25.4 %collective-permute-start.17 = (bf16[512,1024]{1,0:T(8,128)(2,1)S(1)}, bf16[512,1024]{1,0:T(8,128)(2,1)}, u32[]{:S(2)}, u32[]{:S(2)}) collective-permute-start(bf16[512,1024]{1,0:T(8,128)(2,1)S(1)} %copy-done.51), channel_id=1, source_target_pairs={{0,32},{32,64},{64,96},{96,0},{1,33},{33,65},{65,97},{97,1},{2,34}... | collective-permute-start | bytes 3145736 | tf_op jit(solution)/shard_map/ppermute | solution.py:48
  104.6 25.4 %collective-permute-start.16 = (bf16[512,1024]{1,0:T(8,128)(2,1)S(1)}, bf16[512,1024]{1,0:T(8,128)(2,1)}, u32[]{:S(2)}, u32[]{:S(2)}) collective-permute-start(bf16[512,1024]{1,0:T(8,128)(2,1)S(1)} %copy-done.51), channel_id=1, source_target_pairs={{0,96},{32,0},{64,32},{96,64},{1,97},{33,1},{65,33},{97,65},{2,98}... | collective-permute-start | bytes 3145736 | tf_op jit(solution)/shard_map/ppermute | solution.py:48
  107.3 23.9 %collective-permute-start.19 = (bf16[512,1024]{1,0:T(8,128)(2,1)}, bf16[512,1024]{1,0:T(8,128)(2,1)}, u32[]{:S(2)}, u32[]{:S(2)}) collective-permute-start(bf16[512,1024]{1,0:T(8,128)(2,1)} %get-tuple-element.351.refs_19_), channel_id=1, source_target_pairs={{0,20},{4,28},{8,16},{12,24},{16,4},{20,12},{24,0},{28,8},{1,21},{... | collective-permute-start | bytes 3145736 | tf_op jit(solution)/shard_map/ppermute | solution.py:78
  109.1 24.7 %collective-permute-start.18 = (bf16[512,1024]{1,0:T(8,128)(2,1)}, bf16[512,1024]{1,0:T(8,128)(2,1)}, u32[]{:S(2)}, u32[]{:S(2)}) collective-permute-start(bf16[512,1024]{1,0:T(8,128)(2,1)} %get-tuple-element.351.refs_19_), channel_id=1, source_target_pairs={{0,16},{4,24},{8,20},{12,28},{16,0},{20,8},{24,4},{28,12},{1,17},{... | collective-permute-start | bytes 3145736 | tf_op jit(solution)/shard_map/ppermute | solution.py:78
  140.4 67.8 %all-gather.9.cloned.1.call-start = ((), (), s32[]{:S(2)}) async-start(), calls=%async_computation.7 | async-start | bytes 3538944 | tf_op jit(solution)/shard_map/all_gather | solution.py:109
  140.5 38.1 %collective-permute-start.21 = (bf16[512,1024]{1,0:T(8,128)(2,1)S(1)}, bf16[512,1024]{1,0:T(8,128)(2,1)}, u32[]{:S(2)}, u32[]{:S(2)}) collective-permute-start(bf16[512,1024]{1,0:T(8,128)(2,1)S(1)} %copy-done.51), channel_id=1, source_target_pairs={{0,64},{32,96},{64,0},{96,32},{1,65},{33,97},{65,1},{97,33},{2,66}... | collective-permute-start | bytes 3145736 | tf_op jit(solution)/shard_map/ppermute | solution.py:48
  141.2 37.3 %collective-permute-start.23 = (bf16[512,1024]{1,0:T(8,128)(2,1)}, bf16[512,1024]{1,0:T(8,128)(2,1)}, u32[]{:S(2)}, u32[]{:S(2)}) collective-permute-start(bf16[512,1024]{1,0:T(8,128)(2,1)} %get-tuple-element.351.refs_19_), channel_id=1, source_target_pairs={{0,4},{4,12},{8,0},{12,8},{16,20},{20,28},{24,16},{28,24},{1,5},{5... | collective-permute-start | bytes 3145736 | tf_op jit(solution)/shard_map/ppermute | solution.py:78
  141.7 36.9 %collective-permute-start.22 = (bf16[512,1024]{1,0:T(8,128)(2,1)}, bf16[512,1024]{1,0:T(8,128)(2,1)}, u32[]{:S(2)}, u32[]{:S(2)}) collective-permute-start(bf16[512,1024]{1,0:T(8,128)(2,1)} %get-tuple-element.351.refs_19_), channel_id=1, source_target_pairs={{4,8},{8,4},{20,24},{24,20},{5,9},{9,5},{21,25},{25,21},{6,10},{10... | collective-permute-start | bytes 3145736 | tf_op jit(solution)/shard_map/ppermute | solution.py:78
  145.4 33.1 %collective-permute-start.25 = (bf16[512,512]{1,0:T(8,128)(2,1)S(1)}, bf16[512,512]{1,0:T(8,128)(2,1)}, u32[]{:S(2)}, u32[]{:S(2)}) collective-permute-start(bf16[512,512]{1,0:T(8,128)(2,1)S(1)} %copy-done.54), channel_id=1, source_target_pairs={{0,32},{32,64},{64,96},{96,0},{1,33},{33,65},{65,97},{97,1},{2,34}... | collective-permute-start | bytes 1572872 | tf_op jit(solution)/shard_map/ppermute | solution.py:48
  146.6 31.9 %collective-permute-start.24 = (bf16[512,512]{1,0:T(8,128)(2,1)S(1)}, bf16[512,512]{1,0:T(8,128)(2,1)}, u32[]{:S(2)}, u32[]{:S(2)}) collective-permute-start(bf16[512,512]{1,0:T(8,128)(2,1)S(1)} %copy-done.54), channel_id=1, source_target_pairs={{0,96},{32,0},{64,32},{96,64},{1,97},{33,1},{65,33},{97,65},{2,98}... | collective-permute-start | bytes 1572872 | tf_op jit(solution)/shard_map/ppermute | solution.py:48
  179.6 96.7 %reduce-scatter.7.cloned.1.call-start = ((), (), s32[]{:S(2)}) async-start(), calls=%async_computation.8 | async-start | bytes 1966080 | tf_op jit(solution)/shard_map/reduce_scatter | solution.py:760
  179.6 14.6 %collective-permute-start.26 = (bf16[512,512]{1,0:T(8,128)(2,1)S(1)}, bf16[512,512]{1,0:T(8,128)(2,1)S(1)}, u32[]{:S(2)}, u32[]{:S(2)}) collective-permute-start(bf16[512,512]{1,0:T(8,128)(2,1)S(1)} %copy-done.54), channel_id=1, source_target_pairs={{0,64},{32,96},{64,0},{96,32},{1,65},{33,97},{65,1},{97,33},{2,66}... | collective-permute-start | bytes 1572872 | tf_op jit(solution)/shard_map/ppermute | solution.py:48
  180.4 13.9 %collective-permute-start.30 = (bf16[512,512]{1,0:T(8,128)(2,1)}, bf16[512,512]{1,0:T(8,128)(2,1)S(1)}, u32[]{:S(2)}, u32[]{:S(2)}) collective-permute-start(bf16[512,512]{1,0:T(8,128)(2,1)} %get-tuple-element.350.refs_20_.refs_8_), channel_id=1, source_target_pairs={{0,20},{4,28},{8,16},{12,24},{16,4},{20,12},{24,0},{28,8},{1,21},{... | collective-permute-start | bytes 1572872 | tf_op jit(solution)/shard_map/ppermute | solution.py:78
  181.9 24.7 %collective-permute-start.29 = (bf16[512,512]{1,0:T(8,128)(2,1)}, bf16[512,512]{1,0:T(8,128)(2,1)}, u32[]{:S(2)}, u32[]{:S(2)}) collective-permute-start(bf16[512,512]{1,0:T(8,128)(2,1)} %get-tuple-element.350.refs_20_.refs_8_), channel_id=1, source_target_pairs={{0,16},{4,24},{8,20},{12,28},{16,0},{20,8},{24,4},{28,12},{1,17},{... | collective-permute-start | bytes 1572872 | tf_op jit(solution)/shard_map/ppermute | solution.py:78
  184.0 23.8 %collective-permute-start.28 = (bf16[512,512]{1,0:T(8,128)(2,1)}, bf16[512,512]{1,0:T(8,128)(2,1)}, u32[]{:S(2)}, u32[]{:S(2)}) collective-permute-start(bf16[512,512]{1,0:T(8,128)(2,1)} %get-tuple-element.350.refs_20_.refs_8_), channel_id=1, source_target_pairs={{0,4},{4,12},{8,0},{12,8},{16,20},{20,28},{24,16},{28,24},{1,5},{5... | collective-permute-start | bytes 1572872 | tf_op jit(solution)/shard_map/ppermute | solution.py:78
  184.3 23.9 %collective-permute-start.27 = (bf16[512,512]{1,0:T(8,128)(2,1)}, bf16[512,512]{1,0:T(8,128)(2,1)}, u32[]{:S(2)}, u32[]{:S(2)}) collective-permute-start(bf16[512,512]{1,0:T(8,128)(2,1)} %get-tuple-element.350.refs_20_.refs_8_), channel_id=1, source_target_pairs={{4,8},{8,4},{20,24},{24,20},{5,9},{9,5},{21,25},{25,21},{6,10},{10... | collective-permute-start | bytes 1572872 | tf_op jit(solution)/shard_map/ppermute | solution.py:78
  246.2 64.9 %all-gather.11.cloned.1.call-start = ((), (), s32[]{:S(2)}) async-start(), calls=%async_computation.9 | async-start | bytes 3538944 | tf_op jit(solution)/shard_map/all_gather | solution.py:109
  247.7 29.6 %collective-permute-start.32 = (bf16[512,1024]{1,0:T(8,128)(2,1)}, bf16[512,1024]{1,0:T(8,128)(2,1)S(1)}, u32[]{:S(2)}, u32[]{:S(2)}) collective-permute-start(bf16[512,1024]{1,0:T(8,128)(2,1)} %get-tuple-element.365), channel_id=1, source_target_pairs={{16,0},{24,4},{20,8},{28,12},{0,16},{8,20},{4,24},{12,28},{17,1},{... | collective-permute-start | bytes 3145736 | tf_op jit(solution)/shard_map/ppermute | solution.py:82
  251.1 26.3 %collective-permute-start.33 = (bf16[512,1024]{1,0:T(8,128)(2,1)}, bf16[512,1024]{1,0:T(8,128)(2,1)}, u32[]{:S(2)}, u32[]{:S(2)}) collective-permute-start(bf16[512,1024]{1,0:T(8,128)(2,1)} %get-tuple-element.366), channel_id=1, source_target_pairs={{20,0},{28,4},{16,8},{24,12},{4,16},{12,20},{0,24},{8,28},{21,1},{... | collective-permute-start | bytes 3145736 | tf_op jit(solution)/shard_map/ppermute | solution.py:82
  251.1 26.3 %collective-permute-start.34 = (bf16[512,1024]{1,0:T(8,128)(2,1)}, bf16[512,1024]{1,0:T(8,128)(2,1)}, u32[]{:S(2)}, u32[]{:S(2)}) collective-permute-start(bf16[512,1024]{1,0:T(8,128)(2,1)} %get-tuple-element.367), channel_id=1, source_target_pairs={{0,32},{32,64},{64,96},{96,0},{1,33},{33,65},{65,97},{97,1},{2,34}... | collective-permute-start | bytes 3145736 | tf_op jit(solution)/shard_map/ppermute | solution.py:48
  251.8 25.7 %collective-permute-start.35 = (bf16[512,1024]{1,0:T(8,128)(2,1)}, bf16[512,1024]{1,0:T(8,128)(2,1)}, u32[]{:S(2)}, u32[]{:S(2)}) collective-permute-start(bf16[512,1024]{1,0:T(8,128)(2,1)} %get-tuple-element.368), channel_id=1, source_target_pairs={{0,96},{32,0},{64,32},{96,64},{1,97},{33,1},{65,33},{97,65},{2,98}... | collective-permute-start | bytes 3145736 | tf_op jit(solution)/shard_map/ppermute | solution.py:48
  280.7 109.0 %reduce-scatter.9.cloned.1.call-start = ((), (), s32[]{:S(2)}) async-start(), calls=%async_computation.10 | async-start | bytes 1966080 | tf_op jit(solution)/shard_map/reduce_scatter | solution.py:839
  281.2 26.3 %collective-permute-start.37 = (bf16[512,1024]{1,0:T(8,128)(2,1)}, bf16[512,1024]{1,0:T(8,128)(2,1)S(1)}, u32[]{:S(2)}, u32[]{:S(2)}) collective-permute-start(bf16[512,1024]{1,0:T(8,128)(2,1)} %get-tuple-element.384), channel_id=1, source_target_pairs={{0,64},{32,96},{64,0},{96,32},{1,65},{33,97},{65,1},{97,33},{2,66}... | collective-permute-start | bytes 3145736 | tf_op jit(solution)/shard_map/ppermute | solution.py:48
  283.5 24.0 %collective-permute-start.39 = (bf16[512,1024]{1,0:T(8,128)(2,1)}, bf16[512,1024]{1,0:T(8,128)(2,1)}, u32[]{:S(2)}, u32[]{:S(2)}) collective-permute-start(bf16[512,1024]{1,0:T(8,128)(2,1)} %get-tuple-element.388), channel_id=1, source_target_pairs={{4,0},{12,4},{0,8},{8,12},{20,16},{28,20},{16,24},{24,28},{5,1},{1... | collective-permute-start | bytes 3145736 | tf_op jit(solution)/shard_map/ppermute | solution.py:82
  284.6 26.4 %collective-permute-start.38 = (bf16[512,1024]{1,0:T(8,128)(2,1)}, bf16[512,1024]{1,0:T(8,128)(2,1)}, u32[]{:S(2)}, u32[]{:S(2)}) collective-permute-start(bf16[512,1024]{1,0:T(8,128)(2,1)} %get-tuple-element.387.refs_16_), channel_id=1, source_target_pairs={{8,4},{4,8},{24,20},{20,24},{9,5},{5,9},{25,21},{21,25},{10,6},{6,... | collective-permute-start | bytes 3145736 | tf_op jit(solution)/shard_map/ppermute | solution.py:82
  311.0 18.9 %collective-permute-start.40 = (bf16[512,512]{1,0:T(8,128)(2,1)}, bf16[512,512]{1,0:T(8,128)(2,1)S(1)}, u32[]{:S(2)}, u32[]{:S(2)}) collective-permute-start(bf16[512,512]{1,0:T(8,128)(2,1)} %get-tuple-element.411), channel_id=1, source_target_pairs={{0,32},{32,64},{64,96},{96,0},{1,33},{33,65},{65,97},{97,1},{2,34}... | collective-permute-start | bytes 1572872 | tf_op jit(solution)/shard_map/ppermute | solution.py:48
  312.5 17.4 %collective-permute-start.41 = (bf16[512,512]{1,0:T(8,128)(2,1)}, bf16[512,512]{1,0:T(8,128)(2,1)S(1)}, u32[]{:S(2)}, u32[]{:S(2)}) collective-permute-start(bf16[512,512]{1,0:T(8,128)(2,1)} %get-tuple-element.412), channel_id=1, source_target_pairs={{0,96},{32,0},{64,32},{96,64},{1,97},{33,1},{65,33},{97,65},{2,98}... | collective-permute-start | bytes 1572872 | tf_op jit(solution)/shard_map/ppermute | solution.py:48
  313.7 16.2 %collective-permute-start.42 = (bf16[512,512]{1,0:T(8,128)(2,1)}, bf16[512,512]{1,0:T(8,128)(2,1)S(1)}, u32[]{:S(2)}, u32[]{:S(2)}) collective-permute-start(bf16[512,512]{1,0:T(8,128)(2,1)} %get-tuple-element.413), channel_id=1, source_target_pairs={{16,0},{24,4},{20,8},{28,12},{0,16},{8,20},{4,24},{12,28},{17,1},{... | collective-permute-start | bytes 1572872 | tf_op jit(solution)/shard_map/ppermute | solution.py:82
  315.6 14.4 %collective-permute-start.43 = (bf16[512,512]{1,0:T(8,128)(2,1)}, bf16[512,512]{1,0:T(8,128)(2,1)S(1)}, u32[]{:S(2)}, u32[]{:S(2)}) collective-permute-start(bf16[512,512]{1,0:T(8,128)(2,1)} %get-tuple-element.414), channel_id=1, source_target_pairs={{20,0},{28,4},{16,8},{24,12},{4,16},{12,20},{0,24},{8,28},{21,1},{... | collective-permute-start | bytes 1572872 | tf_op jit(solution)/shard_map/ppermute | solution.py:82
  331.0 17.9 %collective-permute-start.44 = (bf16[3072,256]{1,0:T(8,128)(2,1)}, bf16[3072,256]{1,0:T(8,128)(2,1)S(1)}, u32[]{:S(2)}, u32[]{:S(2)}) collective-permute-start(bf16[3072,256]{1,0:T(8,128)(2,1)} %get-tuple-element.416), channel_id=1, source_target_pairs={{0,8},{8,0},{1,9},{9,1},{2,10},{10,2},{3,11},{11,3},{4,12},{12,4},... | collective-permute-start | bytes 4718600 | tf_op jit(solution)/shard_map/ppermute | solution.py:44
  331.3 15.1 %collective-permute-start.45 = (bf16[512,512]{1,0:T(8,128)(2,1)S(1)}, bf16[512,512]{1,0:T(8,128)(2,1)S(1)}, u32[]{:S(2)}, u32[]{:S(2)}) collective-permute-start(bf16[512,512]{1,0:T(8,128)(2,1)S(1)} %copy-done.56), channel_id=1, source_target_pairs={{0,64},{32,96},{64,0},{96,32},{1,65},{33,97},{65,1},{97,33},{2,66}... | collective-permute-start | bytes 1572872 | tf_op jit(solution)/shard_map/ppermute | solution.py:48
  332.8 13.6 %collective-permute-start.47 = (bf16[512,512]{1,0:T(8,128)(2,1)S(1)}, bf16[512,512]{1,0:T(8,128)(2,1)S(1)}, u32[]{:S(2)}, u32[]{:S(2)}) collective-permute-start(bf16[512,512]{1,0:T(8,128)(2,1)S(1)} %copy-done.55), channel_id=1, source_target_pairs={{4,0},{12,4},{0,8},{8,12},{20,16},{28,20},{16,24},{24,28},{5,1},{1... | collective-permute-start | bytes 1572872 | tf_op jit(solution)/shard_map/ppermute | solution.py:82
  334.0 14.9 %collective-permute-start.46 = (bf16[512,512]{1,0:T(8,128)(2,1)S(1)}, bf16[512,512]{1,0:T(8,128)(2,1)S(1)}, u32[]{:S(2)}, u32[]{:S(2)}) collective-permute-start(bf16[512,512]{1,0:T(8,128)(2,1)S(1)} %copy-done.20), channel_id=1, source_target_pairs={{8,4},{4,8},{24,20},{20,24},{9,5},{5,9},{25,21},{21,25},{10,6},{6,... | collective-permute-start | bytes 1572872 | tf_op jit(solution)/shard_map/ppermute | solution.py:82
  351.5 54.9 %reduce-scatter.11.cloned.1.call-start = ((), (), s32[]{:S(2)}) async-start(), calls=%async_computation.11 | async-start | bytes 1966080 | tf_op jit(solution)/shard_map/reduce_scatter | solution.py:899
  353.1 14.5 %collective-permute-start.50 = (bf16[512,512]{1,0:T(8,128)(2,1)}, bf16[512,512]{1,0:T(8,128)(2,1)S(1)}, u32[]{:S(2)}, u32[]{:S(2)}) collective-permute-start(bf16[512,512]{1,0:T(8,128)(2,1)} %get-tuple-element.446), channel_id=1, source_target_pairs={{0,32},{32,64},{64,96},{96,0},{1,33},{33,65},{65,97},{97,1},{2,34}... | collective-permute-start | bytes 1572872 | tf_op jit(solution)/shard_map/ppermute | solution.py:48
  353.4 14.2 %collective-permute-start.51 = (bf16[512,512]{1,0:T(8,128)(2,1)}, bf16[512,512]{1,0:T(8,128)(2,1)S(1)}, u32[]{:S(2)}, u32[]{:S(2)}) collective-permute-start(bf16[512,512]{1,0:T(8,128)(2,1)} %get-tuple-element.447), channel_id=1, source_target_pairs={{0,96},{32,0},{64,32},{96,64},{1,97},{33,1},{65,33},{97,65},{2,98}... | collective-permute-start | bytes 1572872 | tf_op jit(solution)/shard_map/ppermute | solution.py:48
  358.0 13.8 %collective-permute-start.53 = (bf16[512,512]{1,0:T(8,128)(2,1)}, bf16[512,512]{1,0:T(8,128)(2,1)S(1)}, u32[]{:S(2)}, u32[]{:S(2)}) collective-permute-start(bf16[512,512]{1,0:T(8,128)(2,1)} %get-tuple-element.449), channel_id=1, source_target_pairs={{20,0},{28,4},{16,8},{24,12},{4,16},{12,20},{0,24},{8,28},{21,1},{... | collective-permute-start | bytes 1572872 | tf_op jit(solution)/shard_map/ppermute | solution.py:82
  373.6 17.2 %collective-permute-start.54 = (bf16[512,512]{1,0:T(8,128)(2,1)S(1)}, bf16[512,512]{1,0:T(8,128)(2,1)}, u32[]{:S(2)}, u32[]{:S(2)}) collective-permute-start(bf16[512,512]{1,0:T(8,128)(2,1)S(1)} %copy-done.53), channel_id=1, source_target_pairs={{0,64},{32,96},{64,0},{96,32},{1,65},{33,97},{65,1},{97,33},{2,66}... | collective-permute-start | bytes 1572872 | tf_op jit(solution)/shard_map/ppermute | solution.py:48
  374.2 16.6 %collective-permute-start.56 = (bf16[512,512]{1,0:T(8,128)(2,1)S(1)}, bf16[512,512]{1,0:T(8,128)(2,1)}, u32[]{:S(2)}, u32[]{:S(2)}) collective-permute-start(bf16[512,512]{1,0:T(8,128)(2,1)S(1)} %copy-done.52), channel_id=1, source_target_pairs={{4,0},{12,4},{0,8},{8,12},{20,16},{28,20},{16,24},{24,28},{5,1},{1... | collective-permute-start | bytes 1572872 | tf_op jit(solution)/shard_map/ppermute | solution.py:82
  374.9 16.4 %collective-permute-start.55 = (bf16[512,512]{1,0:T(8,128)(2,1)S(1)}, bf16[512,512]{1,0:T(8,128)(2,1)}, u32[]{:S(2)}, u32[]{:S(2)}) collective-permute-start(bf16[512,512]{1,0:T(8,128)(2,1)S(1)} %copy-done.27), channel_id=1, source_target_pairs={{8,4},{4,8},{24,20},{20,24},{9,5},{5,9},{25,21},{21,25},{10,6},{6,... | collective-permute-start | bytes 1572872 | tf_op jit(solution)/shard_map/ppermute | solution.py:82
  399.0 15.6 %collective-permute-start.59 = (bf16[128,2048]{1,0:T(8,128)(2,1)}, bf16[128,2048]{1,0:T(8,128)(2,1)S(1)}, u32[]{:S(2)}, u32[]{:S(2)}) collective-permute-start(bf16[128,2048]{1,0:T(8,128)(2,1)} %get-tuple-element.486), channel_id=1, source_target_pairs={{0,32},{32,64},{64,96},{96,0},{1,33},{33,65},{65,97},{97,1},{2,34}... | collective-permute-start | bytes 1572872 | tf_op jit(solution)/shard_map/ppermute | solution.py:48
  399.0 15.6 %collective-permute-start.60 = (bf16[128,2048]{1,0:T(8,128)(2,1)}, bf16[128,2048]{1,0:T(8,128)(2,1)S(1)}, u32[]{:S(2)}, u32[]{:S(2)}) collective-permute-start(bf16[128,2048]{1,0:T(8,128)(2,1)} %get-tuple-element.487), channel_id=1, source_target_pairs={{0,96},{32,0},{64,32},{96,64},{1,97},{33,1},{65,33},{97,65},{2,98}... | collective-permute-start | bytes 1572872 | tf_op jit(solution)/shard_map/ppermute | solution.py:48
  401.7 13.0 %collective-permute-start.61 = (bf16[128,2048]{1,0:T(8,128)(2,1)}, bf16[128,2048]{1,0:T(8,128)(2,1)S(1)}, u32[]{:S(2)}, u32[]{:S(2)}) collective-permute-start(bf16[128,2048]{1,0:T(8,128)(2,1)} %get-tuple-element.488), channel_id=1, source_target_pairs={{16,0},{24,4},{20,8},{28,12},{0,16},{8,20},{4,24},{12,28},{17,1},{... | collective-permute-start | bytes 1572872 | tf_op jit(solution)/shard_map/ppermute | solution.py:82
  402.9 12.5 %collective-permute-start.62 = (bf16[128,2048]{1,0:T(8,128)(2,1)}, bf16[128,2048]{1,0:T(8,128)(2,1)S(1)}, u32[]{:S(2)}, u32[]{:S(2)}) collective-permute-start(bf16[128,2048]{1,0:T(8,128)(2,1)} %get-tuple-element.489), channel_id=1, source_target_pairs={{20,0},{28,4},{16,8},{24,12},{4,16},{12,20},{0,24},{8,28},{21,1},{... | collective-permute-start | bytes 1572872 | tf_op jit(solution)/shard_map/ppermute | solution.py:82
  416.9 16.0 %collective-permute-start.68 = (bf16[1536,256]{1,0:T(8,128)(2,1)S(1)}, bf16[1536,256]{1,0:T(8,128)(2,1)}, u32[]{:S(2)}, u32[]{:S(2)}) collective-permute-start(bf16[1536,256]{1,0:T(8,128)(2,1)S(1)} %pad_maximum_fusion), channel_id=1, source_target_pairs={{4,8},{8,4},{5,9},{9,5},{6,10},{10,6},{7,11},{11,7},{20,24},{24,20... | collective-permute-start | bytes 2359304 | tf_op jit(solution)/shard_map/ppermute | solution.py:39
  422.9 15.6 %collective-permute-start.65 = (bf16[128,2048]{1,0:T(8,128)(2,1)S(1)}, bf16[128,2048]{1,0:T(8,128)(2,1)S(1)}, u32[]{:S(2)}, u32[]{:S(2)}) collective-permute-start(bf16[128,2048]{1,0:T(8,128)(2,1)S(1)} %copy-done.10), channel_id=1, source_target_pairs={{8,4},{4,8},{24,20},{20,24},{9,5},{5,9},{25,21},{21,25},{10,6},{6,... | collective-permute-start | bytes 1572872 | tf_op jit(solution)/shard_map/ppermute | solution.py:82
  425.7 17.3 %collective-permute-start.66 = (bf16[128,2048]{1,0:T(8,128)(2,1)}, bf16[128,2048]{1,0:T(8,128)(2,1)S(1)}, u32[]{:S(2)}, u32[]{:S(2)}) collective-permute-start(bf16[128,2048]{1,0:T(8,128)(2,1)} %get-tuple-element.495), channel_id=1, source_target_pairs={{4,0},{12,4},{0,8},{8,12},{20,16},{28,20},{16,24},{24,28},{5,1},{1... | collective-permute-start | bytes 1572872 | tf_op jit(solution)/shard_map/ppermute | solution.py:82
  425.8 18.0 %collective-permute-start.67 = (bf16[128,2048]{1,0:T(8,128)(2,1)}, bf16[128,2048]{1,0:T(8,128)(2,1)S(1)}, u32[]{:S(2)}, u32[]{:S(2)}) collective-permute-start(bf16[128,2048]{1,0:T(8,128)(2,1)} %get-tuple-element.499), channel_id=1, source_target_pairs={{0,64},{32,96},{64,0},{96,32},{1,65},{33,97},{65,1},{97,33},{2,66}... | collective-permute-start | bytes 1572872 | tf_op jit(solution)/shard_map/ppermute | solution.py:48
  (76 other events, 879.8 us)
Sparse Core Ops, SparseCore 0:
  44.9 28.6 all-gather.4
  75.8 27.8 all-gather.6
  140.5 24.9 reduce-scatter.4
  179.7 28.3 all-gather.8
  246.3 26.1 reduce-scatter.6
  280.8 28.9 all-gather.10
  351.5 23.1 reduce-scatter.8
  377.1 25.8 reduce-scatter.10

commit v3 on v2

--- a/solution.py
+++ b/solution.py
@@ -147,7 +147,7 @@
     return [pl.BlockSpec(memory_space=pltpu.VMEM)] * n
 
 
-def call(body, name, inputs, outs, scratch, flops, megabytes=56, anywhere=0, outs_anywhere=0):
+def call(body, name, inputs, outs, scratch, flops, megabytes=56, anywhere=0, outs_anywhere=0, alias=0):
     moved = sum(v.size * v.dtype.itemsize for v in inputs[1:])
     moved += sum(math.prod(s) * jnp.dtype(d).itemsize for s, d in outs)
     specs = [pl.BlockSpec(memory_space=pltpu.SMEM)] + in_vmem(len(inputs) - 1 - anywhere)
@@ -159,6 +159,7 @@
         in_specs=specs,
         out_specs=in_vmem(len(outs) - outs_anywhere) + [pl.BlockSpec(memory_space=pl.ANY)] * outs_anywhere,
         scratch_shapes=scratch,
+        input_output_aliases={len(inputs) - alias + i: i for i in range(alias)},
         cost_estimate=pl.CostEstimate(flops=int(flops), bytes_accessed=int(moved), transcendentals=0),
         compiler_params=pltpu.CompilerParams(vmem_limit_bytes=megabytes * 2**20),
     )(*inputs))
@@ -356,8 +357,10 @@
 
 
 def rows_a(refs, to_ref, cols, sem, copies):
-    for i, ref in enumerate(refs):
-        to = to_ref.at[pl.ds(i * 512, 512), cols]
+    row = 0
+    for ref in refs:
+        to = to_ref.at[pl.ds(row, ref.shape[0]), cols]
+        row += ref.shape[0]
         copies.append(pltpu.make_async_copy(ref, to, sem.at[len(copies)]))
         copies[-1].start()
 
@@ -376,12 +379,12 @@
 
 def ffn_body(at, *refs):
     gains, h_in, dy_in = refs[:3]
-    wide_a, down_a, wide_b, down_b = [refs[3 + 4 * i : 7 + 4 * i] for i in range(4)]
-    own_wide, own_down = refs[19:21]
-    h_cols, a2_out, hid_out, dgate_out, dup_out, give_out, keep_out = refs[21:28]
-    up_outs, gate_outs = refs[28:30], refs[30:32]
-    h, dy, a2, hid, dgate, dup, give, keep, up_0, up_1, gate_0, gate_1 = refs[32:44]
-    w_gate, w_up, w_down, sem, out_sem = refs[44:]
+    wide_a, (down_a, wide_b, down_b) = refs[3:8], [refs[8 + 4 * i : 12 + 4 * i] for i in range(3)]
+    own_wide, own_down = refs[20:22]
+    h_cols, a2_out, hid_out, dgate_out, dup_out, give_out, keep_out = refs[22:29]
+    up_outs, gate_outs = refs[29:31], refs[31:33]
+    h, dy, a2, hid, dgate, dup, give, keep, up_0, up_1, gate_0, gate_1 = refs[33:45]
+    w_gate, w_up, w_down, sem, out_sem = refs[45:]
     h_copy = pltpu.make_async_copy(h_in, h, out_sem.at[14])
     h_copy.start()
     copies = []
@@ -543,64 +546,86 @@
             ref[rows, lanes(at[2] ^ j, 128)] = value[:, j * 128 : (j + 1) * 128].astype(bf16)
 
 
-def attention_weight_body(at, a1, dqkv, db, o, *outs):
-    a_outs, b_outs = outs[:4], outs[4:]
+def attention_weight_body(at, a1, dqkv, db, o, *refs):
+    outs, values, sem = refs[:8], refs[8:16], refs[16]
     for i in range(4):
         cols, rows = slice(i * 512, (i + 1) * 512), slice(i * 128, (i + 1) * 128)
-        a_outs[i][...] = kdot(a1[:, cols], dqkv[:, 256:], tn).astype(bf16)
+        values[i][...] = kdot(a1[:, cols], dqkv[:, 256:], tn).astype(bf16)
         for n, left, right in ((slice(0, 256), a1, dqkv.at[:, :256]), (slice(256, 512), db, o)):
             value = kdot(left[:, cols], right[...], tn).astype(bf16)
             for k in range(4):
-                b_outs[k][rows, n] = value[k * 128 : (k + 1) * 128]
-
-
-def ffn_sum_body(at, *refs):
-    wide_a, down_a, wide_b, down_b = [refs[4 * i : 4 * i + 4] for i in range(4)]
-    own_wide, own_down, out_a, out_b = refs[16:]
+                values[4 + k][rows, n] = value[k * 128 : (k + 1) * 128]
+    copies = [pltpu.make_async_copy(v, o_.at[pl.ds(0, 512)], sem.at[i]) for i, (v, o_) in enumerate(zip(values, outs))]
+    for copy in copies:
+        copy.start()
+    for copy in copies:
+        copy.wait()
+
+
+def ffn_sum_body(row, at, *refs):
+    a, b, own, outs, values, sem = refs[:4], refs[4:8], refs[8], refs[17:25], refs[25:33], refs[33]
     mine = at[2] == at[3]
-    for cols, a, b, own in ((slice(0, FF), wide_a, wide_b, own_wide), (slice(FF, 1536), down_a, down_b, own_down)):
-        value = a[0][...].astype(f32) + a[1][...].astype(f32) + a[2][...].astype(f32) + a[3][...].astype(f32)
-        out_a[:, cols] = value.astype(bf16)
-        value = jnp.where(mine, own[...], b[0][...]).astype(f32) + b[1][...].astype(f32)
-        value = value + b[2][...].astype(f32) + b[3][...].astype(f32)
-        out_b[:, cols] = value.astype(bf16)
-
-
-def join_body(at, *refs):
-    ffn_a, ffn_b, a, b, own, outs = refs[0], refs[1], refs[2:6], refs[6:10], refs[10], refs[11:]
+    copies = []
     for i in range(4):
         rows = slice(i * 128, (i + 1) * 128)
-        outs[i][:, :1536] = ffn_a[rows, :]
-        outs[4 + i][:, :1536] = ffn_b[rows, :]
-        value = a[0][rows, :].astype(f32) + a[1][rows, :].astype(f32) + a[2][rows, :].astype(f32)
-        outs[i][:, 1536:] = (value + a[3][rows, :].astype(f32)).astype(bf16)
-        head = jnp.where(at[2] == at[3], own[rows, :], b[0][rows, :])
-        value = head.astype(f32) + b[1][rows, :].astype(f32) + b[2][rows, :].astype(f32)
-        outs[4 + i][:, 1536:] = (value + b[3][rows, :].astype(f32)).astype(bf16)
+        head = jnp.where(mine, own[rows, :], b[0][rows, :])
+        for value, terms in ((values[i], [b[k][rows, :] for k in (1, 2, 3)]), (values[4 + i], [a[k][rows, :] for k in (1, 2, 3)])):
+            first = head if value is values[i] else a[0][rows, :]
+            total = first.astype(f32) + terms[0].astype(f32) + terms[1].astype(f32) + terms[2].astype(f32)
+            for j in range(total.shape[1] // 512):
+                value[j * 128 : (j + 1) * 128, :] = total[:, j * 512 : (j + 1) * 512].astype(bf16)
+    for i in range(8):
+        to = outs[i].at[pl.ds(row, values[i].shape[0])]
+        copies.append(pltpu.make_async_copy(values[i], to, sem.at[i]))
+        copies[-1].start()
+    for copy in copies:
+        copy.wait()
+
+
+def join_body(at, *refs):
+    a, b, own, outs = refs[:4], refs[4:8], refs[8], refs[9:13]
+    kv_give, kv_keep, va, vb, v_own, sem = refs[13], refs[14], refs[15:19], refs[19:23], refs[23], refs[24]
+    pairs = list(zip([*a, *b, own], [*va, *vb, v_own]))
+    copies = [pltpu.make_async_copy(x.at[pl.ds(0, 512)], v, sem.at[i]) for i, (x, v) in enumerate(pairs)]
+    for copy in copies:
+        copy.start()
+    for copy in copies:
+        copy.wait()
+    odd = (at[4] & 1) == 1
+    for i in range(4):
+        rows = slice(i * 128, (i + 1) * 128)
+        head = jnp.where(at[2] == at[3], v_own[rows, :], vb[0][rows, :])
+        value = head.astype(f32) + vb[1][rows, :].astype(f32) + vb[2][rows, :].astype(f32) + vb[3][rows, :].astype(f32)
+        outs[i][...] = value.astype(bf16)
+        value = va[0][rows, :].astype(f32) + va[1][rows, :].astype(f32) + va[2][rows, :].astype(f32) + va[3][rows, :].astype(f32)
+        for half in range(2):
+            one, two = value[:, half * 256 : half * 256 + 128], value[:, half * 256 + 128 : (half + 1) * 256]
+            n = slice(half * 128, (half + 1) * 128)
+            kv_keep[rows, n] = jnp.where(odd, two, one)
+            kv_give[rows, n] = jnp.where(odd, one, two).astype(bf16)
 
 
 def finish_body(at, *refs):
-    own, a, b = refs[0], refs[1:5], refs[5:9]
-    gate, up, down, query, output = refs[9:]
+    a, b, own = refs[:4], refs[4:8], refs[8]
+    gate, up, down, va, vb, v_own, sem = refs[9], refs[10], refs[11], refs[12:16], refs[16:20], refs[20], refs[21]
+    pairs = list(zip([*a, *b, own], [*va, *vb, v_own]))
+    copies = [pltpu.make_async_copy(x.at[pl.ds(512, 384)], v, sem.at[i]) for i, (x, v) in enumerate(pairs)]
+    for copy in copies:
+        copy.start()
+    for copy in copies:
+        copy.wait()
     mine = at[2] == at[3]
-
-    def sum_a(cols):
-        head = jnp.where(mine, own[:, cols], a[0][:, cols])
-        return head.astype(f32) + a[1][:, cols].astype(f32) + a[2][:, cols].astype(f32) + a[3][:, cols].astype(f32)
-
-    def sum_b(cols):
-        return b[0][:, cols].astype(f32) + b[1][:, cols].astype(f32) + b[2][:, cols].astype(f32) + b[3][:, cols].astype(f32)
-
-    for j in range(4):
-        cols = slice(j * 256, (j + 1) * 256)
-        gate[:, cols] = sum_a(cols)
-        up[:, cols] = sum_b(cols)
-    for j in range(2):
-        cols = slice(FF + j * 256, FF + (j + 1) * 256)
-        down[:, j * 256 : (j + 1) * 256] = sum_a(cols)
-        down[:, 512 + j * 256 : 512 + (j + 1) * 256] = sum_b(cols)
-    query[...] = sum_b(slice(1536, 1792))
-    output[...] = sum_b(slice(1792, 2048))
+    for j in range(3):
+        rows = slice(j * 128, (j + 1) * 128)
+        head = jnp.where(mine, v_own[rows, :], vb[0][rows, :])
+        of_a = head.astype(f32) + vb[1][rows, :].astype(f32) + vb[2][rows, :].astype(f32) + vb[3][rows, :].astype(f32)
+        of_b = va[0][rows, :].astype(f32) + va[1][rows, :].astype(f32) + va[2][rows, :].astype(f32) + va[3][rows, :].astype(f32)
+        if j < 2:
+            gate[:, j * 512 : (j + 1) * 512] = of_a
+            up[:, j * 512 : (j + 1) * 512] = of_b
+        else:
+            down[:, :512] = of_a
+            down[:, 512:] = of_b
 
 
 def on_device(
@@ -722,14 +747,15 @@
     )
     wide_a, wide_b, (a_wide, b_wide, a_down, b_down) = done[:2], done[2:4], done[4:]
     attn_own = team_scatter(give, keep)
-    wide_a = [a_wide, wide_a[0], shift(a_wide, Y, 2), wide_a[1]]
+    halves = [shift(wide_a[0][:256], Y, -1), shift(wide_a[1][256:], Y, 1)]
+    wide_a = [a_wide, wide_a[0], *halves, wide_a[1]]
     wide_b = [x_in(b_wide, *flip) for flip in FLIPS[:2]] + wide_b
     down_a = [shift(a_down, Y, -1), shift(a_down, Y, 1)]
     (dy,) = call(reorder_body, "order_upstream", [at, upstream], [((LEN, WIDTH), bf16)], [], 0)
 
 
     attn_own, dy, *done = lax.optimization_barrier((attn_own, dy, *wide_a, *wide_b, *down_a, b_wide, a_down, b_down))
-    wide_a, wide_b, down_a, (b_wide, a_down, b_down) = done[:4], done[4:8], done[8:10], done[10:]
+    wide_a, wide_b, down_a, (b_wide, a_down, b_down) = done[:5], done[5:9], done[9:11], done[11:]
     down_b = [x_in(b_down, *flip) for flip in FLIPS]
     down_a = [a_down, down_a[0], shift(a_down, Y, 2), down_a[1]]
     hidden_own = x_mine.astype(f32) + attn_own
@@ -746,11 +772,11 @@
             pltpu.VMEM((WIDTH, FF), bf16),
             pltpu.VMEM((WIDTH, FF), bf16),
             pltpu.VMEM((WIDTH, FF), bf16),
-            pltpu.SemaphoreType.DMA((40,)),
+            pltpu.SemaphoreType.DMA((44,)),
             pltpu.SemaphoreType.DMA((16,)),
         ],
         14 * LEN * WIDTH * FF,
-        anywhere=20,
+        anywhere=21,
         outs_anywhere=10,
     )
     other = other_core(give)
@@ -825,16 +851,40 @@
     got_down_a = [down_g[0], shift(down_y, Y, 2), *got[:2]]
     got_down_b = [x_out(down_0, 0, 0), x_out(down_1, *FLIPS[1]), *got[2:]]
     part_other = other_core(part_give)
+    message = ((896, 512), bf16)
     blocks = call(
         attention_weight_body,
         "attention_weights",
         [at, a1, dqkv, db, o],
-        [((512, 512), bf16)] * 8,
-        [],
+        [message] * 8,
+        [pltpu.VMEM((512, 512), bf16)] * 8 + [pltpu.SemaphoreType.DMA((8,))],
         2 * LEN * WIDTH * 1024,
+        outs_anywhere=8,
+    )
+    blocks = call(
+        functools.partial(ffn_sum_body, 512),
+        "feed_forward_sums_wide",
+        [at, *got_gate, *got_up, up_b[0], *blocks],
+        [message] * 8,
+        [pltpu.VMEM((256, 512), bf16)] * 8 + [pltpu.SemaphoreType.DMA((8,))],
+        0,
+        anywhere=8,
+        outs_anywhere=8,
+        alias=8,
     )
     part_keep, part_other, *got = lax.optimization_barrier((part_keep, part_other, *blocks, *got_down_a, *got_down_b))
     blocks, got_down_a, got_down_b = got[:8], got[8:12], got[12:]
+    blocks = call(
+        functools.partial(ffn_sum_body, 768),
+        "feed_forward_sums_down",
+        [at, *got_down_a, *got_down_b, down_0, *blocks],
+        [message] * 8,
+        [pltpu.VMEM((128, 512), bf16)] * 8 + [pltpu.SemaphoreType.DMA((8,))],
+        0,
+        anywhere=8,
+        outs_anywhere=8,
+        alias=8,
+    )
     part_both = (part_keep.astype(f32) + part_other.astype(f32)).astype(bf16)
     attn_grad = lax.psum_scatter(part_both, Z, scatter_dimension=0, tiled=True).astype(f32)
     got_attn_a = [shift(blocks[1], Y, 1), shift(blocks[3], Y, 3)]
@@ -858,44 +908,41 @@
     small = join([small, other_core(small)])
     small = join([small, z_other(small, 1)])
 
-    rest = lax.optimization_barrier((blocks[2], blocks[4], blocks[5], small, got_up[2], *got_attn_a, *got_attn_b))
-    (block_y, block_0, block_1, small, got_up[2]), got_attn_a, got_attn_b = rest[:5], rest[5:7], rest[7:]
+    rest = lax.optimization_barrier((blocks[2], blocks[4], blocks[5], small, *got_attn_a, *got_attn_b))
+    (block_y, block_0, block_1, small), got_attn_a, got_attn_b = rest[:4], rest[4:6], rest[6:]
     got_attn_a = [blocks[0], shift(block_y, Y, 2), *got_attn_a]
     got_attn_b = [x_out(block_0, 0, 0), x_out(block_1, *FLIPS[1]), *got_attn_b]
     out_late = after(out_both, part_both)
-    ffn_a, ffn_b = call(
-        ffn_sum_body,
-        "feed_forward_sums",
-        [at, *got_gate, *got_down_a, *got_up, *got_down_b, up_b[0], down_0],
-        [((512, 1536), bf16)] * 2,
-        [],
-        0,
-    )
-
     small = join([small, z_other(small, 2)])
     row_sum = small[:6].reshape(LEN, 1)
     small = small[6:]
     small = join([small, y_other(small, 1)])
-    got_attn_a, got_attn_b, ffn_a, ffn_b, small, attn_grad = lax.optimization_barrier(
-        (got_attn_a, got_attn_b, ffn_a, ffn_b, small, attn_grad)
-    )
-    sums = call(
+    got_attn_a, got_attn_b, small, attn_grad = lax.optimization_barrier((got_attn_a, got_attn_b, small, attn_grad))
+    *sum_b, kv_give, kv_keep = call(
         join_body,
         "join_sums",
-        [at, ffn_a, ffn_b, *got_attn_a, *got_attn_b, block_0],
-        [((128, WIDTH), bf16)] * 8,
-        [],
+        [at, *got_attn_a, *got_attn_b, block_0],
+        [((128, 512), bf16)] * 4 + [((512, HEAD), bf16), ((512, HEAD), f32)],
+        [pltpu.VMEM((512, 512), bf16)] * 9 + [pltpu.SemaphoreType.DMA((9,))],
         0,
-    )
-    sums_a, sums_b = sums[:4], sums[4:]
-    sum_b = [shift(sums_b[i], Y, i) for i in (1, 3)]
-    sum_a = [x_out(sums_a[i], *FLIPS[i]) for i in (2, 3)]
+        anywhere=9,
+    )
+    kv_sum = (kv_keep + kv_partner(kv_give).astype(f32)).astype(bf16)
+    sum_b = [sum_b[0]] + [shift(sum_b[i], Y, i) for i in (1, 2, 3)]
     small = join([small, y_other(small, 2)])
     small = join([small, x_ring(small, 1)])
-    rest = lax.optimization_barrier((*sum_b, *sum_a, sums_b[2], sums_a[0], sums_a[1], small))
-    sum_b, sum_a, (late_y, late_0, late_1, small) = rest[:2], rest[2:4], rest[4:]
-    sum_b = [sums_b[0], shift(late_y, Y, 2), *sum_b]
-    sum_a = [x_out(late_0, 0, 0), x_out(late_1, *FLIPS[1]), *sum_a]
+    kv_sum, small, *sum_b = lax.optimization_barrier((kv_sum, small, *sum_b))
+    sum_a = [x_out(kv_sum[i * 128 : (i + 1) * 128], *flip) for i, flip in enumerate(FLIPS)]
+    sum_a[0] = own_or(sum_a[0], kv_sum[:128])
+    grads = call(
+        finish_body,
+        "finish",
+        [at, *got_attn_a, *got_attn_b, after(block_0, kv_sum)],
+        [((128, FF), f32)] * 3,
+        [pltpu.VMEM((384, 512), bf16)] * 9 + [pltpu.SemaphoreType.DMA((9,))],
+        0,
+        anywhere=9,
+    )
     ffn_own = lax.psum_scatter(out_late, Z, scatter_dimension=0, tiled=True).astype(f32)
     ffn_own = after(ffn_own, small)
 
@@ -907,21 +954,9 @@
     home = [(h_cols.astype(f32) + ffn_own).astype(bf16), grad_inputs.astype(bf16)]
     home = swap(jnp.concatenate(home, 0))
     small = join([small, x_ring(small, 2)])
-    sum_a, sum_b, home, small = lax.optimization_barrier((sum_a, sum_b, home, small))
-    kv_sum = total([own_or(sum_a[0], sums_a[0]), *sum_a[1:]], slice(1536, None))
-    first_halves = jnp.concatenate([kv_sum[:, :half], kv_sum[:, HEAD : HEAD + half]], 1)
-    second_halves = jnp.concatenate([kv_sum[:, half:HEAD], kv_sum[:, HEAD + half :]], 1)
-    kv_done = jnp.where(odd, second_halves, first_halves) + kv_partner(
-        jnp.where(odd, first_halves, second_halves).astype(bf16)
-    ).astype(f32)
-    grads = call(
-        finish_body,
-        "finish",
-        [at, sums_a[0], *sum_a, *sum_b],
-        [((128, FF), f32)] * 3 + [((128, HEAD), f32)] * 2,
-        [],
-        0,
-    )
+    sum_a, home, small, grads = lax.optimization_barrier((sum_a, home, small, grads))
+    query_output = total(sum_b)
+    kv_done = total(sum_a)
     tok = y * 4 + lo * 2 + core
     gains_mine = lax.dynamic_slice(small[:32].reshape(2, 16, 128), (0, tok, 0), (2, 1, 128)).reshape(2, 128)
     peaks = small[32:, 0]
@@ -937,10 +972,10 @@
         home[:LEN],
         home[LEN:].astype(f32),
         gains_mine[0],
-        grads[3],
+        query_output[:, :HEAD],
         kv_done[:, :half],
         kv_done[:, half:],
-        grads[4],
+        query_output[:, HEAD:],
         gains_mine[1],
         grads[0],
         grads[1],

time: 472 us -> 467 us (0.989)
    ppermute x2, waiting for transfers between devices: 13.6 us -> 2.58 us  [x_ring(): return lax.ppermute(a, (XLO, XHI), [(i, i ^ mask) for i in range(4)])]
    reduce_scatter x1, waiting for transfers between devices: 12.5 us -> 5 us  [team_scatter(): lax.psum_scatter(both, Z, scatter_dimension=0, tiled=True).astype(f32)]
    ppermute x24 -> x25, waiting for transfers between devices: 63.1 us -> 66.7 us  [shift(): return lax.ppermute(a, axis, [(i, (i + by) % 4) for i in range(4)])]
    ppermute x24 -> x25, starting transfers between devices: 34.4 us -> 33.6 us  [shift(): return lax.ppermute(a, axis, [(i, (i + by) % 4) for i in range(4)])]
    pallas_call x14 -> x15, Pallas kernels: 126 us -> 127 us  [call(): pl.pallas_call(body, name=name, out_shape=[jax.ShapeDtypeStruct(s, d) for...]
  transfers between devices with their start and end apart: 79 -> 80, of which waited for: 31 -> 38; matrix products, arithmetic and copies ran while one was open for 4% -> 4% of each run, Pallas kernels for 20% -> 20%
where the time goes in v3:
time: 467 us; the launch traced here: 458 us
  waiting for transfers between devices  161 us (34%)
  Pallas kernels  127 us (27%)
  starting transfers between devices  106 us (23%)
  other arithmetic  32.5 us (7%)
  between operations  17.2 us (4%)
  local copies, waits for them, and re-layouts  14 us (3%)
    pallas_call x15, Pallas kernels, call(): pl.pallas_call(body, name=name, out_shape=[jax.ShapeDtypeStruct(s, d) for...  127 us
    ppermute x25, waiting for transfers between devices, shift(): return lax.ppermute(a, axis, [(i, (i + by) % 4) for i in range(4)])  66.7 us
    ppermute x16, waiting for transfers between devices, x_in(): return lax.ppermute(a, (XLO, CORE, XHI), x_pairs(flip_lo, flip_core, False))  42.5 us
    ppermute x25, starting transfers between devices, shift(): return lax.ppermute(a, axis, [(i, (i + by) % 4) for i in range(4)])  33.6 us
    ppermute x16, starting transfers between devices, x_out(): return lax.ppermute(a, (XLO, CORE, XHI), x_pairs(flip_lo, flip_core, True))  30.7 us
    ppermute x16, starting transfers between devices, x_in(): return lax.ppermute(a, (XLO, CORE, XHI), x_pairs(flip_lo, flip_core, False))  22.4 us
    ppermute x16, waiting for transfers between devices, x_out(): return lax.ppermute(a, (XLO, CORE, XHI), x_pairs(flip_lo, flip_core, True))  20.9 us
    ppermute x2, starting transfers between devices, swap(): got = lax.ppermute(a, (CORE, XHI), [(1, 2), (2, 1)])  10.7 us
  transfers between devices with their start and end apart: 80, of which 38 were waited for; matrix products, arithmetic and copies ran while one was open for 4% of the time, Pallas kernels for 20%

profile of v3, /device:TPU:1, one launch (start us, length us, event | category | flops | bytes accessed | tf_op | source)
XLA Modules:
  0.0 458.0 jit_solution(3660470785060634074)
XLA Ops:
  10.4 3.3 lay_out_y.1
  13.7 6.0 %collective-permute-start = (bf16[1552,256]{1,0:T(8,128)(2,1)}, bf16[1552,256]{1,0:T(8,128)(2,1)}, u32[]{:S(2)}, u32[]{:S(2)}) collective-permute-start(bf16[1552,256]{1,0:T(8,128)(2,1)} %get-tuple-element.281), channel_id=1, source_target_pairs={{4,8},{8,4},{5,9},{9,5},{6,10},{10,6},{7,11},{11,7},{20,24},{24,20... | collective-permute-start | bytes 2383880 | tf_op jit(solution)/shard_map/ppermute | solution.py:39
  25.7 2.7 lay_out_x.1
  31.2 4.2 collective-permute-done.3.refs_7_
  36.1 6.8 %collective-permute-done.5.refs_3_ = bf16[512,512]{1,0:T(8,128)(2,1)S(1)} collective-permute-done((bf16[512,512]{1,0:T(8,128)(2,1)}, bf16[512,512]{1,0:T(8,128)(2,1)S(1)}, u32[]{:S(2)}, u32[]{:S(2)}) %collective-permute-start.5) | collective-permute-done | bytes 524320 | tf_op jit(solution)/shard_map/ppermute | solution.py:78
  44.6 2.6 collective-permute-start.6
  47.2 3.0 collective-permute-start.8
  50.2 9.0 %collective-permute-done.6 = bf16[512,512]{1,0:T(8,128)(2,1)S(1)} collective-permute-done((bf16[512,512]{1,0:T(8,128)(2,1)}, bf16[512,512]{1,0:T(8,128)(2,1)S(1)}, u32[]{:S(2)}, u32[]{:S(2)}) %collective-permute-start.6) | collective-permute-done | bytes 524320 | tf_op jit(solution)/shard_map/ppermute | solution.py:78
  60.1 2.4 collective-permute-done.7.refs_1_
  64.1 3.0 pack.1
  69.8 2.3 collective-permute-start.9
  72.1 11.9 %collective-permute-done.10.refs_8_.refs_14_ = bf16[512,512]{1,0:T(8,128)(2,1)S(1)} collective-permute-done((bf16[512,512]{1,0:T(8,128)(2,1)}, bf16[512,512]{1,0:T(8,128)(2,1)S(1)}, u32[]{:S(2)}, u32[]{:S(2)}) %collective-permute-start.10) | collective-permute-done | bytes 524320 | tf_op jit(solution)/shard_map/ppermute | solution.py:48
  84.1 2.3 collective-permute-start.14
  86.8 2.8 collective-permute-start.13
  89.6 2.5 multiply_sine_fusion
  92.1 4.7 %riders.1 = (bf16[512,1024]{1,0:T(8,128)(2,1)}, bf16[512,1024]{1,0:T(8,128)(2,1)}, bf16[512,512]{1,0:T(8,128)(2,1)}, bf16[512,512]{1,0:T(8,128)(2,1)}) custom-call(s32[5]{0:T(128)} %stack.74.at, bf16[512,512]{1,0:T(8,128)(2,1)} %broadcast_select_fusion.3.refs_0_, bf16[512,512]{1,0:T(8,128)(2,1)} %copy-done.9, bf16[512,512]{1,0:T(8,128)(2,1)} %copy-done.8, ...), custom_call_target="tpu_custom_call" | custom-call | bytes 7405568 | tf_op jit(solution)/shard_map/riders/pallas_call | solution.py:155
  96.8 6.2 %collective-permute-done.14 = bf16[576,512]{1,0:T(8,128)(2,1)S(1)} collective-permute-done((bf16[576,512]{1,0:T(8,128)(2,1)}, bf16[576,512]{1,0:T(8,128)(2,1)S(1)}, u32[]{:S(2)}, u32[]{:S(2)}) %collective-permute-start.14) | collective-permute-done | bytes 589856 | tf_op jit(solution)/shard_map/ppermute | solution.py:78
  104.0 2.7 collective-permute-start.16
  110.3 15.7 %attention_forward.1 = (bf16[768,2048]{1,0:T(8,128)(2,1)}, f32[768,1]{1,0:T(8,128)}, bf16[96,2048]{1,0:T(8,128)(2,1)}, bf16[768,256]{1,0:T(8,128)(2,1)}, bf16[76...) custom-call(s32[5]{0:T(128)} %stack.74.at, ...), custom_call_target="tpu_custom_call" | custom-call | flops 3221225472 | bytes 16728064 | tf_op jit(solution)/shard_map/attention_forward/pallas_call | solution.py:155
  126.0 3.9 collective-permute-done.17.refs_7_
  133.1 3.6 collective-permute-done.20
  136.7 3.0 add_convert_fusion.3
  140.2 4.1 collective-permute-start.23
  145.4 2.8 collective-permute-start.21
  148.2 6.5 %collective-permute-done.22.refs_6_ = bf16[256,1024]{1,0:T(8,128)(2,1)S(1)} collective-permute-done((bf16[256,1024]{1,0:T(8,128)(2,1)S(1)}, bf16[256,1024]{1,0:T(8,128)(2,1)S(1)}, u32[]{:S(2)}, u32[]{:S(2)}) %collective-permute-start.22) | collective-permute-done | bytes 524320 | tf_op jit(solution)/shard_map/ppermute | solution.py:48
  155.5 4.5 order_upstream.1.refs_2_.dy
  160.0 5.0 %reduce-scatter.5.cloned.1.call-done = bf16[96,2048]{1,0:T(8,128)(2,1)} async-done(((bf16[384,2048]{1,0:T(8,128)(2,1)}), bf16[96,2048]{1,0:T(8,128)(2,1)}) %reduce-scatter.5.cloned.1.call-update) | async-done | bytes 393232 | tf_op jit(solution)/shard_map/reduce_scatter | solution.py:114
  166.1 4.6 %collective-permute-done.25.refs_9_.refs_1_ = bf16[512,512]{1,0:T(8,128)(2,1)} collective-permute-done((bf16[512,512]{1,0:T(8,128)(2,1)}, bf16[512,512]{1,0:T(8,128)(2,1)}, u32[]{:S(2)}, u32[]{:S(2)}) %collective-permute-start.25) | collective-permute-done | bytes 524320 | tf_op jit(solution)/shard_map/ppermute | solution.py:48
  172.8 2.2 collective-permute-start.27
  175.0 2.5 collective-permute-start.31
  177.9 3.9 collective-permute-start.28
  181.8 5.2 %collective-permute-done.27.refs_10_.refs_2_ = bf16[512,512]{1,0:T(8,128)(2,1)S(1)} collective-permute-done((bf16[512,512]{1,0:T(8,128)(2,1)}, bf16[512,512]{1,0:T(8,128)(2,1)S(1)}, u32[]{:S(2)}, u32[]{:S(2)}) %collective-permute-start.27) | collective-permute-done | bytes 524320 | tf_op jit(solution)/shard_map/ppermute | solution.py:48
  189.0 12.3 %collective-permute-done.30.refs_18_.refs_6_ = bf16[512,512]{1,0:T(8,128)(2,1)S(1)} collective-permute-done((bf16[512,512]{1,0:T(8,128)(2,1)}, bf16[512,512]{1,0:T(8,128)(2,1)S(1)}, u32[]{:S(2)}, u32[]{:S(2)}) %collective-permute-start.30) | collective-permute-done | bytes 524320 | tf_op jit(solution)/shard_map/ppermute | solution.py:78
  202.6 31.0 %feed_forward.1 = (bf16[768,256]{1,0:T(8,128)(2,1)}, bf16[768,2048]{1,0:T(8,128)(2,1)}, bf16[768,1024]{1,0:T(8,128)(2,1)}, bf16[768,1024]{1,0:T(8,128)(2,1)}, bf...) custom-call(s32[5]{0:T(128)} %stack.74.at, ...), custom_call_target="tpu_custom_call" | custom-call | flops 22548578304 | bytes 36110336 | tf_op jit(solution)/shard_map/feed_forward/pallas_call | solution.py:155
  234.0 3.4 collective-permute-done.32
  237.4 3.1 add_convert_fusion.2
  242.1 2.5 collective-permute-start.33
  248.4 13.1 %weight_rest.1 = (bf16[512,1024]{1,0:T(8,128)(2,1)}, bf16[512,1024]{1,0:T(8,128)(2,1)}, bf16[512,1024]{1,0:T(8,128)(2,1)}, bf16[512,1024]{1,0:T(8,128)(2,1)}, bf...) custom-call(s32[5]{0:T(128)} %stack.74.at, ...), custom_call_target="tpu_custom_call" | custom-call | flops 6442450944 | bytes 19398656 | tf_op jit(solution)/shard_map/weight_rest/pallas_call | solution.py:155
  261.6 8.7 %feed_forward_out.1 = (bf16[3072,256]{1,0:T(8,128)(2,1)}, bf16[3072,256]{1,0:T(8,128)(2,1)}) custom-call(s32[5]{0:T(128)} %stack.74.at, bf16[768,1024]{1,0:T(8,128)(2,1)} %get-tuple-element.369.hid, bf16[512,512]{1,0:T(8,128)(2,1)} %get-tuple-element.350.refs_8_.refs_0_, bf16[512,512]{1,0:T(8,128)(2,1)} %collective-permute-done.25.refs_9_.refs_1_, ...), custom_call_target="tpu_custom_call" | custom-call | flops 3221225472 | bytes 9437184 | tf_op jit(solution)/shard_map/feed_forward_out/pallas_call | solution.py:155
  272.8 2.3 subtract_convert_fusion.1
  279.3 4.2 collective-permute-start.39
  285.2 17.3 %collective-permute-done.38.refs_1_ = bf16[512,1024]{1,0:T(8,128)(2,1)S(1)} collective-permute-done((bf16[512,1024]{1,0:T(8,128)(2,1)}, bf16[512,1024]{1,0:T(8,128)(2,1)S(1)}, u32[]{:S(2)}, u32[]{:S(2)}) %collective-permute-start.38) | collective-permute-done | bytes 1048608 | tf_op jit(solution)/shard_map/ppermute | solution.py:48
  302.5 3.1 collective-permute-done.39.refs_4_
  309.4 14.0 %attention_backward.1 = (bf16[768,256]{1,0:T(8,128)(2,1)}, bf16[768,768]{1,0:T(8,128)(2,1)}, f32[768,1]{1,0:T(8,128)}, f32[1,2048]{1,0:T(1,128)}, bf16[3072,256]{1,0:T(8,128)(2,1)}, /*index=5*/bf16[3072,256]{1,0:T(8,128)(2,1)}) custom-call(s32[5]{0:T(128)} %stack.74.at, bf16[768,2048]{1,0:T(8,128)(2,1)} %all-gather.11.cloned.1.call-done.refs_0_.db, ...), custom_call_target="tpu_custom_call" | custom-call | flops 3221225472 | bytes 17518592 | tf_op jit(solution)/shard_map/attention_backward/pallas_call | solution.py:155
  327.9 3.7 collective-permute-start.47
  331.6 8.0 %attention_weights.1 = (bf16[896,512]{1,0:T(8,128)(2,1)}, bf16[896,512]{1,0:T(8,128)(2,1)}, bf16[896,512]{1,0:T(8,128)(2,1)}, bf16[896,512]{1,0:T(8,128)(2,1)}, ...) custom-call(s32[5]{0:T(128)} %stack.74.at, ...), custom_call_target="tpu_custom_call" | custom-call | flops 3221225472 | bytes 15204352 | tf_op jit(solution)/shard_map/attention_weights/pallas_call | solution.py:155
  339.6 5.6 %feed_forward_sums_wide.1 = (bf16[896,512]{1,0:T(8,128)(2,1)}, bf16[896,512]{1,0:T(8,128)(2,1)}, bf16[896,512]{1,0:T(8,128)(2,1)}, bf16[896,512]{1,0:T(8,128)(2,...) custom-call(s32[5]{0:T(128)} %stack.74.at, ...), custom_call_target="tpu_custom_call", output_to_operand_aliasing={{0}: (10, {}), {1}: (11, {}), {2}: (12, {}), {3}: (13, {}),... | custom-call | bytes 24117248 | tf_op jit(solution)/shard_map/feed_forward_sums_wide/pallas_call | solution.py:155
  349.2 3.7 feed_forward_sums_down.1
  353.2 2.4 collective-permute-start.52
  359.5 3.3 collective-permute-done.50
  362.8 10.4 %collective-permute-done.51.refs_2_ = bf16[896,512]{1,0:T(8,128)(2,1)S(1)} collective-permute-done((bf16[896,512]{1,0:T(8,128)(2,1)}, bf16[896,512]{1,0:T(8,128)(2,1)S(1)}, u32[]{:S(2)}, u32[]{:S(2)}) %collective-permute-start.51) | collective-permute-done | bytes 917536 | tf_op jit(solution)/shard_map/ppermute | solution.py:48
  373.2 4.8 %collective-permute-done.54.refs_7_ = bf16[896,512]{1,0:T(8,128)(2,1)} collective-permute-done((bf16[896,512]{1,0:T(8,128)(2,1)}, bf16[896,512]{1,0:T(8,128)(2,1)}, u32[]{:S(2)}, u32[]{:S(2)}) %collective-permute-start.54) | collective-permute-done | bytes 917536 | tf_op jit(solution)/shard_map/ppermute | solution.py:82
  378.7 2.9 collective-permute-start.57
  381.6 5.1 %collective-permute-start.56 = (bf16[896,512]{1,0:T(8,128)(2,1)}, bf16[896,512]{1,0:T(8,128)(2,1)}, u32[]{:S(2)}, u32[]{:S(2)}) collective-permute-start(bf16[896,512]{1,0:T(8,128)(2,1)} %get-tuple-element.520.refs_8_), channel_id=1, source_target_pairs={{8,4},{4,8},{24,20},{20,24},{9,5},{5,9},{25,21},{21,25},{10,6},{6,... | collective-permute-start | bytes 2752520 | tf_op jit(solution)/shard_map/ppermute | solution.py:82
  389.0 3.0 collective-permute-done.58
  392.2 4.6 %collective-permute-done.59 = f32[40,128]{1,0:T(8,128)S(1)} collective-permute-done((f32[40,128]{1,0:T(8,128)S(1)}, f32[40,128]{1,0:T(8,128)S(1)}, u32[]{:S(2)}, u32[]{:S(2)}) %collective-permute-start.59) | collective-permute-done | bytes 20512 | tf_op jit(solution)/shard_map/ppermute | solution.py:56
  399.3 6.7 %collective-permute-done.56.refs_4_ = bf16[896,512]{1,0:T(8,128)(2,1)} collective-permute-done((bf16[896,512]{1,0:T(8,128)(2,1)}, bf16[896,512]{1,0:T(8,128)(2,1)}, u32[]{:S(2)}, u32[]{:S(2)}) %collective-permute-start.56) | collective-permute-done | bytes 917536 | tf_op jit(solution)/shard_map/ppermute | solution.py:82
  408.1 4.6 %join_sums.1 = (bf16[128,512]{1,0:T(8,128)(2,1)}, bf16[128,512]{1,0:T(8,128)(2,1)}, bf16[128,512]{1,0:T(8,128)(2,1)}, bf16[128,512]{1,0:T(8,128)(2,1)}, bf16[512,256]{1,0:T(8,128)(2,1)}, /*index=5*/f32[512,256]{1,0:T(8,128)}) custom-call(s32[5]{0:T(128)} %stack.74.at, bf16[896,512]{1,0:T(8,128)(2,1)} %get-tuple-element.496.refs_0_, ...), custom_call_target="tpu_custom_call" | custom-call | bytes 9568256 | tf_op jit(solution)/shard_map/join_sums/pallas_call | solution.py:155
  417.6 2.6 collective-permute-done.62
  420.2 2.2 collective-permute-done.60
  422.8 4.6 %collective-permute-start.70 = (bf16[1536,256]{1,0:T(8,128)(2,1)S(1)}, bf16[1536,256]{1,0:T(8,128)(2,1)S(1)}, u32[]{:S(2)}, u32[]{:S(2)}) collective-permute-start(bf16[1536,256]{1,0:T(8,128)(2,1)S(1)} %pad_maximum_fusion), channel_id=1, source_target_pairs={{4,8},{8,4},{5,9},{9,5},{6,10},{10,6},{7,11},{11,7},{20,24},{24,20... | collective-permute-start | bytes 2359304 | tf_op jit(solution)/shard_map/ppermute | solution.py:39
  428.3 3.9 finish.1
  432.2 2.6 collective-permute-start.66
  434.9 4.5 collective-permute-done.66
  (304 shorter events, 90.3 us)
Async XLA Ops:
  7.2 96.8 %all-gather.5.cloned.1.call-start = ((), (), s32[]{:S(2)}) async-start(), calls=%async_computation.4 | async-start | bytes 3538944 | tf_op jit(solution)/shard_map/all_gather | solution.py:109
  13.7 16.2 %collective-permute-start = (bf16[1552,256]{1,0:T(8,128)(2,1)}, bf16[1552,256]{1,0:T(8,128)(2,1)}, u32[]{:S(2)}, u32[]{:S(2)}) collective-permute-start(bf16[1552,256]{1,0:T(8,128)(2,1)} %get-tuple-element.281), channel_id=1, source_target_pairs={{4,8},{8,4},{5,9},{9,5},{6,10},{10,6},{7,11},{11,7},{20,24},{24,20... | collective-permute-start | bytes 2383880 | tf_op jit(solution)/shard_map/ppermute | solution.py:39
  22.3 13.2 %collective-permute-start.3 = (bf16[528,512]{1,0:T(8,128)(2,1)}, bf16[528,512]{1,0:T(8,128)(2,1)S(1)}, u32[]{:S(2)}, u32[]{:S(2)}) collective-permute-start(bf16[528,512]{1,0:T(8,128)(2,1)} %get-tuple-element.294.refs_4_), channel_id=1, source_target_pairs={{0,32},{32,64},{64,96},{96,0},{1,33},{33,65},{65,97},{97,1},{2,34}... | collective-permute-start | bytes 1622024 | tf_op jit(solution)/shard_map/ppermute | solution.py:48
  23.6 12.5 %collective-permute-start.2 = (bf16[528,512]{1,0:T(8,128)(2,1)}, bf16[528,512]{1,0:T(8,128)(2,1)S(1)}, u32[]{:S(2)}, u32[]{:S(2)}) collective-permute-start(bf16[528,512]{1,0:T(8,128)(2,1)} %get-tuple-element.294.refs_4_), channel_id=1, source_target_pairs={{0,96},{32,0},{64,32},{96,64},{1,97},{33,1},{65,33},{97,65},{2,98}... | collective-permute-start | bytes 1622024 | tf_op jit(solution)/shard_map/ppermute | solution.py:48
  28.4 14.5 %collective-permute-start.5 = (bf16[512,512]{1,0:T(8,128)(2,1)}, bf16[512,512]{1,0:T(8,128)(2,1)S(1)}, u32[]{:S(2)}, u32[]{:S(2)}) collective-permute-start(bf16[512,512]{1,0:T(8,128)(2,1)} %lay_out_x.1), channel_id=1, source_target_pairs={{0,20},{4,28},{8,16},{12,24},{16,4},{20,12},{24,0},{28,8},{1,21},{... | collective-permute-start | bytes 1572872 | tf_op jit(solution)/shard_map/ppermute | solution.py:78
  28.5 15.1 %collective-permute-start.4 = (bf16[512,512]{1,0:T(8,128)(2,1)}, bf16[512,512]{1,0:T(8,128)(2,1)S(1)}, u32[]{:S(2)}, u32[]{:S(2)}) collective-permute-start(bf16[512,512]{1,0:T(8,128)(2,1)} %lay_out_x.1), channel_id=1, source_target_pairs={{0,16},{4,24},{8,20},{12,28},{16,0},{20,8},{24,4},{28,12},{1,17},{... | collective-permute-start | bytes 1572872 | tf_op jit(solution)/shard_map/ppermute | solution.py:78
  44.6 81.4 %all-gather.7.cloned.1.call-start = ((), (), s32[]{:S(2)}) async-start(), calls=%async_computation.5 | async-start | bytes 3538944 | tf_op jit(solution)/shard_map/all_gather | solution.py:109
  44.6 14.6 %collective-permute-start.6 = (bf16[512,512]{1,0:T(8,128)(2,1)}, bf16[512,512]{1,0:T(8,128)(2,1)S(1)}, u32[]{:S(2)}, u32[]{:S(2)}) collective-permute-start(bf16[512,512]{1,0:T(8,128)(2,1)} %lay_out_x.1), channel_id=1, source_target_pairs={{4,8},{8,4},{20,24},{24,20},{5,9},{9,5},{21,25},{25,21},{6,10},{10... | collective-permute-start | bytes 1572872 | tf_op jit(solution)/shard_map/ppermute | solution.py:78
  47.2 15.3 %collective-permute-start.8 = (bf16[528,512]{1,0:T(8,128)(2,1)S(1)}, bf16[528,512]{1,0:T(8,128)(2,1)S(1)}, u32[]{:S(2)}, u32[]{:S(2)}) collective-permute-start(bf16[528,512]{1,0:T(8,128)(2,1)S(1)} %copy-done.3), channel_id=1, source_target_pairs={{0,64},{32,96},{64,0},{96,32},{1,65},{33,97},{65,1},{97,33},{2,66}... | collective-permute-start | bytes 1622024 | tf_op jit(solution)/shard_map/ppermute | solution.py:48
  50.2 12.3 %collective-permute-start.7 = (bf16[512,512]{1,0:T(8,128)(2,1)}, bf16[512,512]{1,0:T(8,128)(2,1)S(1)}, u32[]{:S(2)}, u32[]{:S(2)}) collective-permute-start(bf16[512,512]{1,0:T(8,128)(2,1)} %lay_out_x.1), channel_id=1, source_target_pairs={{0,4},{4,12},{8,0},{12,8},{16,20},{20,28},{24,16},{28,24},{1,5},{5... | collective-permute-start | bytes 1572872 | tf_op jit(solution)/shard_map/ppermute | solution.py:78
  67.2 97.9 %reduce-scatter.5.cloned.1.call-start = ((), (), s32[]{:S(2)}) async-start(), calls=%async_computation.6 | async-start | bytes 1966080 | tf_op jit(solution)/shard_map/reduce_scatter | solution.py:114
  67.2 16.8 %collective-permute-start.12 = (bf16[576,512]{1,0:T(8,128)(2,1)}, bf16[576,512]{1,0:T(8,128)(2,1)S(1)}, u32[]{:S(2)}, u32[]{:S(2)}) collective-permute-start(bf16[576,512]{1,0:T(8,128)(2,1)} %get-tuple-element.303), channel_id=1, source_target_pairs={{0,20},{4,28},{8,16},{12,24},{16,4},{20,12},{24,0},{28,8},{1,21},{... | collective-permute-start | bytes 1769480 | tf_op jit(solution)/shard_map/ppermute | solution.py:78
  67.3 16.8 %collective-permute-start.11 = (bf16[576,512]{1,0:T(8,128)(2,1)}, bf16[576,512]{1,0:T(8,128)(2,1)S(1)}, u32[]{:S(2)}, u32[]{:S(2)}) collective-permute-start(bf16[576,512]{1,0:T(8,128)(2,1)} %get-tuple-element.303), channel_id=1, source_target_pairs={{0,16},{4,24},{8,20},{12,28},{16,0},{20,8},{24,4},{28,12},{1,17},{... | collective-permute-start | bytes 1769480 | tf_op jit(solution)/shard_map/ppermute | solution.py:78
  69.4 14.6 %collective-permute-start.10 = (bf16[512,512]{1,0:T(8,128)(2,1)}, bf16[512,512]{1,0:T(8,128)(2,1)S(1)}, u32[]{:S(2)}, u32[]{:S(2)}) collective-permute-start(bf16[512,512]{1,0:T(8,128)(2,1)} %get-tuple-element.315.refs_5_.refs_11_), channel_id=1, source_target_pairs={{0,32},{32,64},{64,96},{96,0},{1,33},{33,65},{65,97},{97,1},{2,34}... | collective-permute-start | bytes 1572872 | tf_op jit(solution)/shard_map/ppermute | solution.py:48
  69.8 14.2 %collective-permute-start.9 = (bf16[512,512]{1,0:T(8,128)(2,1)}, bf16[512,512]{1,0:T(8,128)(2,1)S(1)}, u32[]{:S(2)}, u32[]{:S(2)}) collective-permute-start(bf16[512,512]{1,0:T(8,128)(2,1)} %get-tuple-element.315.refs_5_.refs_11_), channel_id=1, source_target_pairs={{0,96},{32,0},{64,32},{96,64},{1,97},{33,1},{65,33},{97,65},{2,98}... | collective-permute-start | bytes 1572872 | tf_op jit(solution)/shard_map/ppermute | solution.py:48
  84.1 19.0 %collective-permute-start.14 = (bf16[576,512]{1,0:T(8,128)(2,1)}, bf16[576,512]{1,0:T(8,128)(2,1)S(1)}, u32[]{:S(2)}, u32[]{:S(2)}) collective-permute-start(bf16[576,512]{1,0:T(8,128)(2,1)} %get-tuple-element.303), channel_id=1, source_target_pairs={{4,8},{8,4},{20,24},{24,20},{5,9},{9,5},{21,25},{25,21},{6,10},{10... | collective-permute-start | bytes 1769480 | tf_op jit(solution)/shard_map/ppermute | solution.py:78
  86.7 17.2 %collective-permute-start.15 = (bf16[576,512]{1,0:T(8,128)(2,1)}, bf16[576,512]{1,0:T(8,128)(2,1)S(1)}, u32[]{:S(2)}, u32[]{:S(2)}) collective-permute-start(bf16[576,512]{1,0:T(8,128)(2,1)} %get-tuple-element.303), channel_id=1, source_target_pairs={{0,4},{4,12},{8,0},{12,8},{16,20},{20,28},{24,16},{28,24},{1,5},{5... | collective-permute-start | bytes 1769480 | tf_op jit(solution)/shard_map/ppermute | solution.py:78
  86.8 17.1 %collective-permute-start.13 = (bf16[512,512]{1,0:T(8,128)(2,1)}, bf16[512,512]{1,0:T(8,128)(2,1)}, u32[]{:S(2)}, u32[]{:S(2)}) collective-permute-start(bf16[512,512]{1,0:T(8,128)(2,1)} %get-tuple-element.315.refs_5_.refs_11_), channel_id=1, source_target_pairs={{0,64},{32,96},{64,0},{96,32},{1,65},{33,97},{65,1},{97,33},{2,66}... | collective-permute-start | bytes 1572872 | tf_op jit(solution)/shard_map/ppermute | solution.py:48
  103.9 26.0 %collective-permute-start.17 = (bf16[512,1024]{1,0:T(8,128)(2,1)}, bf16[512,1024]{1,0:T(8,128)(2,1)S(1)}, u32[]{:S(2)}, u32[]{:S(2)}) collective-permute-start(bf16[512,1024]{1,0:T(8,128)(2,1)} %get-tuple-element.345.refs_3_), channel_id=1, source_target_pairs={{0,32},{32,64},{64,96},{96,0},{1,33},{33,65},{65,97},{97,1},{2,34}... | collective-permute-start | bytes 3145736 | tf_op jit(solution)/shard_map/ppermute | solution.py:48
  104.0 25.9 %collective-permute-start.16 = (bf16[512,1024]{1,0:T(8,128)(2,1)}, bf16[512,1024]{1,0:T(8,128)(2,1)S(1)}, u32[]{:S(2)}, u32[]{:S(2)}) collective-permute-start(bf16[512,1024]{1,0:T(8,128)(2,1)} %get-tuple-element.345.refs_3_), channel_id=1, source_target_pairs={{0,96},{32,0},{64,32},{96,64},{1,97},{33,1},{65,33},{97,65},{2,98}... | collective-permute-start | bytes 3145736 | tf_op jit(solution)/shard_map/ppermute | solution.py:48
  106.7 24.5 %collective-permute-start.19 = (bf16[512,1024]{1,0:T(8,128)(2,1)}, bf16[512,1024]{1,0:T(8,128)(2,1)}, u32[]{:S(2)}, u32[]{:S(2)}) collective-permute-start(bf16[512,1024]{1,0:T(8,128)(2,1)} %get-tuple-element.358.refs_20_), channel_id=1, source_target_pairs={{0,20},{4,28},{8,16},{12,24},{16,4},{20,12},{24,0},{28,8},{1,21},{... | collective-permute-start | bytes 3145736 | tf_op jit(solution)/shard_map/ppermute | solution.py:78
  108.9 24.2 %collective-permute-start.18 = (bf16[512,1024]{1,0:T(8,128)(2,1)}, bf16[512,1024]{1,0:T(8,128)(2,1)}, u32[]{:S(2)}, u32[]{:S(2)}) collective-permute-start(bf16[512,1024]{1,0:T(8,128)(2,1)} %get-tuple-element.358.refs_20_), channel_id=1, source_target_pairs={{0,16},{4,24},{8,20},{12,28},{16,0},{20,8},{24,4},{28,12},{1,17},{... | collective-permute-start | bytes 3145736 | tf_op jit(solution)/shard_map/ppermute | solution.py:78
  139.8 62.8 %all-gather.9.cloned.1.call-start = ((), (), s32[]{:S(2)}) async-start(), calls=%async_computation.7 | async-start | bytes 3538944 | tf_op jit(solution)/shard_map/all_gather | solution.py:109
  139.9 14.8 %collective-permute-start.22 = (bf16[256,1024]{1,0:T(8,128)(2,1)S(1)}, bf16[256,1024]{1,0:T(8,128)(2,1)S(1)}, u32[]{:S(2)}, u32[]{:S(2)}) collective-permute-start(bf16[256,1024]{1,0:T(8,128)(2,1)S(1)} %slice.111), channel_id=1, source_target_pairs={{0,32},{32,64},{64,96},{96,0},{1,33},{33,65},{65,97},{97,1},{2,34}... | collective-permute-start | bytes 1572872 | tf_op jit(solution)/shard_map/ppermute | solution.py:48
  140.0 30.7 %collective-permute-start.24 = (bf16[512,1024]{1,0:T(8,128)(2,1)}, bf16[512,1024]{1,0:T(8,128)(2,1)S(1)}, u32[]{:S(2)}, u32[]{:S(2)}) collective-permute-start(bf16[512,1024]{1,0:T(8,128)(2,1)} %get-tuple-element.358.refs_20_), channel_id=1, source_target_pairs={{0,4},{4,12},{8,0},{12,8},{16,20},{20,28},{24,16},{28,24},{1,5},{5... | collective-permute-start | bytes 3145736 | tf_op jit(solution)/shard_map/ppermute | solution.py:78
  140.2 30.5 %collective-permute-start.23 = (bf16[512,1024]{1,0:T(8,128)(2,1)}, bf16[512,1024]{1,0:T(8,128)(2,1)}, u32[]{:S(2)}, u32[]{:S(2)}) collective-permute-start(bf16[512,1024]{1,0:T(8,128)(2,1)} %get-tuple-element.358.refs_20_), channel_id=1, source_target_pairs={{4,8},{8,4},{20,24},{24,20},{5,9},{9,5},{21,25},{25,21},{6,10},{10... | collective-permute-start | bytes 3145736 | tf_op jit(solution)/shard_map/ppermute | solution.py:78
  145.4 20.7 %collective-permute-start.21 = (bf16[256,1024]{1,0:T(8,128)(2,1)S(1)}, bf16[256,1024]{1,0:T(8,128)(2,1)}, u32[]{:S(2)}, u32[]{:S(2)}) collective-permute-start(bf16[256,1024]{1,0:T(8,128)(2,1)S(1)} %slice.110), channel_id=1, source_target_pairs={{0,96},{32,0},{64,32},{96,64},{1,97},{33,1},{65,33},{97,65},{2,98}... | collective-permute-start | bytes 1572872 | tf_op jit(solution)/shard_map/ppermute | solution.py:48
  148.2 17.9 %collective-permute-start.26 = (bf16[512,512]{1,0:T(8,128)(2,1)}, bf16[512,512]{1,0:T(8,128)(2,1)}, u32[]{:S(2)}, u32[]{:S(2)}) collective-permute-start(bf16[512,512]{1,0:T(8,128)(2,1)} %get-tuple-element.350.refs_8_.refs_0_), channel_id=1, source_target_pairs={{0,32},{32,64},{64,96},{96,0},{1,33},{33,65},{65,97},{97,1},{2,34}... | collective-permute-start | bytes 1572872 | tf_op jit(solution)/shard_map/ppermute | solution.py:48
  155.5 15.3 %collective-permute-start.25 = (bf16[512,512]{1,0:T(8,128)(2,1)}, bf16[512,512]{1,0:T(8,128)(2,1)}, u32[]{:S(2)}, u32[]{:S(2)}) collective-permute-start(bf16[512,512]{1,0:T(8,128)(2,1)} %get-tuple-element.350.refs_8_.refs_0_), channel_id=1, source_target_pairs={{0,96},{32,0},{64,32},{96,64},{1,97},{33,1},{65,33},{97,65},{2,98}... | collective-permute-start | bytes 1572872 | tf_op jit(solution)/shard_map/ppermute | solution.py:48
  172.7 97.6 %reduce-scatter.7.cloned.1.call-start = ((), (), s32[]{:S(2)}) async-start(), calls=%async_computation.8 | async-start | bytes 1966080 | tf_op jit(solution)/shard_map/reduce_scatter | solution.py:786
  172.8 14.3 %collective-permute-start.27 = (bf16[512,512]{1,0:T(8,128)(2,1)}, bf16[512,512]{1,0:T(8,128)(2,1)S(1)}, u32[]{:S(2)}, u32[]{:S(2)}) collective-permute-start(bf16[512,512]{1,0:T(8,128)(2,1)} %get-tuple-element.350.refs_8_.refs_0_), channel_id=1, source_target_pairs={{0,64},{32,96},{64,0},{96,32},{1,65},{33,97},{65,1},{97,33},{2,66}... | collective-permute-start | bytes 1572872 | tf_op jit(solution)/shard_map/ppermute | solution.py:48
  175.0 14.0 %collective-permute-start.31 = (bf16[512,512]{1,0:T(8,128)(2,1)}, bf16[512,512]{1,0:T(8,128)(2,1)S(1)}, u32[]{:S(2)}, u32[]{:S(2)}) collective-permute-start(bf16[512,512]{1,0:T(8,128)(2,1)} %get-tuple-element.357.refs_21_.refs_8_), channel_id=1, source_target_pairs={{0,20},{4,28},{8,16},{12,24},{16,4},{20,12},{24,0},{28,8},{1,21},{... | collective-permute-start | bytes 1572872 | tf_op jit(solution)/shard_map/ppermute | solution.py:78
  177.5 23.8 %collective-permute-start.30 = (bf16[512,512]{1,0:T(8,128)(2,1)}, bf16[512,512]{1,0:T(8,128)(2,1)S(1)}, u32[]{:S(2)}, u32[]{:S(2)}) collective-permute-start(bf16[512,512]{1,0:T(8,128)(2,1)} %get-tuple-element.357.refs_21_.refs_8_), channel_id=1, source_target_pairs={{0,16},{4,24},{8,20},{12,28},{16,0},{20,8},{24,4},{28,12},{1,17},{... | collective-permute-start | bytes 1572872 | tf_op jit(solution)/shard_map/ppermute | solution.py:78
  177.5 23.8 %collective-permute-start.29 = (bf16[512,512]{1,0:T(8,128)(2,1)}, bf16[512,512]{1,0:T(8,128)(2,1)}, u32[]{:S(2)}, u32[]{:S(2)}) collective-permute-start(bf16[512,512]{1,0:T(8,128)(2,1)} %get-tuple-element.357.refs_21_.refs_8_), channel_id=1, source_target_pairs={{0,4},{4,12},{8,0},{12,8},{16,20},{20,28},{24,16},{28,24},{1,5},{5... | collective-permute-start | bytes 1572872 | tf_op jit(solution)/shard_map/ppermute | solution.py:78
  177.9 23.4 %collective-permute-start.28 = (bf16[512,512]{1,0:T(8,128)(2,1)}, bf16[512,512]{1,0:T(8,128)(2,1)}, u32[]{:S(2)}, u32[]{:S(2)}) collective-permute-start(bf16[512,512]{1,0:T(8,128)(2,1)} %get-tuple-element.357.refs_21_.refs_8_), channel_id=1, source_target_pairs={{4,8},{8,4},{20,24},{24,20},{5,9},{9,5},{21,25},{25,21},{6,10},{10... | collective-permute-start | bytes 1572872 | tf_op jit(solution)/shard_map/ppermute | solution.py:78
  240.5 65.1 %all-gather.11.cloned.1.call-start = ((), (), s32[]{:S(2)}) async-start(), calls=%async_computation.9 | async-start | bytes 3538944 | tf_op jit(solution)/shard_map/all_gather | solution.py:109
  242.1 29.3 %collective-permute-start.33 = (bf16[512,1024]{1,0:T(8,128)(2,1)}, bf16[512,1024]{1,0:T(8,128)(2,1)S(1)}, u32[]{:S(2)}, u32[]{:S(2)}) collective-permute-start(bf16[512,1024]{1,0:T(8,128)(2,1)} %get-tuple-element.372), channel_id=1, source_target_pairs={{16,0},{24,4},{20,8},{28,12},{0,16},{8,20},{4,24},{12,28},{17,1},{... | collective-permute-start | bytes 3145736 | tf_op jit(solution)/shard_map/ppermute | solution.py:82
  244.6 26.8 %collective-permute-start.34 = (bf16[512,1024]{1,0:T(8,128)(2,1)}, bf16[512,1024]{1,0:T(8,128)(2,1)}, u32[]{:S(2)}, u32[]{:S(2)}) collective-permute-start(bf16[512,1024]{1,0:T(8,128)(2,1)} %get-tuple-element.373), channel_id=1, source_target_pairs={{20,0},{28,4},{16,8},{24,12},{4,16},{12,20},{0,24},{8,28},{21,1},{... | collective-permute-start | bytes 3145736 | tf_op jit(solution)/shard_map/ppermute | solution.py:82
  245.1 26.4 %collective-permute-start.35 = (bf16[512,1024]{1,0:T(8,128)(2,1)}, bf16[512,1024]{1,0:T(8,128)(2,1)}, u32[]{:S(2)}, u32[]{:S(2)}) collective-permute-start(bf16[512,1024]{1,0:T(8,128)(2,1)} %get-tuple-element.374), channel_id=1, source_target_pairs={{0,32},{32,64},{64,96},{96,0},{1,33},{33,65},{65,97},{97,1},{2,34}... | collective-permute-start | bytes 3145736 | tf_op jit(solution)/shard_map/ppermute | solution.py:48
  246.7 25.2 %collective-permute-start.36 = (bf16[512,1024]{1,0:T(8,128)(2,1)}, bf16[512,1024]{1,0:T(8,128)(2,1)}, u32[]{:S(2)}, u32[]{:S(2)}) collective-permute-start(bf16[512,1024]{1,0:T(8,128)(2,1)} %get-tuple-element.375), channel_id=1, source_target_pairs={{0,96},{32,0},{64,32},{96,64},{1,97},{33,1},{65,33},{97,65},{2,98}... | collective-permute-start | bytes 3145736 | tf_op jit(solution)/shard_map/ppermute | solution.py:48
  275.1 121.7 %reduce-scatter.9.cloned.1.call-start = ((), (), s32[]{:S(2)}) async-start(), calls=%async_computation.10 | async-start | bytes 1966080 | tf_op jit(solution)/shard_map/reduce_scatter | solution.py:889
  276.1 26.4 %collective-permute-start.38 = (bf16[512,1024]{1,0:T(8,128)(2,1)}, bf16[512,1024]{1,0:T(8,128)(2,1)S(1)}, u32[]{:S(2)}, u32[]{:S(2)}) collective-permute-start(bf16[512,1024]{1,0:T(8,128)(2,1)} %get-tuple-element.391), channel_id=1, source_target_pairs={{0,64},{32,96},{64,0},{96,32},{1,65},{33,97},{65,1},{97,33},{2,66}... | collective-permute-start | bytes 3145736 | tf_op jit(solution)/shard_map/ppermute | solution.py:48
  278.1 24.4 %collective-permute-start.40 = (bf16[512,1024]{1,0:T(8,128)(2,1)}, bf16[512,1024]{1,0:T(8,128)(2,1)}, u32[]{:S(2)}, u32[]{:S(2)}) collective-permute-start(bf16[512,1024]{1,0:T(8,128)(2,1)} %get-tuple-element.395), channel_id=1, source_target_pairs={{4,0},{12,4},{0,8},{8,12},{20,16},{28,20},{16,24},{24,28},{5,1},{1... | collective-permute-start | bytes 3145736 | tf_op jit(solution)/shard_map/ppermute | solution.py:82
  279.3 26.4 %collective-permute-start.39 = (bf16[512,1024]{1,0:T(8,128)(2,1)}, bf16[512,1024]{1,0:T(8,128)(2,1)}, u32[]{:S(2)}, u32[]{:S(2)}) collective-permute-start(bf16[512,1024]{1,0:T(8,128)(2,1)} %get-tuple-element.394.refs_8_), channel_id=1, source_target_pairs={{8,4},{4,8},{24,20},{20,24},{9,5},{5,9},{25,21},{21,25},{10,6},{6,... | collective-permute-start | bytes 3145736 | tf_op jit(solution)/shard_map/ppermute | solution.py:82
  305.6 17.8 %collective-permute-start.41 = (bf16[512,512]{1,0:T(8,128)(2,1)}, bf16[512,512]{1,0:T(8,128)(2,1)S(1)}, u32[]{:S(2)}, u32[]{:S(2)}) collective-permute-start(bf16[512,512]{1,0:T(8,128)(2,1)} %get-tuple-element.418), channel_id=1, source_target_pairs={{0,32},{32,64},{64,96},{96,0},{1,33},{33,65},{65,97},{97,1},{2,34}... | collective-permute-start | bytes 1572872 | tf_op jit(solution)/shard_map/ppermute | solution.py:48
  306.4 17.0 %collective-permute-start.42 = (bf16[512,512]{1,0:T(8,128)(2,1)}, bf16[512,512]{1,0:T(8,128)(2,1)S(1)}, u32[]{:S(2)}, u32[]{:S(2)}) collective-permute-start(bf16[512,512]{1,0:T(8,128)(2,1)} %get-tuple-element.419), channel_id=1, source_target_pairs={{0,96},{32,0},{64,32},{96,64},{1,97},{33,1},{65,33},{97,65},{2,98}... | collective-permute-start | bytes 1572872 | tf_op jit(solution)/shard_map/ppermute | solution.py:48
  308.3 15.2 %collective-permute-start.43 = (bf16[512,512]{1,0:T(8,128)(2,1)}, bf16[512,512]{1,0:T(8,128)(2,1)S(1)}, u32[]{:S(2)}, u32[]{:S(2)}) collective-permute-start(bf16[512,512]{1,0:T(8,128)(2,1)} %get-tuple-element.420), channel_id=1, source_target_pairs={{16,0},{24,4},{20,8},{28,12},{0,16},{8,20},{4,24},{12,28},{17,1},{... | collective-permute-start | bytes 1572872 | tf_op jit(solution)/shard_map/ppermute | solution.py:82
  309.2 14.3 %collective-permute-start.44 = (bf16[512,512]{1,0:T(8,128)(2,1)}, bf16[512,512]{1,0:T(8,128)(2,1)S(1)}, u32[]{:S(2)}, u32[]{:S(2)}) collective-permute-start(bf16[512,512]{1,0:T(8,128)(2,1)} %get-tuple-element.421), channel_id=1, source_target_pairs={{20,0},{28,4},{16,8},{24,12},{4,16},{12,20},{0,24},{8,28},{21,1},{... | collective-permute-start | bytes 1572872 | tf_op jit(solution)/shard_map/ppermute | solution.py:82
  324.5 20.8 %collective-permute-start.45 = (bf16[3072,256]{1,0:T(8,128)(2,1)}, bf16[3072,256]{1,0:T(8,128)(2,1)S(1)}, u32[]{:S(2)}, u32[]{:S(2)}) collective-permute-start(bf16[3072,256]{1,0:T(8,128)(2,1)} %get-tuple-element.423), channel_id=1, source_target_pairs={{0,8},{8,0},{1,9},{9,1},{2,10},{10,2},{3,11},{11,3},{4,12},{12,4},... | collective-permute-start | bytes 4718600 | tf_op jit(solution)/shard_map/ppermute | solution.py:44
  325.5 19.8 %collective-permute-start.46 = (bf16[512,512]{1,0:T(8,128)(2,1)S(1)}, bf16[512,512]{1,0:T(8,128)(2,1)S(1)}, u32[]{:S(2)}, u32[]{:S(2)}) collective-permute-start(bf16[512,512]{1,0:T(8,128)(2,1)S(1)} %copy-done.49), channel_id=1, source_target_pairs={{0,64},{32,96},{64,0},{96,32},{1,65},{33,97},{65,1},{97,33},{2,66}... | collective-permute-start | bytes 1572872 | tf_op jit(solution)/shard_map/ppermute | solution.py:48
  326.1 19.2 %collective-permute-start.48 = (bf16[512,512]{1,0:T(8,128)(2,1)S(1)}, bf16[512,512]{1,0:T(8,128)(2,1)S(1)}, u32[]{:S(2)}, u32[]{:S(2)}) collective-permute-start(bf16[512,512]{1,0:T(8,128)(2,1)S(1)} %copy-done.48), channel_id=1, source_target_pairs={{4,0},{12,4},{0,8},{8,12},{20,16},{28,20},{16,24},{24,28},{5,1},{1... | collective-permute-start | bytes 1572872 | tf_op jit(solution)/shard_map/ppermute | solution.py:82
  327.9 17.5 %collective-permute-start.47 = (bf16[512,512]{1,0:T(8,128)(2,1)S(1)}, bf16[512,512]{1,0:T(8,128)(2,1)S(1)}, u32[]{:S(2)}, u32[]{:S(2)}) collective-permute-start(bf16[512,512]{1,0:T(8,128)(2,1)S(1)} %copy-done.21), channel_id=1, source_target_pairs={{8,4},{4,8},{24,20},{20,24},{9,5},{5,9},{25,21},{21,25},{10,6},{6,... | collective-permute-start | bytes 1572872 | tf_op jit(solution)/shard_map/ppermute | solution.py:82
  347.9 68.6 %reduce-scatter.11.cloned.1.call-start = ((), (), s32[]{:S(2)}) async-start(), calls=%async_computation.11 | async-start | bytes 1966080 | tf_op jit(solution)/shard_map/reduce_scatter | solution.py:946
  352.8 20.4 %collective-permute-start.51 = (bf16[896,512]{1,0:T(8,128)(2,1)}, bf16[896,512]{1,0:T(8,128)(2,1)S(1)}, u32[]{:S(2)}, u32[]{:S(2)}) collective-permute-start(bf16[896,512]{1,0:T(8,128)(2,1)} %get-tuple-element.484), channel_id=1, source_target_pairs={{0,32},{32,64},{64,96},{96,0},{1,33},{33,65},{65,97},{97,1},{2,34}... | collective-permute-start | bytes 2752520 | tf_op jit(solution)/shard_map/ppermute | solution.py:48
  353.2 20.0 %collective-permute-start.52 = (bf16[896,512]{1,0:T(8,128)(2,1)}, bf16[896,512]{1,0:T(8,128)(2,1)S(1)}, u32[]{:S(2)}, u32[]{:S(2)}) collective-permute-start(bf16[896,512]{1,0:T(8,128)(2,1)} %get-tuple-element.485), channel_id=1, source_target_pairs={{0,96},{32,0},{64,32},{96,64},{1,97},{33,1},{65,33},{97,65},{2,98}... | collective-permute-start | bytes 2752520 | tf_op jit(solution)/shard_map/ppermute | solution.py:48
  355.6 17.6 %collective-permute-start.53 = (bf16[896,512]{1,0:T(8,128)(2,1)}, bf16[896,512]{1,0:T(8,128)(2,1)}, u32[]{:S(2)}, u32[]{:S(2)}) collective-permute-start(bf16[896,512]{1,0:T(8,128)(2,1)} %get-tuple-element.486), channel_id=1, source_target_pairs={{16,0},{24,4},{20,8},{28,12},{0,16},{8,20},{4,24},{12,28},{17,1},{... | collective-permute-start | bytes 2752520 | tf_op jit(solution)/shard_map/ppermute | solution.py:82
  357.6 20.5 %collective-permute-start.54 = (bf16[896,512]{1,0:T(8,128)(2,1)}, bf16[896,512]{1,0:T(8,128)(2,1)}, u32[]{:S(2)}, u32[]{:S(2)}) collective-permute-start(bf16[896,512]{1,0:T(8,128)(2,1)} %get-tuple-element.487), channel_id=1, source_target_pairs={{20,0},{28,4},{16,8},{24,12},{4,16},{12,20},{0,24},{8,28},{21,1},{... | collective-permute-start | bytes 2752520 | tf_op jit(solution)/shard_map/ppermute | solution.py:82
  378.0 21.3 %collective-permute-start.55 = (bf16[896,512]{1,0:T(8,128)(2,1)}, bf16[896,512]{1,0:T(8,128)(2,1)}, u32[]{:S(2)}, u32[]{:S(2)}) collective-permute-start(bf16[896,512]{1,0:T(8,128)(2,1)} %get-tuple-element.488), channel_id=1, source_target_pairs={{0,64},{32,96},{64,0},{96,32},{1,65},{33,97},{65,1},{97,33},{2,66}... | collective-permute-start | bytes 2752520 | tf_op jit(solution)/shard_map/ppermute | solution.py:48
  378.7 20.6 %collective-permute-start.57 = (bf16[896,512]{1,0:T(8,128)(2,1)}, bf16[896,512]{1,0:T(8,128)(2,1)}, u32[]{:S(2)}, u32[]{:S(2)}) collective-permute-start(bf16[896,512]{1,0:T(8,128)(2,1)} %get-tuple-element.492), channel_id=1, source_target_pairs={{4,0},{12,4},{0,8},{8,12},{20,16},{28,20},{16,24},{24,28},{5,1},{1... | collective-permute-start | bytes 2752520 | tf_op jit(solution)/shard_map/ppermute | solution.py:82
  381.6 24.4 %collective-permute-start.56 = (bf16[896,512]{1,0:T(8,128)(2,1)}, bf16[896,512]{1,0:T(8,128)(2,1)}, u32[]{:S(2)}, u32[]{:S(2)}) collective-permute-start(bf16[896,512]{1,0:T(8,128)(2,1)} %get-tuple-element.520.refs_8_), channel_id=1, source_target_pairs={{8,4},{4,8},{24,20},{20,24},{9,5},{5,9},{25,21},{21,25},{10,6},{6,... | collective-permute-start | bytes 2752520 | tf_op jit(solution)/shard_map/ppermute | solution.py:82
  406.0 9.9 %collective-permute-start.61 = (f32[40,128]{1,0:T(8,128)S(1)}, f32[40,128]{1,0:T(8,128)S(1)}, u32[]{:S(2)}, u32[]{:S(2)}) collective-permute-start(f32[40,128]{1,0:T(8,128)S(1)} %add_select_fusion.6), channel_id=1, source_target_pairs={{0,64},{32,96},{64,0},{96,32},{1,65},{33,97},{65,1},{97,33},{2,66}... | collective-permute-start | bytes 61448 | tf_op jit(solution)/shard_map/ppermute | solution.py:56
  412.7 9.8 %collective-permute-start.63 = (bf16[128,512]{1,0:T(8,128)(2,1)}, bf16[128,512]{1,0:T(8,128)(2,1)S(1)}, u32[]{:S(2)}, u32[]{:S(2)}) collective-permute-start(bf16[128,512]{1,0:T(8,128)(2,1)} %get-tuple-element.508), channel_id=1, source_target_pairs={{0,32},{32,64},{64,96},{96,0},{1,33},{33,65},{65,97},{97,1},{2,34}... | collective-permute-start | bytes 393224 | tf_op jit(solution)/shard_map/ppermute | solution.py:48
  422.5 12.3 %collective-permute-start.71 = (f32[40,128]{1,0:T(8,128)S(1)}, f32[40,128]{1,0:T(8,128)S(1)}, u32[]{:S(2)}, u32[]{:S(2)}) collective-permute-start(f32[40,128]{1,0:T(8,128)S(1)} %add_select_fusion.4), channel_id=1, source_target_pairs={{0,16},{4,20},{16,0},{20,4},{1,17},{5,21},{17,1},{21,5},{2,18},{6,... | collective-permute-start | bytes 61448 | tf_op jit(solution)/shard_map/ppermute | solution.py:101
  422.8 19.8 %collective-permute-start.70 = (bf16[1536,256]{1,0:T(8,128)(2,1)S(1)}, bf16[1536,256]{1,0:T(8,128)(2,1)S(1)}, u32[]{:S(2)}, u32[]{:S(2)}) collective-permute-start(bf16[1536,256]{1,0:T(8,128)(2,1)S(1)} %pad_maximum_fusion), channel_id=1, source_target_pairs={{4,8},{8,4},{5,9},{9,5},{6,10},{10,6},{7,11},{11,7},{20,24},{24,20... | collective-permute-start | bytes 2359304 | tf_op jit(solution)/shard_map/ppermute | solution.py:39
  (72 other events, 715.9 us)
Sparse Core Ops, SparseCore 0:
  44.7 28.6 all-gather.4
  75.6 27.8 all-gather.6
  139.9 25.0 reduce-scatter.4
  172.8 29.7 all-gather.8
  240.6 25.3 reduce-scatter.6
  275.2 27.7 all-gather.10
  348.0 23.9 reduce-scatter.8
  374.4 26.3 reduce-scatter.10

commit v4 on v3

--- a/solution.py
+++ b/solution.py
@@ -109,8 +109,8 @@
     return lax.all_gather(own, (CORE, Z), axis=0, tiled=True)
 
 
-def team_scatter(give, keep):
-    both = (keep.astype(f32) + other_core(give).astype(f32)).astype(bf16)
+def team_scatter(other, keep):
+    both = (keep.astype(f32) + other.astype(f32)).astype(bf16)
     return lax.psum_scatter(both, Z, scatter_dimension=0, tiled=True).astype(f32)
 
 
@@ -412,18 +412,16 @@
     send(a2, a2_out)
     for copy in copies:
         copy.wait()
-    for half in range(2):
-        rows = slice(half * 384, (half + 1) * 384)
-        for j in range(4):
-            cols = slice(j * 256, (j + 1) * 256)
-            gate = kdot(a2[rows, :], w_gate[:, cols])
-            up = kdot(a2[rows, :], w_up[:, cols])
-            grad = kdot(dy[rows, :], w_down[:, cols])
-            sig = 1.0 / (1.0 + jnp.exp(-gate))
-            act = gate * sig
-            hid[rows, cols] = (act * up).astype(bf16)
-            dgate[rows, cols] = (grad * up * sig * (1.0 + gate * (1.0 - sig))).astype(bf16)
-            dup[rows, cols] = (grad * act).astype(bf16)
+    for j in range(4):
+        cols = slice(j * 256, (j + 1) * 256)
+        gate = kdot(a2[...], w_gate[:, cols])
+        up = kdot(a2[...], w_up[:, cols])
+        grad = kdot(dy[...], w_down[:, cols])
+        sig = 1.0 / (1.0 + jnp.exp(-gate))
+        act = gate * sig
+        hid[:, cols] = (act * up).astype(bf16)
+        dgate[:, cols] = (grad * up * sig * (1.0 + gate * (1.0 - sig))).astype(bf16)
+        dup[:, cols] = (grad * act).astype(bf16)
     for source, to in ((hid, hid_out), (dgate, dgate_out), (dup, dup_out)):
         send(source, to)
     for ref, to, c in ((give, give_out, 1 - at[3]), (keep, keep_out, at[3])):
@@ -546,19 +544,45 @@
             ref[rows, lanes(at[2] ^ j, 128)] = value[:, j * 128 : (j + 1) * 128].astype(bf16)
 
 
+def wide_sums(at, a, b, own, values):
+    for i in range(4):
+        rows = slice(i * 128, (i + 1) * 128)
+        head = jnp.where(at[2] == at[3], own[rows, :], b[0][rows, :])
+        of_b = head.astype(f32) + b[1][rows, :].astype(f32) + b[2][rows, :].astype(f32) + b[3][rows, :].astype(f32)
+        of_a = a[0][rows, :].astype(f32) + a[1][rows, :].astype(f32) + a[2][rows, :].astype(f32) + a[3][rows, :].astype(f32)
+        for value, total_ in ((values[i], of_b), (values[4 + i], of_a)):
+            for j in range(2):
+                value[j * 128 : (j + 1) * 128, :] = total_[:, j * 512 : (j + 1) * 512].astype(bf16)
+
+
 def attention_weight_body(at, a1, dqkv, db, o, *refs):
-    outs, values, sem = refs[:8], refs[8:16], refs[16]
+    pieces, outs, values, sums = refs[:9], refs[9:17], refs[17:25], refs[25:33]
+    held, sem, out_sem = refs[33:42], refs[42], refs[43]
+    arriving = [pltpu.make_async_copy(x, v, sem.at[i]) for i, (x, v) in enumerate(zip(pieces, held))]
+    for copy in arriving:
+        copy.start()
+    sent = []
+
+    def send(source, to):
+        sent.append(pltpu.make_async_copy(source, to, out_sem.at[len(sent)]))
+        sent[-1].start()
+
     for i in range(4):
         cols, rows = slice(i * 512, (i + 1) * 512), slice(i * 128, (i + 1) * 128)
         values[i][...] = kdot(a1[:, cols], dqkv[:, 256:], tn).astype(bf16)
+        send(values[i], outs[i].at[pl.ds(0, 512)])
         for n, left, right in ((slice(0, 256), a1, dqkv.at[:, :256]), (slice(256, 512), db, o)):
             value = kdot(left[:, cols], right[...], tn).astype(bf16)
             for k in range(4):
                 values[4 + k][rows, n] = value[k * 128 : (k + 1) * 128]
-    copies = [pltpu.make_async_copy(v, o_.at[pl.ds(0, 512)], sem.at[i]) for i, (v, o_) in enumerate(zip(values, outs))]
-    for copy in copies:
-        copy.start()
-    for copy in copies:
+    for i in range(4, 8):
+        send(values[i], outs[i].at[pl.ds(0, 512)])
+    for copy in arriving:
+        copy.wait()
+    wide_sums(at, held[:4], held[4:8], held[8], sums)
+    for i in range(8):
+        send(sums[i], outs[i].at[pl.ds(512, 256)])
+    for copy in sent:
         copy.wait()
 
 
@@ -746,7 +770,7 @@
         (give, keep, upstream, *wide_a, *wide_b, a_wide, b_wide, a_down, b_down)
     )
     wide_a, wide_b, (a_wide, b_wide, a_down, b_down) = done[:2], done[2:4], done[4:]
-    attn_own = team_scatter(give, keep)
+    attn_own = team_scatter(other_core(give), keep)
     halves = [shift(wide_a[0][:256], Y, -1), shift(wide_a[1][256:], Y, 1)]
     wide_a = [a_wide, wide_a[0], *halves, wide_a[1]]
     wide_b = [x_in(b_wide, *flip) for flip in FLIPS[:2]] + wide_b
@@ -855,22 +879,18 @@
     blocks = call(
         attention_weight_body,
         "attention_weights",
-        [at, a1, dqkv, db, o],
+        [at, a1, dqkv, db, o, *got_gate, *got_up, up_b[0]],
         [message] * 8,
-        [pltpu.VMEM((512, 512), bf16)] * 8 + [pltpu.SemaphoreType.DMA((8,))],
+        [
+            *[pltpu.VMEM((512, 512), bf16)] * 8,
+            *[pltpu.VMEM((256, 512), bf16)] * 8,
+            *[pltpu.VMEM((512, FF), bf16)] * 9,
+            pltpu.SemaphoreType.DMA((9,)),
+            pltpu.SemaphoreType.DMA((16,)),
+        ],
         2 * LEN * WIDTH * 1024,
+        anywhere=9,
         outs_anywhere=8,
-    )
-    blocks = call(
-        functools.partial(ffn_sum_body, 512),
-        "feed_forward_sums_wide",
-        [at, *got_gate, *got_up, up_b[0], *blocks],
-        [message] * 8,
-        [pltpu.VMEM((256, 512), bf16)] * 8 + [pltpu.SemaphoreType.DMA((8,))],
-        0,
-        anywhere=8,
-        outs_anywhere=8,
-        alias=8,
     )
     part_keep, part_other, *got = lax.optimization_barrier((part_keep, part_other, *blocks, *got_down_a, *got_down_b))
     blocks, got_down_a, got_down_b = got[:8], got[8:12], got[12:]
@@ -918,6 +938,15 @@
     small = small[6:]
     small = join([small, y_other(small, 1)])
     got_attn_a, got_attn_b, small, attn_grad = lax.optimization_barrier((got_attn_a, got_attn_b, small, attn_grad))
+    ffn_own = lax.psum_scatter(out_late, Z, scatter_dimension=0, tiled=True).astype(f32)
+
+    gain_pair = jnp.dot(pick, gain_rows[0].reshape(16, 128), precision=lax.Precision.HIGHEST)
+    gain_cols = lax.dynamic_slice(gain_pair, (mine * 2, 0), (2, 128)).reshape(1, HEAD)
+    grad_inputs = (
+        db_cols.astype(f32) + r1 * attn_grad * gain_cols - x_own.astype(f32) * r1**2 * (row_sum / WIDTH)
+    )
+    home = [(h_cols.astype(f32) + ffn_own).astype(bf16), grad_inputs.astype(bf16)]
+    home = swap(jnp.concatenate(home, 0))
     *sum_b, kv_give, kv_keep = call(
         join_body,
         "join_sums",
@@ -929,32 +958,23 @@
     )
     kv_sum = (kv_keep + kv_partner(kv_give).astype(f32)).astype(bf16)
     sum_b = [sum_b[0]] + [shift(sum_b[i], Y, i) for i in (1, 2, 3)]
+    first_y = sum_b[1]
     small = join([small, y_other(small, 2)])
-    small = join([small, x_ring(small, 1)])
-    kv_sum, small, *sum_b = lax.optimization_barrier((kv_sum, small, *sum_b))
+    kv_sum, home, small, *sum_b = lax.optimization_barrier((kv_sum, home, small, *sum_b))
     sum_a = [x_out(kv_sum[i * 128 : (i + 1) * 128], *flip) for i, flip in enumerate(FLIPS)]
     sum_a[0] = own_or(sum_a[0], kv_sum[:128])
     grads = call(
         finish_body,
         "finish",
-        [at, *got_attn_a, *got_attn_b, after(block_0, kv_sum)],
+        [at, *got_attn_a, *got_attn_b, after(block_0, first_y)],
         [((128, FF), f32)] * 3,
         [pltpu.VMEM((384, 512), bf16)] * 9 + [pltpu.SemaphoreType.DMA((9,))],
         0,
         anywhere=9,
     )
-    ffn_own = lax.psum_scatter(out_late, Z, scatter_dimension=0, tiled=True).astype(f32)
-    ffn_own = after(ffn_own, small)
-
-    gain_pair = jnp.dot(pick, gain_rows[0].reshape(16, 128), precision=lax.Precision.HIGHEST)
-    gain_cols = lax.dynamic_slice(gain_pair, (mine * 2, 0), (2, 128)).reshape(1, HEAD)
-    grad_inputs = (
-        db_cols.astype(f32) + r1 * attn_grad * gain_cols - x_own.astype(f32) * r1**2 * (row_sum / WIDTH)
-    )
-    home = [(h_cols.astype(f32) + ffn_own).astype(bf16), grad_inputs.astype(bf16)]
-    home = swap(jnp.concatenate(home, 0))
-    small = join([small, x_ring(small, 2)])
-    sum_a, home, small, grads = lax.optimization_barrier((sum_a, home, small, grads))
+    for mask in (1, 2):
+        small = join([small, x_ring(small, mask)])
+    sum_a, small, grads = lax.optimization_barrier((sum_a, small, grads))
     query_output = total(sum_b)
     kv_done = total(sum_a)
     tok = y * 4 + lo * 2 + core

time: 467 us -> 461 us (0.987)
  waiting for transfers between devices: 161 us -> 156 us
    ppermute x16, waiting for transfers between devices: 20.9 us -> 11.5 us  [x_out(): return lax.ppermute(a, (XLO, CORE, XHI), x_pairs(flip_lo, flip_core, True))]
    ppermute x16, starting transfers between devices: 30.7 us -> 36.3 us  [x_out(): return lax.ppermute(a, (XLO, CORE, XHI), x_pairs(flip_lo, flip_core, True))]
    pallas_call x15 -> x14, Pallas kernels: 127 us -> 123 us  [call(): pl.pallas_call(body, name=name, out_shape=[jax.ShapeDtypeStruct(s, d) for...]
  transfers between devices with their start and end apart: 80 -> 80, of which waited for: 38 -> 37; matrix products, arithmetic and copies ran while one was open for 4% -> 5% of each run, Pallas kernels for 20% -> 20%
where the time goes in v4:
time: 461 us; the launch traced here: 453 us
  waiting for transfers between devices  156 us (34%)
  Pallas kernels  123 us (27%)
  starting transfers between devices  109 us (24%)
  other arithmetic  33.3 us (7%)
  between operations  17.1 us (4%)
  local copies, waits for them, and re-layouts  14.6 us (3%)
    pallas_call x14, Pallas kernels, call(): pl.pallas_call(body, name=name, out_shape=[jax.ShapeDtypeStruct(s, d) for...  123 us
    ppermute x25, waiting for transfers between devices, shift(): return lax.ppermute(a, axis, [(i, (i + by) % 4) for i in range(4)])  71.3 us
    ppermute x16, waiting for transfers between devices, x_in(): return lax.ppermute(a, (XLO, CORE, XHI), x_pairs(flip_lo, flip_core, False))  43.3 us
    ppermute x16, starting transfers between devices, x_out(): return lax.ppermute(a, (XLO, CORE, XHI), x_pairs(flip_lo, flip_core, True))  36.3 us
    ppermute x25, starting transfers between devices, shift(): return lax.ppermute(a, axis, [(i, (i + by) % 4) for i in range(4)])  32.6 us
    ppermute x16, starting transfers between devices, x_in(): return lax.ppermute(a, (XLO, CORE, XHI), x_pairs(flip_lo, flip_core, False))  22.4 us
    ppermute x16, waiting for transfers between devices, x_out(): return lax.ppermute(a, (XLO, CORE, XHI), x_pairs(flip_lo, flip_core, True))  11.5 us
  transfers between devices with their start and end apart: 80, of which 37 were waited for; matrix products, arithmetic and copies ran while one was open for 5% of the time, Pallas kernels for 20%

profile of v4, /device:TPU:1, one launch (start us, length us, event | category | flops | bytes accessed | tf_op | source)
XLA Modules:
  0.0 453.4 jit_solution(2123471056218415436)
XLA Ops:
  10.4 3.3 lay_out_y.1
  13.7 6.2 %collective-permute-start = (bf16[1552,256]{1,0:T(8,128)(2,1)}, bf16[1552,256]{1,0:T(8,128)(2,1)S(1)}, u32[]{:S(2)}, u32[]{:S(2)}) collective-permute-start(bf16[1552,256]{1,0:T(8,128)(2,1)} %get-tuple-element.272), channel_id=1, source_target_pairs={{4,8},{8,4},{5,9},{9,5},{6,10},{10,6},{7,11},{11,7},{20,24},{24,20... | collective-permute-start | bytes 2383880 | tf_op jit(solution)/shard_map/ppermute | solution.py:39
  25.8 2.7 lay_out_x.1
  30.2 4.6 %collective-permute-done.3.refs_7_ = bf16[528,512]{1,0:T(8,128)(2,1)S(1)} collective-permute-done((bf16[528,512]{1,0:T(8,128)(2,1)}, bf16[528,512]{1,0:T(8,128)(2,1)S(1)}, u32[]{:S(2)}, u32[]{:S(2)}) %collective-permute-start.3) | collective-permute-done | bytes 540704 | tf_op jit(solution)/shard_map/ppermute | solution.py:48
  35.5 7.6 %collective-permute-done.5.refs_3_ = bf16[512,512]{1,0:T(8,128)(2,1)} collective-permute-done((bf16[512,512]{1,0:T(8,128)(2,1)}, bf16[512,512]{1,0:T(8,128)(2,1)}, u32[]{:S(2)}, u32[]{:S(2)}) %collective-permute-start.5) | collective-permute-done | bytes 524320 | tf_op jit(solution)/shard_map/ppermute | solution.py:78
  44.7 2.6 collective-permute-start.6
  47.3 3.0 collective-permute-start.8
  50.3 9.0 %collective-permute-done.6 = bf16[512,512]{1,0:T(8,128)(2,1)S(1)} collective-permute-done((bf16[512,512]{1,0:T(8,128)(2,1)}, bf16[512,512]{1,0:T(8,128)(2,1)S(1)}, u32[]{:S(2)}, u32[]{:S(2)}) %collective-permute-start.6) | collective-permute-done | bytes 524320 | tf_op jit(solution)/shard_map/ppermute | solution.py:78
  60.3 2.4 collective-permute-done.7.refs_1_
  64.2 3.0 pack.1
  67.4 2.1 collective-permute-start.11
  69.9 2.3 collective-permute-start.9
  72.2 11.9 %collective-permute-done.10.refs_8_.refs_14_ = bf16[512,512]{1,0:T(8,128)(2,1)S(1)} collective-permute-done((bf16[512,512]{1,0:T(8,128)(2,1)}, bf16[512,512]{1,0:T(8,128)(2,1)S(1)}, u32[]{:S(2)}, u32[]{:S(2)}) %collective-permute-start.10) | collective-permute-done | bytes 524320 | tf_op jit(solution)/shard_map/ppermute | solution.py:48
  84.2 2.3 collective-permute-start.14
  86.9 2.8 collective-permute-start.13
  89.7 2.5 multiply_sine_fusion
  92.2 4.7 %riders.1 = (bf16[512,1024]{1,0:T(8,128)(2,1)}, bf16[512,1024]{1,0:T(8,128)(2,1)}, bf16[512,512]{1,0:T(8,128)(2,1)}, bf16[512,512]{1,0:T(8,128)(2,1)}) custom-call(s32[5]{0:T(128)} %stack.74.at, bf16[512,512]{1,0:T(8,128)(2,1)} %broadcast_select_fusion.3.refs_0_, bf16[512,512]{1,0:T(8,128)(2,1)} %copy-done.7, ...), custom_call_target="tpu_custom_call" | custom-call | bytes 7405568 | tf_op jit(solution)/shard_map/riders/pallas_call | solution.py:155
  96.9 6.2 %collective-permute-done.14 = bf16[576,512]{1,0:T(8,128)(2,1)S(1)} collective-permute-done((bf16[576,512]{1,0:T(8,128)(2,1)}, bf16[576,512]{1,0:T(8,128)(2,1)S(1)}, u32[]{:S(2)}, u32[]{:S(2)}) %collective-permute-start.14) | collective-permute-done | bytes 589856 | tf_op jit(solution)/shard_map/ppermute | solution.py:78
  104.1 2.7 collective-permute-start.16
  106.8 2.2 collective-permute-start.19
  110.4 15.6 %attention_forward.1 = (bf16[768,2048]{1,0:T(8,128)(2,1)}, f32[768,1]{1,0:T(8,128)}, bf16[96,2048]{1,0:T(8,128)(2,1)}, bf16[768,256]{1,0:T(8,128)(2,1)}, bf16[76...) custom-call(s32[5]{0:T(128)} %stack.74.at, ...), custom_call_target="tpu_custom_call" | custom-call | flops 3221225472 | bytes 16728064 | tf_op jit(solution)/shard_map/attention_forward/pallas_call | solution.py:155
  126.0 4.0 collective-permute-done.17.refs_7_
  133.2 3.6 collective-permute-done.20
  136.8 3.0 add_convert_fusion.3
  140.3 4.1 collective-permute-start.23
  145.5 2.8 collective-permute-start.21
  148.3 6.5 %collective-permute-done.22.refs_6_ = bf16[256,1024]{1,0:T(8,128)(2,1)S(1)} collective-permute-done((bf16[256,1024]{1,0:T(8,128)(2,1)S(1)}, bf16[256,1024]{1,0:T(8,128)(2,1)S(1)}, u32[]{:S(2)}, u32[]{:S(2)}) %collective-permute-start.22) | collective-permute-done | bytes 524320 | tf_op jit(solution)/shard_map/ppermute | solution.py:48
  155.5 4.6 %order_upstream.1.refs_2_.dy = bf16[768,2048]{1,0:T(8,128)(2,1)} custom-call(s32[5]{0:T(128)} %stack.74.at, bf16[6144,256]{1,0:T(8,128)(2,1)} %all-gather.7.cloned.1.call-done.whole), custom_call_target="tpu_custom_call" | custom-call | bytes 6291456 | tf_op jit(solution)/shard_map/order_upstream/pallas_call | solution.py:155
  160.1 5.0 %reduce-scatter.5.cloned.1.call-done = bf16[96,2048]{1,0:T(8,128)(2,1)} async-done(((bf16[384,2048]{1,0:T(8,128)(2,1)}), bf16[96,2048]{1,0:T(8,128)(2,1)}) %reduce-scatter.5.cloned.1.call-update) | async-done | bytes 393232 | tf_op jit(solution)/shard_map/reduce_scatter | solution.py:114
  166.2 4.6 %collective-permute-done.25.refs_9_.refs_1_ = bf16[512,512]{1,0:T(8,128)(2,1)} collective-permute-done((bf16[512,512]{1,0:T(8,128)(2,1)}, bf16[512,512]{1,0:T(8,128)(2,1)}, u32[]{:S(2)}, u32[]{:S(2)}) %collective-permute-start.25) | collective-permute-done | bytes 524320 | tf_op jit(solution)/shard_map/ppermute | solution.py:48
  172.8 2.2 collective-permute-start.27
  175.1 2.5 collective-permute-start.31
  178.0 3.9 collective-permute-start.28
  181.9 5.2 %collective-permute-done.27.refs_10_.refs_2_ = bf16[512,512]{1,0:T(8,128)(2,1)S(1)} collective-permute-done((bf16[512,512]{1,0:T(8,128)(2,1)}, bf16[512,512]{1,0:T(8,128)(2,1)S(1)}, u32[]{:S(2)}, u32[]{:S(2)}) %collective-permute-start.27) | collective-permute-done | bytes 524320 | tf_op jit(solution)/shard_map/ppermute | solution.py:48
  189.1 12.3 %collective-permute-done.30.refs_18_.refs_6_ = bf16[512,512]{1,0:T(8,128)(2,1)S(1)} collective-permute-done((bf16[512,512]{1,0:T(8,128)(2,1)}, bf16[512,512]{1,0:T(8,128)(2,1)S(1)}, u32[]{:S(2)}, u32[]{:S(2)}) %collective-permute-start.30) | collective-permute-done | bytes 524320 | tf_op jit(solution)/shard_map/ppermute | solution.py:78
  202.7 31.1 %feed_forward.1 = (bf16[768,256]{1,0:T(8,128)(2,1)}, bf16[768,2048]{1,0:T(8,128)(2,1)}, bf16[768,1024]{1,0:T(8,128)(2,1)}, bf16[768,1024]{1,0:T(8,128)(2,1)}, bf...) custom-call(s32[5]{0:T(128)} %stack.74.at, ...), custom_call_target="tpu_custom_call" | custom-call | flops 22548578304 | bytes 36110336 | tf_op jit(solution)/shard_map/feed_forward/pallas_call | solution.py:155
  234.2 3.3 collective-permute-done.32
  237.5 3.1 add_convert_fusion.2
  242.2 2.5 collective-permute-start.33
  248.6 13.1 %weight_rest.1 = (bf16[512,1024]{1,0:T(8,128)(2,1)}, bf16[512,1024]{1,0:T(8,128)(2,1)}, bf16[512,1024]{1,0:T(8,128)(2,1)}, bf16[512,1024]{1,0:T(8,128)(2,1)}, bf...) custom-call(s32[5]{0:T(128)} %stack.74.at, ...), custom_call_target="tpu_custom_call" | custom-call | flops 6442450944 | bytes 19398656 | tf_op jit(solution)/shard_map/weight_rest/pallas_call | solution.py:155
  261.7 8.7 %feed_forward_out.1 = (bf16[3072,256]{1,0:T(8,128)(2,1)}, bf16[3072,256]{1,0:T(8,128)(2,1)}) custom-call(s32[5]{0:T(128)} %stack.74.at, bf16[768,1024]{1,0:T(8,128)(2,1)} %get-tuple-element.360.hid, bf16[512,512]{1,0:T(8,128)(2,1)} %get-tuple-element.341.refs_8_.refs_0_, bf16[512,512]{1,0:T(8,128)(2,1)} %collective-permute-done.25.refs_9_.refs_1_, ...), custom_call_target="tpu_custom_call" | custom-call | flops 3221225472 | bytes 9437184 | tf_op jit(solution)/shard_map/feed_forward_out/pallas_call | solution.py:155
  272.9 2.3 subtract_convert_fusion.1
  276.1 2.1 collective-permute-start.38
  279.3 4.3 collective-permute-start.39
  285.4 17.2 %collective-permute-done.38.refs_1_ = bf16[512,1024]{1,0:T(8,128)(2,1)S(1)} collective-permute-done((bf16[512,1024]{1,0:T(8,128)(2,1)}, bf16[512,1024]{1,0:T(8,128)(2,1)S(1)}, u32[]{:S(2)}, u32[]{:S(2)}) %collective-permute-start.38) | collective-permute-done | bytes 1048608 | tf_op jit(solution)/shard_map/ppermute | solution.py:48
  302.6 3.2 collective-permute-done.39.refs_4_
  309.5 14.0 %attention_backward.1 = (bf16[768,256]{1,0:T(8,128)(2,1)}, bf16[768,768]{1,0:T(8,128)(2,1)}, f32[768,1]{1,0:T(8,128)}, f32[1,2048]{1,0:T(1,128)}, bf16[3072,256]{1,0:T(8,128)(2,1)}, /*index=5*/bf16[3072,256]{1,0:T(8,128)(2,1)}) custom-call(s32[5]{0:T(128)} %stack.74.at, bf16[768,2048]{1,0:T(8,128)(2,1)} %all-gather.11.cloned.1.call-done.refs_0_.db, ...), custom_call_target="tpu_custom_call" | custom-call | flops 3221225472 | bytes 17518592 | tf_op jit(solution)/shard_map/attention_backward/pallas_call | solution.py:155
  328.0 3.7 collective-permute-start.47
  331.7 10.4 %attention_weights.1 = (bf16[896,512]{1,0:T(8,128)(2,1)}, bf16[896,512]{1,0:T(8,128)(2,1)}, bf16[896,512]{1,0:T(8,128)(2,1)}, bf16[896,512]{1,0:T(8,128)(2,1)}, ...) custom-call(s32[5]{0:T(128)} %stack.74.at, ...), custom_call_target="tpu_custom_call" | custom-call | flops 3221225472 | bytes 24641536 | tf_op jit(solution)/shard_map/attention_weights/pallas_call | solution.py:155
  346.1 3.6 feed_forward_sums_down.1
  350.1 2.4 collective-permute-start.52
  357.4 3.2 collective-permute-done.50
  360.6 12.7 %collective-permute-done.51.refs_2_ = bf16[896,512]{1,0:T(8,128)(2,1)S(1)} collective-permute-done((bf16[896,512]{1,0:T(8,128)(2,1)}, bf16[896,512]{1,0:T(8,128)(2,1)S(1)}, u32[]{:S(2)}, u32[]{:S(2)}) %collective-permute-start.51) | collective-permute-done | bytes 917536 | tf_op jit(solution)/shard_map/ppermute | solution.py:48
  373.3 2.0 collective-permute-done.54.refs_7_
  375.7 2.9 collective-permute-start.57
  378.6 5.1 %collective-permute-start.56 = (bf16[896,512]{1,0:T(8,128)(2,1)}, bf16[896,512]{1,0:T(8,128)(2,1)}, u32[]{:S(2)}, u32[]{:S(2)}) collective-permute-start(bf16[896,512]{1,0:T(8,128)(2,1)} %get-tuple-element.503.refs_8_), channel_id=1, source_target_pairs={{8,4},{4,8},{24,20},{20,24},{9,5},{5,9},{25,21},{21,25},{10,6},{6,... | collective-permute-start | bytes 2752520 | tf_op jit(solution)/shard_map/ppermute | solution.py:82
  386.0 3.3 collective-permute-done.58
  389.5 7.4 %collective-permute-done.59 = f32[40,128]{1,0:T(8,128)S(1)} collective-permute-done((f32[40,128]{1,0:T(8,128)S(1)}, f32[40,128]{1,0:T(8,128)S(1)}, u32[]{:S(2)}, u32[]{:S(2)}) %collective-permute-start.59) | collective-permute-done | bytes 20512 | tf_op jit(solution)/shard_map/ppermute | solution.py:56
  398.1 4.9 %collective-permute-done.56.refs_4_ = bf16[896,512]{1,0:T(8,128)(2,1)} collective-permute-done((bf16[896,512]{1,0:T(8,128)(2,1)}, bf16[896,512]{1,0:T(8,128)(2,1)}, u32[]{:S(2)}, u32[]{:S(2)}) %collective-permute-start.56) | collective-permute-done | bytes 917536 | tf_op jit(solution)/shard_map/ppermute | solution.py:82
  406.7 4.5 join_sums.1
  416.5 3.4 collective-permute-done.63
  420.0 3.9 finish.1
  426.0 6.9 %collective-permute-start.66 = (bf16[128,256]{1,0:T(8,128)(2,1)S(1)}, bf16[128,256]{1,0:T(8,128)(2,1)S(1)}, u32[]{:S(2)}, u32[]{:S(2)}) collective-permute-start(bf16[128,256]{1,0:T(8,128)(2,1)S(1)} %slice.121), channel_id=1, source_target_pairs={{8,4},{4,8},{24,20},{20,24},{9,5},{5,9},{25,21},{21,25},{10,6},{6,... | collective-permute-start | bytes 196616 | tf_op jit(solution)/shard_map/ppermute | solution.py:82
  435.2 2.6 collective-permute-start.68
  (293 shorter events, 84.6 us)
Async XLA Ops:
  7.2 96.8 %all-gather.5.cloned.1.call-start = ((), (), s32[]{:S(2)}) async-start(), calls=%async_computation.4 | async-start | bytes 3538944 | tf_op jit(solution)/shard_map/all_gather | solution.py:109
  13.7 16.3 %collective-permute-start = (bf16[1552,256]{1,0:T(8,128)(2,1)}, bf16[1552,256]{1,0:T(8,128)(2,1)S(1)}, u32[]{:S(2)}, u32[]{:S(2)}) collective-permute-start(bf16[1552,256]{1,0:T(8,128)(2,1)} %get-tuple-element.272), channel_id=1, source_target_pairs={{4,8},{8,4},{5,9},{9,5},{6,10},{10,6},{7,11},{11,7},{20,24},{24,20... | collective-permute-start | bytes 2383880 | tf_op jit(solution)/shard_map/ppermute | solution.py:39
  22.4 12.3 %collective-permute-start.3 = (bf16[528,512]{1,0:T(8,128)(2,1)}, bf16[528,512]{1,0:T(8,128)(2,1)S(1)}, u32[]{:S(2)}, u32[]{:S(2)}) collective-permute-start(bf16[528,512]{1,0:T(8,128)(2,1)} %get-tuple-element.285.refs_4_), channel_id=1, source_target_pairs={{0,32},{32,64},{64,96},{96,0},{1,33},{33,65},{65,97},{97,1},{2,34}... | collective-permute-start | bytes 1622024 | tf_op jit(solution)/shard_map/ppermute | solution.py:48
  23.7 11.8 %collective-permute-start.2 = (bf16[528,512]{1,0:T(8,128)(2,1)}, bf16[528,512]{1,0:T(8,128)(2,1)S(1)}, u32[]{:S(2)}, u32[]{:S(2)}) collective-permute-start(bf16[528,512]{1,0:T(8,128)(2,1)} %get-tuple-element.285.refs_4_), channel_id=1, source_target_pairs={{0,96},{32,0},{64,32},{96,64},{1,97},{33,1},{65,33},{97,65},{2,98}... | collective-permute-start | bytes 1622024 | tf_op jit(solution)/shard_map/ppermute | solution.py:48
  28.5 14.6 %collective-permute-start.5 = (bf16[512,512]{1,0:T(8,128)(2,1)}, bf16[512,512]{1,0:T(8,128)(2,1)}, u32[]{:S(2)}, u32[]{:S(2)}) collective-permute-start(bf16[512,512]{1,0:T(8,128)(2,1)} %lay_out_x.1), channel_id=1, source_target_pairs={{0,20},{4,28},{8,16},{12,24},{16,4},{20,12},{24,0},{28,8},{1,21},{... | collective-permute-start | bytes 1572872 | tf_op jit(solution)/shard_map/ppermute | solution.py:78
  28.6 15.2 %collective-permute-start.4 = (bf16[512,512]{1,0:T(8,128)(2,1)}, bf16[512,512]{1,0:T(8,128)(2,1)}, u32[]{:S(2)}, u32[]{:S(2)}) collective-permute-start(bf16[512,512]{1,0:T(8,128)(2,1)} %lay_out_x.1), channel_id=1, source_target_pairs={{0,16},{4,24},{8,20},{12,28},{16,0},{20,8},{24,4},{28,12},{1,17},{... | collective-permute-start | bytes 1572872 | tf_op jit(solution)/shard_map/ppermute | solution.py:78
  44.7 81.3 %all-gather.7.cloned.1.call-start = ((), (), s32[]{:S(2)}) async-start(), calls=%async_computation.5 | async-start | bytes 3538944 | tf_op jit(solution)/shard_map/all_gather | solution.py:109
  44.7 14.6 %collective-permute-start.6 = (bf16[512,512]{1,0:T(8,128)(2,1)}, bf16[512,512]{1,0:T(8,128)(2,1)S(1)}, u32[]{:S(2)}, u32[]{:S(2)}) collective-permute-start(bf16[512,512]{1,0:T(8,128)(2,1)} %lay_out_x.1), channel_id=1, source_target_pairs={{4,8},{8,4},{20,24},{24,20},{5,9},{9,5},{21,25},{25,21},{6,10},{10... | collective-permute-start | bytes 1572872 | tf_op jit(solution)/shard_map/ppermute | solution.py:78
  47.3 15.3 %collective-permute-start.8 = (bf16[528,512]{1,0:T(8,128)(2,1)S(1)}, bf16[528,512]{1,0:T(8,128)(2,1)S(1)}, u32[]{:S(2)}, u32[]{:S(2)}) collective-permute-start(bf16[528,512]{1,0:T(8,128)(2,1)S(1)} %copy-done.3), channel_id=1, source_target_pairs={{0,64},{32,96},{64,0},{96,32},{1,65},{33,97},{65,1},{97,33},{2,66}... | collective-permute-start | bytes 1622024 | tf_op jit(solution)/shard_map/ppermute | solution.py:48
  50.3 12.3 %collective-permute-start.7 = (bf16[512,512]{1,0:T(8,128)(2,1)}, bf16[512,512]{1,0:T(8,128)(2,1)S(1)}, u32[]{:S(2)}, u32[]{:S(2)}) collective-permute-start(bf16[512,512]{1,0:T(8,128)(2,1)} %lay_out_x.1), channel_id=1, source_target_pairs={{0,4},{4,12},{8,0},{12,8},{16,20},{20,28},{24,16},{28,24},{1,5},{5... | collective-permute-start | bytes 1572872 | tf_op jit(solution)/shard_map/ppermute | solution.py:78
  67.3 97.9 %reduce-scatter.5.cloned.1.call-start = ((), (), s32[]{:S(2)}) async-start(), calls=%async_computation.6 | async-start | bytes 1966080 | tf_op jit(solution)/shard_map/reduce_scatter | solution.py:114
  67.3 16.8 %collective-permute-start.12 = (bf16[576,512]{1,0:T(8,128)(2,1)}, bf16[576,512]{1,0:T(8,128)(2,1)S(1)}, u32[]{:S(2)}, u32[]{:S(2)}) collective-permute-start(bf16[576,512]{1,0:T(8,128)(2,1)} %get-tuple-element.294), channel_id=1, source_target_pairs={{0,20},{4,28},{8,16},{12,24},{16,4},{20,12},{24,0},{28,8},{1,21},{... | collective-permute-start | bytes 1769480 | tf_op jit(solution)/shard_map/ppermute | solution.py:78
  67.4 16.8 %collective-permute-start.11 = (bf16[576,512]{1,0:T(8,128)(2,1)}, bf16[576,512]{1,0:T(8,128)(2,1)S(1)}, u32[]{:S(2)}, u32[]{:S(2)}) collective-permute-start(bf16[576,512]{1,0:T(8,128)(2,1)} %get-tuple-element.294), channel_id=1, source_target_pairs={{0,16},{4,24},{8,20},{12,28},{16,0},{20,8},{24,4},{28,12},{1,17},{... | collective-permute-start | bytes 1769480 | tf_op jit(solution)/shard_map/ppermute | solution.py:78
  69.5 14.6 %collective-permute-start.10 = (bf16[512,512]{1,0:T(8,128)(2,1)}, bf16[512,512]{1,0:T(8,128)(2,1)S(1)}, u32[]{:S(2)}, u32[]{:S(2)}) collective-permute-start(bf16[512,512]{1,0:T(8,128)(2,1)} %get-tuple-element.306.refs_5_.refs_11_), channel_id=1, source_target_pairs={{0,32},{32,64},{64,96},{96,0},{1,33},{33,65},{65,97},{97,1},{2,34}... | collective-permute-start | bytes 1572872 | tf_op jit(solution)/shard_map/ppermute | solution.py:48
  69.9 14.2 %collective-permute-start.9 = (bf16[512,512]{1,0:T(8,128)(2,1)}, bf16[512,512]{1,0:T(8,128)(2,1)S(1)}, u32[]{:S(2)}, u32[]{:S(2)}) collective-permute-start(bf16[512,512]{1,0:T(8,128)(2,1)} %get-tuple-element.306.refs_5_.refs_11_), channel_id=1, source_target_pairs={{0,96},{32,0},{64,32},{96,64},{1,97},{33,1},{65,33},{97,65},{2,98}... | collective-permute-start | bytes 1572872 | tf_op jit(solution)/shard_map/ppermute | solution.py:48
  84.2 18.9 %collective-permute-start.14 = (bf16[576,512]{1,0:T(8,128)(2,1)}, bf16[576,512]{1,0:T(8,128)(2,1)S(1)}, u32[]{:S(2)}, u32[]{:S(2)}) collective-permute-start(bf16[576,512]{1,0:T(8,128)(2,1)} %get-tuple-element.294), channel_id=1, source_target_pairs={{4,8},{8,4},{20,24},{24,20},{5,9},{9,5},{21,25},{25,21},{6,10},{10... | collective-permute-start | bytes 1769480 | tf_op jit(solution)/shard_map/ppermute | solution.py:78
  86.8 17.2 %collective-permute-start.15 = (bf16[576,512]{1,0:T(8,128)(2,1)}, bf16[576,512]{1,0:T(8,128)(2,1)S(1)}, u32[]{:S(2)}, u32[]{:S(2)}) collective-permute-start(bf16[576,512]{1,0:T(8,128)(2,1)} %get-tuple-element.294), channel_id=1, source_target_pairs={{0,4},{4,12},{8,0},{12,8},{16,20},{20,28},{24,16},{28,24},{1,5},{5... | collective-permute-start | bytes 1769480 | tf_op jit(solution)/shard_map/ppermute | solution.py:78
  86.9 17.1 %collective-permute-start.13 = (bf16[512,512]{1,0:T(8,128)(2,1)}, bf16[512,512]{1,0:T(8,128)(2,1)}, u32[]{:S(2)}, u32[]{:S(2)}) collective-permute-start(bf16[512,512]{1,0:T(8,128)(2,1)} %get-tuple-element.306.refs_5_.refs_11_), channel_id=1, source_target_pairs={{0,64},{32,96},{64,0},{96,32},{1,65},{33,97},{65,1},{97,33},{2,66}... | collective-permute-start | bytes 1572872 | tf_op jit(solution)/shard_map/ppermute | solution.py:48
  104.0 26.0 %collective-permute-start.17 = (bf16[512,1024]{1,0:T(8,128)(2,1)}, bf16[512,1024]{1,0:T(8,128)(2,1)S(1)}, u32[]{:S(2)}, u32[]{:S(2)}) collective-permute-start(bf16[512,1024]{1,0:T(8,128)(2,1)} %get-tuple-element.336.refs_3_), channel_id=1, source_target_pairs={{0,32},{32,64},{64,96},{96,0},{1,33},{33,65},{65,97},{97,1},{2,34}... | collective-permute-start | bytes 3145736 | tf_op jit(solution)/shard_map/ppermute | solution.py:48
  104.1 25.9 %collective-permute-start.16 = (bf16[512,1024]{1,0:T(8,128)(2,1)}, bf16[512,1024]{1,0:T(8,128)(2,1)S(1)}, u32[]{:S(2)}, u32[]{:S(2)}) collective-permute-start(bf16[512,1024]{1,0:T(8,128)(2,1)} %get-tuple-element.336.refs_3_), channel_id=1, source_target_pairs={{0,96},{32,0},{64,32},{96,64},{1,97},{33,1},{65,33},{97,65},{2,98}... | collective-permute-start | bytes 3145736 | tf_op jit(solution)/shard_map/ppermute | solution.py:48
  106.8 24.5 %collective-permute-start.19 = (bf16[512,1024]{1,0:T(8,128)(2,1)}, bf16[512,1024]{1,0:T(8,128)(2,1)}, u32[]{:S(2)}, u32[]{:S(2)}) collective-permute-start(bf16[512,1024]{1,0:T(8,128)(2,1)} %get-tuple-element.349.refs_20_), channel_id=1, source_target_pairs={{0,20},{4,28},{8,16},{12,24},{16,4},{20,12},{24,0},{28,8},{1,21},{... | collective-permute-start | bytes 3145736 | tf_op jit(solution)/shard_map/ppermute | solution.py:78
  108.9 24.2 %collective-permute-start.18 = (bf16[512,1024]{1,0:T(8,128)(2,1)}, bf16[512,1024]{1,0:T(8,128)(2,1)}, u32[]{:S(2)}, u32[]{:S(2)}) collective-permute-start(bf16[512,1024]{1,0:T(8,128)(2,1)} %get-tuple-element.349.refs_20_), channel_id=1, source_target_pairs={{0,16},{4,24},{8,20},{12,28},{16,0},{20,8},{24,4},{28,12},{1,17},{... | collective-permute-start | bytes 3145736 | tf_op jit(solution)/shard_map/ppermute | solution.py:78
  139.9 62.8 %all-gather.9.cloned.1.call-start = ((), (), s32[]{:S(2)}) async-start(), calls=%async_computation.7 | async-start | bytes 3538944 | tf_op jit(solution)/shard_map/all_gather | solution.py:109
  140.0 14.8 %collective-permute-start.22 = (bf16[256,1024]{1,0:T(8,128)(2,1)S(1)}, bf16[256,1024]{1,0:T(8,128)(2,1)S(1)}, u32[]{:S(2)}, u32[]{:S(2)}) collective-permute-start(bf16[256,1024]{1,0:T(8,128)(2,1)S(1)} %slice.111), channel_id=1, source_target_pairs={{0,32},{32,64},{64,96},{96,0},{1,33},{33,65},{65,97},{97,1},{2,34}... | collective-permute-start | bytes 1572872 | tf_op jit(solution)/shard_map/ppermute | solution.py:48
  140.1 30.7 %collective-permute-start.24 = (bf16[512,1024]{1,0:T(8,128)(2,1)}, bf16[512,1024]{1,0:T(8,128)(2,1)S(1)}, u32[]{:S(2)}, u32[]{:S(2)}) collective-permute-start(bf16[512,1024]{1,0:T(8,128)(2,1)} %get-tuple-element.349.refs_20_), channel_id=1, source_target_pairs={{0,4},{4,12},{8,0},{12,8},{16,20},{20,28},{24,16},{28,24},{1,5},{5... | collective-permute-start | bytes 3145736 | tf_op jit(solution)/shard_map/ppermute | solution.py:78
  140.3 30.5 %collective-permute-start.23 = (bf16[512,1024]{1,0:T(8,128)(2,1)}, bf16[512,1024]{1,0:T(8,128)(2,1)}, u32[]{:S(2)}, u32[]{:S(2)}) collective-permute-start(bf16[512,1024]{1,0:T(8,128)(2,1)} %get-tuple-element.349.refs_20_), channel_id=1, source_target_pairs={{4,8},{8,4},{20,24},{24,20},{5,9},{9,5},{21,25},{25,21},{6,10},{10... | collective-permute-start | bytes 3145736 | tf_op jit(solution)/shard_map/ppermute | solution.py:78
  145.5 20.7 %collective-permute-start.21 = (bf16[256,1024]{1,0:T(8,128)(2,1)S(1)}, bf16[256,1024]{1,0:T(8,128)(2,1)}, u32[]{:S(2)}, u32[]{:S(2)}) collective-permute-start(bf16[256,1024]{1,0:T(8,128)(2,1)S(1)} %slice.110), channel_id=1, source_target_pairs={{0,96},{32,0},{64,32},{96,64},{1,97},{33,1},{65,33},{97,65},{2,98}... | collective-permute-start | bytes 1572872 | tf_op jit(solution)/shard_map/ppermute | solution.py:48
  148.3 17.9 %collective-permute-start.26 = (bf16[512,512]{1,0:T(8,128)(2,1)}, bf16[512,512]{1,0:T(8,128)(2,1)}, u32[]{:S(2)}, u32[]{:S(2)}) collective-permute-start(bf16[512,512]{1,0:T(8,128)(2,1)} %get-tuple-element.341.refs_8_.refs_0_), channel_id=1, source_target_pairs={{0,32},{32,64},{64,96},{96,0},{1,33},{33,65},{65,97},{97,1},{2,34}... | collective-permute-start | bytes 1572872 | tf_op jit(solution)/shard_map/ppermute | solution.py:48
  155.5 15.3 %collective-permute-start.25 = (bf16[512,512]{1,0:T(8,128)(2,1)}, bf16[512,512]{1,0:T(8,128)(2,1)}, u32[]{:S(2)}, u32[]{:S(2)}) collective-permute-start(bf16[512,512]{1,0:T(8,128)(2,1)} %get-tuple-element.341.refs_8_.refs_0_), channel_id=1, source_target_pairs={{0,96},{32,0},{64,32},{96,64},{1,97},{33,1},{65,33},{97,65},{2,98}... | collective-permute-start | bytes 1572872 | tf_op jit(solution)/shard_map/ppermute | solution.py:48
  172.8 97.6 %reduce-scatter.7.cloned.1.call-start = ((), (), s32[]{:S(2)}) async-start(), calls=%async_computation.8 | async-start | bytes 1966080 | tf_op jit(solution)/shard_map/reduce_scatter | solution.py:810
  172.8 14.3 %collective-permute-start.27 = (bf16[512,512]{1,0:T(8,128)(2,1)}, bf16[512,512]{1,0:T(8,128)(2,1)S(1)}, u32[]{:S(2)}, u32[]{:S(2)}) collective-permute-start(bf16[512,512]{1,0:T(8,128)(2,1)} %get-tuple-element.341.refs_8_.refs_0_), channel_id=1, source_target_pairs={{0,64},{32,96},{64,0},{96,32},{1,65},{33,97},{65,1},{97,33},{2,66}... | collective-permute-start | bytes 1572872 | tf_op jit(solution)/shard_map/ppermute | solution.py:48
  175.1 14.0 %collective-permute-start.31 = (bf16[512,512]{1,0:T(8,128)(2,1)}, bf16[512,512]{1,0:T(8,128)(2,1)S(1)}, u32[]{:S(2)}, u32[]{:S(2)}) collective-permute-start(bf16[512,512]{1,0:T(8,128)(2,1)} %get-tuple-element.348.refs_21_.refs_8_), channel_id=1, source_target_pairs={{0,20},{4,28},{8,16},{12,24},{16,4},{20,12},{24,0},{28,8},{1,21},{... | collective-permute-start | bytes 1572872 | tf_op jit(solution)/shard_map/ppermute | solution.py:78
  177.6 23.8 %collective-permute-start.30 = (bf16[512,512]{1,0:T(8,128)(2,1)}, bf16[512,512]{1,0:T(8,128)(2,1)S(1)}, u32[]{:S(2)}, u32[]{:S(2)}) collective-permute-start(bf16[512,512]{1,0:T(8,128)(2,1)} %get-tuple-element.348.refs_21_.refs_8_), channel_id=1, source_target_pairs={{0,16},{4,24},{8,20},{12,28},{16,0},{20,8},{24,4},{28,12},{1,17},{... | collective-permute-start | bytes 1572872 | tf_op jit(solution)/shard_map/ppermute | solution.py:78
  177.6 23.8 %collective-permute-start.29 = (bf16[512,512]{1,0:T(8,128)(2,1)}, bf16[512,512]{1,0:T(8,128)(2,1)}, u32[]{:S(2)}, u32[]{:S(2)}) collective-permute-start(bf16[512,512]{1,0:T(8,128)(2,1)} %get-tuple-element.348.refs_21_.refs_8_), channel_id=1, source_target_pairs={{0,4},{4,12},{8,0},{12,8},{16,20},{20,28},{24,16},{28,24},{1,5},{5... | collective-permute-start | bytes 1572872 | tf_op jit(solution)/shard_map/ppermute | solution.py:78
  178.0 23.4 %collective-permute-start.28 = (bf16[512,512]{1,0:T(8,128)(2,1)}, bf16[512,512]{1,0:T(8,128)(2,1)}, u32[]{:S(2)}, u32[]{:S(2)}) collective-permute-start(bf16[512,512]{1,0:T(8,128)(2,1)} %get-tuple-element.348.refs_21_.refs_8_), channel_id=1, source_target_pairs={{4,8},{8,4},{20,24},{24,20},{5,9},{9,5},{21,25},{25,21},{6,10},{10... | collective-permute-start | bytes 1572872 | tf_op jit(solution)/shard_map/ppermute | solution.py:78
  240.6 65.2 %all-gather.11.cloned.1.call-start = ((), (), s32[]{:S(2)}) async-start(), calls=%async_computation.9 | async-start | bytes 3538944 | tf_op jit(solution)/shard_map/all_gather | solution.py:109
  242.2 29.3 %collective-permute-start.33 = (bf16[512,1024]{1,0:T(8,128)(2,1)}, bf16[512,1024]{1,0:T(8,128)(2,1)S(1)}, u32[]{:S(2)}, u32[]{:S(2)}) collective-permute-start(bf16[512,1024]{1,0:T(8,128)(2,1)} %get-tuple-element.363), channel_id=1, source_target_pairs={{16,0},{24,4},{20,8},{28,12},{0,16},{8,20},{4,24},{12,28},{17,1},{... | collective-permute-start | bytes 3145736 | tf_op jit(solution)/shard_map/ppermute | solution.py:82
  244.7 26.8 %collective-permute-start.34 = (bf16[512,1024]{1,0:T(8,128)(2,1)}, bf16[512,1024]{1,0:T(8,128)(2,1)}, u32[]{:S(2)}, u32[]{:S(2)}) collective-permute-start(bf16[512,1024]{1,0:T(8,128)(2,1)} %get-tuple-element.364), channel_id=1, source_target_pairs={{20,0},{28,4},{16,8},{24,12},{4,16},{12,20},{0,24},{8,28},{21,1},{... | collective-permute-start | bytes 3145736 | tf_op jit(solution)/shard_map/ppermute | solution.py:82
  245.2 26.4 %collective-permute-start.35 = (bf16[512,1024]{1,0:T(8,128)(2,1)}, bf16[512,1024]{1,0:T(8,128)(2,1)}, u32[]{:S(2)}, u32[]{:S(2)}) collective-permute-start(bf16[512,1024]{1,0:T(8,128)(2,1)} %get-tuple-element.365), channel_id=1, source_target_pairs={{0,32},{32,64},{64,96},{96,0},{1,33},{33,65},{65,97},{97,1},{2,34}... | collective-permute-start | bytes 3145736 | tf_op jit(solution)/shard_map/ppermute | solution.py:48
  246.8 25.2 %collective-permute-start.36 = (bf16[512,1024]{1,0:T(8,128)(2,1)}, bf16[512,1024]{1,0:T(8,128)(2,1)}, u32[]{:S(2)}, u32[]{:S(2)}) collective-permute-start(bf16[512,1024]{1,0:T(8,128)(2,1)} %get-tuple-element.366), channel_id=1, source_target_pairs={{0,96},{32,0},{64,32},{96,64},{1,97},{33,1},{65,33},{97,65},{2,98}... | collective-permute-start | bytes 3145736 | tf_op jit(solution)/shard_map/ppermute | solution.py:48
  275.2 121.8 %reduce-scatter.9.cloned.1.call-start = ((), (), s32[]{:S(2)}) async-start(), calls=%async_computation.10 | async-start | bytes 1966080 | tf_op jit(solution)/shard_map/reduce_scatter | solution.py:909
  276.1 26.4 %collective-permute-start.38 = (bf16[512,1024]{1,0:T(8,128)(2,1)}, bf16[512,1024]{1,0:T(8,128)(2,1)S(1)}, u32[]{:S(2)}, u32[]{:S(2)}) collective-permute-start(bf16[512,1024]{1,0:T(8,128)(2,1)} %get-tuple-element.382), channel_id=1, source_target_pairs={{0,64},{32,96},{64,0},{96,32},{1,65},{33,97},{65,1},{97,33},{2,66}... | collective-permute-start | bytes 3145736 | tf_op jit(solution)/shard_map/ppermute | solution.py:48
  278.2 24.3 %collective-permute-start.40 = (bf16[512,1024]{1,0:T(8,128)(2,1)}, bf16[512,1024]{1,0:T(8,128)(2,1)}, u32[]{:S(2)}, u32[]{:S(2)}) collective-permute-start(bf16[512,1024]{1,0:T(8,128)(2,1)} %get-tuple-element.386), channel_id=1, source_target_pairs={{4,0},{12,4},{0,8},{8,12},{20,16},{28,20},{16,24},{24,28},{5,1},{1... | collective-permute-start | bytes 3145736 | tf_op jit(solution)/shard_map/ppermute | solution.py:82
  279.3 26.4 %collective-permute-start.39 = (bf16[512,1024]{1,0:T(8,128)(2,1)}, bf16[512,1024]{1,0:T(8,128)(2,1)}, u32[]{:S(2)}, u32[]{:S(2)}) collective-permute-start(bf16[512,1024]{1,0:T(8,128)(2,1)} %get-tuple-element.385.refs_8_), channel_id=1, source_target_pairs={{8,4},{4,8},{24,20},{20,24},{9,5},{5,9},{25,21},{21,25},{10,6},{6,... | collective-permute-start | bytes 3145736 | tf_op jit(solution)/shard_map/ppermute | solution.py:82
  305.8 17.8 %collective-permute-start.41 = (bf16[512,512]{1,0:T(8,128)(2,1)}, bf16[512,512]{1,0:T(8,128)(2,1)S(1)}, u32[]{:S(2)}, u32[]{:S(2)}) collective-permute-start(bf16[512,512]{1,0:T(8,128)(2,1)} %get-tuple-element.409), channel_id=1, source_target_pairs={{0,32},{32,64},{64,96},{96,0},{1,33},{33,65},{65,97},{97,1},{2,34}... | collective-permute-start | bytes 1572872 | tf_op jit(solution)/shard_map/ppermute | solution.py:48
  306.6 17.0 %collective-permute-start.42 = (bf16[512,512]{1,0:T(8,128)(2,1)}, bf16[512,512]{1,0:T(8,128)(2,1)S(1)}, u32[]{:S(2)}, u32[]{:S(2)}) collective-permute-start(bf16[512,512]{1,0:T(8,128)(2,1)} %get-tuple-element.410), channel_id=1, source_target_pairs={{0,96},{32,0},{64,32},{96,64},{1,97},{33,1},{65,33},{97,65},{2,98}... | collective-permute-start | bytes 1572872 | tf_op jit(solution)/shard_map/ppermute | solution.py:48
  308.4 15.1 %collective-permute-start.43 = (bf16[512,512]{1,0:T(8,128)(2,1)}, bf16[512,512]{1,0:T(8,128)(2,1)S(1)}, u32[]{:S(2)}, u32[]{:S(2)}) collective-permute-start(bf16[512,512]{1,0:T(8,128)(2,1)} %get-tuple-element.411), channel_id=1, source_target_pairs={{16,0},{24,4},{20,8},{28,12},{0,16},{8,20},{4,24},{12,28},{17,1},{... | collective-permute-start | bytes 1572872 | tf_op jit(solution)/shard_map/ppermute | solution.py:82
  309.3 14.3 %collective-permute-start.44 = (bf16[512,512]{1,0:T(8,128)(2,1)}, bf16[512,512]{1,0:T(8,128)(2,1)S(1)}, u32[]{:S(2)}, u32[]{:S(2)}) collective-permute-start(bf16[512,512]{1,0:T(8,128)(2,1)} %get-tuple-element.412), channel_id=1, source_target_pairs={{20,0},{28,4},{16,8},{24,12},{4,16},{12,20},{0,24},{8,28},{21,1},{... | collective-permute-start | bytes 1572872 | tf_op jit(solution)/shard_map/ppermute | solution.py:82
  324.6 17.6 %collective-permute-start.45 = (bf16[3072,256]{1,0:T(8,128)(2,1)}, bf16[3072,256]{1,0:T(8,128)(2,1)S(1)}, u32[]{:S(2)}, u32[]{:S(2)}) collective-permute-start(bf16[3072,256]{1,0:T(8,128)(2,1)} %get-tuple-element.414), channel_id=1, source_target_pairs={{0,8},{8,0},{1,9},{9,1},{2,10},{10,2},{3,11},{11,3},{4,12},{12,4},... | collective-permute-start | bytes 4718600 | tf_op jit(solution)/shard_map/ppermute | solution.py:44
  325.6 16.5 %collective-permute-start.46 = (bf16[512,512]{1,0:T(8,128)(2,1)S(1)}, bf16[512,512]{1,0:T(8,128)(2,1)S(1)}, u32[]{:S(2)}, u32[]{:S(2)}) collective-permute-start(bf16[512,512]{1,0:T(8,128)(2,1)S(1)} %copy-done.45), channel_id=1, source_target_pairs={{0,64},{32,96},{64,0},{96,32},{1,65},{33,97},{65,1},{97,33},{2,66}... | collective-permute-start | bytes 1572872 | tf_op jit(solution)/shard_map/ppermute | solution.py:48
  326.2 16.0 %collective-permute-start.48 = (bf16[512,512]{1,0:T(8,128)(2,1)S(1)}, bf16[512,512]{1,0:T(8,128)(2,1)S(1)}, u32[]{:S(2)}, u32[]{:S(2)}) collective-permute-start(bf16[512,512]{1,0:T(8,128)(2,1)S(1)} %copy-done.44), channel_id=1, source_target_pairs={{4,0},{12,4},{0,8},{8,12},{20,16},{28,20},{16,24},{24,28},{5,1},{1... | collective-permute-start | bytes 1572872 | tf_op jit(solution)/shard_map/ppermute | solution.py:82
  328.0 14.2 %collective-permute-start.47 = (bf16[512,512]{1,0:T(8,128)(2,1)S(1)}, bf16[512,512]{1,0:T(8,128)(2,1)S(1)}, u32[]{:S(2)}, u32[]{:S(2)}) collective-permute-start(bf16[512,512]{1,0:T(8,128)(2,1)S(1)} %copy-done.19), channel_id=1, source_target_pairs={{8,4},{4,8},{24,20},{20,24},{9,5},{5,9},{25,21},{21,25},{10,6},{6,... | collective-permute-start | bytes 1572872 | tf_op jit(solution)/shard_map/ppermute | solution.py:82
  344.8 58.6 %reduce-scatter.11.cloned.1.call-start = ((), (), s32[]{:S(2)}) async-start(), calls=%async_computation.11 | async-start | bytes 1966080 | tf_op jit(solution)/shard_map/reduce_scatter | solution.py:941
  349.7 23.5 %collective-permute-start.51 = (bf16[896,512]{1,0:T(8,128)(2,1)}, bf16[896,512]{1,0:T(8,128)(2,1)S(1)}, u32[]{:S(2)}, u32[]{:S(2)}) collective-permute-start(bf16[896,512]{1,0:T(8,128)(2,1)} %get-tuple-element.467), channel_id=1, source_target_pairs={{0,32},{32,64},{64,96},{96,0},{1,33},{33,65},{65,97},{97,1},{2,34}... | collective-permute-start | bytes 2752520 | tf_op jit(solution)/shard_map/ppermute | solution.py:48
  350.1 23.1 %collective-permute-start.52 = (bf16[896,512]{1,0:T(8,128)(2,1)}, bf16[896,512]{1,0:T(8,128)(2,1)S(1)}, u32[]{:S(2)}, u32[]{:S(2)}) collective-permute-start(bf16[896,512]{1,0:T(8,128)(2,1)} %get-tuple-element.468), channel_id=1, source_target_pairs={{0,96},{32,0},{64,32},{96,64},{1,97},{33,1},{65,33},{97,65},{2,98}... | collective-permute-start | bytes 2752520 | tf_op jit(solution)/shard_map/ppermute | solution.py:48
  352.5 20.8 %collective-permute-start.53 = (bf16[896,512]{1,0:T(8,128)(2,1)}, bf16[896,512]{1,0:T(8,128)(2,1)}, u32[]{:S(2)}, u32[]{:S(2)}) collective-permute-start(bf16[896,512]{1,0:T(8,128)(2,1)} %get-tuple-element.469), channel_id=1, source_target_pairs={{16,0},{24,4},{20,8},{28,12},{0,16},{8,20},{4,24},{12,28},{17,1},{... | collective-permute-start | bytes 2752520 | tf_op jit(solution)/shard_map/ppermute | solution.py:82
  354.5 20.8 %collective-permute-start.54 = (bf16[896,512]{1,0:T(8,128)(2,1)}, bf16[896,512]{1,0:T(8,128)(2,1)}, u32[]{:S(2)}, u32[]{:S(2)}) collective-permute-start(bf16[896,512]{1,0:T(8,128)(2,1)} %get-tuple-element.470), channel_id=1, source_target_pairs={{20,0},{28,4},{16,8},{24,12},{4,16},{12,20},{0,24},{8,28},{21,1},{... | collective-permute-start | bytes 2752520 | tf_op jit(solution)/shard_map/ppermute | solution.py:82
  375.3 22.8 %collective-permute-start.55 = (bf16[896,512]{1,0:T(8,128)(2,1)}, bf16[896,512]{1,0:T(8,128)(2,1)}, u32[]{:S(2)}, u32[]{:S(2)}) collective-permute-start(bf16[896,512]{1,0:T(8,128)(2,1)} %get-tuple-element.471), channel_id=1, source_target_pairs={{0,64},{32,96},{64,0},{96,32},{1,65},{33,97},{65,1},{97,33},{2,66}... | collective-permute-start | bytes 2752520 | tf_op jit(solution)/shard_map/ppermute | solution.py:48
  375.7 22.4 %collective-permute-start.57 = (bf16[896,512]{1,0:T(8,128)(2,1)}, bf16[896,512]{1,0:T(8,128)(2,1)}, u32[]{:S(2)}, u32[]{:S(2)}) collective-permute-start(bf16[896,512]{1,0:T(8,128)(2,1)} %get-tuple-element.475), channel_id=1, source_target_pairs={{4,0},{12,4},{0,8},{8,12},{20,16},{28,20},{16,24},{24,28},{5,1},{1... | collective-permute-start | bytes 2752520 | tf_op jit(solution)/shard_map/ppermute | solution.py:82
  378.6 24.4 %collective-permute-start.56 = (bf16[896,512]{1,0:T(8,128)(2,1)}, bf16[896,512]{1,0:T(8,128)(2,1)}, u32[]{:S(2)}, u32[]{:S(2)}) collective-permute-start(bf16[896,512]{1,0:T(8,128)(2,1)} %get-tuple-element.503.refs_8_), channel_id=1, source_target_pairs={{8,4},{4,8},{24,20},{20,24},{9,5},{5,9},{25,21},{21,25},{10,6},{6,... | collective-permute-start | bytes 2752520 | tf_op jit(solution)/shard_map/ppermute | solution.py:82
  404.7 21.0 %collective-permute-start.61 = (bf16[1536,256]{1,0:T(8,128)(2,1)S(1)}, bf16[1536,256]{1,0:T(8,128)(2,1)S(1)}, u32[]{:S(2)}, u32[]{:S(2)}) collective-permute-start(bf16[1536,256]{1,0:T(8,128)(2,1)S(1)} %pad_maximum_fusion), channel_id=1, source_target_pairs={{4,8},{8,4},{5,9},{9,5},{6,10},{10,6},{7,11},{11,7},{20,24},{24,20... | collective-permute-start | bytes 2359304 | tf_op jit(solution)/shard_map/ppermute | solution.py:39
  411.2 12.7 %collective-permute-start.60 = (bf16[512,256]{1,0:T(8,128)(2,1)}, bf16[512,256]{1,0:T(8,128)(2,1)S(1)}, u32[]{:S(2)}, u32[]{:S(2)}) collective-permute-start(bf16[512,256]{1,0:T(8,128)(2,1)} %get-tuple-element.488), channel_id=1, source_target_pairs={{0,1},{1,0},{2,3},{3,2},{4,5},{5,4},{6,7},{7,6},{8,9},{9,8},{10,11... | collective-permute-start | bytes 786440 | tf_op jit(solution)/shard_map/ppermute | solution.py:60
  413.3 12.6 %collective-permute-start.64 = (bf16[128,512]{1,0:T(8,128)(2,1)}, bf16[128,512]{1,0:T(8,128)(2,1)S(1)}, u32[]{:S(2)}, u32[]{:S(2)}) collective-permute-start(bf16[128,512]{1,0:T(8,128)(2,1)} %get-tuple-element.498), channel_id=1, source_target_pairs={{0,64},{32,96},{64,0},{96,32},{1,65},{33,97},{65,1},{97,33},{2,66}... | collective-permute-start | bytes 393224 | tf_op jit(solution)/shard_map/ppermute | solution.py:48
  416.0 10.0 %collective-permute-start.65 = (bf16[128,512]{1,0:T(8,128)(2,1)}, bf16[128,512]{1,0:T(8,128)(2,1)S(1)}, u32[]{:S(2)}, u32[]{:S(2)}) collective-permute-start(bf16[128,512]{1,0:T(8,128)(2,1)} %get-tuple-element.499), channel_id=1, source_target_pairs={{0,96},{32,0},{64,32},{96,64},{1,97},{33,1},{65,33},{97,65},{2,98}... | collective-permute-start | bytes 393224 | tf_op jit(solution)/shard_map/ppermute | solution.py:48
  (67 other events, 723.7 us)
Sparse Core Ops, SparseCore 0:
  44.8 28.6 all-gather.4
  75.7 27.8 all-gather.6
  140.0 25.0 reduce-scatter.4
  172.9 29.7 all-gather.8
  240.7 25.4 reduce-scatter.6
  275.3 27.8 all-gather.10
  345.0 23.7 reduce-scatter.8
  371.2 26.4 reduce-scatter.10

commit v5 on v4

--- a/solution.py
+++ b/solution.py
@@ -652,6 +652,33 @@
             down[:, 512:] = of_b
 
 
+def last_body(at, *refs):
+    own, a, b, w_query, w_key = refs[0], refs[1:5], refs[5:9], refs[9], refs[10]
+    query, output, key, value, gain_one, gain_two, clipped_query, clipped_key, small = refs[11:]
+    a = [jnp.where(at[2] == at[3], own[...], a[0][...]), a[1][...], a[2][...], a[3][...]]
+    kv = a[0][:128].astype(f32) + a[1][:128].astype(f32) + a[2][:128].astype(f32) + a[3][:128].astype(f32)
+    key[...] = kv[:, :128]
+    value[...] = kv[:, 128:]
+    parts = [piece[128:, :128].astype(f32) + piece[128:, 128:].astype(f32) for piece in a]
+    added = parts[0] + parts[1] + parts[2] + parts[3]
+    most = jnp.maximum(jnp.maximum(parts[0], parts[1]), jnp.maximum(parts[2], parts[3]))
+    small[...] = jnp.where(lax.broadcasted_iota(jnp.int32, (48, 128), 0) >= 32, most, added)
+    tok, head = at[0] * 4 + at[1] * 2 + at[3], at[2] * 4 + at[4]
+    gain_one[...] = small[pl.ds(tok, 1), :]
+    gain_two[...] = small[pl.ds(16 + tok, 1), :]
+    peak = small[pl.ds(32 + head, 1), :]
+    pair = jnp.maximum(peak, small[pl.ds(32 + (head ^ 1), 1), :])
+    scale = jnp.sqrt(logit_ceiling / (peak + peak_floor_epsilon))
+    for j in range(2):
+        cols = slice(j * 128, (j + 1) * 128)
+        clipped_query[:, cols] = (w_query[:, cols].astype(f32) * scale).astype(bf16)
+    scale = jnp.sqrt(logit_ceiling / (pair + peak_floor_epsilon))
+    clipped_key[...] = (w_key[...].astype(f32) * scale).astype(bf16)
+    total_b = b[0][...].astype(f32) + b[1][...].astype(f32) + b[2][...].astype(f32) + b[3][...].astype(f32)
+    query[...] = total_b[:, :256]
+    output[...] = total_b[:, 256:]
+
+
 def on_device(
     tokens,
     segments,
@@ -961,8 +988,12 @@
     first_y = sum_b[1]
     small = join([small, y_other(small, 2)])
     kv_sum, home, small, *sum_b = lax.optimization_barrier((kv_sum, home, small, *sum_b))
-    sum_a = [x_out(kv_sum[i * 128 : (i + 1) * 128], *flip) for i, flip in enumerate(FLIPS)]
-    sum_a[0] = own_or(sum_a[0], kv_sum[:128])
+    high = lax.reduce_precision(small, 8, 7)
+    rider = jnp.concatenate([high.astype(bf16), (small - high).astype(bf16)], 1)
+    rider = jnp.pad(rider, ((0, 8), (0, 0)))
+    rider = jnp.broadcast_to(rider[None], (4, 48, HEAD))
+    last = jnp.concatenate([kv_sum.reshape(4, 128, HEAD), rider], 1).reshape(4 * 176, HEAD)
+    sum_a = [x_out(last[i * 176 : (i + 1) * 176], *flip) for i, flip in enumerate(FLIPS)]
     grads = call(
         finish_body,
         "finish",
@@ -972,31 +1003,32 @@
         0,
         anywhere=9,
     )
-    for mask in (1, 2):
-        small = join([small, x_ring(small, mask)])
-    sum_a, small, grads = lax.optimization_barrier((sum_a, small, grads))
-    query_output = total(sum_b)
-    kv_done = total(sum_a)
-    tok = y * 4 + lo * 2 + core
-    gains_mine = lax.dynamic_slice(small[:32].reshape(2, 16, 128), (0, tok, 0), (2, 1, 128)).reshape(2, 128)
-    peaks = small[32:, 0]
-
-    head = hi * 4 + z
-    peak_q = lax.dynamic_slice(peaks, (head,), (1,))
-    pair = lax.dynamic_slice(peaks, (head // 2 * 2,), (2,))
-    scale_q = jnp.sqrt(logit_ceiling / (peak_q + peak_floor_epsilon))
-    scale_k = jnp.sqrt(logit_ceiling / (jnp.max(pair, keepdims=True) + peak_floor_epsilon))
-    clipped_query = (w_query.astype(f32) * scale_q[None, :]).astype(bf16)
-    clipped_key = (w_key.astype(f32) * scale_k[None, :]).astype(bf16)
+    query, output, key, value, gain_one, gain_two, clipped_query, clipped_key = call(
+        last_body,
+        "last",
+        [at, last[:176], *sum_a, *sum_b, w_query, w_key],
+        [
+            ((128, HEAD), f32),
+            ((128, HEAD), f32),
+            ((128, 128), f32),
+            ((128, 128), f32),
+            ((1, 128), f32),
+            ((1, 128), f32),
+            ((128, HEAD), bf16),
+            ((128, 128), bf16),
+        ],
+        [pltpu.VMEM((48, 128), f32)],
+        0,
+    )
     return (
         home[:LEN],
         home[LEN:].astype(f32),
-        gains_mine[0],
-        query_output[:, :HEAD],
-        kv_done[:, :half],
-        kv_done[:, half:],
-        query_output[:, HEAD:],
-        gains_mine[1],
+        gain_one.reshape(128),
+        query,
+        key,
+        value,
+        output,
+        gain_two.reshape(128),
         grads[0],
         grads[1],
         grads[2],

time: 461 us -> 455 us (0.987)
    pallas_call x14 -> x15, Pallas kernels: 123 us -> 125 us  [call(): pl.pallas_call(body, name=name, out_shape=[jax.ShapeDtypeStruct(s, d) for...]
  transfers between devices with their start and end apart: 80 -> 78, of which waited for: 37 -> 35; matrix products, arithmetic and copies ran while one was open for 5% -> 4% of each run, Pallas kernels for 20% -> 20%
where the time goes in v5:
time: 455 us; the launch traced here: 448 us
  waiting for transfers between devices  157 us (35%)
  Pallas kernels  125 us (27%)
  starting transfers between devices  107 us (24%)
  other arithmetic  29.7 us (7%)
  between operations  15.7 us (3%)
  local copies, waits for them, and re-layouts  12.7 us (3%)
    pallas_call x15, Pallas kernels, call(): pl.pallas_call(body, name=name, out_shape=[jax.ShapeDtypeStruct(s, d) for...  125 us
    ppermute x25, waiting for transfers between devices, shift(): return lax.ppermute(a, axis, [(i, (i + by) % 4) for i in range(4)])  71.5 us
    ppermute x16, waiting for transfers between devices, x_in(): return lax.ppermute(a, (XLO, CORE, XHI), x_pairs(flip_lo, flip_core, False))  43.3 us
    ppermute x16, starting transfers between devices, x_out(): return lax.ppermute(a, (XLO, CORE, XHI), x_pairs(flip_lo, flip_core, True))  34.8 us
    ppermute x25, starting transfers between devices, shift(): return lax.ppermute(a, axis, [(i, (i + by) % 4) for i in range(4)])  32.6 us
    ppermute x16, starting transfers between devices, x_in(): return lax.ppermute(a, (XLO, CORE, XHI), x_pairs(flip_lo, flip_core, False))  22.4 us
    ppermute x16, waiting for transfers between devices, x_out(): return lax.ppermute(a, (XLO, CORE, XHI), x_pairs(flip_lo, flip_core, True))  12.2 us
  transfers between devices with their start and end apart: 78, of which 35 were waited for; matrix products, arithmetic and copies ran while one was open for 4% of the time, Pallas kernels for 20%

profile of v5, /device:TPU:1, one launch (start us, length us, event | category | flops | bytes accessed | tf_op | source)
XLA Modules:
  0.0 447.7 jit_solution(950746422965417954)
XLA Ops:
  10.4 3.3 lay_out_y.1
  13.7 6.2 %collective-permute-start = (bf16[1552,256]{1,0:T(8,128)(2,1)}, bf16[1552,256]{1,0:T(8,128)(2,1)S(1)}, u32[]{:S(2)}, u32[]{:S(2)}) collective-permute-start(bf16[1552,256]{1,0:T(8,128)(2,1)} %get-tuple-element.272), channel_id=1, source_target_pairs={{4,8},{8,4},{5,9},{9,5},{6,10},{10,6},{7,11},{11,7},{20,24},{24,20... | collective-permute-start | bytes 2383880 | tf_op jit(solution)/shard_map/ppermute | solution.py:39
  25.8 2.7 lay_out_x.1
  30.2 4.6 %collective-permute-done.3.refs_7_ = bf16[528,512]{1,0:T(8,128)(2,1)S(1)} collective-permute-done((bf16[528,512]{1,0:T(8,128)(2,1)}, bf16[528,512]{1,0:T(8,128)(2,1)S(1)}, u32[]{:S(2)}, u32[]{:S(2)}) %collective-permute-start.3) | collective-permute-done | bytes 540704 | tf_op jit(solution)/shard_map/ppermute | solution.py:48
  35.5 7.6 %collective-permute-done.5.refs_3_ = bf16[512,512]{1,0:T(8,128)(2,1)} collective-permute-done((bf16[512,512]{1,0:T(8,128)(2,1)}, bf16[512,512]{1,0:T(8,128)(2,1)}, u32[]{:S(2)}, u32[]{:S(2)}) %collective-permute-start.5) | collective-permute-done | bytes 524320 | tf_op jit(solution)/shard_map/ppermute | solution.py:78
  44.8 2.6 collective-permute-start.6
  47.4 3.0 collective-permute-start.8
  50.4 9.0 %collective-permute-done.6 = bf16[512,512]{1,0:T(8,128)(2,1)S(1)} collective-permute-done((bf16[512,512]{1,0:T(8,128)(2,1)}, bf16[512,512]{1,0:T(8,128)(2,1)S(1)}, u32[]{:S(2)}, u32[]{:S(2)}) %collective-permute-start.6) | collective-permute-done | bytes 524320 | tf_op jit(solution)/shard_map/ppermute | solution.py:78
  60.3 2.4 collective-permute-done.7.refs_1_
  64.3 3.0 pack.1
  67.5 2.1 collective-permute-start.11
  69.9 2.3 collective-permute-start.9
  72.3 11.9 %collective-permute-done.10.refs_8_.refs_14_ = bf16[512,512]{1,0:T(8,128)(2,1)S(1)} collective-permute-done((bf16[512,512]{1,0:T(8,128)(2,1)}, bf16[512,512]{1,0:T(8,128)(2,1)S(1)}, u32[]{:S(2)}, u32[]{:S(2)}) %collective-permute-start.10) | collective-permute-done | bytes 524320 | tf_op jit(solution)/shard_map/ppermute | solution.py:48
  84.2 2.3 collective-permute-start.14
  87.0 2.8 collective-permute-start.13
  89.8 2.5 multiply_sine_fusion
  92.3 4.7 %riders.1 = (bf16[512,1024]{1,0:T(8,128)(2,1)}, bf16[512,1024]{1,0:T(8,128)(2,1)}, bf16[512,512]{1,0:T(8,128)(2,1)}, bf16[512,512]{1,0:T(8,128)(2,1)}) custom-call(s32[5]{0:T(128)} %stack.74.at, bf16[512,512]{1,0:T(8,128)(2,1)} %broadcast_select_fusion.3.refs_0_, bf16[512,512]{1,0:T(8,128)(2,1)} %copy-done.7, ...), custom_call_target="tpu_custom_call" | custom-call | bytes 7405568 | tf_op jit(solution)/shard_map/riders/pallas_call | solution.py:155
  97.0 6.2 %collective-permute-done.14 = bf16[576,512]{1,0:T(8,128)(2,1)S(1)} collective-permute-done((bf16[576,512]{1,0:T(8,128)(2,1)}, bf16[576,512]{1,0:T(8,128)(2,1)S(1)}, u32[]{:S(2)}, u32[]{:S(2)}) %collective-permute-start.14) | collective-permute-done | bytes 589856 | tf_op jit(solution)/shard_map/ppermute | solution.py:78
  104.2 2.7 collective-permute-start.16
  106.8 2.2 collective-permute-start.19
  110.4 15.6 %attention_forward.1 = (bf16[768,2048]{1,0:T(8,128)(2,1)}, f32[768,1]{1,0:T(8,128)}, bf16[96,2048]{1,0:T(8,128)(2,1)}, bf16[768,256]{1,0:T(8,128)(2,1)}, bf16[76...) custom-call(s32[5]{0:T(128)} %stack.74.at, ...), custom_call_target="tpu_custom_call" | custom-call | flops 3221225472 | bytes 16728064 | tf_op jit(solution)/shard_map/attention_forward/pallas_call | solution.py:155
  126.1 4.0 collective-permute-done.17.refs_7_
  133.3 3.6 collective-permute-done.20
  136.9 3.0 add_convert_fusion.3
  140.4 4.1 collective-permute-start.23
  145.6 2.8 collective-permute-start.21
  148.4 6.5 %collective-permute-done.22.refs_6_ = bf16[256,1024]{1,0:T(8,128)(2,1)S(1)} collective-permute-done((bf16[256,1024]{1,0:T(8,128)(2,1)S(1)}, bf16[256,1024]{1,0:T(8,128)(2,1)S(1)}, u32[]{:S(2)}, u32[]{:S(2)}) %collective-permute-start.22) | collective-permute-done | bytes 524320 | tf_op jit(solution)/shard_map/ppermute | solution.py:48
  155.6 4.5 %order_upstream.1.refs_2_.dy = bf16[768,2048]{1,0:T(8,128)(2,1)} custom-call(s32[5]{0:T(128)} %stack.74.at, bf16[6144,256]{1,0:T(8,128)(2,1)} %all-gather.7.cloned.1.call-done.whole), custom_call_target="tpu_custom_call" | custom-call | bytes 6291456 | tf_op jit(solution)/shard_map/order_upstream/pallas_call | solution.py:155
  160.2 5.0 %reduce-scatter.5.cloned.1.call-done = bf16[96,2048]{1,0:T(8,128)(2,1)} async-done(((bf16[384,2048]{1,0:T(8,128)(2,1)}), bf16[96,2048]{1,0:T(8,128)(2,1)}) %reduce-scatter.5.cloned.1.call-update) | async-done | bytes 393232 | tf_op jit(solution)/shard_map/reduce_scatter | solution.py:114
  166.3 4.6 %collective-permute-done.25.refs_9_.refs_1_ = bf16[512,512]{1,0:T(8,128)(2,1)} collective-permute-done((bf16[512,512]{1,0:T(8,128)(2,1)}, bf16[512,512]{1,0:T(8,128)(2,1)}, u32[]{:S(2)}, u32[]{:S(2)}) %collective-permute-start.25) | collective-permute-done | bytes 524320 | tf_op jit(solution)/shard_map/ppermute | solution.py:48
  172.9 2.2 collective-permute-start.27
  175.2 2.5 collective-permute-start.31
  178.1 3.9 collective-permute-start.28
  182.0 5.2 %collective-permute-done.27.refs_10_.refs_2_ = bf16[512,512]{1,0:T(8,128)(2,1)S(1)} collective-permute-done((bf16[512,512]{1,0:T(8,128)(2,1)}, bf16[512,512]{1,0:T(8,128)(2,1)S(1)}, u32[]{:S(2)}, u32[]{:S(2)}) %collective-permute-start.27) | collective-permute-done | bytes 524320 | tf_op jit(solution)/shard_map/ppermute | solution.py:48
  189.1 12.3 %collective-permute-done.30.refs_18_.refs_6_ = bf16[512,512]{1,0:T(8,128)(2,1)S(1)} collective-permute-done((bf16[512,512]{1,0:T(8,128)(2,1)}, bf16[512,512]{1,0:T(8,128)(2,1)S(1)}, u32[]{:S(2)}, u32[]{:S(2)}) %collective-permute-start.30) | collective-permute-done | bytes 524320 | tf_op jit(solution)/shard_map/ppermute | solution.py:78
  202.8 31.0 %feed_forward.1 = (bf16[768,256]{1,0:T(8,128)(2,1)}, bf16[768,2048]{1,0:T(8,128)(2,1)}, bf16[768,1024]{1,0:T(8,128)(2,1)}, bf16[768,1024]{1,0:T(8,128)(2,1)}, bf...) custom-call(s32[5]{0:T(128)} %stack.74.at, ...), custom_call_target="tpu_custom_call" | custom-call | flops 22548578304 | bytes 36110336 | tf_op jit(solution)/shard_map/feed_forward/pallas_call | solution.py:155
  234.2 3.3 collective-permute-done.32
  237.5 3.1 add_convert_fusion.2
  242.2 2.5 collective-permute-start.33
  248.6 13.1 %weight_rest.1 = (bf16[512,1024]{1,0:T(8,128)(2,1)}, bf16[512,1024]{1,0:T(8,128)(2,1)}, bf16[512,1024]{1,0:T(8,128)(2,1)}, bf16[512,1024]{1,0:T(8,128)(2,1)}, bf...) custom-call(s32[5]{0:T(128)} %stack.74.at, ...), custom_call_target="tpu_custom_call" | custom-call | flops 6442450944 | bytes 19398656 | tf_op jit(solution)/shard_map/weight_rest/pallas_call | solution.py:155
  261.8 8.7 %feed_forward_out.1 = (bf16[3072,256]{1,0:T(8,128)(2,1)}, bf16[3072,256]{1,0:T(8,128)(2,1)}) custom-call(s32[5]{0:T(128)} %stack.74.at, bf16[768,1024]{1,0:T(8,128)(2,1)} %get-tuple-element.360.hid, bf16[512,512]{1,0:T(8,128)(2,1)} %get-tuple-element.341.refs_8_.refs_0_, bf16[512,512]{1,0:T(8,128)(2,1)} %collective-permute-done.25.refs_9_.refs_1_, ...), custom_call_target="tpu_custom_call" | custom-call | flops 3221225472 | bytes 9437184 | tf_op jit(solution)/shard_map/feed_forward_out/pallas_call | solution.py:155
  273.0 2.3 subtract_convert_fusion.1
  279.4 4.3 collective-permute-start.39
  285.4 17.3 %collective-permute-done.38.refs_1_ = bf16[512,1024]{1,0:T(8,128)(2,1)S(1)} collective-permute-done((bf16[512,1024]{1,0:T(8,128)(2,1)}, bf16[512,1024]{1,0:T(8,128)(2,1)S(1)}, u32[]{:S(2)}, u32[]{:S(2)}) %collective-permute-start.38) | collective-permute-done | bytes 1048608 | tf_op jit(solution)/shard_map/ppermute | solution.py:48
  302.7 3.1 collective-permute-done.39.refs_4_
  309.6 14.0 %attention_backward.1 = (bf16[768,256]{1,0:T(8,128)(2,1)}, bf16[768,768]{1,0:T(8,128)(2,1)}, f32[768,1]{1,0:T(8,128)}, f32[1,2048]{1,0:T(1,128)}, bf16[3072,256]{1,0:T(8,128)(2,1)}, /*index=5*/bf16[3072,256]{1,0:T(8,128)(2,1)}) custom-call(s32[5]{0:T(128)} %stack.74.at, bf16[768,2048]{1,0:T(8,128)(2,1)} %all-gather.11.cloned.1.call-done.refs_0_.db, ...), custom_call_target="tpu_custom_call" | custom-call | flops 3221225472 | bytes 17518592 | tf_op jit(solution)/shard_map/attention_backward/pallas_call | solution.py:155
  328.1 3.7 collective-permute-start.47
  331.8 10.4 %attention_weights.1 = (bf16[896,512]{1,0:T(8,128)(2,1)}, bf16[896,512]{1,0:T(8,128)(2,1)}, bf16[896,512]{1,0:T(8,128)(2,1)}, bf16[896,512]{1,0:T(8,128)(2,1)}, ...) custom-call(s32[5]{0:T(128)} %stack.74.at, ...), custom_call_target="tpu_custom_call" | custom-call | flops 3221225472 | bytes 24641536 | tf_op jit(solution)/shard_map/attention_weights/pallas_call | solution.py:155
  346.2 3.6 feed_forward_sums_down.1
  350.3 2.4 collective-permute-start.52
  357.5 3.2 collective-permute-done.50
  360.8 12.6 %collective-permute-done.51.refs_2_ = bf16[896,512]{1,0:T(8,128)(2,1)S(1)} collective-permute-done((bf16[896,512]{1,0:T(8,128)(2,1)}, bf16[896,512]{1,0:T(8,128)(2,1)S(1)}, u32[]{:S(2)}, u32[]{:S(2)}) %collective-permute-start.51) | collective-permute-done | bytes 917536 | tf_op jit(solution)/shard_map/ppermute | solution.py:48
  375.8 2.9 collective-permute-start.57
  378.7 5.1 %collective-permute-start.56 = (bf16[896,512]{1,0:T(8,128)(2,1)}, bf16[896,512]{1,0:T(8,128)(2,1)}, u32[]{:S(2)}, u32[]{:S(2)}) collective-permute-start(bf16[896,512]{1,0:T(8,128)(2,1)} %get-tuple-element.513.refs_8_), channel_id=1, source_target_pairs={{8,4},{4,8},{24,20},{20,24},{9,5},{5,9},{25,21},{21,25},{10,6},{6,... | collective-permute-start | bytes 2752520 | tf_op jit(solution)/shard_map/ppermute | solution.py:82
  386.1 3.3 collective-permute-done.58
  389.6 7.4 %collective-permute-done.59 = f32[40,128]{1,0:T(8,128)S(1)} collective-permute-done((f32[40,128]{1,0:T(8,128)S(1)}, f32[40,128]{1,0:T(8,128)S(1)}, u32[]{:S(2)}, u32[]{:S(2)}) %collective-permute-start.59) | collective-permute-done | bytes 20512 | tf_op jit(solution)/shard_map/ppermute | solution.py:56
  398.2 4.9 %collective-permute-done.56.refs_4_ = bf16[896,512]{1,0:T(8,128)(2,1)} collective-permute-done((bf16[896,512]{1,0:T(8,128)(2,1)}, bf16[896,512]{1,0:T(8,128)(2,1)}, u32[]{:S(2)}, u32[]{:S(2)}) %collective-permute-start.56) | collective-permute-done | bytes 917536 | tf_op jit(solution)/shard_map/ppermute | solution.py:82
  406.8 4.5 %join_sums.1 = (bf16[128,512]{1,0:T(8,128)(2,1)}, bf16[128,512]{1,0:T(8,128)(2,1)}, bf16[128,512]{1,0:T(8,128)(2,1)}, bf16[128,512]{1,0:T(8,128)(2,1)}, bf16[512,256]{1,0:T(8,128)(2,1)}, /*index=5*/f32[512,256]{1,0:T(8,128)}) custom-call(s32[5]{0:T(128)} %stack.74.at, bf16[896,512]{1,0:T(8,128)(2,1)} %get-tuple-element.479.refs_0_, ...), custom_call_target="tpu_custom_call" | custom-call | bytes 9568256 | tf_op jit(solution)/shard_map/join_sums/pallas_call | solution.py:155
  416.7 3.5 collective-permute-done.63.refs_6_
  420.1 3.9 finish.1
  424.6 5.6 %collective-permute-start.67 = (bf16[176,256]{1,0:T(8,128)(2,1)S(1)}, bf16[176,256]{1,0:T(8,128)(2,1)S(1)}, u32[]{:S(2)}, u32[]{:S(2)}) collective-permute-start(bf16[176,256]{1,0:T(8,128)(2,1)S(1)} %get-tuple-element.533), channel_id=1, source_target_pairs={{4,0},{12,4},{0,8},{8,12},{20,16},{28,20},{16,24},{24,28},{5,1},{1... | collective-permute-start | bytes 270344 | tf_op jit(solution)/shard_map/ppermute | solution.py:82
  430.3 4.1 collective-permute-start.66
  435.5 2.1 collective-permute-done.66.refs_1_
  438.3 2.1 last.1
  (287 shorter events, 79.9 us)
Async XLA Ops:
  7.2 96.9 %all-gather.5.cloned.1.call-start = ((), (), s32[]{:S(2)}) async-start(), calls=%async_computation.4 | async-start | bytes 3538944 | tf_op jit(solution)/shard_map/all_gather | solution.py:109
  13.7 16.3 %collective-permute-start = (bf16[1552,256]{1,0:T(8,128)(2,1)}, bf16[1552,256]{1,0:T(8,128)(2,1)S(1)}, u32[]{:S(2)}, u32[]{:S(2)}) collective-permute-start(bf16[1552,256]{1,0:T(8,128)(2,1)} %get-tuple-element.272), channel_id=1, source_target_pairs={{4,8},{8,4},{5,9},{9,5},{6,10},{10,6},{7,11},{11,7},{20,24},{24,20... | collective-permute-start | bytes 2383880 | tf_op jit(solution)/shard_map/ppermute | solution.py:39
  22.4 12.3 %collective-permute-start.3 = (bf16[528,512]{1,0:T(8,128)(2,1)}, bf16[528,512]{1,0:T(8,128)(2,1)S(1)}, u32[]{:S(2)}, u32[]{:S(2)}) collective-permute-start(bf16[528,512]{1,0:T(8,128)(2,1)} %get-tuple-element.285.refs_4_), channel_id=1, source_target_pairs={{0,32},{32,64},{64,96},{96,0},{1,33},{33,65},{65,97},{97,1},{2,34}... | collective-permute-start | bytes 1622024 | tf_op jit(solution)/shard_map/ppermute | solution.py:48
  23.7 11.8 %collective-permute-start.2 = (bf16[528,512]{1,0:T(8,128)(2,1)}, bf16[528,512]{1,0:T(8,128)(2,1)S(1)}, u32[]{:S(2)}, u32[]{:S(2)}) collective-permute-start(bf16[528,512]{1,0:T(8,128)(2,1)} %get-tuple-element.285.refs_4_), channel_id=1, source_target_pairs={{0,96},{32,0},{64,32},{96,64},{1,97},{33,1},{65,33},{97,65},{2,98}... | collective-permute-start | bytes 1622024 | tf_op jit(solution)/shard_map/ppermute | solution.py:48
  28.5 14.6 %collective-permute-start.5 = (bf16[512,512]{1,0:T(8,128)(2,1)}, bf16[512,512]{1,0:T(8,128)(2,1)}, u32[]{:S(2)}, u32[]{:S(2)}) collective-permute-start(bf16[512,512]{1,0:T(8,128)(2,1)} %lay_out_x.1), channel_id=1, source_target_pairs={{0,20},{4,28},{8,16},{12,24},{16,4},{20,12},{24,0},{28,8},{1,21},{... | collective-permute-start | bytes 1572872 | tf_op jit(solution)/shard_map/ppermute | solution.py:78
  28.6 15.2 %collective-permute-start.4 = (bf16[512,512]{1,0:T(8,128)(2,1)}, bf16[512,512]{1,0:T(8,128)(2,1)}, u32[]{:S(2)}, u32[]{:S(2)}) collective-permute-start(bf16[512,512]{1,0:T(8,128)(2,1)} %lay_out_x.1), channel_id=1, source_target_pairs={{0,16},{4,24},{8,20},{12,28},{16,0},{20,8},{24,4},{28,12},{1,17},{... | collective-permute-start | bytes 1572872 | tf_op jit(solution)/shard_map/ppermute | solution.py:78
  44.7 81.3 %all-gather.7.cloned.1.call-start = ((), (), s32[]{:S(2)}) async-start(), calls=%async_computation.5 | async-start | bytes 3538944 | tf_op jit(solution)/shard_map/all_gather | solution.py:109
  44.8 14.6 %collective-permute-start.6 = (bf16[512,512]{1,0:T(8,128)(2,1)}, bf16[512,512]{1,0:T(8,128)(2,1)S(1)}, u32[]{:S(2)}, u32[]{:S(2)}) collective-permute-start(bf16[512,512]{1,0:T(8,128)(2,1)} %lay_out_x.1), channel_id=1, source_target_pairs={{4,8},{8,4},{20,24},{24,20},{5,9},{9,5},{21,25},{25,21},{6,10},{10... | collective-permute-start | bytes 1572872 | tf_op jit(solution)/shard_map/ppermute | solution.py:78
  47.4 15.3 %collective-permute-start.8 = (bf16[528,512]{1,0:T(8,128)(2,1)S(1)}, bf16[528,512]{1,0:T(8,128)(2,1)S(1)}, u32[]{:S(2)}, u32[]{:S(2)}) collective-permute-start(bf16[528,512]{1,0:T(8,128)(2,1)S(1)} %copy-done.3), channel_id=1, source_target_pairs={{0,64},{32,96},{64,0},{96,32},{1,65},{33,97},{65,1},{97,33},{2,66}... | collective-permute-start | bytes 1622024 | tf_op jit(solution)/shard_map/ppermute | solution.py:48
  50.4 12.3 %collective-permute-start.7 = (bf16[512,512]{1,0:T(8,128)(2,1)}, bf16[512,512]{1,0:T(8,128)(2,1)S(1)}, u32[]{:S(2)}, u32[]{:S(2)}) collective-permute-start(bf16[512,512]{1,0:T(8,128)(2,1)} %lay_out_x.1), channel_id=1, source_target_pairs={{0,4},{4,12},{8,0},{12,8},{16,20},{20,28},{24,16},{28,24},{1,5},{5... | collective-permute-start | bytes 1572872 | tf_op jit(solution)/shard_map/ppermute | solution.py:78
  67.3 97.9 %reduce-scatter.5.cloned.1.call-start = ((), (), s32[]{:S(2)}) async-start(), calls=%async_computation.6 | async-start | bytes 1966080 | tf_op jit(solution)/shard_map/reduce_scatter | solution.py:114
  67.4 16.8 %collective-permute-start.12 = (bf16[576,512]{1,0:T(8,128)(2,1)}, bf16[576,512]{1,0:T(8,128)(2,1)S(1)}, u32[]{:S(2)}, u32[]{:S(2)}) collective-permute-start(bf16[576,512]{1,0:T(8,128)(2,1)} %get-tuple-element.294), channel_id=1, source_target_pairs={{0,20},{4,28},{8,16},{12,24},{16,4},{20,12},{24,0},{28,8},{1,21},{... | collective-permute-start | bytes 1769480 | tf_op jit(solution)/shard_map/ppermute | solution.py:78
  67.5 16.8 %collective-permute-start.11 = (bf16[576,512]{1,0:T(8,128)(2,1)}, bf16[576,512]{1,0:T(8,128)(2,1)S(1)}, u32[]{:S(2)}, u32[]{:S(2)}) collective-permute-start(bf16[576,512]{1,0:T(8,128)(2,1)} %get-tuple-element.294), channel_id=1, source_target_pairs={{0,16},{4,24},{8,20},{12,28},{16,0},{20,8},{24,4},{28,12},{1,17},{... | collective-permute-start | bytes 1769480 | tf_op jit(solution)/shard_map/ppermute | solution.py:78
  69.5 14.6 %collective-permute-start.10 = (bf16[512,512]{1,0:T(8,128)(2,1)}, bf16[512,512]{1,0:T(8,128)(2,1)S(1)}, u32[]{:S(2)}, u32[]{:S(2)}) collective-permute-start(bf16[512,512]{1,0:T(8,128)(2,1)} %get-tuple-element.306.refs_5_.refs_11_), channel_id=1, source_target_pairs={{0,32},{32,64},{64,96},{96,0},{1,33},{33,65},{65,97},{97,1},{2,34}... | collective-permute-start | bytes 1572872 | tf_op jit(solution)/shard_map/ppermute | solution.py:48
  69.9 14.2 %collective-permute-start.9 = (bf16[512,512]{1,0:T(8,128)(2,1)}, bf16[512,512]{1,0:T(8,128)(2,1)S(1)}, u32[]{:S(2)}, u32[]{:S(2)}) collective-permute-start(bf16[512,512]{1,0:T(8,128)(2,1)} %get-tuple-element.306.refs_5_.refs_11_), channel_id=1, source_target_pairs={{0,96},{32,0},{64,32},{96,64},{1,97},{33,1},{65,33},{97,65},{2,98}... | collective-permute-start | bytes 1572872 | tf_op jit(solution)/shard_map/ppermute | solution.py:48
  84.2 18.9 %collective-permute-start.14 = (bf16[576,512]{1,0:T(8,128)(2,1)}, bf16[576,512]{1,0:T(8,128)(2,1)S(1)}, u32[]{:S(2)}, u32[]{:S(2)}) collective-permute-start(bf16[576,512]{1,0:T(8,128)(2,1)} %get-tuple-element.294), channel_id=1, source_target_pairs={{4,8},{8,4},{20,24},{24,20},{5,9},{9,5},{21,25},{25,21},{6,10},{10... | collective-permute-start | bytes 1769480 | tf_op jit(solution)/shard_map/ppermute | solution.py:78
  86.9 17.2 %collective-permute-start.15 = (bf16[576,512]{1,0:T(8,128)(2,1)}, bf16[576,512]{1,0:T(8,128)(2,1)S(1)}, u32[]{:S(2)}, u32[]{:S(2)}) collective-permute-start(bf16[576,512]{1,0:T(8,128)(2,1)} %get-tuple-element.294), channel_id=1, source_target_pairs={{0,4},{4,12},{8,0},{12,8},{16,20},{20,28},{24,16},{28,24},{1,5},{5... | collective-permute-start | bytes 1769480 | tf_op jit(solution)/shard_map/ppermute | solution.py:78
  87.0 17.1 %collective-permute-start.13 = (bf16[512,512]{1,0:T(8,128)(2,1)}, bf16[512,512]{1,0:T(8,128)(2,1)}, u32[]{:S(2)}, u32[]{:S(2)}) collective-permute-start(bf16[512,512]{1,0:T(8,128)(2,1)} %get-tuple-element.306.refs_5_.refs_11_), channel_id=1, source_target_pairs={{0,64},{32,96},{64,0},{96,32},{1,65},{33,97},{65,1},{97,33},{2,66}... | collective-permute-start | bytes 1572872 | tf_op jit(solution)/shard_map/ppermute | solution.py:48
  104.1 26.0 %collective-permute-start.17 = (bf16[512,1024]{1,0:T(8,128)(2,1)}, bf16[512,1024]{1,0:T(8,128)(2,1)S(1)}, u32[]{:S(2)}, u32[]{:S(2)}) collective-permute-start(bf16[512,1024]{1,0:T(8,128)(2,1)} %get-tuple-element.336.refs_3_), channel_id=1, source_target_pairs={{0,32},{32,64},{64,96},{96,0},{1,33},{33,65},{65,97},{97,1},{2,34}... | collective-permute-start | bytes 3145736 | tf_op jit(solution)/shard_map/ppermute | solution.py:48
  104.2 25.9 %collective-permute-start.16 = (bf16[512,1024]{1,0:T(8,128)(2,1)}, bf16[512,1024]{1,0:T(8,128)(2,1)S(1)}, u32[]{:S(2)}, u32[]{:S(2)}) collective-permute-start(bf16[512,1024]{1,0:T(8,128)(2,1)} %get-tuple-element.336.refs_3_), channel_id=1, source_target_pairs={{0,96},{32,0},{64,32},{96,64},{1,97},{33,1},{65,33},{97,65},{2,98}... | collective-permute-start | bytes 3145736 | tf_op jit(solution)/shard_map/ppermute | solution.py:48
  106.8 24.5 %collective-permute-start.19 = (bf16[512,1024]{1,0:T(8,128)(2,1)}, bf16[512,1024]{1,0:T(8,128)(2,1)}, u32[]{:S(2)}, u32[]{:S(2)}) collective-permute-start(bf16[512,1024]{1,0:T(8,128)(2,1)} %get-tuple-element.349.refs_20_), channel_id=1, source_target_pairs={{0,20},{4,28},{8,16},{12,24},{16,4},{20,12},{24,0},{28,8},{1,21},{... | collective-permute-start | bytes 3145736 | tf_op jit(solution)/shard_map/ppermute | solution.py:78
  109.0 24.2 %collective-permute-start.18 = (bf16[512,1024]{1,0:T(8,128)(2,1)}, bf16[512,1024]{1,0:T(8,128)(2,1)}, u32[]{:S(2)}, u32[]{:S(2)}) collective-permute-start(bf16[512,1024]{1,0:T(8,128)(2,1)} %get-tuple-element.349.refs_20_), channel_id=1, source_target_pairs={{0,16},{4,24},{8,20},{12,28},{16,0},{20,8},{24,4},{28,12},{1,17},{... | collective-permute-start | bytes 3145736 | tf_op jit(solution)/shard_map/ppermute | solution.py:78
  140.0 62.8 %all-gather.9.cloned.1.call-start = ((), (), s32[]{:S(2)}) async-start(), calls=%async_computation.7 | async-start | bytes 3538944 | tf_op jit(solution)/shard_map/all_gather | solution.py:109
  140.1 14.8 %collective-permute-start.22 = (bf16[256,1024]{1,0:T(8,128)(2,1)S(1)}, bf16[256,1024]{1,0:T(8,128)(2,1)S(1)}, u32[]{:S(2)}, u32[]{:S(2)}) collective-permute-start(bf16[256,1024]{1,0:T(8,128)(2,1)S(1)} %slice.91), channel_id=1, source_target_pairs={{0,32},{32,64},{64,96},{96,0},{1,33},{33,65},{65,97},{97,1},{2,34}... | collective-permute-start | bytes 1572872 | tf_op jit(solution)/shard_map/ppermute | solution.py:48
  140.1 30.7 %collective-permute-start.24 = (bf16[512,1024]{1,0:T(8,128)(2,1)}, bf16[512,1024]{1,0:T(8,128)(2,1)S(1)}, u32[]{:S(2)}, u32[]{:S(2)}) collective-permute-start(bf16[512,1024]{1,0:T(8,128)(2,1)} %get-tuple-element.349.refs_20_), channel_id=1, source_target_pairs={{0,4},{4,12},{8,0},{12,8},{16,20},{20,28},{24,16},{28,24},{1,5},{5... | collective-permute-start | bytes 3145736 | tf_op jit(solution)/shard_map/ppermute | solution.py:78
  140.4 30.5 %collective-permute-start.23 = (bf16[512,1024]{1,0:T(8,128)(2,1)}, bf16[512,1024]{1,0:T(8,128)(2,1)}, u32[]{:S(2)}, u32[]{:S(2)}) collective-permute-start(bf16[512,1024]{1,0:T(8,128)(2,1)} %get-tuple-element.349.refs_20_), channel_id=1, source_target_pairs={{4,8},{8,4},{20,24},{24,20},{5,9},{9,5},{21,25},{25,21},{6,10},{10... | collective-permute-start | bytes 3145736 | tf_op jit(solution)/shard_map/ppermute | solution.py:78
  145.6 20.7 %collective-permute-start.21 = (bf16[256,1024]{1,0:T(8,128)(2,1)S(1)}, bf16[256,1024]{1,0:T(8,128)(2,1)}, u32[]{:S(2)}, u32[]{:S(2)}) collective-permute-start(bf16[256,1024]{1,0:T(8,128)(2,1)S(1)} %slice.90), channel_id=1, source_target_pairs={{0,96},{32,0},{64,32},{96,64},{1,97},{33,1},{65,33},{97,65},{2,98}... | collective-permute-start | bytes 1572872 | tf_op jit(solution)/shard_map/ppermute | solution.py:48
  148.4 17.9 %collective-permute-start.26 = (bf16[512,512]{1,0:T(8,128)(2,1)}, bf16[512,512]{1,0:T(8,128)(2,1)}, u32[]{:S(2)}, u32[]{:S(2)}) collective-permute-start(bf16[512,512]{1,0:T(8,128)(2,1)} %get-tuple-element.341.refs_8_.refs_0_), channel_id=1, source_target_pairs={{0,32},{32,64},{64,96},{96,0},{1,33},{33,65},{65,97},{97,1},{2,34}... | collective-permute-start | bytes 1572872 | tf_op jit(solution)/shard_map/ppermute | solution.py:48
  155.6 15.3 %collective-permute-start.25 = (bf16[512,512]{1,0:T(8,128)(2,1)}, bf16[512,512]{1,0:T(8,128)(2,1)}, u32[]{:S(2)}, u32[]{:S(2)}) collective-permute-start(bf16[512,512]{1,0:T(8,128)(2,1)} %get-tuple-element.341.refs_8_.refs_0_), channel_id=1, source_target_pairs={{0,96},{32,0},{64,32},{96,64},{1,97},{33,1},{65,33},{97,65},{2,98}... | collective-permute-start | bytes 1572872 | tf_op jit(solution)/shard_map/ppermute | solution.py:48
  172.9 97.6 %reduce-scatter.7.cloned.1.call-start = ((), (), s32[]{:S(2)}) async-start(), calls=%async_computation.8 | async-start | bytes 1966080 | tf_op jit(solution)/shard_map/reduce_scatter | solution.py:837
  172.9 14.3 %collective-permute-start.27 = (bf16[512,512]{1,0:T(8,128)(2,1)}, bf16[512,512]{1,0:T(8,128)(2,1)S(1)}, u32[]{:S(2)}, u32[]{:S(2)}) collective-permute-start(bf16[512,512]{1,0:T(8,128)(2,1)} %get-tuple-element.341.refs_8_.refs_0_), channel_id=1, source_target_pairs={{0,64},{32,96},{64,0},{96,32},{1,65},{33,97},{65,1},{97,33},{2,66}... | collective-permute-start | bytes 1572872 | tf_op jit(solution)/shard_map/ppermute | solution.py:48
  175.2 14.0 %collective-permute-start.31 = (bf16[512,512]{1,0:T(8,128)(2,1)}, bf16[512,512]{1,0:T(8,128)(2,1)S(1)}, u32[]{:S(2)}, u32[]{:S(2)}) collective-permute-start(bf16[512,512]{1,0:T(8,128)(2,1)} %get-tuple-element.348.refs_21_.refs_8_), channel_id=1, source_target_pairs={{0,20},{4,28},{8,16},{12,24},{16,4},{20,12},{24,0},{28,8},{1,21},{... | collective-permute-start | bytes 1572872 | tf_op jit(solution)/shard_map/ppermute | solution.py:78
  177.6 23.8 %collective-permute-start.30 = (bf16[512,512]{1,0:T(8,128)(2,1)}, bf16[512,512]{1,0:T(8,128)(2,1)S(1)}, u32[]{:S(2)}, u32[]{:S(2)}) collective-permute-start(bf16[512,512]{1,0:T(8,128)(2,1)} %get-tuple-element.348.refs_21_.refs_8_), channel_id=1, source_target_pairs={{0,16},{4,24},{8,20},{12,28},{16,0},{20,8},{24,4},{28,12},{1,17},{... | collective-permute-start | bytes 1572872 | tf_op jit(solution)/shard_map/ppermute | solution.py:78
  177.6 23.8 %collective-permute-start.29 = (bf16[512,512]{1,0:T(8,128)(2,1)}, bf16[512,512]{1,0:T(8,128)(2,1)}, u32[]{:S(2)}, u32[]{:S(2)}) collective-permute-start(bf16[512,512]{1,0:T(8,128)(2,1)} %get-tuple-element.348.refs_21_.refs_8_), channel_id=1, source_target_pairs={{0,4},{4,12},{8,0},{12,8},{16,20},{20,28},{24,16},{28,24},{1,5},{5... | collective-permute-start | bytes 1572872 | tf_op jit(solution)/shard_map/ppermute | solution.py:78
  178.1 23.4 %collective-permute-start.28 = (bf16[512,512]{1,0:T(8,128)(2,1)}, bf16[512,512]{1,0:T(8,128)(2,1)}, u32[]{:S(2)}, u32[]{:S(2)}) collective-permute-start(bf16[512,512]{1,0:T(8,128)(2,1)} %get-tuple-element.348.refs_21_.refs_8_), channel_id=1, source_target_pairs={{4,8},{8,4},{20,24},{24,20},{5,9},{9,5},{21,25},{25,21},{6,10},{10... | collective-permute-start | bytes 1572872 | tf_op jit(solution)/shard_map/ppermute | solution.py:78
  240.6 65.2 %all-gather.11.cloned.1.call-start = ((), (), s32[]{:S(2)}) async-start(), calls=%async_computation.9 | async-start | bytes 3538944 | tf_op jit(solution)/shard_map/all_gather | solution.py:109
  242.2 29.3 %collective-permute-start.33 = (bf16[512,1024]{1,0:T(8,128)(2,1)}, bf16[512,1024]{1,0:T(8,128)(2,1)S(1)}, u32[]{:S(2)}, u32[]{:S(2)}) collective-permute-start(bf16[512,1024]{1,0:T(8,128)(2,1)} %get-tuple-element.363), channel_id=1, source_target_pairs={{16,0},{24,4},{20,8},{28,12},{0,16},{8,20},{4,24},{12,28},{17,1},{... | collective-permute-start | bytes 3145736 | tf_op jit(solution)/shard_map/ppermute | solution.py:82
  244.8 26.8 %collective-permute-start.34 = (bf16[512,1024]{1,0:T(8,128)(2,1)}, bf16[512,1024]{1,0:T(8,128)(2,1)}, u32[]{:S(2)}, u32[]{:S(2)}) collective-permute-start(bf16[512,1024]{1,0:T(8,128)(2,1)} %get-tuple-element.364), channel_id=1, source_target_pairs={{20,0},{28,4},{16,8},{24,12},{4,16},{12,20},{0,24},{8,28},{21,1},{... | collective-permute-start | bytes 3145736 | tf_op jit(solution)/shard_map/ppermute | solution.py:82
  245.3 26.4 %collective-permute-start.35 = (bf16[512,1024]{1,0:T(8,128)(2,1)}, bf16[512,1024]{1,0:T(8,128)(2,1)}, u32[]{:S(2)}, u32[]{:S(2)}) collective-permute-start(bf16[512,1024]{1,0:T(8,128)(2,1)} %get-tuple-element.365), channel_id=1, source_target_pairs={{0,32},{32,64},{64,96},{96,0},{1,33},{33,65},{65,97},{97,1},{2,34}... | collective-permute-start | bytes 3145736 | tf_op jit(solution)/shard_map/ppermute | solution.py:48
  246.9 25.3 %collective-permute-start.36 = (bf16[512,1024]{1,0:T(8,128)(2,1)}, bf16[512,1024]{1,0:T(8,128)(2,1)}, u32[]{:S(2)}, u32[]{:S(2)}) collective-permute-start(bf16[512,1024]{1,0:T(8,128)(2,1)} %get-tuple-element.366), channel_id=1, source_target_pairs={{0,96},{32,0},{64,32},{96,64},{1,97},{33,1},{65,33},{97,65},{2,98}... | collective-permute-start | bytes 3145736 | tf_op jit(solution)/shard_map/ppermute | solution.py:48
  275.4 121.8 %reduce-scatter.9.cloned.1.call-start = ((), (), s32[]{:S(2)}) async-start(), calls=%async_computation.10 | async-start | bytes 1966080 | tf_op jit(solution)/shard_map/reduce_scatter | solution.py:936
  276.3 26.4 %collective-permute-start.38 = (bf16[512,1024]{1,0:T(8,128)(2,1)}, bf16[512,1024]{1,0:T(8,128)(2,1)S(1)}, u32[]{:S(2)}, u32[]{:S(2)}) collective-permute-start(bf16[512,1024]{1,0:T(8,128)(2,1)} %get-tuple-element.382), channel_id=1, source_target_pairs={{0,64},{32,96},{64,0},{96,32},{1,65},{33,97},{65,1},{97,33},{2,66}... | collective-permute-start | bytes 3145736 | tf_op jit(solution)/shard_map/ppermute | solution.py:48
  278.3 24.4 %collective-permute-start.40 = (bf16[512,1024]{1,0:T(8,128)(2,1)}, bf16[512,1024]{1,0:T(8,128)(2,1)}, u32[]{:S(2)}, u32[]{:S(2)}) collective-permute-start(bf16[512,1024]{1,0:T(8,128)(2,1)} %get-tuple-element.386), channel_id=1, source_target_pairs={{4,0},{12,4},{0,8},{8,12},{20,16},{28,20},{16,24},{24,28},{5,1},{1... | collective-permute-start | bytes 3145736 | tf_op jit(solution)/shard_map/ppermute | solution.py:82
  279.4 26.4 %collective-permute-start.39 = (bf16[512,1024]{1,0:T(8,128)(2,1)}, bf16[512,1024]{1,0:T(8,128)(2,1)}, u32[]{:S(2)}, u32[]{:S(2)}) collective-permute-start(bf16[512,1024]{1,0:T(8,128)(2,1)} %get-tuple-element.385.refs_8_), channel_id=1, source_target_pairs={{8,4},{4,8},{24,20},{20,24},{9,5},{5,9},{25,21},{21,25},{10,6},{6,... | collective-permute-start | bytes 3145736 | tf_op jit(solution)/shard_map/ppermute | solution.py:82
  305.8 17.8 %collective-permute-start.41 = (bf16[512,512]{1,0:T(8,128)(2,1)}, bf16[512,512]{1,0:T(8,128)(2,1)S(1)}, u32[]{:S(2)}, u32[]{:S(2)}) collective-permute-start(bf16[512,512]{1,0:T(8,128)(2,1)} %get-tuple-element.409), channel_id=1, source_target_pairs={{0,32},{32,64},{64,96},{96,0},{1,33},{33,65},{65,97},{97,1},{2,34}... | collective-permute-start | bytes 1572872 | tf_op jit(solution)/shard_map/ppermute | solution.py:48
  306.6 17.0 %collective-permute-start.42 = (bf16[512,512]{1,0:T(8,128)(2,1)}, bf16[512,512]{1,0:T(8,128)(2,1)S(1)}, u32[]{:S(2)}, u32[]{:S(2)}) collective-permute-start(bf16[512,512]{1,0:T(8,128)(2,1)} %get-tuple-element.410), channel_id=1, source_target_pairs={{0,96},{32,0},{64,32},{96,64},{1,97},{33,1},{65,33},{97,65},{2,98}... | collective-permute-start | bytes 1572872 | tf_op jit(solution)/shard_map/ppermute | solution.py:48
  308.5 15.2 %collective-permute-start.43 = (bf16[512,512]{1,0:T(8,128)(2,1)}, bf16[512,512]{1,0:T(8,128)(2,1)S(1)}, u32[]{:S(2)}, u32[]{:S(2)}) collective-permute-start(bf16[512,512]{1,0:T(8,128)(2,1)} %get-tuple-element.411), channel_id=1, source_target_pairs={{16,0},{24,4},{20,8},{28,12},{0,16},{8,20},{4,24},{12,28},{17,1},{... | collective-permute-start | bytes 1572872 | tf_op jit(solution)/shard_map/ppermute | solution.py:82
  309.3 14.3 %collective-permute-start.44 = (bf16[512,512]{1,0:T(8,128)(2,1)}, bf16[512,512]{1,0:T(8,128)(2,1)S(1)}, u32[]{:S(2)}, u32[]{:S(2)}) collective-permute-start(bf16[512,512]{1,0:T(8,128)(2,1)} %get-tuple-element.412), channel_id=1, source_target_pairs={{20,0},{28,4},{16,8},{24,12},{4,16},{12,20},{0,24},{8,28},{21,1},{... | collective-permute-start | bytes 1572872 | tf_op jit(solution)/shard_map/ppermute | solution.py:82
  324.7 17.7 %collective-permute-start.45 = (bf16[3072,256]{1,0:T(8,128)(2,1)}, bf16[3072,256]{1,0:T(8,128)(2,1)S(1)}, u32[]{:S(2)}, u32[]{:S(2)}) collective-permute-start(bf16[3072,256]{1,0:T(8,128)(2,1)} %get-tuple-element.414), channel_id=1, source_target_pairs={{0,8},{8,0},{1,9},{9,1},{2,10},{10,2},{3,11},{11,3},{4,12},{12,4},... | collective-permute-start | bytes 4718600 | tf_op jit(solution)/shard_map/ppermute | solution.py:44
  325.7 16.6 %collective-permute-start.46 = (bf16[512,512]{1,0:T(8,128)(2,1)S(1)}, bf16[512,512]{1,0:T(8,128)(2,1)S(1)}, u32[]{:S(2)}, u32[]{:S(2)}) collective-permute-start(bf16[512,512]{1,0:T(8,128)(2,1)S(1)} %copy-done.49), channel_id=1, source_target_pairs={{0,64},{32,96},{64,0},{96,32},{1,65},{33,97},{65,1},{97,33},{2,66}... | collective-permute-start | bytes 1572872 | tf_op jit(solution)/shard_map/ppermute | solution.py:48
  326.3 16.0 %collective-permute-start.48 = (bf16[512,512]{1,0:T(8,128)(2,1)S(1)}, bf16[512,512]{1,0:T(8,128)(2,1)S(1)}, u32[]{:S(2)}, u32[]{:S(2)}) collective-permute-start(bf16[512,512]{1,0:T(8,128)(2,1)S(1)} %copy-done.48), channel_id=1, source_target_pairs={{4,0},{12,4},{0,8},{8,12},{20,16},{28,20},{16,24},{24,28},{5,1},{1... | collective-permute-start | bytes 1572872 | tf_op jit(solution)/shard_map/ppermute | solution.py:82
  328.1 14.3 %collective-permute-start.47 = (bf16[512,512]{1,0:T(8,128)(2,1)S(1)}, bf16[512,512]{1,0:T(8,128)(2,1)S(1)}, u32[]{:S(2)}, u32[]{:S(2)}) collective-permute-start(bf16[512,512]{1,0:T(8,128)(2,1)S(1)} %copy-done.19), channel_id=1, source_target_pairs={{8,4},{4,8},{24,20},{20,24},{9,5},{5,9},{25,21},{21,25},{10,6},{6,... | collective-permute-start | bytes 1572872 | tf_op jit(solution)/shard_map/ppermute | solution.py:82
  345.0 58.5 %reduce-scatter.11.cloned.1.call-start = ((), (), s32[]{:S(2)}) async-start(), calls=%async_computation.11 | async-start | bytes 1966080 | tf_op jit(solution)/shard_map/reduce_scatter | solution.py:968
  349.9 23.5 %collective-permute-start.51 = (bf16[896,512]{1,0:T(8,128)(2,1)}, bf16[896,512]{1,0:T(8,128)(2,1)S(1)}, u32[]{:S(2)}, u32[]{:S(2)}) collective-permute-start(bf16[896,512]{1,0:T(8,128)(2,1)} %get-tuple-element.467), channel_id=1, source_target_pairs={{0,32},{32,64},{64,96},{96,0},{1,33},{33,65},{65,97},{97,1},{2,34}... | collective-permute-start | bytes 2752520 | tf_op jit(solution)/shard_map/ppermute | solution.py:48
  350.3 23.1 %collective-permute-start.52 = (bf16[896,512]{1,0:T(8,128)(2,1)}, bf16[896,512]{1,0:T(8,128)(2,1)S(1)}, u32[]{:S(2)}, u32[]{:S(2)}) collective-permute-start(bf16[896,512]{1,0:T(8,128)(2,1)} %get-tuple-element.468), channel_id=1, source_target_pairs={{0,96},{32,0},{64,32},{96,64},{1,97},{33,1},{65,33},{97,65},{2,98}... | collective-permute-start | bytes 2752520 | tf_op jit(solution)/shard_map/ppermute | solution.py:48
  352.6 20.7 %collective-permute-start.53 = (bf16[896,512]{1,0:T(8,128)(2,1)}, bf16[896,512]{1,0:T(8,128)(2,1)}, u32[]{:S(2)}, u32[]{:S(2)}) collective-permute-start(bf16[896,512]{1,0:T(8,128)(2,1)} %get-tuple-element.469), channel_id=1, source_target_pairs={{16,0},{24,4},{20,8},{28,12},{0,16},{8,20},{4,24},{12,28},{17,1},{... | collective-permute-start | bytes 2752520 | tf_op jit(solution)/shard_map/ppermute | solution.py:82
  354.7 20.8 %collective-permute-start.54 = (bf16[896,512]{1,0:T(8,128)(2,1)}, bf16[896,512]{1,0:T(8,128)(2,1)}, u32[]{:S(2)}, u32[]{:S(2)}) collective-permute-start(bf16[896,512]{1,0:T(8,128)(2,1)} %get-tuple-element.470), channel_id=1, source_target_pairs={{20,0},{28,4},{16,8},{24,12},{4,16},{12,20},{0,24},{8,28},{21,1},{... | collective-permute-start | bytes 2752520 | tf_op jit(solution)/shard_map/ppermute | solution.py:82
  375.4 22.8 %collective-permute-start.55 = (bf16[896,512]{1,0:T(8,128)(2,1)}, bf16[896,512]{1,0:T(8,128)(2,1)}, u32[]{:S(2)}, u32[]{:S(2)}) collective-permute-start(bf16[896,512]{1,0:T(8,128)(2,1)} %get-tuple-element.471), channel_id=1, source_target_pairs={{0,64},{32,96},{64,0},{96,32},{1,65},{33,97},{65,1},{97,33},{2,66}... | collective-permute-start | bytes 2752520 | tf_op jit(solution)/shard_map/ppermute | solution.py:48
  375.8 22.4 %collective-permute-start.57 = (bf16[896,512]{1,0:T(8,128)(2,1)}, bf16[896,512]{1,0:T(8,128)(2,1)}, u32[]{:S(2)}, u32[]{:S(2)}) collective-permute-start(bf16[896,512]{1,0:T(8,128)(2,1)} %get-tuple-element.475), channel_id=1, source_target_pairs={{4,0},{12,4},{0,8},{8,12},{20,16},{28,20},{16,24},{24,28},{5,1},{1... | collective-permute-start | bytes 2752520 | tf_op jit(solution)/shard_map/ppermute | solution.py:82
  378.7 24.4 %collective-permute-start.56 = (bf16[896,512]{1,0:T(8,128)(2,1)}, bf16[896,512]{1,0:T(8,128)(2,1)}, u32[]{:S(2)}, u32[]{:S(2)}) collective-permute-start(bf16[896,512]{1,0:T(8,128)(2,1)} %get-tuple-element.513.refs_8_), channel_id=1, source_target_pairs={{8,4},{4,8},{24,20},{20,24},{9,5},{5,9},{25,21},{21,25},{10,6},{6,... | collective-permute-start | bytes 2752520 | tf_op jit(solution)/shard_map/ppermute | solution.py:82
  404.8 19.4 %collective-permute-start.61 = (bf16[1536,256]{1,0:T(8,128)(2,1)S(1)}, bf16[1536,256]{1,0:T(8,128)(2,1)S(1)}, u32[]{:S(2)}, u32[]{:S(2)}) collective-permute-start(bf16[1536,256]{1,0:T(8,128)(2,1)S(1)} %pad_maximum_fusion), channel_id=1, source_target_pairs={{4,8},{8,4},{5,9},{9,5},{6,10},{10,6},{7,11},{11,7},{20,24},{24,20... | collective-permute-start | bytes 2359304 | tf_op jit(solution)/shard_map/ppermute | solution.py:39
  411.3 12.8 %collective-permute-start.60 = (bf16[512,256]{1,0:T(8,128)(2,1)}, bf16[512,256]{1,0:T(8,128)(2,1)S(1)}, u32[]{:S(2)}, u32[]{:S(2)}) collective-permute-start(bf16[512,256]{1,0:T(8,128)(2,1)} %get-tuple-element.488), channel_id=1, source_target_pairs={{0,1},{1,0},{2,3},{3,2},{4,5},{5,4},{6,7},{7,6},{8,9},{9,8},{10,11... | collective-permute-start | bytes 786440 | tf_op jit(solution)/shard_map/ppermute | solution.py:60
  413.5 10.9 %collective-permute-start.64 = (bf16[128,512]{1,0:T(8,128)(2,1)}, bf16[128,512]{1,0:T(8,128)(2,1)S(1)}, u32[]{:S(2)}, u32[]{:S(2)}) collective-permute-start(bf16[128,512]{1,0:T(8,128)(2,1)} %get-tuple-element.498), channel_id=1, source_target_pairs={{0,64},{32,96},{64,0},{96,32},{1,65},{33,97},{65,1},{97,33},{2,66}... | collective-permute-start | bytes 393224 | tf_op jit(solution)/shard_map/ppermute | solution.py:48
  424.5 10.9 %collective-permute-start.69 = (bf16[176,256]{1,0:T(8,128)(2,1)S(1)}, bf16[176,256]{1,0:T(8,128)(2,1)S(1)}, u32[]{:S(2)}, u32[]{:S(2)}) collective-permute-start(bf16[176,256]{1,0:T(8,128)(2,1)S(1)} %get-tuple-element.531), channel_id=1, source_target_pairs={{20,0},{28,4},{16,8},{24,12},{4,16},{12,20},{0,24},{8,28},{21,1},{... | collective-permute-start | bytes 270344 | tf_op jit(solution)/shard_map/ppermute | solution.py:82
  (69 other events, 739.8 us)
Sparse Core Ops, SparseCore 0:
  44.9 28.6 all-gather.4
  75.8 27.8 all-gather.6
  140.1 25.0 reduce-scatter.4
  173.0 29.7 all-gather.8
  240.8 25.4 reduce-scatter.6
  275.5 27.7 all-gather.10
  345.1 23.8 reduce-scatter.8
  371.4 26.4 reduce-scatter.10

commit v6 on v5

--- a/solution.py
+++ b/solution.py
@@ -190,16 +190,14 @@
 
 
 def along_y_body(at, *refs):
-    riders, gain_one, gain_two = refs[:3]
-    tokens, cotangent, w_query, w_output, w_up, w_down, out, mixed, sem = refs[3:]
+    gain_one, gain_two = refs[:2]
+    w_query, w_output, w_up, w_down, out, sem = refs[2:]
     pairs = [
         (w_query, out.at[pl.ds(0, 128), pl.ds(0, 256)]),
         (w_output, out.at[pl.ds(0, 128), pl.ds(256, 256)]),
         (w_up.at[:, pl.ds(0, 512)], out.at[pl.ds(144, 128)]),
         (w_up.at[:, pl.ds(512, 512)], out.at[pl.ds(272, 128)]),
         (w_down.at[:, pl.ds(512, 512)], out.at[pl.ds(400, 128)]),
-        (tokens, mixed.at[pl.ds(0, 768)]),
-        (cotangent, mixed.at[pl.ds(784, 768)]),
     ]
     copies = [pltpu.make_async_copy(a, b, sem.at[i]) for i, (a, b) in enumerate(pairs)]
     for copy in copies:
@@ -208,13 +206,14 @@
     gains = jnp.where(row == 0, gain_one[...], jnp.where(row == 1, gain_two[...], 0.0))
     out[128:144, :128] = gains.astype(bf16)
     out[128:144, 128:] = jnp.zeros((16, 384), bf16)
-    mixed[768:784, :] = riders[...]
     for copy in copies:
         copy.wait()
 
 
 def along_x_body(at, *refs):
-    key, value, other, w_gate, w_down, out, sem = refs
+    riders, key, value, other, w_gate, w_down, out, sem = refs
+    out[512:528, :256] = riders[...]
+    out[512:528, 256:] = jnp.zeros((16, 256), bf16)
     pairs = [
         (w_gate.at[:, pl.ds(0, 512)], out.at[pl.ds(128, 128)]),
         (w_gate.at[:, pl.ds(512, 512)], out.at[pl.ds(256, 128)]),
@@ -703,39 +702,38 @@
     odd = z % 2 == 1
     half = HEAD // 2
     kv_other = kv_partner(jnp.concatenate([w_key, w_value], 1))
-    y_rows, mixed = call(
+    (y_rows,) = call(
         along_y_body,
         "lay_out_y",
         [
             at,
-            riders,
-            gain_attn.astype(f32).reshape(1, 128),
+            after(gain_attn.astype(f32).reshape(1, 128), kv_other),
             gain_ffn.astype(f32).reshape(1, 128),
-            tokens,
-            cotangent,
             w_query,
             w_output,
             w_up,
             w_down,
         ],
-        [((528, 2 * HEAD), bf16), ((1552, HEAD), bf16)],
-        [pltpu.SemaphoreType.DMA((7,))],
+        [((528, 2 * HEAD), bf16)],
+        [pltpu.SemaphoreType.DMA((5,))],
         0,
-        anywhere=6,
+        anywhere=4,
     )
     (x_rows,) = call(
         along_x_body,
         "lay_out_x",
-        [at, w_key, w_value, kv_other, w_gate, w_down],
-        [((512, 2 * HEAD), bf16)],
+        [at, riders, w_key, w_value, kv_other, w_gate, w_down],
+        [((528, 2 * HEAD), bf16)],
         [pltpu.SemaphoreType.DMA((3,))],
         0,
         anywhere=2,
     )
-    got = swap(mixed)
+    x_own, upstream_own = swap(tokens), swap(cotangent)
     along_y = [shift(y_rows, Y, -1), shift(y_rows, Y, 1)]
     along_x = [x_in(x_rows, *flip) for flip in FLIPS[2:]]
-    got, late_y, late_x, *rest = lax.optimization_barrier((got, y_rows, x_rows, *along_y, *along_x))
+    x_own, upstream_own, late_y, late_x, *rest = lax.optimization_barrier(
+        (x_own, upstream_own, y_rows, x_rows, *along_y, *along_x)
+    )
     along_y = [y_rows, rest[0], shift(late_y, Y, 2), rest[1]]
     along_x = [own_or(x_in(late_x, 0, 0), x_rows), x_in(late_x, *FLIPS[1]), *rest[2:]]
     rest = lax.optimization_barrier((*along_x, *along_y))
@@ -757,10 +755,9 @@
         0,
         anywhere=8,
     )
-    x_own = got[:LEN]
     x_all = team_gather(x_own)
-    upstream = team_gather(after(got[784:1552], to_x))
-    segment_row = got[LEN : LEN + 3].astype(f32).reshape(1, LEN)
+    upstream = team_gather(after(upstream_own, to_x))
+    segment_row = rest[0][512:515, :HEAD].astype(f32).reshape(1, LEN)
     segment_col = segment_row.reshape(LEN, 1)
     cosine, sine = rope_tables(segment_row[0])
     first = [shift(to_y, Y, -1), shift(to_y, Y, 1)]

time: 455 us -> 460 us (1.011)
  waiting for transfers between devices: 157 us -> 142 us
  other arithmetic: 29.7 us -> 41.1 us
  starting transfers between devices: 107 us -> 115 us
    ppermute x16, starting transfers between devices: 22.4 us -> 29.9 us  [x_in(): return lax.ppermute(a, (XLO, CORE, XHI), x_pairs(flip_lo, flip_core, False))]
    ppermute x25, waiting for transfers between devices: 71.5 us -> 64.5 us  [shift(): return lax.ppermute(a, axis, [(i, (i + by) % 4) for i in range(4)])]
    ppermute x2 -> x3, starting transfers between devices: 8.16 us -> 9.33 us  [swap(): got = lax.ppermute(a, (CORE, XHI), [(1, 2), (2, 1)])]
  transfers between devices with their start and end apart: 78 -> 79, of which waited for: 35 -> 34; matrix products, arithmetic and copies ran while one was open for 4% -> 8% of each run, Pallas kernels for 20% -> 20%
where the time goes in v6:
time: 460 us; the launch traced here: 452 us
  waiting for transfers between devices  142 us (31%)
  Pallas kernels  125 us (27%)
  starting transfers between devices  115 us (25%)
  other arithmetic  41.1 us (9%)
  between operations  15.8 us (3%)
  local copies, waits for them, and re-layouts  12.6 us (3%)
    pallas_call x15, Pallas kernels, call(): pl.pallas_call(body, name=name, out_shape=[jax.ShapeDtypeStruct(s, d) for...  125 us
    ppermute x25, waiting for transfers between devices, shift(): return lax.ppermute(a, axis, [(i, (i + by) % 4) for i in range(4)])  64.5 us
    ppermute x16, waiting for transfers between devices, x_in(): return lax.ppermute(a, (XLO, CORE, XHI), x_pairs(flip_lo, flip_core, False))  40.1 us
    ppermute x16, starting transfers between devices, x_out(): return lax.ppermute(a, (XLO, CORE, XHI), x_pairs(flip_lo, flip_core, True))  34.5 us
    ppermute x25, starting transfers between devices, shift(): return lax.ppermute(a, axis, [(i, (i + by) % 4) for i in range(4)])  31.1 us
    ppermute x16, starting transfers between devices, x_in(): return lax.ppermute(a, (XLO, CORE, XHI), x_pairs(flip_lo, flip_core, False))  29.9 us
    ppermute x16, waiting for transfers between devices, x_out(): return lax.ppermute(a, (XLO, CORE, XHI), x_pairs(flip_lo, flip_core, True))  11.3 us
    ppermute x3, starting transfers between devices, swap(): got = lax.ppermute(a, (CORE, XHI), [(1, 2), (2, 1)])  9.33 us
  transfers between devices with their start and end apart: 79, of which 34 were waited for; matrix products, arithmetic and copies ran while one was open for 8% of the time, Pallas kernels for 20%

profile of v6, /device:TPU:1, one launch (start us, length us, event | category | flops | bytes accessed | tf_op | source)
XLA Modules:
  0.0 451.9 jit_solution(16877857536595797833)
XLA Ops:
  8.1 2.5 collective-permute-start.2
  10.6 5.5 %collective-permute-start = (bf16[768,256]{1,0:T(8,128)(2,1)}, bf16[768,256]{1,0:T(8,128)(2,1)}, u32[]{:S(2)}, u32[]{:S(2)}) collective-permute-start(bf16[768,256]{1,0:T(8,128)(2,1)} %param.14), channel_id=1, source_target_pairs={{4,8},{8,4},{5,9},{9,5},{6,10},{10,6},{7,11},{11,7},{20,24},{24,20... | collective-permute-start | bytes 1179656 | tf_op jit(solution)/shard_map/ppermute | solution.py:39
  22.4 2.8 lay_out_y.1.refs_4_
  28.0 2.8 lay_out_x.1
  30.9 3.5 collective-permute-start.5
  38.1 7.1 %collective-permute-done.6.refs_3_ = bf16[528,512]{1,0:T(8,128)(2,1)S(1)} collective-permute-done((bf16[528,512]{1,0:T(8,128)(2,1)}, bf16[528,512]{1,0:T(8,128)(2,1)S(1)}, u32[]{:S(2)}, u32[]{:S(2)}) %collective-permute-start.6) | collective-permute-done | bytes 540704 | tf_op jit(solution)/shard_map/ppermute | solution.py:78
  46.5 5.0 %collective-permute-start.7 = (bf16[528,512]{1,0:T(8,128)(2,1)}, bf16[528,512]{1,0:T(8,128)(2,1)S(1)}, u32[]{:S(2)}, u32[]{:S(2)}) collective-permute-start(bf16[528,512]{1,0:T(8,128)(2,1)} %lay_out_x.1), channel_id=1, source_target_pairs={{4,8},{8,4},{20,24},{24,20},{5,9},{9,5},{21,25},{25,21},{6,10},{10... | collective-permute-start | bytes 1622024 | tf_op jit(solution)/shard_map/ppermute | solution.py:78
  53.2 7.6 %collective-permute-done.7 = bf16[528,512]{1,0:T(8,128)(2,1)S(1)} collective-permute-done((bf16[528,512]{1,0:T(8,128)(2,1)}, bf16[528,512]{1,0:T(8,128)(2,1)S(1)}, u32[]{:S(2)}, u32[]{:S(2)}) %collective-permute-start.7) | collective-permute-done | bytes 540704 | tf_op jit(solution)/shard_map/ppermute | solution.py:78
  61.8 2.3 collective-permute-done.9.refs_6_
  65.7 3.1 pack.1
  69.7 3.1 collective-permute-start.12
  72.9 2.6 collective-permute-start.10
  76.2 11.2 %collective-permute-done.11.refs_8_.refs_14_ = bf16[512,512]{1,0:T(8,128)(2,1)S(1)} collective-permute-done((bf16[512,512]{1,0:T(8,128)(2,1)}, bf16[512,512]{1,0:T(8,128)(2,1)S(1)}, u32[]{:S(2)}, u32[]{:S(2)}) %collective-permute-start.11) | collective-permute-done | bytes 524320 | tf_op jit(solution)/shard_map/ppermute | solution.py:48
  87.5 2.9 collective-permute-start.15
  92.4 4.6 %riders.1 = (bf16[512,1024]{1,0:T(8,128)(2,1)}, bf16[512,1024]{1,0:T(8,128)(2,1)}, bf16[512,512]{1,0:T(8,128)(2,1)}, bf16[512,512]{1,0:T(8,128)(2,1)}) custom-call(s32[5]{0:T(128)} %stack.74.at, bf16[528,512]{1,0:T(8,128)(2,1)} %broadcast_select_fusion.2.refs_0_, bf16[528,512]{1,0:T(8,128)(2,1)} %copy-done.11, bf16[528,512]{1,0:T(8,128)(2,1)} %copy-done.9, ...), custom_call_target="tpu_custom_call" | custom-call | bytes 7471104 | tf_op jit(solution)/shard_map/riders/pallas_call | solution.py:155
  97.1 2.5 multiply_sine_fusion
  99.6 6.5 %collective-permute-done.15 = bf16[576,512]{1,0:T(8,128)(2,1)S(1)} collective-permute-done((bf16[576,512]{1,0:T(8,128)(2,1)}, bf16[576,512]{1,0:T(8,128)(2,1)S(1)}, u32[]{:S(2)}, u32[]{:S(2)}) %collective-permute-start.15) | collective-permute-done | bytes 589856 | tf_op jit(solution)/shard_map/ppermute | solution.py:78
  107.2 2.7 collective-permute-start.17
  109.8 2.4 collective-permute-start.20
  113.9 15.5 %attention_forward.1 = (bf16[768,2048]{1,0:T(8,128)(2,1)}, f32[768,1]{1,0:T(8,128)}, bf16[96,2048]{1,0:T(8,128)(2,1)}, bf16[768,256]{1,0:T(8,128)(2,1)}, bf16[76...) custom-call(s32[5]{0:T(128)} %stack.74.at, ...), custom_call_target="tpu_custom_call" | custom-call | flops 3221225472 | bytes 16728064 | tf_op jit(solution)/shard_map/attention_forward/pallas_call | solution.py:155
  129.4 4.0 collective-permute-done.18.refs_7_
  133.9 2.3 collective-permute-done.19.refs_14_
  136.6 3.3 collective-permute-done.21
  139.9 3.2 add_convert_fusion.3
  143.7 4.4 collective-permute-start.24
  149.2 2.8 collective-permute-start.22
  152.0 5.7 %collective-permute-done.23.refs_6_ = bf16[256,1024]{1,0:T(8,128)(2,1)S(1)} collective-permute-done((bf16[256,1024]{1,0:T(8,128)(2,1)S(1)}, bf16[256,1024]{1,0:T(8,128)(2,1)S(1)}, u32[]{:S(2)}, u32[]{:S(2)}) %collective-permute-start.23) | collective-permute-done | bytes 524320 | tf_op jit(solution)/shard_map/ppermute | solution.py:48
  158.5 4.6 %order_upstream.1.refs_2_.dy = bf16[768,2048]{1,0:T(8,128)(2,1)} custom-call(s32[5]{0:T(128)} %stack.74.at, bf16[6144,256]{1,0:T(8,128)(2,1)} %all-gather.7.cloned.1.call-done.whole), custom_call_target="tpu_custom_call" | custom-call | bytes 6291456 | tf_op jit(solution)/shard_map/order_upstream/pallas_call | solution.py:155
  163.1 5.1 %reduce-scatter.5.cloned.1.call-done = bf16[96,2048]{1,0:T(8,128)(2,1)} async-done(((bf16[384,2048]{1,0:T(8,128)(2,1)}), bf16[96,2048]{1,0:T(8,128)(2,1)}) %reduce-scatter.5.cloned.1.call-update) | async-done | bytes 393232 | tf_op jit(solution)/shard_map/reduce_scatter | solution.py:114
  169.2 5.2 %collective-permute-done.26.refs_9_.refs_1_ = bf16[512,512]{1,0:T(8,128)(2,1)} collective-permute-done((bf16[512,512]{1,0:T(8,128)(2,1)}, bf16[512,512]{1,0:T(8,128)(2,1)}, u32[]{:S(2)}, u32[]{:S(2)}) %collective-permute-start.26) | collective-permute-done | bytes 524320 | tf_op jit(solution)/shard_map/ppermute | solution.py:48
  175.7 2.2 collective-permute-start.28
  177.9 2.4 collective-permute-start.32
  180.8 3.7 collective-permute-start.29
  184.5 5.5 %collective-permute-done.28.refs_10_.refs_2_ = bf16[512,512]{1,0:T(8,128)(2,1)S(1)} collective-permute-done((bf16[512,512]{1,0:T(8,128)(2,1)}, bf16[512,512]{1,0:T(8,128)(2,1)S(1)}, u32[]{:S(2)}, u32[]{:S(2)}) %collective-permute-start.28) | collective-permute-done | bytes 524320 | tf_op jit(solution)/shard_map/ppermute | solution.py:48
  191.5 12.5 %collective-permute-done.31.refs_18_.refs_6_ = bf16[512,512]{1,0:T(8,128)(2,1)S(1)} collective-permute-done((bf16[512,512]{1,0:T(8,128)(2,1)S(1)}, bf16[512,512]{1,0:T(8,128)(2,1)S(1)}, u32[]{:S(2)}, u32[]{:S(2)}) %collective-permute-start.31) | collective-permute-done | bytes 524320 | tf_op jit(solution)/shard_map/ppermute | solution.py:78
  205.7 31.1 %feed_forward.1 = (bf16[768,256]{1,0:T(8,128)(2,1)}, bf16[768,2048]{1,0:T(8,128)(2,1)}, bf16[768,1024]{1,0:T(8,128)(2,1)}, bf16[768,1024]{1,0:T(8,128)(2,1)}, bf...) custom-call(s32[5]{0:T(128)} %stack.74.at, ...), custom_call_target="tpu_custom_call" | custom-call | flops 22548578304 | bytes 36110336 | tf_op jit(solution)/shard_map/feed_forward/pallas_call | solution.py:155
  237.0 3.5 collective-permute-done.33
  240.5 3.3 add_convert_fusion.2
  245.3 2.5 collective-permute-start.34
  251.0 13.1 %weight_rest.1 = (bf16[512,1024]{1,0:T(8,128)(2,1)}, bf16[512,1024]{1,0:T(8,128)(2,1)}, bf16[512,1024]{1,0:T(8,128)(2,1)}, bf16[512,1024]{1,0:T(8,128)(2,1)}, bf...) custom-call(s32[5]{0:T(128)} %stack.74.at, ...), custom_call_target="tpu_custom_call" | custom-call | flops 6442450944 | bytes 19398656 | tf_op jit(solution)/shard_map/weight_rest/pallas_call | solution.py:155
  264.2 8.7 %feed_forward_out.1 = (bf16[3072,256]{1,0:T(8,128)(2,1)}, bf16[3072,256]{1,0:T(8,128)(2,1)}) custom-call(s32[5]{0:T(128)} %stack.74.at, bf16[768,1024]{1,0:T(8,128)(2,1)} %get-tuple-element.360.hid, bf16[512,512]{1,0:T(8,128)(2,1)} %get-tuple-element.341.refs_8_.refs_0_, bf16[512,512]{1,0:T(8,128)(2,1)} %collective-permute-done.26.refs_9_.refs_1_, ...), custom_call_target="tpu_custom_call" | custom-call | flops 3221225472 | bytes 9437184 | tf_op jit(solution)/shard_map/feed_forward_out/pallas_call | solution.py:155
  275.3 2.3 subtract_convert_fusion.1
  281.8 4.2 collective-permute-start.40
  287.8 17.3 %collective-permute-done.39.refs_1_ = bf16[512,1024]{1,0:T(8,128)(2,1)S(1)} collective-permute-done((bf16[512,1024]{1,0:T(8,128)(2,1)}, bf16[512,1024]{1,0:T(8,128)(2,1)S(1)}, u32[]{:S(2)}, u32[]{:S(2)}) %collective-permute-start.39) | collective-permute-done | bytes 1048608 | tf_op jit(solution)/shard_map/ppermute | solution.py:48
  305.1 3.1 collective-permute-done.40.refs_4_
  312.2 14.0 %attention_backward.1 = (bf16[768,256]{1,0:T(8,128)(2,1)}, bf16[768,768]{1,0:T(8,128)(2,1)}, f32[768,1]{1,0:T(8,128)}, f32[1,2048]{1,0:T(1,128)}, bf16[3072,256]{1,0:T(8,128)(2,1)}, /*index=5*/bf16[3072,256]{1,0:T(8,128)(2,1)}) custom-call(s32[5]{0:T(128)} %stack.74.at, bf16[768,2048]{1,0:T(8,128)(2,1)} %all-gather.11.cloned.1.call-done.refs_0_.db, ...), custom_call_target="tpu_custom_call" | custom-call | flops 3221225472 | bytes 17518592 | tf_op jit(solution)/shard_map/attention_backward/pallas_call | solution.py:155
  330.3 4.2 collective-permute-start.48
  334.5 10.4 %attention_weights.1 = (bf16[896,512]{1,0:T(8,128)(2,1)}, bf16[896,512]{1,0:T(8,128)(2,1)}, bf16[896,512]{1,0:T(8,128)(2,1)}, bf16[896,512]{1,0:T(8,128)(2,1)}, ...) custom-call(s32[5]{0:T(128)} %stack.74.at, ...), custom_call_target="tpu_custom_call" | custom-call | flops 3221225472 | bytes 24641536 | tf_op jit(solution)/shard_map/attention_weights/pallas_call | solution.py:155
  349.4 3.6 feed_forward_sums_down.1
  353.5 2.4 collective-permute-start.53
  364.2 2.6 collective-permute-done.51
  367.7 8.5 %collective-permute-done.52.refs_2_ = bf16[896,512]{1,0:T(8,128)(2,1)S(1)} collective-permute-done((bf16[896,512]{1,0:T(8,128)(2,1)}, bf16[896,512]{1,0:T(8,128)(2,1)S(1)}, u32[]{:S(2)}, u32[]{:S(2)}) %collective-permute-start.52) | collective-permute-done | bytes 917536 | tf_op jit(solution)/shard_map/ppermute | solution.py:48
  378.5 2.9 collective-permute-start.58
  381.4 5.2 %collective-permute-start.57 = (bf16[896,512]{1,0:T(8,128)(2,1)}, bf16[896,512]{1,0:T(8,128)(2,1)}, u32[]{:S(2)}, u32[]{:S(2)}) collective-permute-start(bf16[896,512]{1,0:T(8,128)(2,1)} %get-tuple-element.513.refs_8_), channel_id=1, source_target_pairs={{8,4},{4,8},{24,20},{20,24},{9,5},{5,9},{25,21},{21,25},{10,6},{6,... | collective-permute-start | bytes 2752520 | tf_op jit(solution)/shard_map/ppermute | solution.py:82
  389.7 3.5 collective-permute-done.59
  394.0 5.5 %collective-permute-done.60 = f32[40,128]{1,0:T(8,128)S(1)} collective-permute-done((f32[40,128]{1,0:T(8,128)S(1)}, f32[40,128]{1,0:T(8,128)S(1)}, u32[]{:S(2)}, u32[]{:S(2)}) %collective-permute-start.60) | collective-permute-done | bytes 20512 | tf_op jit(solution)/shard_map/ppermute | solution.py:56
  402.0 4.0 collective-permute-done.57.refs_4_
  410.6 4.5 join_sums.1
  415.4 2.3 collective-permute-start.63
  421.0 3.9 collective-permute-done.64.refs_6_
  424.8 3.9 finish.1
  429.3 5.1 %collective-permute-start.68 = (bf16[176,256]{1,0:T(8,128)(2,1)S(1)}, bf16[176,256]{1,0:T(8,128)(2,1)S(1)}, u32[]{:S(2)}, u32[]{:S(2)}) collective-permute-start(bf16[176,256]{1,0:T(8,128)(2,1)S(1)} %get-tuple-element.531), channel_id=1, source_target_pairs={{4,0},{12,4},{0,8},{8,12},{20,16},{28,20},{16,24},{24,28},{5,1},{1... | collective-permute-start | bytes 270344 | tf_op jit(solution)/shard_map/ppermute | solution.py:82
  434.4 4.1 collective-permute-start.67
  442.5 2.1 last.1
  (306 shorter events, 91.1 us)
Async XLA Ops:
  7.2 99.9 %all-gather.5.cloned.1.call-start = ((), (), s32[]{:S(2)}) async-start(), calls=%async_computation.4 | async-start | bytes 3538944 | tf_op jit(solution)/shard_map/all_gather | solution.py:109
  8.1 14.3 %collective-permute-start.2 = (bf16[128,256]{1,0:T(8,128)(2,1)S(1)}, bf16[128,256]{1,0:T(8,128)(2,1)S(1)}, u32[]{:S(2)}, u32[]{:S(2)}) collective-permute-start(bf16[128,256]{1,0:T(8,128)(2,1)S(1)} %pad_maximum_fusion.2), channel_id=1, source_target_pairs={{0,1},{1,0},{2,3},{3,2},{4,5},{5,4},{6,7},{7,6},{8,9},{9,8},{10,11... | collective-permute-start | bytes 196616 | tf_op jit(solution)/shard_map/ppermute | solution.py:60
  10.6 20.3 %collective-permute-start = (bf16[768,256]{1,0:T(8,128)(2,1)}, bf16[768,256]{1,0:T(8,128)(2,1)}, u32[]{:S(2)}, u32[]{:S(2)}) collective-permute-start(bf16[768,256]{1,0:T(8,128)(2,1)} %param.14), channel_id=1, source_target_pairs={{4,8},{8,4},{5,9},{9,5},{6,10},{10,6},{7,11},{11,7},{20,24},{24,20... | collective-permute-start | bytes 1179656 | tf_op jit(solution)/shard_map/ppermute | solution.py:39
  16.1 20.1 %collective-permute-start.1 = (bf16[768,256]{1,0:T(8,128)(2,1)}, bf16[768,256]{1,0:T(8,128)(2,1)}, u32[]{:S(2)}, u32[]{:S(2)}) collective-permute-start(bf16[768,256]{1,0:T(8,128)(2,1)} %param.25), channel_id=1, source_target_pairs={{4,8},{8,4},{5,9},{9,5},{6,10},{10,6},{7,11},{11,7},{20,24},{24,20... | collective-permute-start | bytes 1179656 | tf_op jit(solution)/shard_map/ppermute | solution.py:39
  25.1 12.8 %collective-permute-start.4 = (bf16[528,512]{1,0:T(8,128)(2,1)}, bf16[528,512]{1,0:T(8,128)(2,1)S(1)}, u32[]{:S(2)}, u32[]{:S(2)}) collective-permute-start(bf16[528,512]{1,0:T(8,128)(2,1)} %lay_out_y.1.refs_4_), channel_id=1, source_target_pairs={{0,32},{32,64},{64,96},{96,0},{1,33},{33,65},{65,97},{97,1},{2,34}... | collective-permute-start | bytes 1622024 | tf_op jit(solution)/shard_map/ppermute | solution.py:48
  26.5 11.6 %collective-permute-start.3 = (bf16[528,512]{1,0:T(8,128)(2,1)}, bf16[528,512]{1,0:T(8,128)(2,1)S(1)}, u32[]{:S(2)}, u32[]{:S(2)}) collective-permute-start(bf16[528,512]{1,0:T(8,128)(2,1)} %lay_out_y.1.refs_4_), channel_id=1, source_target_pairs={{0,96},{32,0},{64,32},{96,64},{1,97},{33,1},{65,33},{97,65},{2,98}... | collective-permute-start | bytes 1622024 | tf_op jit(solution)/shard_map/ppermute | solution.py:48
  30.8 14.4 %collective-permute-start.6 = (bf16[528,512]{1,0:T(8,128)(2,1)}, bf16[528,512]{1,0:T(8,128)(2,1)S(1)}, u32[]{:S(2)}, u32[]{:S(2)}) collective-permute-start(bf16[528,512]{1,0:T(8,128)(2,1)} %lay_out_x.1), channel_id=1, source_target_pairs={{0,20},{4,28},{8,16},{12,24},{16,4},{20,12},{24,0},{28,8},{1,21},{... | collective-permute-start | bytes 1622024 | tf_op jit(solution)/shard_map/ppermute | solution.py:78
  30.9 15.5 %collective-permute-start.5 = (bf16[528,512]{1,0:T(8,128)(2,1)}, bf16[528,512]{1,0:T(8,128)(2,1)S(1)}, u32[]{:S(2)}, u32[]{:S(2)}) collective-permute-start(bf16[528,512]{1,0:T(8,128)(2,1)} %lay_out_x.1), channel_id=1, source_target_pairs={{0,16},{4,24},{8,20},{12,28},{16,0},{20,8},{24,4},{28,12},{1,17},{... | collective-permute-start | bytes 1622024 | tf_op jit(solution)/shard_map/ppermute | solution.py:78
  46.4 83.0 %all-gather.7.cloned.1.call-start = ((), (), s32[]{:S(2)}) async-start(), calls=%async_computation.5 | async-start | bytes 3538944 | tf_op jit(solution)/shard_map/all_gather | solution.py:109
  46.5 14.4 %collective-permute-start.7 = (bf16[528,512]{1,0:T(8,128)(2,1)}, bf16[528,512]{1,0:T(8,128)(2,1)S(1)}, u32[]{:S(2)}, u32[]{:S(2)}) collective-permute-start(bf16[528,512]{1,0:T(8,128)(2,1)} %lay_out_x.1), channel_id=1, source_target_pairs={{4,8},{8,4},{20,24},{24,20},{5,9},{9,5},{21,25},{25,21},{6,10},{10... | collective-permute-start | bytes 1622024 | tf_op jit(solution)/shard_map/ppermute | solution.py:78
  51.4 12.6 %collective-permute-start.9 = (bf16[528,512]{1,0:T(8,128)(2,1)S(1)}, bf16[528,512]{1,0:T(8,128)(2,1)S(1)}, u32[]{:S(2)}, u32[]{:S(2)}) collective-permute-start(bf16[528,512]{1,0:T(8,128)(2,1)S(1)} %copy-done), channel_id=1, source_target_pairs={{0,64},{32,96},{64,0},{96,32},{1,65},{33,97},{65,1},{97,33},{2,66}... | collective-permute-start | bytes 1622024 | tf_op jit(solution)/shard_map/ppermute | solution.py:48
  53.2 11.5 %collective-permute-start.8 = (bf16[528,512]{1,0:T(8,128)(2,1)}, bf16[528,512]{1,0:T(8,128)(2,1)S(1)}, u32[]{:S(2)}, u32[]{:S(2)}) collective-permute-start(bf16[528,512]{1,0:T(8,128)(2,1)} %lay_out_x.1), channel_id=1, source_target_pairs={{0,4},{4,12},{8,0},{12,8},{16,20},{20,28},{24,16},{28,24},{1,5},{5... | collective-permute-start | bytes 1622024 | tf_op jit(solution)/shard_map/ppermute | solution.py:78
  68.8 99.3 %reduce-scatter.5.cloned.1.call-start = ((), (), s32[]{:S(2)}) async-start(), calls=%async_computation.6 | async-start | bytes 1966080 | tf_op jit(solution)/shard_map/reduce_scatter | solution.py:114
  68.9 18.6 %collective-permute-start.13 = (bf16[576,512]{1,0:T(8,128)(2,1)}, bf16[576,512]{1,0:T(8,128)(2,1)S(1)}, u32[]{:S(2)}, u32[]{:S(2)}) collective-permute-start(bf16[576,512]{1,0:T(8,128)(2,1)} %get-tuple-element.293), channel_id=1, source_target_pairs={{0,20},{4,28},{8,16},{12,24},{16,4},{20,12},{24,0},{28,8},{1,21},{... | collective-permute-start | bytes 1769480 | tf_op jit(solution)/shard_map/ppermute | solution.py:78
  69.7 17.8 %collective-permute-start.12 = (bf16[576,512]{1,0:T(8,128)(2,1)}, bf16[576,512]{1,0:T(8,128)(2,1)S(1)}, u32[]{:S(2)}, u32[]{:S(2)}) collective-permute-start(bf16[576,512]{1,0:T(8,128)(2,1)} %get-tuple-element.293), channel_id=1, source_target_pairs={{0,16},{4,24},{8,20},{12,28},{16,0},{20,8},{24,4},{28,12},{1,17},{... | collective-permute-start | bytes 1769480 | tf_op jit(solution)/shard_map/ppermute | solution.py:78
  72.8 14.6 %collective-permute-start.11 = (bf16[512,512]{1,0:T(8,128)(2,1)}, bf16[512,512]{1,0:T(8,128)(2,1)S(1)}, u32[]{:S(2)}, u32[]{:S(2)}) collective-permute-start(bf16[512,512]{1,0:T(8,128)(2,1)} %get-tuple-element.305.refs_5_.refs_11_), channel_id=1, source_target_pairs={{0,32},{32,64},{64,96},{96,0},{1,33},{33,65},{65,97},{97,1},{2,34}... | collective-permute-start | bytes 1572872 | tf_op jit(solution)/shard_map/ppermute | solution.py:48
  72.9 14.6 %collective-permute-start.10 = (bf16[512,512]{1,0:T(8,128)(2,1)}, bf16[512,512]{1,0:T(8,128)(2,1)S(1)}, u32[]{:S(2)}, u32[]{:S(2)}) collective-permute-start(bf16[512,512]{1,0:T(8,128)(2,1)} %get-tuple-element.305.refs_5_.refs_11_), channel_id=1, source_target_pairs={{0,96},{32,0},{64,32},{96,64},{1,97},{33,1},{65,33},{97,65},{2,98}... | collective-permute-start | bytes 1572872 | tf_op jit(solution)/shard_map/ppermute | solution.py:48
  87.5 18.6 %collective-permute-start.15 = (bf16[576,512]{1,0:T(8,128)(2,1)}, bf16[576,512]{1,0:T(8,128)(2,1)S(1)}, u32[]{:S(2)}, u32[]{:S(2)}) collective-permute-start(bf16[576,512]{1,0:T(8,128)(2,1)} %get-tuple-element.293), channel_id=1, source_target_pairs={{4,8},{8,4},{20,24},{24,20},{5,9},{9,5},{21,25},{25,21},{6,10},{10... | collective-permute-start | bytes 1769480 | tf_op jit(solution)/shard_map/ppermute | solution.py:78
  90.8 16.2 %collective-permute-start.16 = (bf16[576,512]{1,0:T(8,128)(2,1)}, bf16[576,512]{1,0:T(8,128)(2,1)S(1)}, u32[]{:S(2)}, u32[]{:S(2)}) collective-permute-start(bf16[576,512]{1,0:T(8,128)(2,1)} %get-tuple-element.293), channel_id=1, source_target_pairs={{0,4},{4,12},{8,0},{12,8},{16,20},{20,28},{24,16},{28,24},{1,5},{5... | collective-permute-start | bytes 1769480 | tf_op jit(solution)/shard_map/ppermute | solution.py:78
  90.9 16.1 %collective-permute-start.14 = (bf16[512,512]{1,0:T(8,128)(2,1)}, bf16[512,512]{1,0:T(8,128)(2,1)S(1)}, u32[]{:S(2)}, u32[]{:S(2)}) collective-permute-start(bf16[512,512]{1,0:T(8,128)(2,1)} %get-tuple-element.305.refs_5_.refs_11_), channel_id=1, source_target_pairs={{0,64},{32,96},{64,0},{96,32},{1,65},{33,97},{65,1},{97,33},{2,66}... | collective-permute-start | bytes 1572872 | tf_op jit(solution)/shard_map/ppermute | solution.py:48
  107.1 26.3 %collective-permute-start.18 = (bf16[512,1024]{1,0:T(8,128)(2,1)}, bf16[512,1024]{1,0:T(8,128)(2,1)S(1)}, u32[]{:S(2)}, u32[]{:S(2)}) collective-permute-start(bf16[512,1024]{1,0:T(8,128)(2,1)} %get-tuple-element.336.refs_3_), channel_id=1, source_target_pairs={{0,32},{32,64},{64,96},{96,0},{1,33},{33,65},{65,97},{97,1},{2,34}... | collective-permute-start | bytes 3145736 | tf_op jit(solution)/shard_map/ppermute | solution.py:48
  107.2 26.2 %collective-permute-start.17 = (bf16[512,1024]{1,0:T(8,128)(2,1)}, bf16[512,1024]{1,0:T(8,128)(2,1)S(1)}, u32[]{:S(2)}, u32[]{:S(2)}) collective-permute-start(bf16[512,1024]{1,0:T(8,128)(2,1)} %get-tuple-element.336.refs_3_), channel_id=1, source_target_pairs={{0,96},{32,0},{64,32},{96,64},{1,97},{33,1},{65,33},{97,65},{2,98}... | collective-permute-start | bytes 3145736 | tf_op jit(solution)/shard_map/ppermute | solution.py:48
  109.8 24.1 %collective-permute-start.20 = (bf16[512,1024]{1,0:T(8,128)(2,1)}, bf16[512,1024]{1,0:T(8,128)(2,1)}, u32[]{:S(2)}, u32[]{:S(2)}) collective-permute-start(bf16[512,1024]{1,0:T(8,128)(2,1)} %get-tuple-element.349.refs_20_), channel_id=1, source_target_pairs={{0,20},{4,28},{8,16},{12,24},{16,4},{20,12},{24,0},{28,8},{1,21},{... | collective-permute-start | bytes 3145736 | tf_op jit(solution)/shard_map/ppermute | solution.py:78
  112.2 24.0 %collective-permute-start.19 = (bf16[512,1024]{1,0:T(8,128)(2,1)}, bf16[512,1024]{1,0:T(8,128)(2,1)}, u32[]{:S(2)}, u32[]{:S(2)}) collective-permute-start(bf16[512,1024]{1,0:T(8,128)(2,1)} %get-tuple-element.349.refs_20_), channel_id=1, source_target_pairs={{0,16},{4,24},{8,20},{12,28},{16,0},{20,8},{24,4},{28,12},{1,17},{... | collective-permute-start | bytes 3145736 | tf_op jit(solution)/shard_map/ppermute | solution.py:78
  143.1 62.6 %all-gather.9.cloned.1.call-start = ((), (), s32[]{:S(2)}) async-start(), calls=%async_computation.7 | async-start | bytes 3538944 | tf_op jit(solution)/shard_map/all_gather | solution.py:109
  143.2 14.5 %collective-permute-start.23 = (bf16[256,1024]{1,0:T(8,128)(2,1)S(1)}, bf16[256,1024]{1,0:T(8,128)(2,1)S(1)}, u32[]{:S(2)}, u32[]{:S(2)}) collective-permute-start(bf16[256,1024]{1,0:T(8,128)(2,1)S(1)} %slice.83), channel_id=1, source_target_pairs={{0,32},{32,64},{64,96},{96,0},{1,33},{33,65},{65,97},{97,1},{2,34}... | collective-permute-start | bytes 1572872 | tf_op jit(solution)/shard_map/ppermute | solution.py:48
  143.2 31.3 %collective-permute-start.25 = (bf16[512,1024]{1,0:T(8,128)(2,1)}, bf16[512,1024]{1,0:T(8,128)(2,1)S(1)}, u32[]{:S(2)}, u32[]{:S(2)}) collective-permute-start(bf16[512,1024]{1,0:T(8,128)(2,1)} %get-tuple-element.349.refs_20_), channel_id=1, source_target_pairs={{0,4},{4,12},{8,0},{12,8},{16,20},{20,28},{24,16},{28,24},{1,5},{5... | collective-permute-start | bytes 3145736 | tf_op jit(solution)/shard_map/ppermute | solution.py:78
  143.7 30.8 %collective-permute-start.24 = (bf16[512,1024]{1,0:T(8,128)(2,1)}, bf16[512,1024]{1,0:T(8,128)(2,1)}, u32[]{:S(2)}, u32[]{:S(2)}) collective-permute-start(bf16[512,1024]{1,0:T(8,128)(2,1)} %get-tuple-element.349.refs_20_), channel_id=1, source_target_pairs={{4,8},{8,4},{20,24},{24,20},{5,9},{9,5},{21,25},{25,21},{6,10},{10... | collective-permute-start | bytes 3145736 | tf_op jit(solution)/shard_map/ppermute | solution.py:78
  149.2 20.1 %collective-permute-start.22 = (bf16[256,1024]{1,0:T(8,128)(2,1)S(1)}, bf16[256,1024]{1,0:T(8,128)(2,1)}, u32[]{:S(2)}, u32[]{:S(2)}) collective-permute-start(bf16[256,1024]{1,0:T(8,128)(2,1)S(1)} %slice.82), channel_id=1, source_target_pairs={{0,96},{32,0},{64,32},{96,64},{1,97},{33,1},{65,33},{97,65},{2,98}... | collective-permute-start | bytes 1572872 | tf_op jit(solution)/shard_map/ppermute | solution.py:48
  152.0 17.3 %collective-permute-start.27 = (bf16[512,512]{1,0:T(8,128)(2,1)}, bf16[512,512]{1,0:T(8,128)(2,1)}, u32[]{:S(2)}, u32[]{:S(2)}) collective-permute-start(bf16[512,512]{1,0:T(8,128)(2,1)} %get-tuple-element.341.refs_8_.refs_0_), channel_id=1, source_target_pairs={{0,32},{32,64},{64,96},{96,0},{1,33},{33,65},{65,97},{97,1},{2,34}... | collective-permute-start | bytes 1572872 | tf_op jit(solution)/shard_map/ppermute | solution.py:48
  158.5 16.0 %collective-permute-start.26 = (bf16[512,512]{1,0:T(8,128)(2,1)}, bf16[512,512]{1,0:T(8,128)(2,1)}, u32[]{:S(2)}, u32[]{:S(2)}) collective-permute-start(bf16[512,512]{1,0:T(8,128)(2,1)} %get-tuple-element.341.refs_8_.refs_0_), channel_id=1, source_target_pairs={{0,96},{32,0},{64,32},{96,64},{1,97},{33,1},{65,33},{97,65},{2,98}... | collective-permute-start | bytes 1572872 | tf_op jit(solution)/shard_map/ppermute | solution.py:48
  175.7 97.3 %reduce-scatter.7.cloned.1.call-start = ((), (), s32[]{:S(2)}) async-start(), calls=%async_computation.8 | async-start | bytes 1966080 | tf_op jit(solution)/shard_map/reduce_scatter | solution.py:834
  175.7 14.3 %collective-permute-start.28 = (bf16[512,512]{1,0:T(8,128)(2,1)}, bf16[512,512]{1,0:T(8,128)(2,1)S(1)}, u32[]{:S(2)}, u32[]{:S(2)}) collective-permute-start(bf16[512,512]{1,0:T(8,128)(2,1)} %get-tuple-element.341.refs_8_.refs_0_), channel_id=1, source_target_pairs={{0,64},{32,96},{64,0},{96,32},{1,65},{33,97},{65,1},{97,33},{2,66}... | collective-permute-start | bytes 1572872 | tf_op jit(solution)/shard_map/ppermute | solution.py:48
  177.9 13.6 %collective-permute-start.32 = (bf16[512,512]{1,0:T(8,128)(2,1)S(1)}, bf16[512,512]{1,0:T(8,128)(2,1)S(1)}, u32[]{:S(2)}, u32[]{:S(2)}) collective-permute-start(bf16[512,512]{1,0:T(8,128)(2,1)S(1)} %copy-done.54), channel_id=1, source_target_pairs={{0,20},{4,28},{8,16},{12,24},{16,4},{20,12},{24,0},{28,8},{1,21},{... | collective-permute-start | bytes 1572872 | tf_op jit(solution)/shard_map/ppermute | solution.py:78
  180.3 23.7 %collective-permute-start.31 = (bf16[512,512]{1,0:T(8,128)(2,1)S(1)}, bf16[512,512]{1,0:T(8,128)(2,1)S(1)}, u32[]{:S(2)}, u32[]{:S(2)}) collective-permute-start(bf16[512,512]{1,0:T(8,128)(2,1)S(1)} %copy-done.54), channel_id=1, source_target_pairs={{0,16},{4,24},{8,20},{12,28},{16,0},{20,8},{24,4},{28,12},{1,17},{... | collective-permute-start | bytes 1572872 | tf_op jit(solution)/shard_map/ppermute | solution.py:78
  180.3 23.7 %collective-permute-start.30 = (bf16[512,512]{1,0:T(8,128)(2,1)S(1)}, bf16[512,512]{1,0:T(8,128)(2,1)S(1)}, u32[]{:S(2)}, u32[]{:S(2)}) collective-permute-start(bf16[512,512]{1,0:T(8,128)(2,1)S(1)} %copy-done.54), channel_id=1, source_target_pairs={{0,4},{4,12},{8,0},{12,8},{16,20},{20,28},{24,16},{28,24},{1,5},{5... | collective-permute-start | bytes 1572872 | tf_op jit(solution)/shard_map/ppermute | solution.py:78
  180.8 24.9 %collective-permute-start.29 = (bf16[512,512]{1,0:T(8,128)(2,1)S(1)}, bf16[512,512]{1,0:T(8,128)(2,1)}, u32[]{:S(2)}, u32[]{:S(2)}) collective-permute-start(bf16[512,512]{1,0:T(8,128)(2,1)S(1)} %copy-done.54), channel_id=1, source_target_pairs={{4,8},{8,4},{20,24},{24,20},{5,9},{9,5},{21,25},{25,21},{6,10},{10... | collective-permute-start | bytes 1572872 | tf_op jit(solution)/shard_map/ppermute | solution.py:78
  243.7 64.4 %all-gather.11.cloned.1.call-start = ((), (), s32[]{:S(2)}) async-start(), calls=%async_computation.9 | async-start | bytes 3538944 | tf_op jit(solution)/shard_map/all_gather | solution.py:109
  245.3 28.7 %collective-permute-start.34 = (bf16[512,1024]{1,0:T(8,128)(2,1)}, bf16[512,1024]{1,0:T(8,128)(2,1)S(1)}, u32[]{:S(2)}, u32[]{:S(2)}) collective-permute-start(bf16[512,1024]{1,0:T(8,128)(2,1)} %get-tuple-element.363), channel_id=1, source_target_pairs={{16,0},{24,4},{20,8},{28,12},{0,16},{8,20},{4,24},{12,28},{17,1},{... | collective-permute-start | bytes 3145736 | tf_op jit(solution)/shard_map/ppermute | solution.py:82
  247.8 26.3 %collective-permute-start.35 = (bf16[512,1024]{1,0:T(8,128)(2,1)}, bf16[512,1024]{1,0:T(8,128)(2,1)S(1)}, u32[]{:S(2)}, u32[]{:S(2)}) collective-permute-start(bf16[512,1024]{1,0:T(8,128)(2,1)} %get-tuple-element.364), channel_id=1, source_target_pairs={{20,0},{28,4},{16,8},{24,12},{4,16},{12,20},{0,24},{8,28},{21,1},{... | collective-permute-start | bytes 3145736 | tf_op jit(solution)/shard_map/ppermute | solution.py:82
  248.2 26.4 %collective-permute-start.36 = (bf16[512,1024]{1,0:T(8,128)(2,1)}, bf16[512,1024]{1,0:T(8,128)(2,1)}, u32[]{:S(2)}, u32[]{:S(2)}) collective-permute-start(bf16[512,1024]{1,0:T(8,128)(2,1)} %get-tuple-element.365), channel_id=1, source_target_pairs={{0,32},{32,64},{64,96},{96,0},{1,33},{33,65},{65,97},{97,1},{2,34}... | collective-permute-start | bytes 3145736 | tf_op jit(solution)/shard_map/ppermute | solution.py:48
  249.8 24.9 %collective-permute-start.37 = (bf16[512,1024]{1,0:T(8,128)(2,1)}, bf16[512,1024]{1,0:T(8,128)(2,1)}, u32[]{:S(2)}, u32[]{:S(2)}) collective-permute-start(bf16[512,1024]{1,0:T(8,128)(2,1)} %get-tuple-element.366), channel_id=1, source_target_pairs={{0,96},{32,0},{64,32},{96,64},{1,97},{33,1},{65,33},{97,65},{2,98}... | collective-permute-start | bytes 3145736 | tf_op jit(solution)/shard_map/ppermute | solution.py:48
  277.6 123.3 %reduce-scatter.9.cloned.1.call-start = ((), (), s32[]{:S(2)}) async-start(), calls=%async_computation.10 | async-start | bytes 1966080 | tf_op jit(solution)/shard_map/reduce_scatter | solution.py:933
  278.6 26.4 %collective-permute-start.39 = (bf16[512,1024]{1,0:T(8,128)(2,1)}, bf16[512,1024]{1,0:T(8,128)(2,1)S(1)}, u32[]{:S(2)}, u32[]{:S(2)}) collective-permute-start(bf16[512,1024]{1,0:T(8,128)(2,1)} %get-tuple-element.382), channel_id=1, source_target_pairs={{0,64},{32,96},{64,0},{96,32},{1,65},{33,97},{65,1},{97,33},{2,66}... | collective-permute-start | bytes 3145736 | tf_op jit(solution)/shard_map/ppermute | solution.py:48
  280.7 24.4 %collective-permute-start.41 = (bf16[512,1024]{1,0:T(8,128)(2,1)}, bf16[512,1024]{1,0:T(8,128)(2,1)}, u32[]{:S(2)}, u32[]{:S(2)}) collective-permute-start(bf16[512,1024]{1,0:T(8,128)(2,1)} %get-tuple-element.386), channel_id=1, source_target_pairs={{4,0},{12,4},{0,8},{8,12},{20,16},{28,20},{16,24},{24,28},{5,1},{1... | collective-permute-start | bytes 3145736 | tf_op jit(solution)/shard_map/ppermute | solution.py:82
  281.8 26.4 %collective-permute-start.40 = (bf16[512,1024]{1,0:T(8,128)(2,1)}, bf16[512,1024]{1,0:T(8,128)(2,1)}, u32[]{:S(2)}, u32[]{:S(2)}) collective-permute-start(bf16[512,1024]{1,0:T(8,128)(2,1)} %get-tuple-element.385.refs_8_), channel_id=1, source_target_pairs={{8,4},{4,8},{24,20},{20,24},{9,5},{5,9},{25,21},{21,25},{10,6},{6,... | collective-permute-start | bytes 3145736 | tf_op jit(solution)/shard_map/ppermute | solution.py:82
  308.2 18.0 %collective-permute-start.42 = (bf16[512,512]{1,0:T(8,128)(2,1)}, bf16[512,512]{1,0:T(8,128)(2,1)S(1)}, u32[]{:S(2)}, u32[]{:S(2)}) collective-permute-start(bf16[512,512]{1,0:T(8,128)(2,1)} %get-tuple-element.409), channel_id=1, source_target_pairs={{0,32},{32,64},{64,96},{96,0},{1,33},{33,65},{65,97},{97,1},{2,34}... | collective-permute-start | bytes 1572872 | tf_op jit(solution)/shard_map/ppermute | solution.py:48
  309.0 17.2 %collective-permute-start.43 = (bf16[512,512]{1,0:T(8,128)(2,1)}, bf16[512,512]{1,0:T(8,128)(2,1)S(1)}, u32[]{:S(2)}, u32[]{:S(2)}) collective-permute-start(bf16[512,512]{1,0:T(8,128)(2,1)} %get-tuple-element.410), channel_id=1, source_target_pairs={{0,96},{32,0},{64,32},{96,64},{1,97},{33,1},{65,33},{97,65},{2,98}... | collective-permute-start | bytes 1572872 | tf_op jit(solution)/shard_map/ppermute | solution.py:48
  310.9 15.4 %collective-permute-start.44 = (bf16[512,512]{1,0:T(8,128)(2,1)}, bf16[512,512]{1,0:T(8,128)(2,1)S(1)}, u32[]{:S(2)}, u32[]{:S(2)}) collective-permute-start(bf16[512,512]{1,0:T(8,128)(2,1)} %get-tuple-element.411), channel_id=1, source_target_pairs={{16,0},{24,4},{20,8},{28,12},{0,16},{8,20},{4,24},{12,28},{17,1},{... | collective-permute-start | bytes 1572872 | tf_op jit(solution)/shard_map/ppermute | solution.py:82
  311.9 14.3 %collective-permute-start.45 = (bf16[512,512]{1,0:T(8,128)(2,1)}, bf16[512,512]{1,0:T(8,128)(2,1)S(1)}, u32[]{:S(2)}, u32[]{:S(2)}) collective-permute-start(bf16[512,512]{1,0:T(8,128)(2,1)} %get-tuple-element.412), channel_id=1, source_target_pairs={{20,0},{28,4},{16,8},{24,12},{4,16},{12,20},{0,24},{8,28},{21,1},{... | collective-permute-start | bytes 1572872 | tf_op jit(solution)/shard_map/ppermute | solution.py:82
  327.1 17.9 %collective-permute-start.46 = (bf16[3072,256]{1,0:T(8,128)(2,1)}, bf16[3072,256]{1,0:T(8,128)(2,1)S(1)}, u32[]{:S(2)}, u32[]{:S(2)}) collective-permute-start(bf16[3072,256]{1,0:T(8,128)(2,1)} %get-tuple-element.414), channel_id=1, source_target_pairs={{0,8},{8,0},{1,9},{9,1},{2,10},{10,2},{3,11},{11,3},{4,12},{12,4},... | collective-permute-start | bytes 4718600 | tf_op jit(solution)/shard_map/ppermute | solution.py:44
  328.0 16.9 %collective-permute-start.47 = (bf16[512,512]{1,0:T(8,128)(2,1)S(1)}, bf16[512,512]{1,0:T(8,128)(2,1)S(1)}, u32[]{:S(2)}, u32[]{:S(2)}) collective-permute-start(bf16[512,512]{1,0:T(8,128)(2,1)S(1)} %copy-done.56), channel_id=1, source_target_pairs={{0,64},{32,96},{64,0},{96,32},{1,65},{33,97},{65,1},{97,33},{2,66}... | collective-permute-start | bytes 1572872 | tf_op jit(solution)/shard_map/ppermute | solution.py:48
  328.9 16.0 %collective-permute-start.49 = (bf16[512,512]{1,0:T(8,128)(2,1)S(1)}, bf16[512,512]{1,0:T(8,128)(2,1)S(1)}, u32[]{:S(2)}, u32[]{:S(2)}) collective-permute-start(bf16[512,512]{1,0:T(8,128)(2,1)S(1)} %copy-done.55), channel_id=1, source_target_pairs={{4,0},{12,4},{0,8},{8,12},{20,16},{28,20},{16,24},{24,28},{5,1},{1... | collective-permute-start | bytes 1572872 | tf_op jit(solution)/shard_map/ppermute | solution.py:82
  330.3 14.8 %collective-permute-start.48 = (bf16[512,512]{1,0:T(8,128)(2,1)S(1)}, bf16[512,512]{1,0:T(8,128)(2,1)S(1)}, u32[]{:S(2)}, u32[]{:S(2)}) collective-permute-start(bf16[512,512]{1,0:T(8,128)(2,1)S(1)} %copy-done.24), channel_id=1, source_target_pairs={{8,4},{4,8},{24,20},{20,24},{9,5},{5,9},{25,21},{21,25},{10,6},{6,... | collective-permute-start | bytes 1572872 | tf_op jit(solution)/shard_map/ppermute | solution.py:82
  347.6 59.8 %reduce-scatter.11.cloned.1.call-start = ((), (), s32[]{:S(2)}) async-start(), calls=%async_computation.11 | async-start | bytes 1966080 | tf_op jit(solution)/shard_map/reduce_scatter | solution.py:965
  353.1 23.2 %collective-permute-start.52 = (bf16[896,512]{1,0:T(8,128)(2,1)}, bf16[896,512]{1,0:T(8,128)(2,1)S(1)}, u32[]{:S(2)}, u32[]{:S(2)}) collective-permute-start(bf16[896,512]{1,0:T(8,128)(2,1)} %get-tuple-element.467), channel_id=1, source_target_pairs={{0,32},{32,64},{64,96},{96,0},{1,33},{33,65},{65,97},{97,1},{2,34}... | collective-permute-start | bytes 2752520 | tf_op jit(solution)/shard_map/ppermute | solution.py:48
  353.5 22.8 %collective-permute-start.53 = (bf16[896,512]{1,0:T(8,128)(2,1)}, bf16[896,512]{1,0:T(8,128)(2,1)S(1)}, u32[]{:S(2)}, u32[]{:S(2)}) collective-permute-start(bf16[896,512]{1,0:T(8,128)(2,1)} %get-tuple-element.468), channel_id=1, source_target_pairs={{0,96},{32,0},{64,32},{96,64},{1,97},{33,1},{65,33},{97,65},{2,98}... | collective-permute-start | bytes 2752520 | tf_op jit(solution)/shard_map/ppermute | solution.py:48
  355.8 20.4 %collective-permute-start.54 = (bf16[896,512]{1,0:T(8,128)(2,1)}, bf16[896,512]{1,0:T(8,128)(2,1)S(1)}, u32[]{:S(2)}, u32[]{:S(2)}) collective-permute-start(bf16[896,512]{1,0:T(8,128)(2,1)} %get-tuple-element.469), channel_id=1, source_target_pairs={{16,0},{24,4},{20,8},{28,12},{0,16},{8,20},{4,24},{12,28},{17,1},{... | collective-permute-start | bytes 2752520 | tf_op jit(solution)/shard_map/ppermute | solution.py:82
  357.8 20.5 %collective-permute-start.55 = (bf16[896,512]{1,0:T(8,128)(2,1)}, bf16[896,512]{1,0:T(8,128)(2,1)}, u32[]{:S(2)}, u32[]{:S(2)}) collective-permute-start(bf16[896,512]{1,0:T(8,128)(2,1)} %get-tuple-element.470), channel_id=1, source_target_pairs={{20,0},{28,4},{16,8},{24,12},{4,16},{12,20},{0,24},{8,28},{21,1},{... | collective-permute-start | bytes 2752520 | tf_op jit(solution)/shard_map/ppermute | solution.py:82
  378.3 23.7 %collective-permute-start.56 = (bf16[896,512]{1,0:T(8,128)(2,1)}, bf16[896,512]{1,0:T(8,128)(2,1)}, u32[]{:S(2)}, u32[]{:S(2)}) collective-permute-start(bf16[896,512]{1,0:T(8,128)(2,1)} %get-tuple-element.471), channel_id=1, source_target_pairs={{0,64},{32,96},{64,0},{96,32},{1,65},{33,97},{65,1},{97,33},{2,66}... | collective-permute-start | bytes 2752520 | tf_op jit(solution)/shard_map/ppermute | solution.py:48
  378.5 23.5 %collective-permute-start.58 = (bf16[896,512]{1,0:T(8,128)(2,1)}, bf16[896,512]{1,0:T(8,128)(2,1)}, u32[]{:S(2)}, u32[]{:S(2)}) collective-permute-start(bf16[896,512]{1,0:T(8,128)(2,1)} %get-tuple-element.475), channel_id=1, source_target_pairs={{4,0},{12,4},{0,8},{8,12},{20,16},{28,20},{16,24},{24,28},{5,1},{1... | collective-permute-start | bytes 2752520 | tf_op jit(solution)/shard_map/ppermute | solution.py:82
  381.4 24.6 %collective-permute-start.57 = (bf16[896,512]{1,0:T(8,128)(2,1)}, bf16[896,512]{1,0:T(8,128)(2,1)}, u32[]{:S(2)}, u32[]{:S(2)}) collective-permute-start(bf16[896,512]{1,0:T(8,128)(2,1)} %get-tuple-element.513.refs_8_), channel_id=1, source_target_pairs={{8,4},{4,8},{24,20},{20,24},{9,5},{5,9},{25,21},{21,25},{10,6},{6,... | collective-permute-start | bytes 2752520 | tf_op jit(solution)/shard_map/ppermute | solution.py:82
  408.7 20.2 %collective-permute-start.62 = (bf16[1536,256]{1,0:T(8,128)(2,1)S(1)}, bf16[1536,256]{1,0:T(8,128)(2,1)S(1)}, u32[]{:S(2)}, u32[]{:S(2)}) collective-permute-start(bf16[1536,256]{1,0:T(8,128)(2,1)S(1)} %pad_maximum_fusion), channel_id=1, source_target_pairs={{4,8},{8,4},{5,9},{9,5},{6,10},{10,6},{7,11},{11,7},{20,24},{24,20... | collective-permute-start | bytes 2359304 | tf_op jit(solution)/shard_map/ppermute | solution.py:39
  415.1 13.7 %collective-permute-start.61 = (bf16[512,256]{1,0:T(8,128)(2,1)}, bf16[512,256]{1,0:T(8,128)(2,1)S(1)}, u32[]{:S(2)}, u32[]{:S(2)}) collective-permute-start(bf16[512,256]{1,0:T(8,128)(2,1)} %get-tuple-element.488), channel_id=1, source_target_pairs={{0,1},{1,0},{2,3},{3,2},{4,5},{5,4},{6,7},{7,6},{8,9},{9,8},{10,11... | collective-permute-start | bytes 786440 | tf_op jit(solution)/shard_map/ppermute | solution.py:60
  (78 other events, 891.0 us)
Sparse Core Ops, SparseCore 0:
  46.5 29.7 all-gather.4
  78.1 27.8 all-gather.6
  143.2 24.9 reduce-scatter.4
  175.8 29.8 all-gather.8
  243.9 25.2 reduce-scatter.6
  277.8 28.2 all-gather.10
  347.7 23.2 reduce-scatter.8
  373.4 26.4 reduce-scatter.10

commit v7 on v5

--- a/solution.py
+++ b/solution.py
@@ -973,7 +973,6 @@
         db_cols.astype(f32) + r1 * attn_grad * gain_cols - x_own.astype(f32) * r1**2 * (row_sum / WIDTH)
     )
     home = [(h_cols.astype(f32) + ffn_own).astype(bf16), grad_inputs.astype(bf16)]
-    home = swap(jnp.concatenate(home, 0))
     *sum_b, kv_give, kv_keep = call(
         join_body,
         "join_sums",
@@ -983,6 +982,7 @@
         0,
         anywhere=9,
     )
+    home = swap(after(jnp.concatenate(home, 0), kv_give))
     kv_sum = (kv_keep + kv_partner(kv_give).astype(f32)).astype(bf16)
     sum_b = [sum_b[0]] + [shift(sum_b[i], Y, i) for i in (1, 2, 3)]
     first_y = sum_b[1]

time: 455 us -> 455 us (level)
  transfers between devices with their start and end apart: 78 -> 78, of which waited for: 35 -> 35; matrix products, arithmetic and copies ran while one was open for 4% -> 4% of each run, Pallas kernels for 20% -> 19%
where the time goes in v7:
time: 455 us; the launch traced here: 448 us
  waiting for transfers between devices  157 us (35%)
  Pallas kernels  125 us (27%)
  starting transfers between devices  107 us (24%)
  other arithmetic  29.6 us (7%)
  between operations  15.7 us (3%)
  local copies, waits for them, and re-layouts  12.7 us (3%)
    pallas_call x15, Pallas kernels, call(): pl.pallas_call(body, name=name, out_shape=[jax.ShapeDtypeStruct(s, d) for...  125 us
    ppermute x25, waiting for transfers between devices, shift(): return lax.ppermute(a, axis, [(i, (i + by) % 4) for i in range(4)])  71.5 us
    ppermute x16, waiting for transfers between devices, x_in(): return lax.ppermute(a, (XLO, CORE, XHI), x_pairs(flip_lo, flip_core, False))  43.3 us
    ppermute x16, starting transfers between devices, x_out(): return lax.ppermute(a, (XLO, CORE, XHI), x_pairs(flip_lo, flip_core, True))  34.8 us
    ppermute x25, starting transfers between devices, shift(): return lax.ppermute(a, axis, [(i, (i + by) % 4) for i in range(4)])  32.6 us
    ppermute x16, starting transfers between devices, x_in(): return lax.ppermute(a, (XLO, CORE, XHI), x_pairs(flip_lo, flip_core, False))  22.4 us
    ppermute x16, waiting for transfers between devices, x_out(): return lax.ppermute(a, (XLO, CORE, XHI), x_pairs(flip_lo, flip_core, True))  12.3 us
  transfers between devices with their start and end apart: 78, of which 35 were waited for; matrix products, arithmetic and copies ran while one was open for 4% of the time, Pallas kernels for 19%

profile of v7, /device:TPU:1, one launch (start us, length us, event | category | flops | bytes accessed | tf_op | source)
XLA Modules:
  0.0 447.6 jit_solution(6982807227052925621)
XLA Ops:
  10.4 3.3 lay_out_y.1
  13.7 6.2 %collective-permute-start = (bf16[1552,256]{1,0:T(8,128)(2,1)}, bf16[1552,256]{1,0:T(8,128)(2,1)S(1)}, u32[]{:S(2)}, u32[]{:S(2)}) collective-permute-start(bf16[1552,256]{1,0:T(8,128)(2,1)} %get-tuple-element.273), channel_id=1, source_target_pairs={{4,8},{8,4},{5,9},{9,5},{6,10},{10,6},{7,11},{11,7},{20,24},{24,20... | collective-permute-start | bytes 2383880 | tf_op jit(solution)/shard_map/ppermute | solution.py:39
  25.8 2.7 lay_out_x.1
  30.2 4.6 %collective-permute-done.3.refs_7_ = bf16[528,512]{1,0:T(8,128)(2,1)S(1)} collective-permute-done((bf16[528,512]{1,0:T(8,128)(2,1)}, bf16[528,512]{1,0:T(8,128)(2,1)S(1)}, u32[]{:S(2)}, u32[]{:S(2)}) %collective-permute-start.3) | collective-permute-done | bytes 540704 | tf_op jit(solution)/shard_map/ppermute | solution.py:48
  35.5 7.6 %collective-permute-done.5.refs_3_ = bf16[512,512]{1,0:T(8,128)(2,1)} collective-permute-done((bf16[512,512]{1,0:T(8,128)(2,1)}, bf16[512,512]{1,0:T(8,128)(2,1)}, u32[]{:S(2)}, u32[]{:S(2)}) %collective-permute-start.5) | collective-permute-done | bytes 524320 | tf_op jit(solution)/shard_map/ppermute | solution.py:78
  44.8 2.6 collective-permute-start.6
  47.4 3.0 collective-permute-start.8
  50.4 9.0 %collective-permute-done.6 = bf16[512,512]{1,0:T(8,128)(2,1)S(1)} collective-permute-done((bf16[512,512]{1,0:T(8,128)(2,1)}, bf16[512,512]{1,0:T(8,128)(2,1)S(1)}, u32[]{:S(2)}, u32[]{:S(2)}) %collective-permute-start.6) | collective-permute-done | bytes 524320 | tf_op jit(solution)/shard_map/ppermute | solution.py:78
  60.3 2.4 collective-permute-done.7.refs_1_
  64.3 3.0 pack.1
  67.5 2.1 collective-permute-start.11
  69.9 2.3 collective-permute-start.9
  72.3 11.9 %collective-permute-done.10.refs_8_.refs_14_ = bf16[512,512]{1,0:T(8,128)(2,1)S(1)} collective-permute-done((bf16[512,512]{1,0:T(8,128)(2,1)}, bf16[512,512]{1,0:T(8,128)(2,1)S(1)}, u32[]{:S(2)}, u32[]{:S(2)}) %collective-permute-start.10) | collective-permute-done | bytes 524320 | tf_op jit(solution)/shard_map/ppermute | solution.py:48
  84.2 2.3 collective-permute-start.14
  87.0 2.8 collective-permute-start.13
  89.8 2.5 multiply_sine_fusion
  92.3 4.7 %riders.1 = (bf16[512,1024]{1,0:T(8,128)(2,1)}, bf16[512,1024]{1,0:T(8,128)(2,1)}, bf16[512,512]{1,0:T(8,128)(2,1)}, bf16[512,512]{1,0:T(8,128)(2,1)}) custom-call(s32[5]{0:T(128)} %stack.74.at, bf16[512,512]{1,0:T(8,128)(2,1)} %broadcast_select_fusion.3.refs_0_, bf16[512,512]{1,0:T(8,128)(2,1)} %copy-done.7, ...), custom_call_target="tpu_custom_call" | custom-call | bytes 7405568 | tf_op jit(solution)/shard_map/riders/pallas_call | solution.py:155
  97.0 6.2 %collective-permute-done.14 = bf16[576,512]{1,0:T(8,128)(2,1)S(1)} collective-permute-done((bf16[576,512]{1,0:T(8,128)(2,1)}, bf16[576,512]{1,0:T(8,128)(2,1)S(1)}, u32[]{:S(2)}, u32[]{:S(2)}) %collective-permute-start.14) | collective-permute-done | bytes 589856 | tf_op jit(solution)/shard_map/ppermute | solution.py:78
  104.2 2.7 collective-permute-start.16
  106.8 2.2 collective-permute-start.19
  110.4 15.6 %attention_forward.1 = (bf16[768,2048]{1,0:T(8,128)(2,1)}, f32[768,1]{1,0:T(8,128)}, bf16[96,2048]{1,0:T(8,128)(2,1)}, bf16[768,256]{1,0:T(8,128)(2,1)}, bf16[76...) custom-call(s32[5]{0:T(128)} %stack.74.at, ...), custom_call_target="tpu_custom_call" | custom-call | flops 3221225472 | bytes 16728064 | tf_op jit(solution)/shard_map/attention_forward/pallas_call | solution.py:155
  126.1 4.0 collective-permute-done.17.refs_7_
  133.3 3.6 collective-permute-done.20
  136.9 3.0 add_convert_fusion.3
  140.4 4.1 collective-permute-start.23
  145.6 2.8 collective-permute-start.21
  148.4 6.5 %collective-permute-done.22.refs_6_ = bf16[256,1024]{1,0:T(8,128)(2,1)S(1)} collective-permute-done((bf16[256,1024]{1,0:T(8,128)(2,1)S(1)}, bf16[256,1024]{1,0:T(8,128)(2,1)S(1)}, u32[]{:S(2)}, u32[]{:S(2)}) %collective-permute-start.22) | collective-permute-done | bytes 524320 | tf_op jit(solution)/shard_map/ppermute | solution.py:48
  155.6 4.5 %order_upstream.1.refs_2_.dy = bf16[768,2048]{1,0:T(8,128)(2,1)} custom-call(s32[5]{0:T(128)} %stack.74.at, bf16[6144,256]{1,0:T(8,128)(2,1)} %all-gather.7.cloned.1.call-done.whole), custom_call_target="tpu_custom_call" | custom-call | bytes 6291456 | tf_op jit(solution)/shard_map/order_upstream/pallas_call | solution.py:155
  160.2 5.0 %reduce-scatter.5.cloned.1.call-done = bf16[96,2048]{1,0:T(8,128)(2,1)} async-done(((bf16[384,2048]{1,0:T(8,128)(2,1)}), bf16[96,2048]{1,0:T(8,128)(2,1)}) %reduce-scatter.5.cloned.1.call-update) | async-done | bytes 393232 | tf_op jit(solution)/shard_map/reduce_scatter | solution.py:114
  166.3 4.6 %collective-permute-done.25.refs_9_.refs_1_ = bf16[512,512]{1,0:T(8,128)(2,1)} collective-permute-done((bf16[512,512]{1,0:T(8,128)(2,1)}, bf16[512,512]{1,0:T(8,128)(2,1)}, u32[]{:S(2)}, u32[]{:S(2)}) %collective-permute-start.25) | collective-permute-done | bytes 524320 | tf_op jit(solution)/shard_map/ppermute | solution.py:48
  172.9 2.2 collective-permute-start.27
  175.2 2.5 collective-permute-start.31
  178.1 3.9 collective-permute-start.28
  182.0 5.2 %collective-permute-done.27.refs_10_.refs_2_ = bf16[512,512]{1,0:T(8,128)(2,1)S(1)} collective-permute-done((bf16[512,512]{1,0:T(8,128)(2,1)}, bf16[512,512]{1,0:T(8,128)(2,1)S(1)}, u32[]{:S(2)}, u32[]{:S(2)}) %collective-permute-start.27) | collective-permute-done | bytes 524320 | tf_op jit(solution)/shard_map/ppermute | solution.py:48
  189.1 12.3 %collective-permute-done.30.refs_18_.refs_6_ = bf16[512,512]{1,0:T(8,128)(2,1)S(1)} collective-permute-done((bf16[512,512]{1,0:T(8,128)(2,1)}, bf16[512,512]{1,0:T(8,128)(2,1)S(1)}, u32[]{:S(2)}, u32[]{:S(2)}) %collective-permute-start.30) | collective-permute-done | bytes 524320 | tf_op jit(solution)/shard_map/ppermute | solution.py:78
  202.8 31.0 %feed_forward.1 = (bf16[768,256]{1,0:T(8,128)(2,1)}, bf16[768,2048]{1,0:T(8,128)(2,1)}, bf16[768,1024]{1,0:T(8,128)(2,1)}, bf16[768,1024]{1,0:T(8,128)(2,1)}, bf...) custom-call(s32[5]{0:T(128)} %stack.74.at, ...), custom_call_target="tpu_custom_call" | custom-call | flops 22548578304 | bytes 36110336 | tf_op jit(solution)/shard_map/feed_forward/pallas_call | solution.py:155
  234.2 3.3 collective-permute-done.32
  237.5 3.1 add_convert_fusion.2
  242.2 2.5 collective-permute-start.33
  248.6 13.1 %weight_rest.1 = (bf16[512,1024]{1,0:T(8,128)(2,1)}, bf16[512,1024]{1,0:T(8,128)(2,1)}, bf16[512,1024]{1,0:T(8,128)(2,1)}, bf16[512,1024]{1,0:T(8,128)(2,1)}, bf...) custom-call(s32[5]{0:T(128)} %stack.74.at, ...), custom_call_target="tpu_custom_call" | custom-call | flops 6442450944 | bytes 19398656 | tf_op jit(solution)/shard_map/weight_rest/pallas_call | solution.py:155
  261.8 8.7 %feed_forward_out.1 = (bf16[3072,256]{1,0:T(8,128)(2,1)}, bf16[3072,256]{1,0:T(8,128)(2,1)}) custom-call(s32[5]{0:T(128)} %stack.74.at, bf16[768,1024]{1,0:T(8,128)(2,1)} %get-tuple-element.361.hid, bf16[512,512]{1,0:T(8,128)(2,1)} %get-tuple-element.342.refs_8_.refs_0_, bf16[512,512]{1,0:T(8,128)(2,1)} %collective-permute-done.25.refs_9_.refs_1_, ...), custom_call_target="tpu_custom_call" | custom-call | flops 3221225472 | bytes 9437184 | tf_op jit(solution)/shard_map/feed_forward_out/pallas_call | solution.py:155
  273.0 2.3 subtract_convert_fusion.1
  279.4 4.3 collective-permute-start.39
  285.4 17.3 %collective-permute-done.38.refs_1_ = bf16[512,1024]{1,0:T(8,128)(2,1)S(1)} collective-permute-done((bf16[512,1024]{1,0:T(8,128)(2,1)}, bf16[512,1024]{1,0:T(8,128)(2,1)S(1)}, u32[]{:S(2)}, u32[]{:S(2)}) %collective-permute-start.38) | collective-permute-done | bytes 1048608 | tf_op jit(solution)/shard_map/ppermute | solution.py:48
  302.7 3.1 collective-permute-done.39.refs_4_
  309.6 14.0 %attention_backward.1 = (bf16[768,256]{1,0:T(8,128)(2,1)}, bf16[768,768]{1,0:T(8,128)(2,1)}, f32[768,1]{1,0:T(8,128)}, f32[1,2048]{1,0:T(1,128)}, bf16[3072,256]{1,0:T(8,128)(2,1)}, /*index=5*/bf16[3072,256]{1,0:T(8,128)(2,1)}) custom-call(s32[5]{0:T(128)} %stack.74.at, bf16[768,2048]{1,0:T(8,128)(2,1)} %all-gather.11.cloned.1.call-done.refs_0_.db, ...), custom_call_target="tpu_custom_call" | custom-call | flops 3221225472 | bytes 17518592 | tf_op jit(solution)/shard_map/attention_backward/pallas_call | solution.py:155
  328.1 3.7 collective-permute-start.47
  331.8 10.4 %attention_weights.1 = (bf16[896,512]{1,0:T(8,128)(2,1)}, bf16[896,512]{1,0:T(8,128)(2,1)}, bf16[896,512]{1,0:T(8,128)(2,1)}, bf16[896,512]{1,0:T(8,128)(2,1)}, ...) custom-call(s32[5]{0:T(128)} %stack.74.at, ...), custom_call_target="tpu_custom_call" | custom-call | flops 3221225472 | bytes 24641536 | tf_op jit(solution)/shard_map/attention_weights/pallas_call | solution.py:155
  346.2 3.6 feed_forward_sums_down.1
  350.3 2.4 collective-permute-start.52
  357.5 3.2 collective-permute-done.50
  360.8 12.6 %collective-permute-done.51.refs_2_ = bf16[896,512]{1,0:T(8,128)(2,1)S(1)} collective-permute-done((bf16[896,512]{1,0:T(8,128)(2,1)}, bf16[896,512]{1,0:T(8,128)(2,1)S(1)}, u32[]{:S(2)}, u32[]{:S(2)}) %collective-permute-start.51) | collective-permute-done | bytes 917536 | tf_op jit(solution)/shard_map/ppermute | solution.py:48
  375.8 2.9 collective-permute-start.57
  378.7 5.1 %collective-permute-start.56 = (bf16[896,512]{1,0:T(8,128)(2,1)}, bf16[896,512]{1,0:T(8,128)(2,1)}, u32[]{:S(2)}, u32[]{:S(2)}) collective-permute-start(bf16[896,512]{1,0:T(8,128)(2,1)} %get-tuple-element.515.refs_8_), channel_id=1, source_target_pairs={{8,4},{4,8},{24,20},{20,24},{9,5},{5,9},{25,21},{21,25},{10,6},{6,... | collective-permute-start | bytes 2752520 | tf_op jit(solution)/shard_map/ppermute | solution.py:82
  386.1 3.3 collective-permute-done.58
  389.6 7.4 %collective-permute-done.59 = f32[40,128]{1,0:T(8,128)S(1)} collective-permute-done((f32[40,128]{1,0:T(8,128)S(1)}, f32[40,128]{1,0:T(8,128)S(1)}, u32[]{:S(2)}, u32[]{:S(2)}) %collective-permute-start.59) | collective-permute-done | bytes 20512 | tf_op jit(solution)/shard_map/ppermute | solution.py:56
  398.2 4.9 %collective-permute-done.56.refs_4_ = bf16[896,512]{1,0:T(8,128)(2,1)} collective-permute-done((bf16[896,512]{1,0:T(8,128)(2,1)}, bf16[896,512]{1,0:T(8,128)(2,1)}, u32[]{:S(2)}, u32[]{:S(2)}) %collective-permute-start.56) | collective-permute-done | bytes 917536 | tf_op jit(solution)/shard_map/ppermute | solution.py:82
  404.8 4.5 %join_sums.1 = (bf16[128,512]{1,0:T(8,128)(2,1)}, bf16[128,512]{1,0:T(8,128)(2,1)}, bf16[128,512]{1,0:T(8,128)(2,1)}, bf16[128,512]{1,0:T(8,128)(2,1)}, bf16[512,256]{1,0:T(8,128)(2,1)}, /*index=5*/f32[512,256]{1,0:T(8,128)}) custom-call(s32[5]{0:T(128)} %stack.74.at, bf16[896,512]{1,0:T(8,128)(2,1)} %get-tuple-element.480.refs_0_, ...), custom_call_target="tpu_custom_call" | custom-call | bytes 9568256 | tf_op jit(solution)/shard_map/join_sums/pallas_call | solution.py:155
  416.7 3.5 collective-permute-done.63.refs_6_
  420.1 3.9 finish.1
  424.5 5.6 %collective-permute-start.67 = (bf16[176,256]{1,0:T(8,128)(2,1)S(1)}, bf16[176,256]{1,0:T(8,128)(2,1)S(1)}, u32[]{:S(2)}, u32[]{:S(2)}) collective-permute-start(bf16[176,256]{1,0:T(8,128)(2,1)S(1)} %get-tuple-element.535), channel_id=1, source_target_pairs={{4,0},{12,4},{0,8},{8,12},{20,16},{28,20},{16,24},{24,28},{5,1},{1... | collective-permute-start | bytes 270344 | tf_op jit(solution)/shard_map/ppermute | solution.py:82
  430.2 4.1 collective-permute-start.66
  435.4 2.1 collective-permute-done.66.refs_1_
  438.2 2.1 last.1
  (287 shorter events, 79.8 us)
Async XLA Ops:
  7.2 96.9 %all-gather.5.cloned.1.call-start = ((), (), s32[]{:S(2)}) async-start(), calls=%async_computation.4 | async-start | bytes 3538944 | tf_op jit(solution)/shard_map/all_gather | solution.py:109
  13.7 16.3 %collective-permute-start = (bf16[1552,256]{1,0:T(8,128)(2,1)}, bf16[1552,256]{1,0:T(8,128)(2,1)S(1)}, u32[]{:S(2)}, u32[]{:S(2)}) collective-permute-start(bf16[1552,256]{1,0:T(8,128)(2,1)} %get-tuple-element.273), channel_id=1, source_target_pairs={{4,8},{8,4},{5,9},{9,5},{6,10},{10,6},{7,11},{11,7},{20,24},{24,20... | collective-permute-start | bytes 2383880 | tf_op jit(solution)/shard_map/ppermute | solution.py:39
  22.4 12.3 %collective-permute-start.3 = (bf16[528,512]{1,0:T(8,128)(2,1)}, bf16[528,512]{1,0:T(8,128)(2,1)S(1)}, u32[]{:S(2)}, u32[]{:S(2)}) collective-permute-start(bf16[528,512]{1,0:T(8,128)(2,1)} %get-tuple-element.286.refs_4_), channel_id=1, source_target_pairs={{0,32},{32,64},{64,96},{96,0},{1,33},{33,65},{65,97},{97,1},{2,34}... | collective-permute-start | bytes 1622024 | tf_op jit(solution)/shard_map/ppermute | solution.py:48
  23.7 11.8 %collective-permute-start.2 = (bf16[528,512]{1,0:T(8,128)(2,1)}, bf16[528,512]{1,0:T(8,128)(2,1)S(1)}, u32[]{:S(2)}, u32[]{:S(2)}) collective-permute-start(bf16[528,512]{1,0:T(8,128)(2,1)} %get-tuple-element.286.refs_4_), channel_id=1, source_target_pairs={{0,96},{32,0},{64,32},{96,64},{1,97},{33,1},{65,33},{97,65},{2,98}... | collective-permute-start | bytes 1622024 | tf_op jit(solution)/shard_map/ppermute | solution.py:48
  28.5 14.6 %collective-permute-start.5 = (bf16[512,512]{1,0:T(8,128)(2,1)}, bf16[512,512]{1,0:T(8,128)(2,1)}, u32[]{:S(2)}, u32[]{:S(2)}) collective-permute-start(bf16[512,512]{1,0:T(8,128)(2,1)} %lay_out_x.1), channel_id=1, source_target_pairs={{0,20},{4,28},{8,16},{12,24},{16,4},{20,12},{24,0},{28,8},{1,21},{... | collective-permute-start | bytes 1572872 | tf_op jit(solution)/shard_map/ppermute | solution.py:78
  28.6 15.2 %collective-permute-start.4 = (bf16[512,512]{1,0:T(8,128)(2,1)}, bf16[512,512]{1,0:T(8,128)(2,1)}, u32[]{:S(2)}, u32[]{:S(2)}) collective-permute-start(bf16[512,512]{1,0:T(8,128)(2,1)} %lay_out_x.1), channel_id=1, source_target_pairs={{0,16},{4,24},{8,20},{12,28},{16,0},{20,8},{24,4},{28,12},{1,17},{... | collective-permute-start | bytes 1572872 | tf_op jit(solution)/shard_map/ppermute | solution.py:78
  44.7 81.3 %all-gather.7.cloned.1.call-start = ((), (), s32[]{:S(2)}) async-start(), calls=%async_computation.5 | async-start | bytes 3538944 | tf_op jit(solution)/shard_map/all_gather | solution.py:109
  44.8 14.6 %collective-permute-start.6 = (bf16[512,512]{1,0:T(8,128)(2,1)}, bf16[512,512]{1,0:T(8,128)(2,1)S(1)}, u32[]{:S(2)}, u32[]{:S(2)}) collective-permute-start(bf16[512,512]{1,0:T(8,128)(2,1)} %lay_out_x.1), channel_id=1, source_target_pairs={{4,8},{8,4},{20,24},{24,20},{5,9},{9,5},{21,25},{25,21},{6,10},{10... | collective-permute-start | bytes 1572872 | tf_op jit(solution)/shard_map/ppermute | solution.py:78
  47.4 15.3 %collective-permute-start.8 = (bf16[528,512]{1,0:T(8,128)(2,1)S(1)}, bf16[528,512]{1,0:T(8,128)(2,1)S(1)}, u32[]{:S(2)}, u32[]{:S(2)}) collective-permute-start(bf16[528,512]{1,0:T(8,128)(2,1)S(1)} %copy-done.3), channel_id=1, source_target_pairs={{0,64},{32,96},{64,0},{96,32},{1,65},{33,97},{65,1},{97,33},{2,66}... | collective-permute-start | bytes 1622024 | tf_op jit(solution)/shard_map/ppermute | solution.py:48
  50.4 12.3 %collective-permute-start.7 = (bf16[512,512]{1,0:T(8,128)(2,1)}, bf16[512,512]{1,0:T(8,128)(2,1)S(1)}, u32[]{:S(2)}, u32[]{:S(2)}) collective-permute-start(bf16[512,512]{1,0:T(8,128)(2,1)} %lay_out_x.1), channel_id=1, source_target_pairs={{0,4},{4,12},{8,0},{12,8},{16,20},{20,28},{24,16},{28,24},{1,5},{5... | collective-permute-start | bytes 1572872 | tf_op jit(solution)/shard_map/ppermute | solution.py:78
  67.3 97.9 %reduce-scatter.5.cloned.1.call-start = ((), (), s32[]{:S(2)}) async-start(), calls=%async_computation.6 | async-start | bytes 1966080 | tf_op jit(solution)/shard_map/reduce_scatter | solution.py:114
  67.4 16.8 %collective-permute-start.12 = (bf16[576,512]{1,0:T(8,128)(2,1)}, bf16[576,512]{1,0:T(8,128)(2,1)S(1)}, u32[]{:S(2)}, u32[]{:S(2)}) collective-permute-start(bf16[576,512]{1,0:T(8,128)(2,1)} %get-tuple-element.295), channel_id=1, source_target_pairs={{0,20},{4,28},{8,16},{12,24},{16,4},{20,12},{24,0},{28,8},{1,21},{... | collective-permute-start | bytes 1769480 | tf_op jit(solution)/shard_map/ppermute | solution.py:78
  67.5 16.8 %collective-permute-start.11 = (bf16[576,512]{1,0:T(8,128)(2,1)}, bf16[576,512]{1,0:T(8,128)(2,1)S(1)}, u32[]{:S(2)}, u32[]{:S(2)}) collective-permute-start(bf16[576,512]{1,0:T(8,128)(2,1)} %get-tuple-element.295), channel_id=1, source_target_pairs={{0,16},{4,24},{8,20},{12,28},{16,0},{20,8},{24,4},{28,12},{1,17},{... | collective-permute-start | bytes 1769480 | tf_op jit(solution)/shard_map/ppermute | solution.py:78
  69.5 14.6 %collective-permute-start.10 = (bf16[512,512]{1,0:T(8,128)(2,1)}, bf16[512,512]{1,0:T(8,128)(2,1)S(1)}, u32[]{:S(2)}, u32[]{:S(2)}) collective-permute-start(bf16[512,512]{1,0:T(8,128)(2,1)} %get-tuple-element.307.refs_5_.refs_11_), channel_id=1, source_target_pairs={{0,32},{32,64},{64,96},{96,0},{1,33},{33,65},{65,97},{97,1},{2,34}... | collective-permute-start | bytes 1572872 | tf_op jit(solution)/shard_map/ppermute | solution.py:48
  69.9 14.2 %collective-permute-start.9 = (bf16[512,512]{1,0:T(8,128)(2,1)}, bf16[512,512]{1,0:T(8,128)(2,1)S(1)}, u32[]{:S(2)}, u32[]{:S(2)}) collective-permute-start(bf16[512,512]{1,0:T(8,128)(2,1)} %get-tuple-element.307.refs_5_.refs_11_), channel_id=1, source_target_pairs={{0,96},{32,0},{64,32},{96,64},{1,97},{33,1},{65,33},{97,65},{2,98}... | collective-permute-start | bytes 1572872 | tf_op jit(solution)/shard_map/ppermute | solution.py:48
  84.2 18.9 %collective-permute-start.14 = (bf16[576,512]{1,0:T(8,128)(2,1)}, bf16[576,512]{1,0:T(8,128)(2,1)S(1)}, u32[]{:S(2)}, u32[]{:S(2)}) collective-permute-start(bf16[576,512]{1,0:T(8,128)(2,1)} %get-tuple-element.295), channel_id=1, source_target_pairs={{4,8},{8,4},{20,24},{24,20},{5,9},{9,5},{21,25},{25,21},{6,10},{10... | collective-permute-start | bytes 1769480 | tf_op jit(solution)/shard_map/ppermute | solution.py:78
  86.9 17.2 %collective-permute-start.15 = (bf16[576,512]{1,0:T(8,128)(2,1)}, bf16[576,512]{1,0:T(8,128)(2,1)S(1)}, u32[]{:S(2)}, u32[]{:S(2)}) collective-permute-start(bf16[576,512]{1,0:T(8,128)(2,1)} %get-tuple-element.295), channel_id=1, source_target_pairs={{0,4},{4,12},{8,0},{12,8},{16,20},{20,28},{24,16},{28,24},{1,5},{5... | collective-permute-start | bytes 1769480 | tf_op jit(solution)/shard_map/ppermute | solution.py:78
  87.0 17.1 %collective-permute-start.13 = (bf16[512,512]{1,0:T(8,128)(2,1)}, bf16[512,512]{1,0:T(8,128)(2,1)}, u32[]{:S(2)}, u32[]{:S(2)}) collective-permute-start(bf16[512,512]{1,0:T(8,128)(2,1)} %get-tuple-element.307.refs_5_.refs_11_), channel_id=1, source_target_pairs={{0,64},{32,96},{64,0},{96,32},{1,65},{33,97},{65,1},{97,33},{2,66}... | collective-permute-start | bytes 1572872 | tf_op jit(solution)/shard_map/ppermute | solution.py:48
  104.1 26.0 %collective-permute-start.17 = (bf16[512,1024]{1,0:T(8,128)(2,1)}, bf16[512,1024]{1,0:T(8,128)(2,1)S(1)}, u32[]{:S(2)}, u32[]{:S(2)}) collective-permute-start(bf16[512,1024]{1,0:T(8,128)(2,1)} %get-tuple-element.337.refs_3_), channel_id=1, source_target_pairs={{0,32},{32,64},{64,96},{96,0},{1,33},{33,65},{65,97},{97,1},{2,34}... | collective-permute-start | bytes 3145736 | tf_op jit(solution)/shard_map/ppermute | solution.py:48
  104.2 25.9 %collective-permute-start.16 = (bf16[512,1024]{1,0:T(8,128)(2,1)}, bf16[512,1024]{1,0:T(8,128)(2,1)S(1)}, u32[]{:S(2)}, u32[]{:S(2)}) collective-permute-start(bf16[512,1024]{1,0:T(8,128)(2,1)} %get-tuple-element.337.refs_3_), channel_id=1, source_target_pairs={{0,96},{32,0},{64,32},{96,64},{1,97},{33,1},{65,33},{97,65},{2,98}... | collective-permute-start | bytes 3145736 | tf_op jit(solution)/shard_map/ppermute | solution.py:48
  106.8 24.5 %collective-permute-start.19 = (bf16[512,1024]{1,0:T(8,128)(2,1)}, bf16[512,1024]{1,0:T(8,128)(2,1)}, u32[]{:S(2)}, u32[]{:S(2)}) collective-permute-start(bf16[512,1024]{1,0:T(8,128)(2,1)} %get-tuple-element.350.refs_20_), channel_id=1, source_target_pairs={{0,20},{4,28},{8,16},{12,24},{16,4},{20,12},{24,0},{28,8},{1,21},{... | collective-permute-start | bytes 3145736 | tf_op jit(solution)/shard_map/ppermute | solution.py:78
  109.0 24.2 %collective-permute-start.18 = (bf16[512,1024]{1,0:T(8,128)(2,1)}, bf16[512,1024]{1,0:T(8,128)(2,1)}, u32[]{:S(2)}, u32[]{:S(2)}) collective-permute-start(bf16[512,1024]{1,0:T(8,128)(2,1)} %get-tuple-element.350.refs_20_), channel_id=1, source_target_pairs={{0,16},{4,24},{8,20},{12,28},{16,0},{20,8},{24,4},{28,12},{1,17},{... | collective-permute-start | bytes 3145736 | tf_op jit(solution)/shard_map/ppermute | solution.py:78
  140.0 62.8 %all-gather.9.cloned.1.call-start = ((), (), s32[]{:S(2)}) async-start(), calls=%async_computation.7 | async-start | bytes 3538944 | tf_op jit(solution)/shard_map/all_gather | solution.py:109
  140.1 14.8 %collective-permute-start.22 = (bf16[256,1024]{1,0:T(8,128)(2,1)S(1)}, bf16[256,1024]{1,0:T(8,128)(2,1)S(1)}, u32[]{:S(2)}, u32[]{:S(2)}) collective-permute-start(bf16[256,1024]{1,0:T(8,128)(2,1)S(1)} %slice.91), channel_id=1, source_target_pairs={{0,32},{32,64},{64,96},{96,0},{1,33},{33,65},{65,97},{97,1},{2,34}... | collective-permute-start | bytes 1572872 | tf_op jit(solution)/shard_map/ppermute | solution.py:48
  140.1 30.7 %collective-permute-start.24 = (bf16[512,1024]{1,0:T(8,128)(2,1)}, bf16[512,1024]{1,0:T(8,128)(2,1)S(1)}, u32[]{:S(2)}, u32[]{:S(2)}) collective-permute-start(bf16[512,1024]{1,0:T(8,128)(2,1)} %get-tuple-element.350.refs_20_), channel_id=1, source_target_pairs={{0,4},{4,12},{8,0},{12,8},{16,20},{20,28},{24,16},{28,24},{1,5},{5... | collective-permute-start | bytes 3145736 | tf_op jit(solution)/shard_map/ppermute | solution.py:78
  140.4 30.5 %collective-permute-start.23 = (bf16[512,1024]{1,0:T(8,128)(2,1)}, bf16[512,1024]{1,0:T(8,128)(2,1)}, u32[]{:S(2)}, u32[]{:S(2)}) collective-permute-start(bf16[512,1024]{1,0:T(8,128)(2,1)} %get-tuple-element.350.refs_20_), channel_id=1, source_target_pairs={{4,8},{8,4},{20,24},{24,20},{5,9},{9,5},{21,25},{25,21},{6,10},{10... | collective-permute-start | bytes 3145736 | tf_op jit(solution)/shard_map/ppermute | solution.py:78
  145.6 20.7 %collective-permute-start.21 = (bf16[256,1024]{1,0:T(8,128)(2,1)S(1)}, bf16[256,1024]{1,0:T(8,128)(2,1)}, u32[]{:S(2)}, u32[]{:S(2)}) collective-permute-start(bf16[256,1024]{1,0:T(8,128)(2,1)S(1)} %slice.90), channel_id=1, source_target_pairs={{0,96},{32,0},{64,32},{96,64},{1,97},{33,1},{65,33},{97,65},{2,98}... | collective-permute-start | bytes 1572872 | tf_op jit(solution)/shard_map/ppermute | solution.py:48
  148.4 17.9 %collective-permute-start.26 = (bf16[512,512]{1,0:T(8,128)(2,1)}, bf16[512,512]{1,0:T(8,128)(2,1)}, u32[]{:S(2)}, u32[]{:S(2)}) collective-permute-start(bf16[512,512]{1,0:T(8,128)(2,1)} %get-tuple-element.342.refs_8_.refs_0_), channel_id=1, source_target_pairs={{0,32},{32,64},{64,96},{96,0},{1,33},{33,65},{65,97},{97,1},{2,34}... | collective-permute-start | bytes 1572872 | tf_op jit(solution)/shard_map/ppermute | solution.py:48
  155.6 15.3 %collective-permute-start.25 = (bf16[512,512]{1,0:T(8,128)(2,1)}, bf16[512,512]{1,0:T(8,128)(2,1)}, u32[]{:S(2)}, u32[]{:S(2)}) collective-permute-start(bf16[512,512]{1,0:T(8,128)(2,1)} %get-tuple-element.342.refs_8_.refs_0_), channel_id=1, source_target_pairs={{0,96},{32,0},{64,32},{96,64},{1,97},{33,1},{65,33},{97,65},{2,98}... | collective-permute-start | bytes 1572872 | tf_op jit(solution)/shard_map/ppermute | solution.py:48
  172.9 97.6 %reduce-scatter.7.cloned.1.call-start = ((), (), s32[]{:S(2)}) async-start(), calls=%async_computation.8 | async-start | bytes 1966080 | tf_op jit(solution)/shard_map/reduce_scatter | solution.py:837
  172.9 14.3 %collective-permute-start.27 = (bf16[512,512]{1,0:T(8,128)(2,1)}, bf16[512,512]{1,0:T(8,128)(2,1)S(1)}, u32[]{:S(2)}, u32[]{:S(2)}) collective-permute-start(bf16[512,512]{1,0:T(8,128)(2,1)} %get-tuple-element.342.refs_8_.refs_0_), channel_id=1, source_target_pairs={{0,64},{32,96},{64,0},{96,32},{1,65},{33,97},{65,1},{97,33},{2,66}... | collective-permute-start | bytes 1572872 | tf_op jit(solution)/shard_map/ppermute | solution.py:48
  175.2 14.0 %collective-permute-start.31 = (bf16[512,512]{1,0:T(8,128)(2,1)}, bf16[512,512]{1,0:T(8,128)(2,1)S(1)}, u32[]{:S(2)}, u32[]{:S(2)}) collective-permute-start(bf16[512,512]{1,0:T(8,128)(2,1)} %get-tuple-element.349.refs_21_.refs_8_), channel_id=1, source_target_pairs={{0,20},{4,28},{8,16},{12,24},{16,4},{20,12},{24,0},{28,8},{1,21},{... | collective-permute-start | bytes 1572872 | tf_op jit(solution)/shard_map/ppermute | solution.py:78
  177.6 23.8 %collective-permute-start.30 = (bf16[512,512]{1,0:T(8,128)(2,1)}, bf16[512,512]{1,0:T(8,128)(2,1)S(1)}, u32[]{:S(2)}, u32[]{:S(2)}) collective-permute-start(bf16[512,512]{1,0:T(8,128)(2,1)} %get-tuple-element.349.refs_21_.refs_8_), channel_id=1, source_target_pairs={{0,16},{4,24},{8,20},{12,28},{16,0},{20,8},{24,4},{28,12},{1,17},{... | collective-permute-start | bytes 1572872 | tf_op jit(solution)/shard_map/ppermute | solution.py:78
  177.6 23.8 %collective-permute-start.29 = (bf16[512,512]{1,0:T(8,128)(2,1)}, bf16[512,512]{1,0:T(8,128)(2,1)}, u32[]{:S(2)}, u32[]{:S(2)}) collective-permute-start(bf16[512,512]{1,0:T(8,128)(2,1)} %get-tuple-element.349.refs_21_.refs_8_), channel_id=1, source_target_pairs={{0,4},{4,12},{8,0},{12,8},{16,20},{20,28},{24,16},{28,24},{1,5},{5... | collective-permute-start | bytes 1572872 | tf_op jit(solution)/shard_map/ppermute | solution.py:78
  178.1 23.4 %collective-permute-start.28 = (bf16[512,512]{1,0:T(8,128)(2,1)}, bf16[512,512]{1,0:T(8,128)(2,1)}, u32[]{:S(2)}, u32[]{:S(2)}) collective-permute-start(bf16[512,512]{1,0:T(8,128)(2,1)} %get-tuple-element.349.refs_21_.refs_8_), channel_id=1, source_target_pairs={{4,8},{8,4},{20,24},{24,20},{5,9},{9,5},{21,25},{25,21},{6,10},{10... | collective-permute-start | bytes 1572872 | tf_op jit(solution)/shard_map/ppermute | solution.py:78
  240.6 65.2 %all-gather.11.cloned.1.call-start = ((), (), s32[]{:S(2)}) async-start(), calls=%async_computation.9 | async-start | bytes 3538944 | tf_op jit(solution)/shard_map/all_gather | solution.py:109
  242.2 29.3 %collective-permute-start.33 = (bf16[512,1024]{1,0:T(8,128)(2,1)}, bf16[512,1024]{1,0:T(8,128)(2,1)S(1)}, u32[]{:S(2)}, u32[]{:S(2)}) collective-permute-start(bf16[512,1024]{1,0:T(8,128)(2,1)} %get-tuple-element.364), channel_id=1, source_target_pairs={{16,0},{24,4},{20,8},{28,12},{0,16},{8,20},{4,24},{12,28},{17,1},{... | collective-permute-start | bytes 3145736 | tf_op jit(solution)/shard_map/ppermute | solution.py:82
  244.8 26.8 %collective-permute-start.34 = (bf16[512,1024]{1,0:T(8,128)(2,1)}, bf16[512,1024]{1,0:T(8,128)(2,1)}, u32[]{:S(2)}, u32[]{:S(2)}) collective-permute-start(bf16[512,1024]{1,0:T(8,128)(2,1)} %get-tuple-element.365), channel_id=1, source_target_pairs={{20,0},{28,4},{16,8},{24,12},{4,16},{12,20},{0,24},{8,28},{21,1},{... | collective-permute-start | bytes 3145736 | tf_op jit(solution)/shard_map/ppermute | solution.py:82
  245.3 26.4 %collective-permute-start.35 = (bf16[512,1024]{1,0:T(8,128)(2,1)}, bf16[512,1024]{1,0:T(8,128)(2,1)}, u32[]{:S(2)}, u32[]{:S(2)}) collective-permute-start(bf16[512,1024]{1,0:T(8,128)(2,1)} %get-tuple-element.366), channel_id=1, source_target_pairs={{0,32},{32,64},{64,96},{96,0},{1,33},{33,65},{65,97},{97,1},{2,34}... | collective-permute-start | bytes 3145736 | tf_op jit(solution)/shard_map/ppermute | solution.py:48
  246.9 25.3 %collective-permute-start.36 = (bf16[512,1024]{1,0:T(8,128)(2,1)}, bf16[512,1024]{1,0:T(8,128)(2,1)}, u32[]{:S(2)}, u32[]{:S(2)}) collective-permute-start(bf16[512,1024]{1,0:T(8,128)(2,1)} %get-tuple-element.367), channel_id=1, source_target_pairs={{0,96},{32,0},{64,32},{96,64},{1,97},{33,1},{65,33},{97,65},{2,98}... | collective-permute-start | bytes 3145736 | tf_op jit(solution)/shard_map/ppermute | solution.py:48
  275.4 121.8 %reduce-scatter.9.cloned.1.call-start = ((), (), s32[]{:S(2)}) async-start(), calls=%async_computation.10 | async-start | bytes 1966080 | tf_op jit(solution)/shard_map/reduce_scatter | solution.py:936
  276.3 26.4 %collective-permute-start.38 = (bf16[512,1024]{1,0:T(8,128)(2,1)}, bf16[512,1024]{1,0:T(8,128)(2,1)S(1)}, u32[]{:S(2)}, u32[]{:S(2)}) collective-permute-start(bf16[512,1024]{1,0:T(8,128)(2,1)} %get-tuple-element.383), channel_id=1, source_target_pairs={{0,64},{32,96},{64,0},{96,32},{1,65},{33,97},{65,1},{97,33},{2,66}... | collective-permute-start | bytes 3145736 | tf_op jit(solution)/shard_map/ppermute | solution.py:48
  278.3 24.4 %collective-permute-start.40 = (bf16[512,1024]{1,0:T(8,128)(2,1)}, bf16[512,1024]{1,0:T(8,128)(2,1)}, u32[]{:S(2)}, u32[]{:S(2)}) collective-permute-start(bf16[512,1024]{1,0:T(8,128)(2,1)} %get-tuple-element.387), channel_id=1, source_target_pairs={{4,0},{12,4},{0,8},{8,12},{20,16},{28,20},{16,24},{24,28},{5,1},{1... | collective-permute-start | bytes 3145736 | tf_op jit(solution)/shard_map/ppermute | solution.py:82
  279.4 26.4 %collective-permute-start.39 = (bf16[512,1024]{1,0:T(8,128)(2,1)}, bf16[512,1024]{1,0:T(8,128)(2,1)}, u32[]{:S(2)}, u32[]{:S(2)}) collective-permute-start(bf16[512,1024]{1,0:T(8,128)(2,1)} %get-tuple-element.386.refs_8_), channel_id=1, source_target_pairs={{8,4},{4,8},{24,20},{20,24},{9,5},{5,9},{25,21},{21,25},{10,6},{6,... | collective-permute-start | bytes 3145736 | tf_op jit(solution)/shard_map/ppermute | solution.py:82
  305.8 17.8 %collective-permute-start.41 = (bf16[512,512]{1,0:T(8,128)(2,1)}, bf16[512,512]{1,0:T(8,128)(2,1)S(1)}, u32[]{:S(2)}, u32[]{:S(2)}) collective-permute-start(bf16[512,512]{1,0:T(8,128)(2,1)} %get-tuple-element.410), channel_id=1, source_target_pairs={{0,32},{32,64},{64,96},{96,0},{1,33},{33,65},{65,97},{97,1},{2,34}... | collective-permute-start | bytes 1572872 | tf_op jit(solution)/shard_map/ppermute | solution.py:48
  306.6 17.0 %collective-permute-start.42 = (bf16[512,512]{1,0:T(8,128)(2,1)}, bf16[512,512]{1,0:T(8,128)(2,1)S(1)}, u32[]{:S(2)}, u32[]{:S(2)}) collective-permute-start(bf16[512,512]{1,0:T(8,128)(2,1)} %get-tuple-element.411), channel_id=1, source_target_pairs={{0,96},{32,0},{64,32},{96,64},{1,97},{33,1},{65,33},{97,65},{2,98}... | collective-permute-start | bytes 1572872 | tf_op jit(solution)/shard_map/ppermute | solution.py:48
  308.5 15.2 %collective-permute-start.43 = (bf16[512,512]{1,0:T(8,128)(2,1)}, bf16[512,512]{1,0:T(8,128)(2,1)S(1)}, u32[]{:S(2)}, u32[]{:S(2)}) collective-permute-start(bf16[512,512]{1,0:T(8,128)(2,1)} %get-tuple-element.412), channel_id=1, source_target_pairs={{16,0},{24,4},{20,8},{28,12},{0,16},{8,20},{4,24},{12,28},{17,1},{... | collective-permute-start | bytes 1572872 | tf_op jit(solution)/shard_map/ppermute | solution.py:82
  309.3 14.3 %collective-permute-start.44 = (bf16[512,512]{1,0:T(8,128)(2,1)}, bf16[512,512]{1,0:T(8,128)(2,1)S(1)}, u32[]{:S(2)}, u32[]{:S(2)}) collective-permute-start(bf16[512,512]{1,0:T(8,128)(2,1)} %get-tuple-element.413), channel_id=1, source_target_pairs={{20,0},{28,4},{16,8},{24,12},{4,16},{12,20},{0,24},{8,28},{21,1},{... | collective-permute-start | bytes 1572872 | tf_op jit(solution)/shard_map/ppermute | solution.py:82
  324.7 17.7 %collective-permute-start.45 = (bf16[3072,256]{1,0:T(8,128)(2,1)}, bf16[3072,256]{1,0:T(8,128)(2,1)S(1)}, u32[]{:S(2)}, u32[]{:S(2)}) collective-permute-start(bf16[3072,256]{1,0:T(8,128)(2,1)} %get-tuple-element.415), channel_id=1, source_target_pairs={{0,8},{8,0},{1,9},{9,1},{2,10},{10,2},{3,11},{11,3},{4,12},{12,4},... | collective-permute-start | bytes 4718600 | tf_op jit(solution)/shard_map/ppermute | solution.py:44
  325.7 16.6 %collective-permute-start.46 = (bf16[512,512]{1,0:T(8,128)(2,1)S(1)}, bf16[512,512]{1,0:T(8,128)(2,1)S(1)}, u32[]{:S(2)}, u32[]{:S(2)}) collective-permute-start(bf16[512,512]{1,0:T(8,128)(2,1)S(1)} %copy-done.49), channel_id=1, source_target_pairs={{0,64},{32,96},{64,0},{96,32},{1,65},{33,97},{65,1},{97,33},{2,66}... | collective-permute-start | bytes 1572872 | tf_op jit(solution)/shard_map/ppermute | solution.py:48
  326.3 16.0 %collective-permute-start.48 = (bf16[512,512]{1,0:T(8,128)(2,1)S(1)}, bf16[512,512]{1,0:T(8,128)(2,1)S(1)}, u32[]{:S(2)}, u32[]{:S(2)}) collective-permute-start(bf16[512,512]{1,0:T(8,128)(2,1)S(1)} %copy-done.48), channel_id=1, source_target_pairs={{4,0},{12,4},{0,8},{8,12},{20,16},{28,20},{16,24},{24,28},{5,1},{1... | collective-permute-start | bytes 1572872 | tf_op jit(solution)/shard_map/ppermute | solution.py:82
  328.1 14.3 %collective-permute-start.47 = (bf16[512,512]{1,0:T(8,128)(2,1)S(1)}, bf16[512,512]{1,0:T(8,128)(2,1)S(1)}, u32[]{:S(2)}, u32[]{:S(2)}) collective-permute-start(bf16[512,512]{1,0:T(8,128)(2,1)S(1)} %copy-done.19), channel_id=1, source_target_pairs={{8,4},{4,8},{24,20},{20,24},{9,5},{5,9},{25,21},{21,25},{10,6},{6,... | collective-permute-start | bytes 1572872 | tf_op jit(solution)/shard_map/ppermute | solution.py:82
  345.0 58.5 %reduce-scatter.11.cloned.1.call-start = ((), (), s32[]{:S(2)}) async-start(), calls=%async_computation.11 | async-start | bytes 1966080 | tf_op jit(solution)/shard_map/reduce_scatter | solution.py:968
  349.9 23.5 %collective-permute-start.51 = (bf16[896,512]{1,0:T(8,128)(2,1)}, bf16[896,512]{1,0:T(8,128)(2,1)S(1)}, u32[]{:S(2)}, u32[]{:S(2)}) collective-permute-start(bf16[896,512]{1,0:T(8,128)(2,1)} %get-tuple-element.468), channel_id=1, source_target_pairs={{0,32},{32,64},{64,96},{96,0},{1,33},{33,65},{65,97},{97,1},{2,34}... | collective-permute-start | bytes 2752520 | tf_op jit(solution)/shard_map/ppermute | solution.py:48
  350.3 23.1 %collective-permute-start.52 = (bf16[896,512]{1,0:T(8,128)(2,1)}, bf16[896,512]{1,0:T(8,128)(2,1)S(1)}, u32[]{:S(2)}, u32[]{:S(2)}) collective-permute-start(bf16[896,512]{1,0:T(8,128)(2,1)} %get-tuple-element.469), channel_id=1, source_target_pairs={{0,96},{32,0},{64,32},{96,64},{1,97},{33,1},{65,33},{97,65},{2,98}... | collective-permute-start | bytes 2752520 | tf_op jit(solution)/shard_map/ppermute | solution.py:48
  352.6 20.7 %collective-permute-start.53 = (bf16[896,512]{1,0:T(8,128)(2,1)}, bf16[896,512]{1,0:T(8,128)(2,1)}, u32[]{:S(2)}, u32[]{:S(2)}) collective-permute-start(bf16[896,512]{1,0:T(8,128)(2,1)} %get-tuple-element.470), channel_id=1, source_target_pairs={{16,0},{24,4},{20,8},{28,12},{0,16},{8,20},{4,24},{12,28},{17,1},{... | collective-permute-start | bytes 2752520 | tf_op jit(solution)/shard_map/ppermute | solution.py:82
  354.7 20.8 %collective-permute-start.54 = (bf16[896,512]{1,0:T(8,128)(2,1)}, bf16[896,512]{1,0:T(8,128)(2,1)}, u32[]{:S(2)}, u32[]{:S(2)}) collective-permute-start(bf16[896,512]{1,0:T(8,128)(2,1)} %get-tuple-element.471), channel_id=1, source_target_pairs={{20,0},{28,4},{16,8},{24,12},{4,16},{12,20},{0,24},{8,28},{21,1},{... | collective-permute-start | bytes 2752520 | tf_op jit(solution)/shard_map/ppermute | solution.py:82
  375.4 22.8 %collective-permute-start.55 = (bf16[896,512]{1,0:T(8,128)(2,1)}, bf16[896,512]{1,0:T(8,128)(2,1)}, u32[]{:S(2)}, u32[]{:S(2)}) collective-permute-start(bf16[896,512]{1,0:T(8,128)(2,1)} %get-tuple-element.472), channel_id=1, source_target_pairs={{0,64},{32,96},{64,0},{96,32},{1,65},{33,97},{65,1},{97,33},{2,66}... | collective-permute-start | bytes 2752520 | tf_op jit(solution)/shard_map/ppermute | solution.py:48
  375.8 22.4 %collective-permute-start.57 = (bf16[896,512]{1,0:T(8,128)(2,1)}, bf16[896,512]{1,0:T(8,128)(2,1)}, u32[]{:S(2)}, u32[]{:S(2)}) collective-permute-start(bf16[896,512]{1,0:T(8,128)(2,1)} %get-tuple-element.476), channel_id=1, source_target_pairs={{4,0},{12,4},{0,8},{8,12},{20,16},{28,20},{16,24},{24,28},{5,1},{1... | collective-permute-start | bytes 2752520 | tf_op jit(solution)/shard_map/ppermute | solution.py:82
  378.7 24.4 %collective-permute-start.56 = (bf16[896,512]{1,0:T(8,128)(2,1)}, bf16[896,512]{1,0:T(8,128)(2,1)}, u32[]{:S(2)}, u32[]{:S(2)}) collective-permute-start(bf16[896,512]{1,0:T(8,128)(2,1)} %get-tuple-element.515.refs_8_), channel_id=1, source_target_pairs={{8,4},{4,8},{24,20},{20,24},{9,5},{5,9},{25,21},{21,25},{10,6},{6,... | collective-permute-start | bytes 2752520 | tf_op jit(solution)/shard_map/ppermute | solution.py:82
  409.3 14.9 %collective-permute-start.61 = (bf16[1536,256]{1,0:T(8,128)(2,1)S(1)}, bf16[1536,256]{1,0:T(8,128)(2,1)S(1)}, u32[]{:S(2)}, u32[]{:S(2)}) collective-permute-start(bf16[1536,256]{1,0:T(8,128)(2,1)S(1)} %pad_maximum_fusion), channel_id=1, source_target_pairs={{4,8},{8,4},{5,9},{9,5},{6,10},{10,6},{7,11},{11,7},{20,24},{24,20... | collective-permute-start | bytes 2359304 | tf_op jit(solution)/shard_map/ppermute | solution.py:39
  411.3 12.8 %collective-permute-start.60 = (bf16[512,256]{1,0:T(8,128)(2,1)}, bf16[512,256]{1,0:T(8,128)(2,1)S(1)}, u32[]{:S(2)}, u32[]{:S(2)}) collective-permute-start(bf16[512,256]{1,0:T(8,128)(2,1)} %get-tuple-element.489), channel_id=1, source_target_pairs={{0,1},{1,0},{2,3},{3,2},{4,5},{5,4},{6,7},{7,6},{8,9},{9,8},{10,11... | collective-permute-start | bytes 786440 | tf_op jit(solution)/shard_map/ppermute | solution.py:60
  424.4 10.9 %collective-permute-start.69 = (bf16[176,256]{1,0:T(8,128)(2,1)S(1)}, bf16[176,256]{1,0:T(8,128)(2,1)S(1)}, u32[]{:S(2)}, u32[]{:S(2)}) collective-permute-start(bf16[176,256]{1,0:T(8,128)(2,1)S(1)} %get-tuple-element.533), channel_id=1, source_target_pairs={{20,0},{28,4},{16,8},{24,12},{4,16},{12,20},{0,24},{8,28},{21,1},{... | collective-permute-start | bytes 270344 | tf_op jit(solution)/shard_map/ppermute | solution.py:82
  424.5 10.9 %collective-permute-start.67 = (bf16[176,256]{1,0:T(8,128)(2,1)S(1)}, bf16[176,256]{1,0:T(8,128)(2,1)S(1)}, u32[]{:S(2)}, u32[]{:S(2)}) collective-permute-start(bf16[176,256]{1,0:T(8,128)(2,1)S(1)} %get-tuple-element.535), channel_id=1, source_target_pairs={{4,0},{12,4},{0,8},{8,12},{20,16},{28,20},{16,24},{24,28},{5,1},{1... | collective-permute-start | bytes 270344 | tf_op jit(solution)/shard_map/ppermute | solution.py:82
  (69 other events, 739.6 us)
Sparse Core Ops, SparseCore 0:
  44.9 28.6 all-gather.4
  75.8 27.8 all-gather.6
  140.1 25.0 reduce-scatter.4
  173.0 29.7 all-gather.8
  240.8 25.4 reduce-scatter.6
  275.5 27.7 all-gather.10
  345.1 23.8 reduce-scatter.8
  371.4 26.4 reduce-scatter.10
